TPU v7x, 32 devices: a whole 2x2x4 slice. The times are simulated.
32 devices in a mesh: grp: 2 (over y), ep: 16 (over z, x, core).
Axes of the slice: x: 2, y: 2, z: 4, core: 2. Of those that a mesh axis runs over, the one named last changes fastest.
Arguments:
- hidden_in: bfloat16 [1024, 2048], P('ep'), may hold values from -45 to 45
- query_nope: bfloat16 [1024, 2048], P('ep', 'grp'), may hold values from -6 to 6
- query_rope: bfloat16 [1024, 1024], P('ep', 'grp'), may hold values from -56 to 56
- new_latent: bfloat16 [256, 2304], P('ep'), may hold values from -6 to 6
- latent_cache: bfloat16 [1024, 9216], P('ep'), may hold values from -6 to 6
- key_absorb: bfloat16 [16, 128, 512], P('grp'), may hold values from -0.5 to 0.5
- value_absorb: bfloat16 [16, 512, 128], P('grp'), may hold values from -1 to 1
- output_proj: bfloat16 [2048, 2048], P('grp'), may hold values from -0.125 to 0.125
- norm_gain: bfloat16 [2048], replicated, may hold values from 0.099609375 to 1.8984375
- router_proj: bfloat16 [2048, 16], replicated, may hold values from -0.125 to 0.125
- expert_ids: int32 [1024, 6], P('ep'), may hold values from 0 to 15, all different within a row; in each aligned block of 64 rows (0 to 63, 64 to 127, ...) at most 32 rows name the same one
- expert_gate: bfloat16 [16, 2048, 1408], P('ep', None, 'grp'), may hold values from -0.125 to 0.125
- expert_up: bfloat16 [16, 2048, 1408], P('ep', None, 'grp'), may hold values from -0.125 to 0.125
- expert_down: bfloat16 [16, 1408, 2048], P('ep', 'grp'), may hold values from -0.15625 to 0.15625
- block_table: int32 [256, 64], P('ep'), may hold values from 0 to 95, as said below
- lengths: int32 [256], P('ep'), may hold values from 1 to 1024
- subtree_moves: int32 [16, 16, 2], P('ep'), may hold values from -1 to 63, as said below
Outputs:
- mixed: bfloat16 [1024, 2048], P('ep', 'grp')
Inputs may be any that keep to these rules, and one draw needn't show every extreme that they name: `expert_ids`: within the rows of one ep index no expert is named by more than 32 entries, a bound that some block reaches. `subtree_moves`: never the source itself; a live entry is a block id of the source; for every destination the rank after it sends 2 live blocks. `block_table`: an address names a resident block or a live moved block of that request's rank; the addresses of one request are distinct; the requests of a rank share a leading run of moved blocks.
All inputs are finite; a program needn't handle non-finite values.
Results may differ from a plain program's by a relative error of at most 0.0074.
Values may be sent and summed in bfloat16 or wider, within the bound.
No kernel may reach another device: no remote copies, remote signals or barrier semaphores. Data moves between devices by JAX's collectives and lax.ppermute only.
A program may use at most 64 MiB of HBM per device.

v0:
```python
import jax
import jax.numpy as jnp
from jax import lax
from jax.sharding import PartitionSpec as P


def local(
    hidden_in,
    query_nope,
    query_rope,
    new_latent,
    latent_cache,
    key_absorb,
    value_absorb,
    output_proj,
    norm_gain,
    router_proj,
    expert_ids,
    expert_gate,
    expert_up,
    expert_down,
    block_table,
    lengths,
    subtree_moves,
):
    head_count = key_absorb.shape[0]
    nope_dim = key_absorb.shape[1]
    latent_dim = key_absorb.shape[2]
    rope_dim = query_rope.shape[1] // head_count
    key_width = latent_dim + rope_dim
    requests, table_len = block_table.shape
    step_count = new_latent.shape[1] // key_width
    row_count = hidden_in.shape[0]
    model_dim = hidden_in.shape[1]
    block_size = latent_cache.shape[1] // key_width
    cached = table_len * block_size
    scale_of_scores = (nope_dim + rope_dim) ** (-0.5)
    local_blocks = latent_cache.shape[0]
    group_size = lax.axis_size("grp")
    group_index = lax.axis_index("grp")
    sent_ids = subtree_moves[0]
    picked_blocks = latent_cache[jnp.clip(sent_ids, 0, local_blocks - 1)]
    outgoing = jnp.where((sent_ids >= 0)[:, :, None], picked_blocks, jnp.zeros_like(picked_blocks))
    arrived = lax.all_to_all(outgoing, "ep", split_axis=0, concat_axis=0, tiled=True)
    block_pool = jnp.concatenate([latent_cache, arrived.reshape(-1, latent_cache.shape[1])], axis=0)
    q_latent = jnp.einsum(
        "rhc,hcl->rhl",
        query_nope.reshape(row_count, head_count, nope_dim),
        key_absorb,
        preferred_element_type=jnp.float32,
    ).astype(jnp.bfloat16)
    queries = jnp.concatenate(
        [q_latent, query_rope.reshape(row_count, head_count, rope_dim)], axis=2
    ).reshape(requests, step_count * head_count, key_width)
    fresh_keys = new_latent.reshape(requests, step_count, key_width)
    per_step = 2
    key_pos = jnp.arange(cached + step_count, dtype=jnp.int32)
    row_step = jnp.arange(step_count * head_count, dtype=jnp.int32) // head_count

    def attend(request_group):
        start_row = request_group * per_step
        table_rows = lax.dynamic_slice_in_dim(block_table, start_row, per_step, 0)
        key_rows = block_pool[table_rows].reshape(per_step, cached, key_width)
        key_rows = jnp.concatenate(
            [key_rows, lax.dynamic_slice_in_dim(fresh_keys, start_row, per_step, 0)], axis=1
        )
        query_rows = lax.dynamic_slice_in_dim(queries, start_row, per_step, 0)
        limits = lax.dynamic_slice_in_dim(lengths, start_row, per_step, 0)
        score_values = (
            jnp.einsum("gqw,gkw->gqk", query_rows, key_rows, preferred_element_type=jnp.float32)
            * scale_of_scores
        )
        visible = jnp.where(
            key_pos[None, None, :] < cached,
            key_pos[None, None, :] < limits[:, None, None],
            key_pos[None, None, :] - cached <= row_step[None, :, None],
        )
        score_values = jnp.where(visible, score_values, -1e30)
        row_peak = jnp.max(score_values, axis=2, keepdims=True)
        exp_scores = jnp.exp(score_values - row_peak)
        attention = (exp_scores / jnp.sum(exp_scores, axis=2, keepdims=True)).astype(jnp.bfloat16)
        return jnp.einsum(
            "gqk,gkl->gql",
            attention,
            key_rows[:, :, :latent_dim],
            preferred_element_type=jnp.float32,
        ).astype(jnp.bfloat16)

    latent_out = lax.map(attend, jnp.arange(requests // per_step, dtype=jnp.int32)).reshape(
        row_count, head_count, latent_dim
    )
    head_out = (
        jnp.einsum("rhl,hlv->rhv", latent_out, value_absorb, preferred_element_type=jnp.float32)
        .astype(jnp.bfloat16)
        .reshape(row_count, -1)
    )
    partial_value = jnp.dot(head_out, output_proj, preferred_element_type=jnp.float32)
    attention_out = lax.psum(partial_value, "grp")
    residual_state = hidden_in.astype(jnp.float32) + attention_out
    normed = (
        residual_state
        * lax.rsqrt(jnp.mean(residual_state * residual_state, axis=1, keepdims=True) + 1e-06)
        * norm_gain.astype(jnp.float32)
    ).astype(jnp.bfloat16)
    logits = jnp.dot(normed, router_proj, preferred_element_type=jnp.float32)
    chosen = jax.nn.sigmoid(jnp.take_along_axis(logits, expert_ids, axis=1))
    gate_weights = chosen / jnp.sum(chosen, axis=1, keepdims=True)
    experts = router_proj.shape[1]
    top_count = expert_ids.shape[1]
    per_device = expert_gate.shape[0]
    capacity = max(2, (4 * row_count * top_count + 3 * experts - 1) // (3 * experts))
    flat_ids = expert_ids.reshape(-1)
    onehot = (flat_ids[:, None] == jnp.arange(experts, dtype=jnp.int32)[None, :]).astype(jnp.int32)
    slot_index = jnp.sum((jnp.cumsum(onehot, axis=0) - 1) * onehot, axis=1)
    target = (flat_ids * capacity + slot_index).reshape(row_count, top_count)
    selector = jnp.any(
        target[None, :, :] == jnp.arange(experts * capacity, dtype=jnp.int32)[:, None, None], axis=2
    ).astype(jnp.bfloat16)
    buffer = (
        jnp.dot(selector, normed, preferred_element_type=jnp.float32)
        .astype(jnp.bfloat16)
        .reshape(experts // per_device, per_device, capacity, model_dim)
    )
    width_out = model_dim // group_size
    column_index = group_index * width_out
    expert_rows = lax.all_to_all(buffer, "ep", split_axis=0, concat_axis=0, tiled=True)
    gate_proj = jnp.einsum(
        "sekd,edf->sekf", expert_rows, expert_gate, preferred_element_type=jnp.float32
    )
    up_proj = jnp.einsum(
        "sekd,edf->sekf", expert_rows, expert_up, preferred_element_type=jnp.float32
    )
    activated = (jax.nn.silu(gate_proj) * up_proj).astype(jnp.bfloat16)
    results = jnp.einsum(
        "sekf,efd->sekd", activated, expert_down, preferred_element_type=jnp.float32
    )
    returned = lax.all_to_all(
        results.astype(jnp.bfloat16), "ep", split_axis=0, concat_axis=0, tiled=True
    ).astype(results.dtype)
    gathered = returned.reshape(experts * capacity, -1)[target]
    expert_mix = lax.psum_scatter(
        jnp.sum(gate_weights[:, :, None] * gathered, axis=1).astype(jnp.bfloat16),
        "grp",
        scatter_dimension=1,
        tiled=True,
    ).astype(jnp.float32)
    state_part = lax.dynamic_slice_in_dim(residual_state, column_index, width_out, 1)
    return (state_part + expert_mix).astype(jnp.bfloat16)


def solution(mesh):
    in_specs = (
        P("ep", None),
        P("ep", "grp"),
        P("ep", "grp"),
        P("ep", None),
        P("ep", None),
        P("grp", None, None),
        P("grp", None, None),
        P("grp", None),
        P(),
        P(),
        P("ep", None),
        P("ep", None, "grp"),
        P("ep", None, "grp"),
        P("ep", "grp", None),
        P("ep", None),
        P("ep"),
        P("ep", None, None),
    )
    out_specs = P("ep", "grp")
    return jax.shard_map(local, mesh=mesh, in_specs=in_specs, out_specs=out_specs, check_vma=False)
```

profile of v0, /device:TPU:0, one launch (start us, length us, event | category | flops | bytes accessed | tf_op | source)
XLA Modules:
  0.0 405.0 jit_solution(10236648225157645328)
XLA Ops:
  14.8 7.4 %all-to-all-start = ((bf16[16,2,9216]{2,1,0:T(2,128)(2,1)}), bf16[16,2,9216]{2,1,0:T(2,128)(2,1)}, u32[]{:S(2)}, u32[]{:S(2)}) async-start(bf16[16,2,9216]{2,1,0:T(2,128)(2,1)} %broadcast_select_fusion), calls=%async_computation | async-start | bytes 1179648 | tf_op jit(solution)/shard_map/all_to_all | solution.py:44
  30.1 7.7 %all-to-all-done = bf16[16,2,9216]{2,1,0:T(2,128)(2,1)} async-done(((bf16[16,2,9216]{2,1,0:T(2,128)(2,1)}), bf16[16,2,9216]{2,1,0:T(2,128)(2,1)}, u32[]{:S(2)}, u32[]{:S(2)}) %all-to-all-start) | async-done | bytes 589856 | tf_op jit(solution)/shard_map/all_to_all | solution.py:44
  41.7 168.8 %while.14 = (s32[]{:T(128)}, bf16[8,2,32,512]{3,2,1,0:T(8,128)(2,1)}, s32[8]{0:T(128)S(1)}, s32[16]{0:T(128)S(1)}, bf16[16,32,576]{2,1,0:T(8,128)(2,1)}, /*index...) while((s32[]{:T(128)}, ...), condition=%wide.region_3.4_spmd.clone.clone, body=%wide.region_0.3_spmd.clone.clone.sunk | while | flops 152644128 | bytes 15479567 | solution.py:89
  43.9 7.3 %gather_fusion = bf16[128,9216]{1,0:T(8,128)(2,1)} fusion(bf16[96,9216]{1,0:T(8,128)(2,1)} %get-tuple-element.286, s32[1024]{0:T(1024)S(1)} %pad_clamp_fusion.4), kind=kCustom, calls=%fused_computation.clone.clone.1 | custom fusion | bytes 4719104 | tf_op jit(solution)/shard_map/while/body/eval_jaxpr/gather | solution.py:63
  51.2 5.0 %reshape.293 = bf16[2,1024,576]{2,1,0:T(8,128)(2,1)} reshape(bf16[128,9216]{1,0:T(8,128)(2,1)} %gather_fusion) | data formatting | bytes 4718592 | tf_op jit(solution)/shard_map/while/body/eval_jaxpr/reshape | solution.py:63
  65.0 7.3 %gather_fusion = bf16[128,9216]{1,0:T(8,128)(2,1)} fusion(bf16[96,9216]{1,0:T(8,128)(2,1)} %get-tuple-element.286, s32[1024]{0:T(1024)S(1)} %pad_clamp_fusion.4), kind=kCustom, calls=%fused_computation.clone.clone.1 | custom fusion | bytes 4719104 | tf_op jit(solution)/shard_map/while/body/eval_jaxpr/gather | solution.py:63
  72.2 5.0 %reshape.293 = bf16[2,1024,576]{2,1,0:T(8,128)(2,1)} reshape(bf16[128,9216]{1,0:T(8,128)(2,1)} %gather_fusion) | data formatting | bytes 4718592 | tf_op jit(solution)/shard_map/while/body/eval_jaxpr/reshape | solution.py:63
  86.1 7.3 %gather_fusion = bf16[128,9216]{1,0:T(8,128)(2,1)} fusion(bf16[96,9216]{1,0:T(8,128)(2,1)} %get-tuple-element.286, s32[1024]{0:T(1024)S(1)} %pad_clamp_fusion.4), kind=kCustom, calls=%fused_computation.clone.clone.1 | custom fusion | bytes 4719104 | tf_op jit(solution)/shard_map/while/body/eval_jaxpr/gather | solution.py:63
  93.3 5.0 %reshape.293 = bf16[2,1024,576]{2,1,0:T(8,128)(2,1)} reshape(bf16[128,9216]{1,0:T(8,128)(2,1)} %gather_fusion) | data formatting | bytes 4718592 | tf_op jit(solution)/shard_map/while/body/eval_jaxpr/reshape | solution.py:63
  107.2 7.3 %gather_fusion = bf16[128,9216]{1,0:T(8,128)(2,1)} fusion(bf16[96,9216]{1,0:T(8,128)(2,1)} %get-tuple-element.286, s32[1024]{0:T(1024)S(1)} %pad_clamp_fusion.4), kind=kCustom, calls=%fused_computation.clone.clone.1 | custom fusion | bytes 4719104 | tf_op jit(solution)/shard_map/while/body/eval_jaxpr/gather | solution.py:63
  114.4 5.0 %reshape.293 = bf16[2,1024,576]{2,1,0:T(8,128)(2,1)} reshape(bf16[128,9216]{1,0:T(8,128)(2,1)} %gather_fusion) | data formatting | bytes 4718592 | tf_op jit(solution)/shard_map/while/body/eval_jaxpr/reshape | solution.py:63
  128.2 7.3 %gather_fusion = bf16[128,9216]{1,0:T(8,128)(2,1)} fusion(bf16[96,9216]{1,0:T(8,128)(2,1)} %get-tuple-element.286, s32[1024]{0:T(1024)S(1)} %pad_clamp_fusion.4), kind=kCustom, calls=%fused_computation.clone.clone.1 | custom fusion | bytes 4719104 | tf_op jit(solution)/shard_map/while/body/eval_jaxpr/gather | solution.py:63
  135.5 5.0 %reshape.293 = bf16[2,1024,576]{2,1,0:T(8,128)(2,1)} reshape(bf16[128,9216]{1,0:T(8,128)(2,1)} %gather_fusion) | data formatting | bytes 4718592 | tf_op jit(solution)/shard_map/while/body/eval_jaxpr/reshape | solution.py:63
  149.3 7.3 %gather_fusion = bf16[128,9216]{1,0:T(8,128)(2,1)} fusion(bf16[96,9216]{1,0:T(8,128)(2,1)} %get-tuple-element.286, s32[1024]{0:T(1024)S(1)} %pad_clamp_fusion.4), kind=kCustom, calls=%fused_computation.clone.clone.1 | custom fusion | bytes 4719104 | tf_op jit(solution)/shard_map/while/body/eval_jaxpr/gather | solution.py:63
  170.4 7.3 %gather_fusion = bf16[128,9216]{1,0:T(8,128)(2,1)} fusion(bf16[96,9216]{1,0:T(8,128)(2,1)} %get-tuple-element.286, s32[1024]{0:T(1024)S(1)} %pad_clamp_fusion.4), kind=kCustom, calls=%fused_computation.clone.clone.1 | custom fusion | bytes 4719104 | tf_op jit(solution)/shard_map/while/body/eval_jaxpr/gather | solution.py:63
  177.7 5.0 %reshape.293 = bf16[2,1024,576]{2,1,0:T(8,128)(2,1)} reshape(bf16[128,9216]{1,0:T(8,128)(2,1)} %gather_fusion) | data formatting | bytes 4718592 | tf_op jit(solution)/shard_map/while/body/eval_jaxpr/reshape | solution.py:63
  191.5 7.3 %gather_fusion = bf16[128,9216]{1,0:T(8,128)(2,1)} fusion(bf16[96,9216]{1,0:T(8,128)(2,1)} %get-tuple-element.286, s32[1024]{0:T(1024)S(1)} %pad_clamp_fusion.4), kind=kCustom, calls=%fused_computation.clone.clone.1 | custom fusion | bytes 4719104 | tf_op jit(solution)/shard_map/while/body/eval_jaxpr/gather | solution.py:63
  216.9 27.7 %all-reduce.2.cloned.1.call-done = f32[64,2048]{1,0:T(8,128)} async-done(((f32[64,2048]{1,0:T(8,128)}), f32[64,2048]{1,0:T(8,128)}) %all-reduce.2.cloned.1.call-update) | async-done | bytes 524304 | tf_op jit(solution)/shard_map/psum | solution.py:98
  246.8 53.0 %all_to_all.15 = bf16[16,1,32,2048]{3,2,1,0:T(8,128)(2,1)S(1)} all-to-all(bf16[16,1,32,2048]{3,2,1,0:T(8,128)(2,1)S(1)} %bitcast.139), channel_id=1, replica_groups=mesh['grp'=2,'ep'=16] {'ep'}, dimensions={0} | all-to-all | bytes 4194304 | tf_op jit(solution)/shard_map/all_to_all | solution.py:126
  304.1 8.3 %fusion.55 = bf16[16,1,32,2048]{3,2,1,0:T(8,128)(2,1)} fusion(bf16[1,704,2048]{2,1,0:T(8,128)(2,1)S(1)} %copy-done, bf16[1,2048,704]{1,2,0:T(8,128)(2,1)} %param.31, bf16[16,1,32,2048]{3,2,1,0:T(8,128)(2,1)} %copy-done.1, f32[16,32,704]{2,1,0:T(8,128)} %fusion.53), kind=kOutput, calls=%fused_computation.52 | convolution fusion | flops 2956001280 | bytes 11403264 | tf_op jit(solution)/shard_map/sekf,efd->sekd/dot_general | solution.py:134
  312.3 5.3 %all-to-all-start.2 = ((bf16[16,1,32,2048]{3,2,1,0:T(8,128)(2,1)}), bf16[16,1,32,2048]{3,2,1,0:T(8,128)(2,1)}, u32[]{:S(2)}, u32[]{:S(2)}) async-start(bf16[16,1,32,2048]{3,2,1,0:T(8,128)(2,1)} %fusion.55), calls=%async_computation.2 | async-start | bytes 4194304 | tf_op jit(solution)/shard_map/all_to_all | solution.py:137
  321.8 37.0 %all-to-all-done.2 = bf16[16,1,32,2048]{3,2,1,0:T(8,128)(2,1)} async-done(((bf16[16,1,32,2048]{3,2,1,0:T(8,128)(2,1)}), bf16[16,1,32,2048]{3,2,1,0:T(8,128)(2,1)}, u32[]{:S(2)}, u32[]{:S(2)}) %all-to-all-start.2) | async-done | bytes 2097184 | tf_op jit(solution)/shard_map/all_to_all | solution.py:137
  362.8 7.3 %gather_fusion.2 = f32[384,2048]{1,0:T(8,128)} fusion(f32[512,2048]{1,0:T(8,128)} %bitcast_convert_fusion, s32[1024]{0:T(1024)S(1)} %pad_clamp_fusion.1), kind=kCustom, calls=%fused_computation.2 | custom fusion | bytes 6292992 | tf_op jit(solution)/shard_map/gather | solution.py:140
  379.2 17.4 %reduce-scatter.2.cloned.1.call-done = bf16[64,1024]{1,0:T(8,128)(2,1)} async-done(((bf16[64,2048]{1,0:T(8,128)(2,1)}), bf16[64,1024]{1,0:T(8,128)(2,1)}) %reduce-scatter.2.cloned.1.call-update) | async-done | bytes 131088 | tf_op jit(solution)/shard_map/reduce_scatter | solution.py:141
  (180 shorter events, 126.3 us)
Async XLA Ops:
  6.5 297.5 %copy-start = (bf16[1,704,2048]{2,1,0:T(8,128)(2,1)S(1)}, bf16[1,704,2048]{2,1,0:T(8,128)(2,1)}, u32[]{:S(2)}) copy-start(bf16[1,704,2048]{2,1,0:T(8,128)(2,1)} %param.32) | copy-start | bytes 8650756
  12.0 10.4 %copy-start.3 = (s32[64,6]{0,1:T(8,128)S(1)}, s32[64,6]{0,1:T(8,128)}, u32[]{:S(2)}) copy-start(s32[64,6]{0,1:T(8,128)} %param.29) | copy-start | bytes 4612
  14.8 23.0 %all-to-all-start = ((bf16[16,2,9216]{2,1,0:T(2,128)(2,1)}), bf16[16,2,9216]{2,1,0:T(2,128)(2,1)}, u32[]{:S(2)}, u32[]{:S(2)}) async-start(bf16[16,2,9216]{2,1,0:T(2,128)(2,1)} %broadcast_select_fusion), calls=%async_computation | async-start | bytes 1179648 | tf_op jit(solution)/shard_map/all_to_all | solution.py:44
  22.2 222.5 %all-reduce.2.cloned.1.call-start = ((), (), s32[]{:S(2)}) async-start(), calls=%async_computation.4 | async-start | bytes 1048576 | tf_op jit(solution)/shard_map/psum | solution.py:98
  30.1 11.6 %copy-start.7 = (s32[16]{0:T(128)S(1)}, s32[16]{0:T(128)}, u32[]{:S(2)}) copy-start(s32[16]{0:T(128)} %param.34) | copy-start | bytes 196
  212.2 3.9 copy-start.2
  212.3 4.5 %copy-start.5 = (bf16[2048]{0:T(1024)(128)(2,1)S(1)}, bf16[2048]{0:T(1024)(128)(2,1)}, u32[]{:S(2)}) copy-start(bf16[2048]{0:T(1024)(128)(2,1)} %param.27) | copy-start | bytes 12292
  246.8 54.3 %copy-start.6 = (bf16[1,2048,704]{1,2,0:T(8,128)(2,1)S(1)}, bf16[1,2048,704]{1,2,0:T(8,128)(2,1)}, u32[]{:S(2)}) copy-start(bf16[1,2048,704]{1,2,0:T(8,128)(2,1)} %param.30) | copy-start | bytes 8650756
  299.8 1.3 copy-start.1
  312.3 5.9 %copy-start.4 = (bf16[2048,16]{0,1:T(8,128)(2,1)S(1)}, bf16[2048,16]{0,1:T(8,128)(2,1)}, u32[]{:S(2)}) copy-start(bf16[2048,16]{0,1:T(8,128)(2,1)} %param.28) | copy-start | bytes 196612
  312.3 46.5 %all-to-all-start.2 = ((bf16[16,1,32,2048]{3,2,1,0:T(8,128)(2,1)}), bf16[16,1,32,2048]{3,2,1,0:T(8,128)(2,1)}, u32[]{:S(2)}, u32[]{:S(2)}) async-start(bf16[16,1,32,2048]{3,2,1,0:T(8,128)(2,1)} %fusion.55), calls=%async_computation.2 | async-start | bytes 4194304 | tf_op jit(solution)/shard_map/all_to_all | solution.py:137
  317.6 79.0 %reduce-scatter.2.cloned.1.call-start = ((), (), s32[]{:S(2)}) async-start(), calls=%async_computation.5 | async-start | bytes 393216 | tf_op jit(solution)/shard_map/reduce_scatter | solution.py:141
Sparse Core Ops, SparseCore 0:
  216.3 28.3 all-reduce.1
  379.3 17.2 reduce-scatter.1
where the time goes:
time: 408 us; the launch traced here: 405 us
  local copies, waits for them, and re-layouts  138 us (34%)
  waiting for transfers between devices  89.9 us (22%)
  matrix products  64.9 us (16%)
  blocking collectives  53 us (13%)
  other arithmetic  27.2 us (7%)
  between operations  13.6 us (3%)
  starting transfers between devices  13 us (3%)
  loops' own time  5.8 us (1%)
    gather x8, local copies, waits for them, and re-layouts, attend(): key_rows = block_pool[table_rows].reshape(per_step, cached, key_width)  58.2 us
    all_to_all x1, blocking collectives, local(): lax.all_to_all(buffer, 'ep', split_axis=0, concat_axis=0, tiled=True)  53 us
    reshape x8, local copies, waits for them, and re-layouts, attend(): key_rows = block_pool[table_rows].reshape(per_step, cached, key_width)  40 us
    all_to_all x1, waiting for transfers between devices, local(): lax.all_to_all(results.astype(jnp.bfloat16), 'ep', split_axis=0, concat_a...  37 us
    psum x1, waiting for transfers between devices, local(): attention_out = lax.psum(partial_value, 'grp')  27.7 us
    sub x8, matrix products, attend(): exp_scores = jnp.exp(score_values - row_peak)  22.9 us
    dot_general x8, matrix products, attend(): jnp.einsum('gqk,gkl->gql', attention, key_rows[:, :, :latent_dim], prefer...  22.4 us
    reduce_scatter x1, waiting for transfers between devices, local(): lax.psum_scatter(jnp.sum(gate_weights[:, :, None] * gathered, axis=1).ast...  17.4 us
  transfers between devices with their start and end apart: 4, of which 4 were waited for; matrix products, arithmetic and copies ran while one was open for 3% of the time, Pallas kernels for 0%

commit v1 on v0

v1 whole, which is shorter than its diff:
```python
import functools

import jax
import jax.numpy as jnp
from jax import lax
from jax.experimental import pallas as pl
from jax.experimental.pallas import tpu as pltpu
from jax.sharding import PartitionSpec as P

F32 = jnp.float32
BF16 = jnp.bfloat16
HIDDEN = -1e30
VMEM = pltpu.VMEM
ANY = pl.BlockSpec(memory_space=pl.ANY)
WHOLE = pl.BlockSpec(memory_space=pltpu.VMEM)


def dot(a, b):
    return jnp.dot(a, b, preferred_element_type=F32)


def dot_rows(a, b):
    return lax.dot_general(a, b, (((1,), (1,)), ((), ())), preferred_element_type=F32)


def cost(products, moved_bytes):
    return pl.CostEstimate(flops=2 * products, bytes_accessed=moved_bytes, transcendentals=0)


def fetch_all(sources, buffers, sems):
    copies = []
    for at, (source, buffer) in enumerate(zip(sources, buffers)):
        copy = pltpu.make_async_copy(source, buffer, sems.at[at])
        copy.start()
        copies.append(copy)
    return copies


def lay_tokens(keys, start, ref, tokens, width):
    count = ref.shape[0]
    for token in range(tokens):
        keys[start : start + count, :width] = ref[:, token * width : (token + 1) * width]
        start += count
    return start


def resident_kernel(
    dims, nope, rope_rows, fresh, cache, absorb, bias_ref,
    query_ref, mixed_ref,
    keys,
):
    head_count, nope_dim, latent, rope, block_size, steps = dims
    width = latent + rope
    rows = nope.shape[0]
    padding = keys.shape[1] - width
    keys[:, latent:] = jnp.zeros((keys.shape[0], keys.shape[1] - latent), BF16)
    start = lay_tokens(keys, 0, cache, block_size, width)
    lay_tokens(keys, start, fresh, steps, width)
    for head in range(head_count):
        q_latent = dot(nope[:, head * nope_dim : (head + 1) * nope_dim], absorb[head])
        q_rope = rope_rows[:, head * rope : (head + 1) * rope]
        fill = jnp.zeros((rows, padding), BF16)
        query_ref[head * rows : (head + 1) * rows, :] = jnp.concatenate(
            [q_latent.astype(BF16), q_rope, fill], axis=1
        )
    scale = (nope_dim + rope) ** (-0.5)
    part = min(4, head_count) * rows
    for first in range(0, head_count * rows, part):
        score = dot_rows(query_ref[first : first + part, :], keys[...])
        score = score.reshape(part // rows, rows, -1) * scale + bias_ref[...][None]
        score = score.reshape(part, -1)
        peak = jnp.max(score, axis=1, keepdims=True)
        weight = jnp.exp(score - peak)
        total = jnp.sum(weight, axis=1, keepdims=True)
        mixed_ref[first : first + part, :latent] = dot(weight.astype(BF16), keys[:, :latent])
        lane = lax.broadcasted_iota(jnp.int32, (part, 128), 1)
        mixed_ref[first : first + part, latent:] = jnp.where(lane < 64, peak, total)


def moved_kernel(
    dims, moved_any, query_any, bias_any, mixed_any, value_any, proj_any,
    share_ref,
    moved, query, bias, mixed, value, proj, keys, heads_out, sems,
):
    head_count, nope_dim, latent, rope, block_size, steps = dims
    width = latent + rope
    rows = heads_out.shape[0]
    got = fetch_all(
        (moved_any, query_any, bias_any, mixed_any, value_any, proj_any),
        (moved, query, bias, mixed, value, proj),
        sems,
    )
    keys[:, latent:] = jnp.zeros((keys.shape[0], keys.shape[1] - latent), BF16)
    scale = (nope_dim + rope) ** (-0.5)
    value_dim = value.shape[2]
    got[0].wait()
    count = moved.shape[0] * moved.shape[1]
    for half in range(2):
        part = moved[:, :, half * width : (half + 1) * width]
        keys[half * count : (half + 1) * count, :width] = part.reshape(count, width)
    got[1].wait()
    got[2].wait()
    group = min(4, head_count)
    for first in range(0, head_count, group):
        at = slice(first * rows, (first + group) * rows)
        score = dot_rows(query[at, :], keys[...])
        score = score.reshape(group, rows, -1) * scale + bias[...][None]
        score = score.reshape(group * rows, -1)
        if first == 0:
            got[3].wait()
        before = mixed[at, latent : latent + 1]
        peak = jnp.maximum(jnp.max(score, axis=1, keepdims=True), before)
        weight = jnp.exp(score - peak)
        keep = jnp.exp(before - peak)
        total = jnp.sum(weight, axis=1, keepdims=True) + mixed[at, latent + 64 : latent + 65] * keep
        joined = dot(weight.astype(BF16), keys[:, :latent]) + mixed[at, :latent] * keep
        joined = (joined / total).astype(BF16)
        if first == 0:
            got[4].wait()
        for head in range(first, first + group):
            own = joined[(head - first) * rows : (head - first + 1) * rows]
            heads_out[:, head * value_dim : (head + 1) * value_dim] = dot(own, value[head]).astype(BF16)
    got[5].wait()
    share_ref[...] = dot(heads_out[...], proj[...]).astype(BF16)


def own_columns(ref, shift):
    groups = lax.axis_size("grp")
    columns = ref.shape[1] // groups
    first = (lax.axis_index("grp") + shift) % groups * columns
    return ref[:, pl.ds(pl.multiple_of(first, 128), columns)]


def norm_kernel(experts, hidden_any, gain_ref, router_ref, ids_ref, *refs):
    parts, (state_ref, packet_ref, hidden, whole, sem) = refs[:-5], refs[-5:]
    copy = pltpu.make_async_copy(hidden_any, hidden, sem)
    copy.start()
    rows, model = hidden.shape
    state = parts[0][...].astype(F32)
    for part in parts[1:]:
        state = state + part[...].astype(F32)
    copy.wait()
    state = state + hidden[...].astype(F32)
    whole[...] = state
    state_ref[...] = own_columns(whole, 0)
    square = jnp.mean(state * state, axis=1, keepdims=True)
    normed = (state * lax.rsqrt(square + 1e-06) * gain_ref[...].astype(F32)).astype(BF16)
    packet_ref[:, :model] = normed
    logits = dot_rows(router_ref[...], normed)
    names = lax.broadcasted_iota(jnp.int32, (experts, rows), 0)
    named = names == ids_ref[0:1, :]
    for k in range(1, ids_ref.shape[0]):
        named = named | (names == ids_ref[k : k + 1, :])
    chosen = jnp.where(named, jax.nn.sigmoid(logits), 0.0)
    weight = chosen / jnp.sum(chosen, axis=0, keepdims=True)
    high = weight.astype(BF16)
    low = (weight - high.astype(F32)).astype(BF16)
    extra = packet_ref.shape[1] - model
    both = jnp.concatenate([high, low], axis=0)
    place = lax.broadcasted_iota(jnp.int32, (2 * experts, extra), 0)
    lane = lax.broadcasted_iota(jnp.int32, (2 * experts, extra), 1)
    turned = lax.dot_general(
        both, (place == lane).astype(BF16), (((0,), (0,)), ((), ())), preferred_element_type=F32
    )
    packet_ref[:, model:] = turned.astype(BF16)


def expert_kernel(experts, *refs):
    rows_refs, (gate_ref, up_ref, down_ref, near_ref, far_ref) = refs[:-5], refs[-5:]
    model = gate_ref.shape[1]
    packet = jnp.concatenate([ref[...] for ref in rows_refs], axis=0)
    rows = packet[:, :model]
    extra = packet[:, model:].astype(F32)
    names = lax.broadcasted_iota(jnp.int32, extra.shape, 1)
    me = lax.axis_index("ep")
    mine = (names == me) | (names == me + experts)
    weight = jnp.sum(jnp.where(mine, extra, 0.0), axis=1, keepdims=True)
    gate = dot_rows(rows, gate_ref[...])
    up = dot_rows(rows, up_ref[...])
    inner = (gate * jax.nn.sigmoid(gate) * up * weight).astype(BF16)
    result = dot(inner, down_ref[...]).astype(BF16)
    half = near_ref.shape[0]
    near_ref[...] = result[:half]
    far_ref[...] = result[half:]


def own_kernel(state_ref, own_ref, over_ref, base_ref, other_ref, whole):
    whole[...] = own_ref[...] + over_ref[...].astype(F32)
    base_ref[...] = state_ref[...] + own_columns(whole, 0)
    other_ref[...] = own_columns(whole, 1).astype(BF16)


def near_kernel(near_ref, far_ref, side_ref, two_ref, mine_ref, other_ref, whole):
    total = near_ref[...] + far_ref[...].astype(F32)
    whole[...] = total + side_ref[...].astype(F32) + two_ref[...].astype(F32)
    mine_ref[...] = own_columns(whole, 0).astype(BF16)
    other_ref[...] = own_columns(whole, 1).astype(BF16)


def local(
    hidden_in,
    query_nope,
    query_rope,
    new_latent,
    latent_cache,
    key_absorb,
    value_absorb,
    output_proj,
    norm_gain,
    router_proj,
    expert_ids,
    expert_gate,
    expert_up,
    expert_down,
    block_table,
    lengths,
    subtree_moves,
):
    head_count, nope_dim, latent = key_absorb.shape
    rope = query_rope.shape[1] // head_count
    width = latent + rope
    requests, table_len = block_table.shape
    steps = new_latent.shape[1] // width
    row_count, model = hidden_in.shape
    block_size = latent_cache.shape[1] // width
    resident = latent_cache.shape[0]
    experts = router_proj.shape[1]
    groups = lax.axis_size("grp")
    group = lax.axis_index("grp")
    ranks = lax.axis_size("ep")
    me = lax.axis_index("ep")
    ring = ranks // 4
    core_swap = [(i, i ^ 1) for i in range(ranks)]
    side_swap = [(i, i ^ 2) for i in range(ranks)]
    ring_next = [(i, (i + 4) % ranks) for i in range(ranks)]
    both_axes = ("grp", "ep")

    def turn(by):
        return [(g, (g + by) % groups) for g in range(groups)]

    sent = jnp.clip(subtree_moves.reshape(-1), 0, resident - 1)
    slots = subtree_moves.shape[2]
    pick = (sent[:, None] == jnp.arange(resident, dtype=jnp.int32)[None, :]).astype(BF16)
    pieces = block_size // 2
    outgoing = dot(pick, latent_cache).astype(BF16).reshape(ranks, slots * pieces, 2 * width)
    arrived = lax.all_to_all(outgoing, "ep", split_axis=0, concat_axis=0, tiled=True)

    place = jnp.arange(table_len, dtype=jnp.int32)
    usable = jnp.clip(lengths[:, None] - place[None, :] * block_size, 0, block_size)
    blocks = jnp.arange(resident + ranks * slots, dtype=jnp.int32)
    limit = jnp.sum(
        jnp.where(block_table[:, :, None] == blocks[None, None, :], usable[:, :, None], 0), axis=1
    )
    token = jnp.arange(block_size, dtype=jnp.int32)
    row = jnp.arange(row_count, dtype=jnp.int32)
    fresh = jnp.arange(steps * requests, dtype=jnp.int32)
    fresh_open = ((row // steps)[:, None] == (fresh % requests)[None, :]) & (
        (fresh // requests)[None, :] <= (row % steps)[:, None]
    )
    near_open = (limit[:, None, :resident] > token[None, :, None]).reshape(requests, -1)
    near_open = jnp.concatenate([jnp.repeat(near_open, steps, axis=0), fresh_open], axis=1)
    near_bias = jnp.where(near_open, 0.0, HIDDEN).astype(F32)
    by_key = jnp.repeat(limit[:, resident:], pieces, axis=1)
    at_token = 2 * (jnp.arange(ranks * slots * pieces, dtype=jnp.int32) % pieces)
    moved_open = jnp.concatenate([by_key > at_token[None], by_key > at_token[None] + 1], axis=1)
    moved_bias = jnp.repeat(jnp.where(moved_open, 0.0, HIDDEN).astype(F32), steps, axis=0)

    padded = -(-width // 128) * 128
    query_rows = head_count * row_count
    dims = (head_count, nope_dim, latent, rope, block_size, steps)
    query, mixed = pl.pallas_call(
        functools.partial(resident_kernel, dims),
        out_shape=(
            jax.ShapeDtypeStruct((query_rows, padded), BF16),
            jax.ShapeDtypeStruct((query_rows, latent + 128), F32),
        ),
        scratch_shapes=[VMEM((near_bias.shape[1], padded), BF16)],
        compiler_params=pltpu.CompilerParams(vmem_limit_bytes=16 * 2**20),
        cost_estimate=cost(query_rows * near_bias.shape[1] * (padded + latent), 8 * 2**20),
        name="attend_resident",
    )(query_nope, query_rope, new_latent, latent_cache, key_absorb, near_bias)
    share = pl.pallas_call(
        functools.partial(moved_kernel, dims),
        out_shape=jax.ShapeDtypeStruct((row_count, model), BF16),
        in_specs=[ANY] * 6,
        scratch_shapes=[
            VMEM(arrived.shape, BF16),
            VMEM(query.shape, BF16),
            VMEM(moved_bias.shape, F32),
            VMEM(mixed.shape, F32),
            VMEM(value_absorb.shape, BF16),
            VMEM(output_proj.shape, BF16),
            VMEM((moved_bias.shape[1], padded), BF16),
            VMEM((row_count, head_count * value_absorb.shape[2]), BF16),
            pltpu.SemaphoreType.DMA((6,)),
        ],
        compiler_params=pltpu.CompilerParams(vmem_limit_bytes=60 * 2**20),
        cost_estimate=cost(query_rows * moved_bias.shape[1] * (padded + latent), 10 * 2**20),
        name="attend_moved",
    )(arrived, query, moved_bias, mixed, value_absorb, output_proj)
    shares = [share]
    shares += [lax.ppermute(share, "grp", turn(by)) for by in range(1, groups)]

    extra = -(-2 * experts // 128) * 128
    columns = model // groups
    state, packet = pl.pallas_call(
        functools.partial(norm_kernel, experts),
        out_shape=(
            jax.ShapeDtypeStruct((row_count, columns), F32),
            jax.ShapeDtypeStruct((row_count, model + extra), BF16),
        ),
        in_specs=[ANY] + [WHOLE] * (3 + groups),
        scratch_shapes=[
            VMEM((row_count, model), BF16),
            VMEM((row_count, model), F32),
            pltpu.SemaphoreType.DMA(()),
        ],
        compiler_params=pltpu.CompilerParams(vmem_limit_bytes=16 * 2**20),
        cost_estimate=cost(row_count * model * 128, 4 * 2**20),
        name="norm",
    )(hidden_in, norm_gain[None, :], router_proj.T, expert_ids.T, *shares)

    gate_rows = jnp.swapaxes(expert_gate[0], 0, 1)
    up_rows = jnp.swapaxes(expert_up[0], 0, 1)

    def run_expert(rows):
        half = len(rows) * row_count
        out = jax.ShapeDtypeStruct((half, model), BF16)
        across = [lax.ppermute(part, "ep", core_swap) for part in rows]
        near, far = pl.pallas_call(
            functools.partial(expert_kernel, experts),
            out_shape=(out, out),
            in_specs=[WHOLE] * (2 * len(rows) + 3),
            compiler_params=pltpu.CompilerParams(vmem_limit_bytes=16 * 2**20),
            cost_estimate=cost(6 * half * model * gate_rows.shape[0], 12 * 2**20),
            name="expert",
        )(*rows, *across, gate_rows, up_rows, expert_down[0])
        return near.astype(F32) + lax.ppermute(far, "ep", core_swap).astype(F32)

    def send(value, axes, pairs):
        return lax.ppermute(value.astype(BF16), axes, pairs).astype(F32)

    if ring == 4 and groups == 2:
        def ring_step(sign):
            return [
                (g * ranks + i, g * ranks + (i + sign * 4 * (1 - 2 * g)) % ranks)
                for g in range(2)
                for i in range(ranks)
            ]

        onward, backward, plane_swap = ring_step(1), ring_step(-1), [(0, 1), (1, 0)]
        near = lax.ppermute(packet, both_axes, onward)
        side = lax.ppermute(packet, "ep", side_swap)
        two = lax.ppermute(near, both_axes, onward)
        near_side = lax.ppermute(near, "ep", side_swap)
        far = lax.ppermute(near, "grp", plane_swap)
        two_side = lax.ppermute(two, "ep", side_swap)
        far_side = lax.ppermute(near_side, "grp", plane_swap)
        cut = row_count
        own_sum = run_expert([side, packet])
        near_sum = run_expert([near_side, near])
        ahead_sum = run_expert([far, two])
        ahead_side = run_expert([far_side, two_side])
        far_side_in = lax.ppermute(ahead_side[:cut].astype(BF16), "grp", plane_swap)
        two_side_in = send(ahead_side[cut:], "ep", side_swap)
        far_in = lax.ppermute(ahead_sum[:cut].astype(BF16), "grp", plane_swap)
        own_in = lax.ppermute(own_sum[:cut].astype(BF16), "ep", side_swap)
        near_side = near_sum[:cut] + far_side_in.astype(F32)
        near_side_in = lax.ppermute(near_side.astype(BF16), "ep", side_swap)
        two_in = lax.ppermute((ahead_sum[cut:] + two_side_in).astype(BF16), both_axes, backward)
        part = (row_count, columns)

        def by_columns(kernel, first_type, *operands):
            return pl.pallas_call(
                kernel,
                out_shape=(
                    jax.ShapeDtypeStruct(part, first_type),
                    jax.ShapeDtypeStruct(part, BF16),
                ),
                scratch_shapes=[VMEM((row_count, model), F32)],
                compiler_params=pltpu.CompilerParams(vmem_limit_bytes=16 * 2**20),
                cost_estimate=cost(row_count * model, 2**20),
                name=kernel.__name__,
            )(*operands)

        base, own_other = by_columns(own_kernel, F32, state, own_sum[cut:], own_in)
        own_over = lax.ppermute(own_other, "grp", plane_swap)
        mine, other = by_columns(near_kernel, BF16, near_sum[cut:], far_in, near_side_in, two_in)
        crossed = [(source, (target + ranks) % (2 * ranks)) for source, target in backward]
        result = base + own_over.astype(F32)
        result = result + send(mine, both_axes, backward) + send(other, both_axes, crossed)
        return result.astype(BF16)

    line = [packet]
    for _ in range(1, ring):
        line.append(lax.ppermute(line[-1], "ep", ring_next))
    totals = []
    for part in line:
        both = run_expert([lax.ppermute(part, "ep", side_swap), part])
        totals.append(both[row_count:] + send(both[:row_count], "ep", side_swap))
    moving = totals[1 % ring]
    for hop in list(range(2, ring)) + [0]:
        moving = totals[hop] + send(moving, "ep", ring_next)

    result = state + lax.dynamic_slice_in_dim(moving, group * columns, columns, 1)
    for by in range(1, groups):
        to = (group + by) % groups
        part = lax.dynamic_slice_in_dim(moving, to * columns, columns, 1)
        result = result + send(part, "grp", turn(by))
    return result.astype(BF16)


def solution(mesh):
    in_specs = (
        P("ep", None),
        P("ep", "grp"),
        P("ep", "grp"),
        P("ep", None),
        P("ep", None),
        P("grp", None, None),
        P("grp", None, None),
        P("grp", None),
        P(),
        P(),
        P("ep", None),
        P("ep", None, "grp"),
        P("ep", None, "grp"),
        P("ep", "grp", None),
        P("ep", None),
        P("ep"),
        P("ep", None, None),
    )
    out_specs = P("ep", "grp")
    return jax.shard_map(local, mesh=mesh, in_specs=in_specs, out_specs=out_specs, check_vma=False)
```

time: 408 us -> 117 us (0.29)
  local copies, waits for them, and re-layouts: 138 us -> 10.1 us
  matrix products: 64.9 us -> 1.64 us
  blocking collectives: 53 us -> 0 us
  waiting for transfers between devices: 89.9 us -> 47.7 us
  other arithmetic: 27.2 us -> 2.74 us
  starting transfers between devices: 13 us -> 34.3 us
  Pallas kernels: 0 us -> 19.3 us
  between operations: 13.6 us -> 0.42 us
  loops' own time: 5.8 us -> 0 us
    gather x17 -> x0, local copies, waits for them, and re-layouts: 78.5 us -> none  [the longest x8 58.2 us: attend(): key_rows = block_pool[table_rows].reshape(per_step, cached, key_width)]
    all_to_all x1 -> x0, blocking collectives: 53 us -> none  [local(): lax.all_to_all(buffer, 'ep', split_axis=0, concat_axis=0, tiled=True)]
    reshape x10 -> x3, local copies, waits for them, and re-layouts: 43 us -> 1.83 us  [the longest x1 1.09 us: local(): dot(pick, latent_cache).astype(BF16)]
    dot_general x15 -> x1, matrix products: 42 us -> 1.64 us  [dot(): return jnp.dot(a, b, preferred_element_type=F32)]
    ppermute x0 -> x29, waiting for transfers between devices: none -> 39 us  [the longest x3 14.4 us: send(): return lax.ppermute(value.astype(BF16), axes, pairs).astype(F32)]
    all_to_all x1 -> x0, waiting for transfers between devices: 37 us -> none  [local(): lax.all_to_all(results.astype(jnp.bfloat16), 'ep', split_axis=0, concat_a...]
    psum x1 -> x0, waiting for transfers between devices: 27.7 us -> none  [local(): attention_out = lax.psum(partial_value, 'grp')]
    ppermute x0 -> x29, starting transfers between devices: none -> 26.8 us  [the longest x3 5.55 us: send(): return lax.ppermute(value.astype(BF16), axes, pairs).astype(F32)]
  transfers between devices with their start and end apart: 4 -> 30, of which waited for: 4 -> 12; matrix products, arithmetic and copies ran while one was open for 3% -> 2% of each run, Pallas kernels for 0% -> 12%
where the time goes in v1:
time: 117 us; the launch traced here: 116 us
  waiting for transfers between devices  47.7 us (41%)
  starting transfers between devices  34.3 us (29%)
  Pallas kernels  19.3 us (16%)
  local copies, waits for them, and re-layouts  10.1 us (9%)
  other arithmetic  2.74 us (2%)
  matrix products  1.64 us (1%)
    ppermute x3, waiting for transfers between devices, send(): return lax.ppermute(value.astype(BF16), axes, pairs).astype(F32)  14.4 us
    pallas_call x4, Pallas kernels, run_expert(): pl.pallas_call(functools.partial(expert_kernel, experts), out_shape=(out,...  10.5 us
    all_to_all x1, waiting for transfers between devices, local(): lax.all_to_all(outgoing, 'ep', split_axis=0, concat_axis=0, tiled=True)  8.71 us
    all_to_all x1, starting transfers between devices, local(): lax.all_to_all(outgoing, 'ep', split_axis=0, concat_axis=0, tiled=True)  7.5 us
    unnamed x38, local copies, waits for them, and re-layouts  7.37 us
    ppermute x1, waiting for transfers between devices, local(): shares += [lax.ppermute(share, 'grp', turn(by)) for by in range(1, groups)]  6.9 us
    ppermute x1, waiting for transfers between devices, local(): near = lax.ppermute(packet, both_axes, onward)  6.52 us
    ppermute x3, starting transfers between devices, send(): return lax.ppermute(value.astype(BF16), axes, pairs).astype(F32)  5.55 us
  transfers between devices with their start and end apart: 30, of which 12 were waited for; matrix products, arithmetic and copies ran while one was open for 2% of the time, Pallas kernels for 12%

profile of v1, /device:TPU:0, one launch (start us, length us, event | category | flops | bytes accessed | tf_op | source)
XLA Modules:
  0.0 116.2 jit_solution(7823745750686944399)
XLA Ops:
  0.9 1.6 %convolution_convert_fusion = bf16[32,9216]{1,0:T(8,128)(2,1)S(1)} fusion(bf16[64,9216]{1,0:T(8,128)(2,1)} %cache.1, s32[32]{0:T(128)S(1)} %min.20), kind=kOutput, calls=%fused_computation | convolution fusion | flops 38045696 | bytes 1769600 | tf_op jit(solution)/shard_map/dot_general | solution.py:19
  3.6 7.5 %all-to-all-start = ((bf16[16,16,1152]{2,1,0:T(8,128)(2,1)}), bf16[16,16,1152]{2,1,0:T(8,128)(2,1)S(1)}, u32[]{:S(2)}, u32[]{:S(2)}) async-start(bf16[16,16,1152]{2,1,0:T(8,128)(2,1)} %reshape.120), calls=%async_computation | async-start | bytes 1179648 | tf_op jit(solution)/shard_map/all_to_all | solution.py:246
  13.4 2.7 %attend_resident.1 = (bf16[512,640]{1,0:T(8,128)(2,1)S(1)}, f32[512,640]{1,0:T(8,128)S(1)}) custom-call(bf16[64,1024]{1,0:T(8,128)(2,1)S(1)} %copy-done.12, bf16[64,512]{1,0:T(8,128)(2,1)S(1)} %copy-done.14, bf16[16,2304]{1,0:T(8,128)(2,1)S(1)} %copy-done.13, bf16[64,9216]{1,0:T(8,128)(2,1)S(1)} %copy-done.5, bf16[8,128,512]{2,1,0:T(8,128)(2,1)S(1)} %copy-done.11, ...), custom_call_target="tpu_custom_call" | custom-call | flops 1283457024 | bytes 8388608 | tf_op jit(solution)/shard_map/attend_resident/pallas_call | solution.py:271
  18.0 8.7 %all-to-all-done.moved_any = bf16[16,16,1152]{2,1,0:T(8,128)(2,1)S(1)} async-done(((bf16[16,16,1152]{2,1,0:T(8,128)(2,1)}), bf16[16,16,1152]{2,1,0:T(8,128)(2,1)S(1)}, u32[]{:S(2)}, u32[]{:S(2)}) %all-to-all-start) | async-done | bytes 589856 | tf_op jit(solution)/shard_map/all_to_all | solution.py:246
  27.5 5.1 %attend_moved.1.refs_0_ = bf16[64,2048]{1,0:T(8,128)(2,1)} custom-call(bf16[16,16,1152]{2,1,0:T(8,128)(2,1)} %copy-done.15, bf16[512,640]{1,0:T(8,128)(2,1)} %copy-done.7, f32[64,512]{1,0:T(8,128)} %reshape.123.bias_any, f32[512,640]{1,0:T(8,128)} %copy-done.4, bf16[8,512,128]{2,1,0:T(8,128)(2,1)} %value_any.1, bf16[1024,2048]{1,0:T(8,128)(2,1)} %proj_any.1), custom_call_target="tpu_custom_call" | custom-call | flops 603979776 | bytes 10485760 | tf_op jit(solution)/shard_map/attend_moved/pallas_call | solution.py:282
  32.6 1.6 %collective-permute-start = (bf16[64,2048]{1,0:T(8,128)(2,1)}, bf16[64,2048]{1,0:T(8,128)(2,1)S(1)}, u32[]{:S(2)}, u32[]{:S(2)}) collective-permute-start(bf16[64,2048]{1,0:T(8,128)(2,1)} %attend_moved.1.refs_0_), channel_id=1, source_target_pairs={{0,16},{16,0},{1,17},{17,1},{2,18},{18,2},{3,19},{19,3},{4,20},{20... | collective-permute-start | bytes 786440 | tf_op jit(solution)/shard_map/ppermute | solution.py:302
  34.2 6.9 %collective-permute-done.refs_1_ = bf16[64,2048]{1,0:T(8,128)(2,1)S(1)} collective-permute-done((bf16[64,2048]{1,0:T(8,128)(2,1)}, bf16[64,2048]{1,0:T(8,128)(2,1)S(1)}, u32[]{:S(2)}, u32[]{:S(2)}) %collective-permute-start) | collective-permute-done | bytes 262176 | tf_op jit(solution)/shard_map/ppermute | solution.py:302
  42.8 2.1 %collective-permute-start.7 = (bf16[64,2176]{1,0:T(8,128)(2,1)S(1)}, bf16[64,2176]{1,0:T(8,128)(2,1)S(1)}, u32[]{:S(2)}, u32[]{:S(2)}) collective-permute-start(bf16[64,2176]{1,0:T(8,128)(2,1)S(1)} %get-tuple-element.24.refs_1_), channel_id=1, source_target_pairs={{0,4},{1,5},{2,6},{3,7},{4,8},{5,9},{6,10},{7,11},{8,12},{9,13},{1... | collective-permute-start | bytes 835592 | tf_op jit(solution)/shard_map/ppermute | solution.py:352
  45.8 6.5 %collective-permute-done.7.refs_1_ = bf16[64,2176]{1,0:T(8,128)(2,1)S(1)} collective-permute-done((bf16[64,2176]{1,0:T(8,128)(2,1)S(1)}, bf16[64,2176]{1,0:T(8,128)(2,1)S(1)}, u32[]{:S(2)}, u32[]{:S(2)}) %collective-permute-start.7) | collective-permute-done | bytes 278560 | tf_op jit(solution)/shard_map/ppermute | solution.py:352
  53.3 3.4 %collective-permute-start.12 = (bf16[64,2176]{1,0:T(8,128)(2,1)S(1)}, bf16[64,2176]{1,0:T(8,128)(2,1)S(1)}, u32[]{:S(2)}, u32[]{:S(2)}) collective-permute-start(bf16[64,2176]{1,0:T(8,128)(2,1)S(1)} %collective-permute-done.7.refs_1_), channel_id=1, source_target_pairs={{0,16},{16,0},{1,17},{17,1},{2,18},{18,2},{3,19},{19,3},{4,20},{20... | collective-permute-start | bytes 835592 | tf_op jit(solution)/shard_map/ppermute | solution.py:356
  58.6 2.3 %collective-permute-done.13.refs_1_ = bf16[64,2176]{1,0:T(8,128)(2,1)S(1)} collective-permute-done((bf16[64,2176]{1,0:T(8,128)(2,1)S(1)}, bf16[64,2176]{1,0:T(8,128)(2,1)S(1)}, u32[]{:S(2)}, u32[]{:S(2)}) %collective-permute-start.13) | collective-permute-done | bytes 278560 | tf_op jit(solution)/shard_map/ppermute | solution.py:354
  65.5 1.8 %copy-done.1 = bf16[1,2048,704]{1,2,0:T(8,128)(2,1)S(1)} copy-done((bf16[1,2048,704]{1,2,0:T(8,128)(2,1)S(1)}, bf16[1,2048,704]{1,2,0:T(8,128)(2,1)}, u32[]{:S(2)}) %copy-start.1) | copy-done | bytes 2883608
  67.3 1.8 %copy-done.3 = bf16[1,704,2048]{2,1,0:T(8,128)(2,1)S(1)} copy-done((bf16[1,704,2048]{2,1,0:T(8,128)(2,1)S(1)}, bf16[1,704,2048]{2,1,0:T(8,128)(2,1)}, u32[]{:S(2)}) %copy-start.3) | copy-done | bytes 2883608
  69.1 2.6 %expert.4 = (bf16[128,2048]{1,0:T(8,128)(2,1)S(1)}, bf16[128,2048]{1,0:T(8,128)(2,1)S(1)}) custom-call(bf16[64,2176]{1,0:T(8,128)(2,1)S(1)} %collective-permute-done.1.refs_0_, bf16[64,2176]{1,0:T(8,128)(2,1)S(1)} %get-tuple-element.24.refs_1_, bf16[64,2176]{1,0:T(8,128)(2,1)S(1)} %collective-permute-done.2.refs_2_, ...), custom_call_target="tpu_custom_call" | custom-call | flops 2214592512 | bytes 12582912 | tf_op jit(solution)/shard_map/expert/pallas_call | solution.py:330
  72.6 2.6 %expert.6 = (bf16[128,2048]{1,0:T(8,128)(2,1)S(1)}, bf16[128,2048]{1,0:T(8,128)(2,1)S(1)}) custom-call(bf16[64,2176]{1,0:T(8,128)(2,1)S(1)} %collective-permute-done.12.refs_0_, bf16[64,2176]{1,0:T(8,128)(2,1)S(1)} %collective-permute-done.13.refs_1_, bf16[64,2176]{1,0:T(8,128)(2,1)S(1)} %collective-permute-done.14.refs_2_, ...), custom_call_target="tpu_custom_call" | custom-call | flops 2214592512 | bytes 12582912 | tf_op jit(solution)/shard_map/expert/pallas_call | solution.py:330
  75.9 2.6 %expert.5 = (bf16[128,2048]{1,0:T(8,128)(2,1)S(1)}, bf16[128,2048]{1,0:T(8,128)(2,1)S(1)}) custom-call(bf16[64,2176]{1,0:T(8,128)(2,1)S(1)} %collective-permute-done.8.refs_0_, bf16[64,2176]{1,0:T(8,128)(2,1)S(1)} %collective-permute-done.7.refs_1_, bf16[64,2176]{1,0:T(8,128)(2,1)S(1)} %collective-permute-done.9.refs_2_, ...), custom_call_target="tpu_custom_call" | custom-call | flops 2214592512 | bytes 12582912 | tf_op jit(solution)/shard_map/expert/pallas_call | solution.py:330
  78.6 2.6 %expert.7 = (bf16[128,2048]{1,0:T(8,128)(2,1)S(1)}, bf16[128,2048]{1,0:T(8,128)(2,1)S(1)}) custom-call(bf16[64,2176]{1,0:T(8,128)(2,1)S(1)} %collective-permute-done.18.refs_0_, bf16[64,2176]{1,0:T(8,128)(2,1)S(1)} %collective-permute-done.19.refs_1_, bf16[64,2176]{1,0:T(8,128)(2,1)S(1)} %collective-permute-done.20.refs_2_, ...), custom_call_target="tpu_custom_call" | custom-call | flops 2214592512 | bytes 12582912 | tf_op jit(solution)/shard_map/expert/pallas_call | solution.py:330
  86.8 9.1 %collective-permute-done.25 = bf16[64,2048]{1,0:T(8,128)(2,1)S(1)} collective-permute-done((bf16[64,2048]{1,0:T(8,128)(2,1)S(1)}, bf16[64,2048]{1,0:T(8,128)(2,1)S(1)}, u32[]{:S(2)}, u32[]{:S(2)}) %collective-permute-start.25) | collective-permute-done | bytes 262176 | tf_op jit(solution)/shard_map/ppermute | solution.py:341
  96.0 2.4 %collective-permute-start.26 = (bf16[64,2048]{1,0:T(8,128)(2,1)S(1)}, bf16[64,2048]{1,0:T(8,128)(2,1)S(1)}, u32[]{:S(2)}, u32[]{:S(2)}) collective-permute-start(bf16[64,2048]{1,0:T(8,128)(2,1)S(1)} %fusion), channel_id=1, source_target_pairs={{0,12},{1,13},{2,14},{3,15},{4,0},{5,1},{6,2},{7,3},{8,4},{9,5},{1... | collective-permute-start | bytes 786440 | tf_op jit(solution)/shard_map/ppermute | solution.py:370
  99.8 3.6 %collective-permute-done.26.two_ref = bf16[64,2048]{1,0:T(8,128)(2,1)S(1)} collective-permute-done((bf16[64,2048]{1,0:T(8,128)(2,1)S(1)}, bf16[64,2048]{1,0:T(8,128)(2,1)S(1)}, u32[]{:S(2)}, u32[]{:S(2)}) %collective-permute-start.26) | collective-permute-done | bytes 262176 | tf_op jit(solution)/shard_map/ppermute | solution.py:370
  103.4 2.3 %collective-permute-done.24.side_ref = bf16[64,2048]{1,0:T(8,128)(2,1)S(1)} collective-permute-done((bf16[64,2048]{1,0:T(8,128)(2,1)S(1)}, bf16[64,2048]{1,0:T(8,128)(2,1)S(1)}, u32[]{:S(2)}, u32[]{:S(2)}) %collective-permute-start.24) | collective-permute-done | bytes 262176 | tf_op jit(solution)/shard_map/ppermute | solution.py:369
  105.9 2.0 %collective-permute-start.27 = (bf16[64,1024]{1,0:T(8,128)(2,1)S(1)}, bf16[64,1024]{1,0:T(8,128)(2,1)S(1)}, u32[]{:S(2)}, u32[]{:S(2)}) collective-permute-start(bf16[64,1024]{1,0:T(8,128)(2,1)S(1)} %get-tuple-element.35), channel_id=1, source_target_pairs={{0,12},{1,13},{2,14},{3,15},{4,0},{5,1},{6,2},{7,3},{8,4},{9,5},{1... | collective-permute-start | bytes 393224 | tf_op jit(solution)/shard_map/ppermute | solution.py:341
  107.9 2.4 %collective-permute-start.28 = (bf16[64,1024]{1,0:T(8,128)(2,1)S(1)}, bf16[64,1024]{1,0:T(8,128)(2,1)S(1)}, u32[]{:S(2)}, u32[]{:S(2)}) collective-permute-start(bf16[64,1024]{1,0:T(8,128)(2,1)S(1)} %get-tuple-element.36), channel_id=1, source_target_pairs={{0,28},{1,29},{2,30},{3,31},{4,16},{5,17},{6,18},{7,19},{8,20},{9,... | collective-permute-start | bytes 393224 | tf_op jit(solution)/shard_map/ppermute | solution.py:341
  111.2 4.3 %collective-permute-done.28 = bf16[64,1024]{1,0:T(8,128)(2,1)S(1)} collective-permute-done((bf16[64,1024]{1,0:T(8,128)(2,1)S(1)}, bf16[64,1024]{1,0:T(8,128)(2,1)S(1)}, u32[]{:S(2)}, u32[]{:S(2)}) %collective-permute-start.28) | collective-permute-done | bytes 131104 | tf_op jit(solution)/shard_map/ppermute | solution.py:341
  (123 shorter events, 27.1 us)
Async XLA Ops:
  3.6 23.1 %all-to-all-start = ((bf16[16,16,1152]{2,1,0:T(8,128)(2,1)}), bf16[16,16,1152]{2,1,0:T(8,128)(2,1)S(1)}, u32[]{:S(2)}, u32[]{:S(2)}) async-start(bf16[16,16,1152]{2,1,0:T(8,128)(2,1)} %reshape.120), calls=%async_computation | async-start | bytes 1179648 | tf_op jit(solution)/shard_map/all_to_all | solution.py:246
  32.6 8.5 %collective-permute-start = (bf16[64,2048]{1,0:T(8,128)(2,1)}, bf16[64,2048]{1,0:T(8,128)(2,1)S(1)}, u32[]{:S(2)}, u32[]{:S(2)}) collective-permute-start(bf16[64,2048]{1,0:T(8,128)(2,1)} %attend_moved.1.refs_0_), channel_id=1, source_target_pairs={{0,16},{16,0},{1,17},{17,1},{2,18},{18,2},{3,19},{19,3},{4,20},{20... | collective-permute-start | bytes 786440 | tf_op jit(solution)/shard_map/ppermute | solution.py:302
  42.8 9.6 %collective-permute-start.7 = (bf16[64,2176]{1,0:T(8,128)(2,1)S(1)}, bf16[64,2176]{1,0:T(8,128)(2,1)S(1)}, u32[]{:S(2)}, u32[]{:S(2)}) collective-permute-start(bf16[64,2176]{1,0:T(8,128)(2,1)S(1)} %get-tuple-element.24.refs_1_), channel_id=1, source_target_pairs={{0,4},{1,5},{2,6},{3,7},{4,8},{5,9},{6,10},{7,11},{8,12},{9,13},{1... | collective-permute-start | bytes 835592 | tf_op jit(solution)/shard_map/ppermute | solution.py:352
  44.9 13.2 %collective-permute-start.1 = (bf16[64,2176]{1,0:T(8,128)(2,1)S(1)}, bf16[64,2176]{1,0:T(8,128)(2,1)S(1)}, u32[]{:S(2)}, u32[]{:S(2)}) collective-permute-start(bf16[64,2176]{1,0:T(8,128)(2,1)S(1)} %get-tuple-element.24.refs_1_), channel_id=1, source_target_pairs={{0,2},{1,3},{2,0},{3,1},{4,6},{5,7},{6,4},{7,5},{8,10},{9,11},{10,... | collective-permute-start | bytes 835592 | tf_op jit(solution)/shard_map/ppermute | solution.py:353
  52.3 8.6 %collective-permute-start.13 = (bf16[64,2176]{1,0:T(8,128)(2,1)S(1)}, bf16[64,2176]{1,0:T(8,128)(2,1)S(1)}, u32[]{:S(2)}, u32[]{:S(2)}) collective-permute-start(bf16[64,2176]{1,0:T(8,128)(2,1)S(1)} %collective-permute-done.7.refs_1_), channel_id=1, source_target_pairs={{0,4},{1,5},{2,6},{3,7},{4,8},{5,9},{6,10},{7,11},{8,12},{9,13},{1... | collective-permute-start | bytes 835592 | tf_op jit(solution)/shard_map/ppermute | solution.py:354
  53.3 8.8 %collective-permute-start.12 = (bf16[64,2176]{1,0:T(8,128)(2,1)S(1)}, bf16[64,2176]{1,0:T(8,128)(2,1)S(1)}, u32[]{:S(2)}, u32[]{:S(2)}) collective-permute-start(bf16[64,2176]{1,0:T(8,128)(2,1)S(1)} %collective-permute-done.7.refs_1_), channel_id=1, source_target_pairs={{0,16},{16,0},{1,17},{17,1},{2,18},{18,2},{3,19},{19,3},{4,20},{20... | collective-permute-start | bytes 835592 | tf_op jit(solution)/shard_map/ppermute | solution.py:356
  56.6 6.9 %collective-permute-start.8 = (bf16[64,2176]{1,0:T(8,128)(2,1)S(1)}, bf16[64,2176]{1,0:T(8,128)(2,1)S(1)}, u32[]{:S(2)}, u32[]{:S(2)}) collective-permute-start(bf16[64,2176]{1,0:T(8,128)(2,1)S(1)} %collective-permute-done.7.refs_1_), channel_id=1, source_target_pairs={{0,2},{1,3},{2,0},{3,1},{4,6},{5,7},{6,4},{7,5},{8,10},{9,11},{10,... | collective-permute-start | bytes 835592 | tf_op jit(solution)/shard_map/ppermute | solution.py:355
  58.1 6.9 %collective-permute-start.2 = (bf16[64,2176]{1,0:T(8,128)(2,1)S(1)}, bf16[64,2176]{1,0:T(8,128)(2,1)S(1)}, u32[]{:S(2)}, u32[]{:S(2)}) collective-permute-start(bf16[64,2176]{1,0:T(8,128)(2,1)S(1)} %collective-permute-done.1.refs_0_), channel_id=1, source_target_pairs={{0,1},{1,0},{2,3},{3,2},{4,5},{5,4},{6,7},{7,6},{8,9},{9,8},{10,11... | collective-permute-start | bytes 835592 | tf_op jit(solution)/shard_map/ppermute | solution.py:329
  62.1 9.6 %collective-permute-start.14 = (bf16[64,2176]{1,0:T(8,128)(2,1)S(1)}, bf16[64,2176]{1,0:T(8,128)(2,1)S(1)}, u32[]{:S(2)}, u32[]{:S(2)}) collective-permute-start(bf16[64,2176]{1,0:T(8,128)(2,1)S(1)} %collective-permute-done.12.refs_0_), channel_id=1, source_target_pairs={{0,1},{1,0},{2,3},{3,2},{4,5},{5,4},{6,7},{7,6},{8,9},{9,8},{10,11... | collective-permute-start | bytes 835592 | tf_op jit(solution)/shard_map/ppermute | solution.py:329
  63.6 8.3 %collective-permute-start.18 = (bf16[64,2176]{1,0:T(8,128)(2,1)S(1)}, bf16[64,2176]{1,0:T(8,128)(2,1)S(1)}, u32[]{:S(2)}, u32[]{:S(2)}) collective-permute-start(bf16[64,2176]{1,0:T(8,128)(2,1)S(1)} %collective-permute-done.8.refs_0_), channel_id=1, source_target_pairs={{0,16},{16,0},{1,17},{17,1},{2,18},{18,2},{3,19},{19,3},{4,20},{20... | collective-permute-start | bytes 835592 | tf_op jit(solution)/shard_map/ppermute | solution.py:358
  63.8 8.8 %collective-permute-start.19 = (bf16[64,2176]{1,0:T(8,128)(2,1)S(1)}, bf16[64,2176]{1,0:T(8,128)(2,1)S(1)}, u32[]{:S(2)}, u32[]{:S(2)}) collective-permute-start(bf16[64,2176]{1,0:T(8,128)(2,1)S(1)} %collective-permute-done.13.refs_1_), channel_id=1, source_target_pairs={{0,2},{1,3},{2,0},{3,1},{4,6},{5,7},{6,4},{7,5},{8,10},{9,11},{10,... | collective-permute-start | bytes 835592 | tf_op jit(solution)/shard_map/ppermute | solution.py:357
  64.9 10.3 %collective-permute-start.10 = (bf16[64,2176]{1,0:T(8,128)(2,1)S(1)}, bf16[64,2176]{1,0:T(8,128)(2,1)S(1)}, u32[]{:S(2)}, u32[]{:S(2)}) collective-permute-start(bf16[64,2176]{1,0:T(8,128)(2,1)S(1)} %collective-permute-done.7.refs_1_), channel_id=1, source_target_pairs={{0,1},{1,0},{2,3},{3,2},{4,5},{5,4},{6,7},{7,6},{8,9},{9,8},{10,11... | collective-permute-start | bytes 835592 | tf_op jit(solution)/shard_map/ppermute | solution.py:329
  65.0 10.9 %collective-permute-start.9 = (bf16[64,2176]{1,0:T(8,128)(2,1)S(1)}, bf16[64,2176]{1,0:T(8,128)(2,1)S(1)}, u32[]{:S(2)}, u32[]{:S(2)}) collective-permute-start(bf16[64,2176]{1,0:T(8,128)(2,1)S(1)} %collective-permute-done.8.refs_0_), channel_id=1, source_target_pairs={{0,1},{1,0},{2,3},{3,2},{4,5},{5,4},{6,7},{7,6},{8,9},{9,8},{10,11... | collective-permute-start | bytes 835592 | tf_op jit(solution)/shard_map/ppermute | solution.py:329
  71.7 10.1 %collective-permute-start.4 = (bf16[128,2048]{1,0:T(8,128)(2,1)S(1)}, bf16[128,2048]{1,0:T(8,128)(2,1)S(1)}, u32[]{:S(2)}, u32[]{:S(2)}) collective-permute-start(bf16[128,2048]{1,0:T(8,128)(2,1)S(1)} %get-tuple-element.26), channel_id=1, source_target_pairs={{0,1},{1,0},{2,3},{3,2},{4,5},{5,4},{6,7},{7,6},{8,9},{9,8},{10,11... | collective-permute-start | bytes 1572872 | tf_op jit(solution)/shard_map/ppermute | solution.py:338
  75.3 7.8 %collective-permute-start.16 = (bf16[128,2048]{1,0:T(8,128)(2,1)S(1)}, bf16[128,2048]{1,0:T(8,128)(2,1)S(1)}, u32[]{:S(2)}, u32[]{:S(2)}) collective-permute-start(bf16[128,2048]{1,0:T(8,128)(2,1)S(1)} %get-tuple-element.32), channel_id=1, source_target_pairs={{0,1},{1,0},{2,3},{3,2},{4,5},{5,4},{6,7},{7,6},{8,9},{9,8},{10,11... | collective-permute-start | bytes 1572872 | tf_op jit(solution)/shard_map/ppermute | solution.py:338
  78.5 7.5 %collective-permute-start.11 = (bf16[128,2048]{1,0:T(8,128)(2,1)S(1)}, bf16[128,2048]{1,0:T(8,128)(2,1)S(1)}, u32[]{:S(2)}, u32[]{:S(2)}) collective-permute-start(bf16[128,2048]{1,0:T(8,128)(2,1)S(1)} %get-tuple-element.30), channel_id=1, source_target_pairs={{0,1},{1,0},{2,3},{3,2},{4,5},{5,4},{6,7},{7,6},{8,9},{9,8},{10,11... | collective-permute-start | bytes 1572872 | tf_op jit(solution)/shard_map/ppermute | solution.py:338
  82.0 17.5 %collective-permute-start.5 = (bf16[64,2048]{1,0:T(8,128)(2,1)S(1)}, bf16[64,2048]{1,0:T(8,128)(2,1)S(1)}, u32[]{:S(2)}, u32[]{:S(2)}) collective-permute-start(bf16[64,2048]{1,0:T(8,128)(2,1)S(1)} %slice.63), channel_id=1, source_target_pairs={{0,2},{1,3},{2,0},{3,1},{4,6},{5,7},{6,4},{7,5},{8,10},{9,11},{10,... | collective-permute-start | bytes 786440 | tf_op jit(solution)/shard_map/ppermute | solution.py:367
  83.3 16.4 %collective-permute-start.17 = (bf16[64,2048]{1,0:T(8,128)(2,1)S(1)}, bf16[64,2048]{1,0:T(8,128)(2,1)S(1)}, u32[]{:S(2)}, u32[]{:S(2)}) collective-permute-start(bf16[64,2048]{1,0:T(8,128)(2,1)S(1)} %slice.62), channel_id=1, source_target_pairs={{0,16},{16,0},{1,17},{17,1},{2,18},{18,2},{3,19},{19,3},{4,20},{20... | collective-permute-start | bytes 786440 | tf_op jit(solution)/shard_map/ppermute | solution.py:366
  84.8 11.1 %collective-permute-start.25 = (bf16[64,2048]{1,0:T(8,128)(2,1)S(1)}, bf16[64,2048]{1,0:T(8,128)(2,1)S(1)}, u32[]{:S(2)}, u32[]{:S(2)}) collective-permute-start(bf16[64,2048]{1,0:T(8,128)(2,1)S(1)} %get-tuple-element.39), channel_id=1, source_target_pairs={{0,2},{1,3},{2,0},{3,1},{4,6},{5,7},{6,4},{7,5},{8,10},{9,11},{10,... | collective-permute-start | bytes 786440 | tf_op jit(solution)/shard_map/ppermute | solution.py:341
  86.1 12.2 %collective-permute-start.23 = (bf16[64,2048]{1,0:T(8,128)(2,1)S(1)}, bf16[64,2048]{1,0:T(8,128)(2,1)S(1)}, u32[]{:S(2)}, u32[]{:S(2)}) collective-permute-start(bf16[64,2048]{1,0:T(8,128)(2,1)S(1)} %get-tuple-element.40), channel_id=1, source_target_pairs={{0,16},{16,0},{1,17},{17,1},{2,18},{18,2},{3,19},{19,3},{4,20},{20... | collective-permute-start | bytes 786440 | tf_op jit(solution)/shard_map/ppermute | solution.py:364
  96.0 7.4 %collective-permute-start.26 = (bf16[64,2048]{1,0:T(8,128)(2,1)S(1)}, bf16[64,2048]{1,0:T(8,128)(2,1)S(1)}, u32[]{:S(2)}, u32[]{:S(2)}) collective-permute-start(bf16[64,2048]{1,0:T(8,128)(2,1)S(1)} %fusion), channel_id=1, source_target_pairs={{0,12},{1,13},{2,14},{3,15},{4,0},{5,1},{6,2},{7,3},{8,4},{9,5},{1... | collective-permute-start | bytes 786440 | tf_op jit(solution)/shard_map/ppermute | solution.py:370
  98.4 7.2 %collective-permute-start.24 = (bf16[64,2048]{1,0:T(8,128)(2,1)S(1)}, bf16[64,2048]{1,0:T(8,128)(2,1)S(1)}, u32[]{:S(2)}, u32[]{:S(2)}) collective-permute-start(bf16[64,2048]{1,0:T(8,128)(2,1)S(1)} %get-tuple-element.37), channel_id=1, source_target_pairs={{0,2},{1,3},{2,0},{3,1},{4,6},{5,7},{6,4},{7,5},{8,10},{9,11},{10,... | collective-permute-start | bytes 786440 | tf_op jit(solution)/shard_map/ppermute | solution.py:369
  99.6 10.7 %collective-permute-start.6 = (bf16[64,1024]{1,0:T(8,128)(2,1)S(1)}, bf16[64,1024]{1,0:T(8,128)(2,1)S(1)}, u32[]{:S(2)}, u32[]{:S(2)}) collective-permute-start(bf16[64,1024]{1,0:T(8,128)(2,1)S(1)} %get-tuple-element.28), channel_id=1, source_target_pairs={{0,16},{16,0},{1,17},{17,1},{2,18},{18,2},{3,19},{19,3},{4,20},{20... | collective-permute-start | bytes 393224 | tf_op jit(solution)/shard_map/ppermute | solution.py:387
  107.9 7.7 %collective-permute-start.28 = (bf16[64,1024]{1,0:T(8,128)(2,1)S(1)}, bf16[64,1024]{1,0:T(8,128)(2,1)S(1)}, u32[]{:S(2)}, u32[]{:S(2)}) collective-permute-start(bf16[64,1024]{1,0:T(8,128)(2,1)S(1)} %get-tuple-element.36), channel_id=1, source_target_pairs={{0,28},{1,29},{2,30},{3,31},{4,16},{5,17},{6,18},{7,19},{8,20},{9,... | collective-permute-start | bytes 393224 | tf_op jit(solution)/shard_map/ppermute | solution.py:341
  (25 other events, 193.2 us)

commit v2 on v1

--- a/solution.py
+++ b/solution.py
@@ -131,16 +131,16 @@
     return ref[:, pl.ds(pl.multiple_of(first, 128), columns)]
 
 
-def norm_kernel(experts, hidden_any, gain_ref, router_ref, ids_ref, *refs):
-    parts, (state_ref, packet_ref, hidden, whole, sem) = refs[:-5], refs[-5:]
-    copy = pltpu.make_async_copy(hidden_any, hidden, sem)
-    copy.start()
+def norm_kernel(experts, own_any, hidden_any, loaded_any, gain_ref, router_ref, ids_ref, *refs):
+    parts, (state_ref, packet_ref, own, hidden, whole, sems) = refs[:-6], refs[-6:]
+    got = fetch_all((own_any, hidden_any), (own, hidden), sems)
     rows, model = hidden.shape
     state = parts[0][...].astype(F32)
     for part in parts[1:]:
         state = state + part[...].astype(F32)
-    copy.wait()
-    state = state + hidden[...].astype(F32)
+    for copy in got:
+        copy.wait()
+    state = state + own[...].astype(F32) + hidden[...].astype(F32)
     whole[...] = state
     state_ref[...] = own_columns(whole, 0)
     square = jnp.mean(state * state, axis=1, keepdims=True)
@@ -165,10 +165,22 @@
     packet_ref[:, model:] = turned.astype(BF16)
 
 
-def expert_kernel(experts, *refs):
-    rows_refs, (gate_ref, up_ref, down_ref, near_ref, far_ref) = refs[:-5], refs[-5:]
+def load_kernel(after_any, gate_any, up_any, down_any, gate_ref, up_ref, down_ref, sems):
+    sources, targets = (gate_any, up_any, down_any), (gate_ref, up_ref, down_ref)
+    for copy in fetch_all(sources, targets, sems):
+        copy.wait()
+
+
+def pack_kernel(after_any, *refs):
+    out_ref = refs[-1]
+    count = refs[0].shape[0]
+    for at, ref in enumerate(refs[:-1]):
+        out_ref[at * count : (at + 1) * count, :] = ref[...]
+
+
+def expert_kernel(experts, here_ref, across_ref, gate_ref, up_ref, down_ref, near_ref, far_ref):
     model = gate_ref.shape[1]
-    packet = jnp.concatenate([ref[...] for ref in rows_refs], axis=0)
+    packet = jnp.concatenate([here_ref[...], across_ref[...]], axis=0)
     rows = packet[:, :model]
     extra = packet[:, model:].astype(F32)
     names = lax.broadcasted_iota(jnp.int32, extra.shape, 1)
@@ -184,17 +196,26 @@
     far_ref[...] = result[half:]
 
 
-def own_kernel(state_ref, own_ref, over_ref, base_ref, other_ref, whole):
-    whole[...] = own_ref[...] + over_ref[...].astype(F32)
-    base_ref[...] = state_ref[...] + own_columns(whole, 0)
-    other_ref[...] = own_columns(whole, 1).astype(BF16)
-
-
-def near_kernel(near_ref, far_ref, side_ref, two_ref, mine_ref, other_ref, whole):
-    total = near_ref[...] + far_ref[...].astype(F32)
-    whole[...] = total + side_ref[...].astype(F32) + two_ref[...].astype(F32)
-    mine_ref[...] = own_columns(whole, 0).astype(BF16)
-    other_ref[...] = own_columns(whole, 1).astype(BF16)
+def join_kernel(first, after_count, near_ref, back_ref, *refs):
+    out_refs = refs[after_count:]
+    count = out_refs[0].shape[0]
+    for at, ref in enumerate(out_refs, first):
+        rows = slice(at * count, (at + 1) * count)
+        ref[...] = (near_ref[rows, :].astype(F32) + back_ref[rows, :].astype(F32)).astype(ref.dtype)
+
+
+def own_kernel(state_ref, own_ref, base_ref, other_ref):
+    base_ref[...] = state_ref[...] + own_columns(own_ref, 0)
+    other_ref[...] = own_columns(own_ref, 1).astype(BF16)
+
+
+def sum_kernel(*refs):
+    parts, (mine_ref, other_ref) = refs[:-2], refs[-2:]
+    for shift, ref in ((0, mine_ref), (1, other_ref)):
+        total = own_columns(parts[0], shift).astype(F32)
+        for part in parts[1:]:
+            total = total + own_columns(part, shift).astype(F32)
+        ref[...] = total.astype(BF16)
 
 
 def local(
@@ -298,8 +319,19 @@
         cost_estimate=cost(query_rows * moved_bias.shape[1] * (padded + latent), 10 * 2**20),
         name="attend_moved",
     )(arrived, query, moved_bias, mixed, value_absorb, output_proj)
-    shares = [share]
-    shares += [lax.ppermute(share, "grp", turn(by)) for by in range(1, groups)]
+    shares = [lax.ppermute(share, "grp", turn(by)) for by in range(1, groups)]
+
+    held = [jnp.swapaxes(expert_gate[0], 0, 1), jnp.swapaxes(expert_up[0], 0, 1), expert_down[0]]
+    gate_rows, up_rows, down_rows = pl.pallas_call(
+        load_kernel,
+        out_shape=[jax.ShapeDtypeStruct(array.shape, BF16) for array in held],
+        in_specs=[ANY] * 4,
+        out_specs=[WHOLE] * 3,
+        scratch_shapes=[pltpu.SemaphoreType.DMA((3,))],
+        compiler_params=pltpu.CompilerParams(vmem_limit_bytes=44 * 2**20),
+        cost_estimate=cost(0, 12 * 2**20),
+        name="load",
+    )(share, *held)
 
     extra = -(-2 * experts // 128) * 128
     columns = model // groups
@@ -309,33 +341,49 @@
             jax.ShapeDtypeStruct((row_count, columns), F32),
             jax.ShapeDtypeStruct((row_count, model + extra), BF16),
         ),
-        in_specs=[ANY] + [WHOLE] * (3 + groups),
+        in_specs=[ANY] * 3 + [WHOLE] * (2 + groups),
         scratch_shapes=[
             VMEM((row_count, model), BF16),
+            VMEM((row_count, model), BF16),
             VMEM((row_count, model), F32),
-            pltpu.SemaphoreType.DMA(()),
+            pltpu.SemaphoreType.DMA((2,)),
         ],
         compiler_params=pltpu.CompilerParams(vmem_limit_bytes=16 * 2**20),
         cost_estimate=cost(row_count * model * 128, 4 * 2**20),
         name="norm",
-    )(hidden_in, norm_gain[None, :], router_proj.T, expert_ids.T, *shares)
-
-    gate_rows = jnp.swapaxes(expert_gate[0], 0, 1)
-    up_rows = jnp.swapaxes(expert_up[0], 0, 1)
-
-    def run_expert(rows):
+    )(share, hidden_in, down_rows, norm_gain[None, :], router_proj.T, expert_ids.T, *shares)
+
+    def run_expert(rows, after):
         half = len(rows) * row_count
         out = jax.ShapeDtypeStruct((half, model), BF16)
-        across = [lax.ppermute(part, "ep", core_swap) for part in rows]
+        here = pl.pallas_call(
+            pack_kernel,
+            out_shape=jax.ShapeDtypeStruct((half, model + extra), BF16),
+            in_specs=[ANY] + [WHOLE] * len(rows),
+            compiler_params=pltpu.CompilerParams(vmem_limit_bytes=16 * 2**20),
+            cost_estimate=cost(0, 2 * half * model * 2),
+            name="pack",
+        )(after, *rows)
+        across = lax.ppermute(here, "ep", core_swap)
         near, far = pl.pallas_call(
             functools.partial(expert_kernel, experts),
             out_shape=(out, out),
-            in_specs=[WHOLE] * (2 * len(rows) + 3),
-            compiler_params=pltpu.CompilerParams(vmem_limit_bytes=16 * 2**20),
+            in_specs=[WHOLE] * 5,
+            compiler_params=pltpu.CompilerParams(vmem_limit_bytes=24 * 2**20),
             cost_estimate=cost(6 * half * model * gate_rows.shape[0], 12 * 2**20),
             name="expert",
-        )(*rows, *across, gate_rows, up_rows, expert_down[0])
-        return near.astype(F32) + lax.ppermute(far, "ep", core_swap).astype(F32)
+        )(here, across, gate_rows, up_rows, down_rows)
+        return near, lax.ppermute(far, "ep", core_swap)
+
+    def join(near, back, types, first=0, after=()):
+        return pl.pallas_call(
+            functools.partial(join_kernel, first, len(after)),
+            out_shape=[jax.ShapeDtypeStruct((row_count, model), kind) for kind in types],
+            in_specs=[WHOLE] * 2 + [ANY] * len(after),
+            compiler_params=pltpu.CompilerParams(vmem_limit_bytes=16 * 2**20),
+            cost_estimate=cost(row_count * model, 2**20),
+            name="join",
+        )(near, back, *after)
 
     def send(value, axes, pairs):
         return lax.ppermute(value.astype(BF16), axes, pairs).astype(F32)
@@ -356,18 +404,20 @@
         far = lax.ppermute(near, "grp", plane_swap)
         two_side = lax.ppermute(two, "ep", side_swap)
         far_side = lax.ppermute(near_side, "grp", plane_swap)
-        cut = row_count
-        own_sum = run_expert([side, packet])
-        near_sum = run_expert([near_side, near])
-        ahead_sum = run_expert([far, two])
-        ahead_side = run_expert([far_side, two_side])
-        far_side_in = lax.ppermute(ahead_side[:cut].astype(BF16), "grp", plane_swap)
-        two_side_in = send(ahead_side[cut:], "ep", side_swap)
-        far_in = lax.ppermute(ahead_sum[:cut].astype(BF16), "grp", plane_swap)
-        own_in = lax.ppermute(own_sum[:cut].astype(BF16), "ep", side_swap)
-        near_side = near_sum[:cut] + far_side_in.astype(F32)
-        near_side_in = lax.ppermute(near_side.astype(BF16), "ep", side_swap)
-        two_in = lax.ppermute((ahead_sum[cut:] + two_side_in).astype(BF16), both_axes, backward)
+        early = run_expert([packet, side, near], packet)
+        later = run_expert([near_side, two, far], early[0])
+        last = run_expert([far_side, two_side], later[0])
+        own_sum, side_sum, near_sum = join(*early, [F32, BF16, F32])
+        near_side_sum, two_sum = join(*later, [F32, F32])
+        far_side_sum, two_side_sum = join(*last, [BF16, BF16])
+        far_side_in = lax.ppermute(far_side_sum, "grp", plane_swap)
+        two_side_in = lax.ppermute(two_side_sum, "ep", side_swap)
+        [near_side_sum] = join(near_side_sum, far_side_in, [BF16])
+        [two_sum] = join(two_sum, two_side_in, [BF16])
+        near_side_in = lax.ppermute(near_side_sum, "ep", side_swap)
+        two_in = lax.ppermute(two_sum, both_axes, backward)
+        [far_sum] = join(*later, [BF16], 2, [far_side_in])
+        far_in = lax.ppermute(far_sum, "grp", plane_swap)
         part = (row_count, columns)
 
         def by_columns(kernel, first_type, *operands):
@@ -377,18 +427,25 @@
                     jax.ShapeDtypeStruct(part, first_type),
                     jax.ShapeDtypeStruct(part, BF16),
                 ),
-                scratch_shapes=[VMEM((row_count, model), F32)],
                 compiler_params=pltpu.CompilerParams(vmem_limit_bytes=16 * 2**20),
                 cost_estimate=cost(row_count * model, 2**20),
                 name=kernel.__name__,
             )(*operands)
 
-        base, own_other = by_columns(own_kernel, F32, state, own_sum[cut:], own_in)
-        own_over = lax.ppermute(own_other, "grp", plane_swap)
-        mine, other = by_columns(near_kernel, BF16, near_sum[cut:], far_in, near_side_in, two_in)
-        crossed = [(source, (target + ranks) % (2 * ranks)) for source, target in backward]
-        result = base + own_over.astype(F32)
-        result = result + send(mine, both_axes, backward) + send(other, both_axes, crossed)
+        def crossed(pairs):
+            return [(source, (target + ranks) % (2 * ranks)) for source, target in pairs]
+
+        sideways = [(i, i ^ 2) for i in range(2 * ranks)]
+        base, own_other = by_columns(own_kernel, F32, state, own_sum)
+        side_mine, side_other = by_columns(sum_kernel, BF16, side_sum)
+        near_mine, near_other = by_columns(
+            sum_kernel, BF16, near_sum, far_in, near_side_in, two_in
+        )
+        result = base + send(own_other, "grp", plane_swap)
+        result = result + send(side_mine, both_axes, sideways)
+        result = result + send(side_other, both_axes, crossed(sideways))
+        result = result + send(near_mine, both_axes, backward)
+        result = result + send(near_other, both_axes, crossed(backward))
         return result.astype(BF16)
 
     line = [packet]
@@ -396,8 +453,9 @@
         line.append(lax.ppermute(line[-1], "ep", ring_next))
     totals = []
     for part in line:
-        both = run_expert([lax.ppermute(part, "ep", side_swap), part])
-        totals.append(both[row_count:] + send(both[:row_count], "ep", side_swap))
+        sums = run_expert([lax.ppermute(part, "ep", side_swap), part], packet)
+        over, here = join(*sums, [BF16, F32])
+        totals.append(here + send(over, "ep", side_swap))
     moving = totals[1 % ring]
     for hop in list(range(2, ring)) + [0]:
         moving = totals[hop] + send(moving, "ep", ring_next)

time: 117 us -> 113 us (0.966)
  starting transfers between devices: 34.3 us -> 29.8 us
  Pallas kernels: 19.3 us -> 23.2 us
  local copies, waits for them, and re-layouts: 10.1 us -> 6.39 us
    ppermute x3 -> x5, waiting for transfers between devices: 14.4 us -> 4.9 us  [send(): return lax.ppermute(value.astype(BF16), axes, pairs).astype(F32)]
    ppermute x19 -> x12, waiting for transfers between devices: 12.9 us -> 18.7 us  [the longest x1 7.3 us: local(): two_side_in = lax.ppermute(two_side_sum, 'ep', side_swap)]
    ppermute x19 -> x12, starting transfers between devices: 11.1 us -> 5.92 us  [the longest x1 1.8 us: local(): two_in = lax.ppermute(two_sum, both_axes, backward)]
    pallas_call x0 -> x10, Pallas kernels: none -> 4.3 us  [the longest x1 3.6 us: local(): pl.pallas_call(load_kernel, out_shape=[jax.ShapeDtypeStruct(array.shape,...]
    unnamed x38 -> x30, local copies, waits for them, and re-layouts: 7.37 us -> 3.8 us
    ppermute x3 -> x5, starting transfers between devices: 5.55 us -> 8.56 us  [send(): return lax.ppermute(value.astype(BF16), axes, pairs).astype(F32)]
    ppermute x1, waiting for transfers between devices: 0.31 us -> 2.87 us  [local(): two_side = lax.ppermute(two, 'ep', side_swap)]
    ppermute x1, starting transfers between devices: 3.37 us -> 1.64 us  [local(): far = lax.ppermute(near, 'grp', plane_swap)]
  transfers between devices with their start and end apart: 30 -> 25, of which waited for: 12 -> 18; matrix products, arithmetic and copies ran while one was open for 2% -> 2% of each run, Pallas kernels for 12% -> 13%
where the time goes in v2:
time: 113 us; the launch traced here: 112 us
  waiting for transfers between devices  48.7 us (43%)
  starting transfers between devices  29.8 us (26%)
  Pallas kernels  23.2 us (21%)
  local copies, waits for them, and re-layouts  6.39 us (6%)
  other arithmetic  2.19 us (2%)
  matrix products  1.79 us (2%)
    pallas_call x3, Pallas kernels, run_expert(): pl.pallas_call(functools.partial(expert_kernel, experts), out_shape=(out,...  10.3 us
    all_to_all x1, waiting for transfers between devices, local(): lax.all_to_all(outgoing, 'ep', split_axis=0, concat_axis=0, tiled=True)  8.67 us
    ppermute x5, starting transfers between devices, send(): return lax.ppermute(value.astype(BF16), axes, pairs).astype(F32)  8.56 us
    all_to_all x1, starting transfers between devices, local(): lax.all_to_all(outgoing, 'ep', split_axis=0, concat_axis=0, tiled=True)  7.36 us
    ppermute x1, waiting for transfers between devices, local(): two_side_in = lax.ppermute(two_side_sum, 'ep', side_swap)  7.3 us
    ppermute x1, waiting for transfers between devices, local(): near = lax.ppermute(packet, both_axes, onward)  6.55 us
    pallas_call x1, Pallas kernels, local(): pl.pallas_call(functools.partial(moved_kernel, dims), out_shape=jax.Shape...  4.97 us
    ppermute x5, waiting for transfers between devices, send(): return lax.ppermute(value.astype(BF16), axes, pairs).astype(F32)  4.9 us
  transfers between devices with their start and end apart: 25, of which 18 were waited for; matrix products, arithmetic and copies ran while one was open for 2% of the time, Pallas kernels for 13%

profile of v2, /device:TPU:0, one launch (start us, length us, event | category | flops | bytes accessed | tf_op | source)
XLA Modules:
  0.0 112.4 jit_solution(16586241016195694947)
XLA Ops:
  0.9 1.8 %convolution_convert_fusion = bf16[32,9216]{1,0:T(8,128)(2,1)S(1)} fusion(bf16[64,9216]{1,0:T(8,128)(2,1)} %cache.1, s32[32]{0:T(128)S(1)} %min.20), kind=kOutput, calls=%fused_computation | convolution fusion | flops 38045696 | bytes 1769600 | tf_op jit(solution)/shard_map/dot_general | solution.py:19
  3.8 7.4 %all-to-all-start = ((bf16[16,16,1152]{2,1,0:T(8,128)(2,1)}), bf16[16,16,1152]{2,1,0:T(8,128)(2,1)S(1)}, u32[]{:S(2)}, u32[]{:S(2)}) async-start(bf16[16,16,1152]{2,1,0:T(8,128)(2,1)} %reshape.120), calls=%async_computation | async-start | bytes 1179648 | tf_op jit(solution)/shard_map/all_to_all | solution.py:267
  13.4 2.7 %attend_resident.1 = (bf16[512,640]{1,0:T(8,128)(2,1)S(1)}, f32[512,640]{1,0:T(8,128)S(1)}) custom-call(bf16[64,1024]{1,0:T(8,128)(2,1)S(1)} %copy-done.8, bf16[64,512]{1,0:T(8,128)(2,1)S(1)} %copy-done.10, bf16[16,2304]{1,0:T(8,128)(2,1)S(1)} %copy-done.9, bf16[64,9216]{1,0:T(8,128)(2,1)S(1)} %copy-done.2, bf16[8,128,512]{2,1,0:T(8,128)(2,1)S(1)} %copy-done.7, ...), custom_call_target="tpu_custom_call" | custom-call | flops 1283457024 | bytes 8388608 | tf_op jit(solution)/shard_map/attend_resident/pallas_call | solution.py:292
  18.1 8.7 %all-to-all-done.moved_any = bf16[16,16,1152]{2,1,0:T(8,128)(2,1)S(1)} async-done(((bf16[16,16,1152]{2,1,0:T(8,128)(2,1)}), bf16[16,16,1152]{2,1,0:T(8,128)(2,1)S(1)}, u32[]{:S(2)}, u32[]{:S(2)}) %all-to-all-start) | async-done | bytes 589856 | tf_op jit(solution)/shard_map/all_to_all | solution.py:267
  27.6 5.0 %attend_moved.1.after_any.own_any = bf16[64,2048]{1,0:T(8,128)(2,1)} custom-call(bf16[16,16,1152]{2,1,0:T(8,128)(2,1)} %copy-done.11, bf16[512,640]{1,0:T(8,128)(2,1)} %copy-done.3, f32[64,512]{1,0:T(8,128)} %reshape.123.bias_any, f32[512,640]{1,0:T(8,128)} %copy-done.1, bf16[8,512,128]{2,1,0:T(8,128)(2,1)} %value_any.1, bf16[1024,2048]{1,0:T(8,128)(2,1)} %proj_any.1), custom_call_target="tpu_custom_call" | custom-call | flops 603979776 | bytes 10485760 | tf_op jit(solution)/shard_map/attend_moved/pallas_call | solution.py:303
  35.1 3.6 %load.1 = (bf16[704,2048]{1,0:T(8,128)(2,1)S(1)}, bf16[704,2048]{1,0:T(8,128)(2,1)S(1)}, bf16[704,2048]{1,0:T(8,128)(2,1)S(1)}) custom-call(bf16[64,2048]{1,0:T(8,128)(2,1)S(1)} %copy-done, bf16[704,2048]{1,0:T(8,128)(2,1)} %bitcast.16, bf16[704,2048]{1,0:T(8,128)(2,1)} %bitcast.17, bf16[704,2048]{1,0:T(8,128)(2,1)} %bitcast.18), custom_call_target="tpu_custom_call" | custom-call | bytes 12582912 | tf_op jit(solution)/shard_map/load/pallas_call | solution.py:325
  38.7 2.3 %collective-permute-done.refs_0_ = bf16[64,2048]{1,0:T(8,128)(2,1)S(1)} collective-permute-done((bf16[64,2048]{1,0:T(8,128)(2,1)}, bf16[64,2048]{1,0:T(8,128)(2,1)S(1)}, u32[]{:S(2)}, u32[]{:S(2)}) %collective-permute-start) | collective-permute-done | bytes 262176 | tf_op jit(solution)/shard_map/ppermute | solution.py:322
  41.8 2.1 %collective-permute-start.2 = (bf16[64,2176]{1,0:T(8,128)(2,1)S(1)}, bf16[64,2176]{1,0:T(8,128)(2,1)S(1)}, u32[]{:S(2)}, u32[]{:S(2)}) collective-permute-start(bf16[64,2176]{1,0:T(8,128)(2,1)S(1)} %get-tuple-element.35.after_any.refs_0_), channel_id=1, source_target_pairs={{0,4},{1,5},{2,6},{3,7},{4,8},{5,9},{6,10},{7,11},{8,12},{9,13},{1... | collective-permute-start | bytes 835592 | tf_op jit(solution)/shard_map/ppermute | solution.py:400
  44.8 6.6 %collective-permute-done.2.refs_2_ = bf16[64,2176]{1,0:T(8,128)(2,1)S(1)} collective-permute-done((bf16[64,2176]{1,0:T(8,128)(2,1)S(1)}, bf16[64,2176]{1,0:T(8,128)(2,1)S(1)}, u32[]{:S(2)}, u32[]{:S(2)}) %collective-permute-start.2) | collective-permute-done | bytes 278560 | tf_op jit(solution)/shard_map/ppermute | solution.py:400
  55.2 3.8 %expert.3 = (bf16[192,2048]{1,0:T(8,128)(2,1)S(1)}, bf16[192,2048]{1,0:T(8,128)(2,1)S(1)}) custom-call(bf16[192,2176]{1,0:T(8,128)(2,1)S(1)} %pack.3.here_ref, bf16[192,2176]{1,0:T(8,128)(2,1)S(1)} %collective-permute-done.3.across_ref, bf16[704,2048]{1,0:T(8,128)(2,1)S(1)} %get-tuple-element.36.gate_ref, bf16[704,2048]{1,0:T(8,128)(2,1)S(1)} %get-tuple-element.37.up_ref, ...), custom_call_target="tpu_custom_call" | custom-call | flops 3321888768 | bytes 12582912 | tf_op jit(solution)/shard_map/expert/pallas_call | solution.py:368
  59.1 2.1 %collective-permute-done.10.refs_2_ = bf16[64,2176]{1,0:T(8,128)(2,1)S(1)} collective-permute-done((bf16[64,2176]{1,0:T(8,128)(2,1)S(1)}, bf16[64,2176]{1,0:T(8,128)(2,1)S(1)}, u32[]{:S(2)}, u32[]{:S(2)}) %collective-permute-start.10) | collective-permute-done | bytes 278560 | tf_op jit(solution)/shard_map/ppermute | solution.py:404
  61.2 3.1 %collective-permute-done.9.refs_1_ = bf16[64,2176]{1,0:T(8,128)(2,1)S(1)} collective-permute-done((bf16[64,2176]{1,0:T(8,128)(2,1)S(1)}, bf16[64,2176]{1,0:T(8,128)(2,1)S(1)}, u32[]{:S(2)}, u32[]{:S(2)}) %collective-permute-start.9) | collective-permute-done | bytes 278560 | tf_op jit(solution)/shard_map/ppermute | solution.py:402
  66.8 3.9 %expert.4 = (bf16[192,2048]{1,0:T(8,128)(2,1)S(1)}, bf16[192,2048]{1,0:T(8,128)(2,1)S(1)}) custom-call(bf16[192,2176]{1,0:T(8,128)(2,1)S(1)} %pack.4.here_ref, bf16[192,2176]{1,0:T(8,128)(2,1)S(1)} %collective-permute-done.11.across_ref, bf16[704,2048]{1,0:T(8,128)(2,1)S(1)} %get-tuple-element.36.gate_ref, bf16[704,2048]{1,0:T(8,128)(2,1)S(1)} %get-tuple-element.37.up_ref, ...), custom_call_target="tpu_custom_call" | custom-call | flops 3321888768 | bytes 12582912 | tf_op jit(solution)/shard_map/expert/pallas_call | solution.py:368
  70.6 2.9 %collective-permute-done.14.refs_1_ = bf16[64,2176]{1,0:T(8,128)(2,1)S(1)} collective-permute-done((bf16[64,2176]{1,0:T(8,128)(2,1)S(1)}, bf16[64,2176]{1,0:T(8,128)(2,1)S(1)}, u32[]{:S(2)}, u32[]{:S(2)}) %collective-permute-start.14) | collective-permute-done | bytes 278560 | tf_op jit(solution)/shard_map/ppermute | solution.py:405
  74.8 1.9 %collective-permute-done.15.across_ref = bf16[128,2176]{1,0:T(8,128)(2,1)S(1)} collective-permute-done((bf16[128,2176]{1,0:T(8,128)(2,1)S(1)}, bf16[128,2176]{1,0:T(8,128)(2,1)S(1)}, u32[]{:S(2)}, u32[]{:S(2)}) %collective-permute-start.15) | collective-permute-done | bytes 557088 | tf_op jit(solution)/shard_map/ppermute | solution.py:367
  76.7 2.6 %expert.5 = (bf16[128,2048]{1,0:T(8,128)(2,1)S(1)}, bf16[128,2048]{1,0:T(8,128)(2,1)S(1)}) custom-call(bf16[128,2176]{1,0:T(8,128)(2,1)S(1)} %pack.5.here_ref, bf16[128,2176]{1,0:T(8,128)(2,1)S(1)} %collective-permute-done.15.across_ref, bf16[704,2048]{1,0:T(8,128)(2,1)S(1)} %get-tuple-element.36.gate_ref, bf16[704,2048]{1,0:T(8,128)(2,1)S(1)} %get-tuple-element.37.up_ref, ...), custom_call_target="tpu_custom_call" | custom-call | flops 2214592512 | bytes 12582912 | tf_op jit(solution)/shard_map/expert/pallas_call | solution.py:368
  82.6 7.3 %collective-permute-done.20.back_ref = bf16[64,2048]{1,0:T(8,128)(2,1)S(1)} collective-permute-done((bf16[64,2048]{1,0:T(8,128)(2,1)S(1)}, bf16[64,2048]{1,0:T(8,128)(2,1)S(1)}, u32[]{:S(2)}, u32[]{:S(2)}) %collective-permute-start.20) | collective-permute-done | bytes 262176 | tf_op jit(solution)/shard_map/ppermute | solution.py:414
  89.9 1.8 %collective-permute-start.21 = (bf16[64,2048]{1,0:T(8,128)(2,1)S(1)}, bf16[64,2048]{1,0:T(8,128)(2,1)S(1)}, u32[]{:S(2)}, u32[]{:S(2)}) collective-permute-start(bf16[64,2048]{1,0:T(8,128)(2,1)S(1)} %join.11), channel_id=1, source_target_pairs={{0,12},{1,13},{2,14},{3,15},{4,0},{5,1},{6,2},{7,3},{8,4},{9,5},{1... | collective-permute-start | bytes 786440 | tf_op jit(solution)/shard_map/ppermute | solution.py:418
  92.8 2.1 %collective-permute-start.5 = (bf16[64,1024]{1,0:T(8,128)(2,1)S(1)}, bf16[64,1024]{1,0:T(8,128)(2,1)S(1)}, u32[]{:S(2)}, u32[]{:S(2)}) collective-permute-start(bf16[64,1024]{1,0:T(8,128)(2,1)S(1)} %get-tuple-element.42), channel_id=1, source_target_pairs={{0,16},{16,0},{1,17},{17,1},{2,18},{18,2},{3,19},{19,3},{4,20},{20... | collective-permute-start | bytes 393224 | tf_op jit(solution)/shard_map/ppermute | solution.py:389
  97.5 2.1 %collective-permute-start.7 = (bf16[64,1024]{1,0:T(8,128)(2,1)S(1)}, bf16[64,1024]{1,0:T(8,128)(2,1)S(1)}, u32[]{:S(2)}, u32[]{:S(2)}) collective-permute-start(bf16[64,1024]{1,0:T(8,128)(2,1)S(1)} %get-tuple-element.45), channel_id=1, source_target_pairs={{0,18},{1,19},{2,16},{3,17},{4,22},{5,23},{6,20},{7,21},{8,26},{9,... | collective-permute-start | bytes 393224 | tf_op jit(solution)/shard_map/ppermute | solution.py:389
  100.9 2.8 %collective-permute-done.18.refs_1_ = bf16[64,2048]{1,0:T(8,128)(2,1)S(1)} collective-permute-done((bf16[64,2048]{1,0:T(8,128)(2,1)S(1)}, bf16[64,2048]{1,0:T(8,128)(2,1)S(1)}, u32[]{:S(2)}, u32[]{:S(2)}) %collective-permute-start.18) | collective-permute-done | bytes 262176 | tf_op jit(solution)/shard_map/ppermute | solution.py:420
  103.9 2.8 %collective-permute-start.23 = (bf16[64,1024]{1,0:T(8,128)(2,1)S(1)}, bf16[64,1024]{1,0:T(8,128)(2,1)S(1)}, u32[]{:S(2)}, u32[]{:S(2)}) collective-permute-start(bf16[64,1024]{1,0:T(8,128)(2,1)S(1)} %get-tuple-element.56), channel_id=1, source_target_pairs={{0,28},{1,29},{2,30},{3,31},{4,16},{5,17},{6,18},{7,19},{8,20},{9,... | collective-permute-start | bytes 393224 | tf_op jit(solution)/shard_map/ppermute | solution.py:389
  106.7 2.1 %collective-permute-done.22 = bf16[64,1024]{1,0:T(8,128)(2,1)S(1)} collective-permute-done((bf16[64,1024]{1,0:T(8,128)(2,1)S(1)}, bf16[64,1024]{1,0:T(8,128)(2,1)S(1)}, u32[]{:S(2)}, u32[]{:S(2)}) %collective-permute-start.22) | collective-permute-done | bytes 131104 | tf_op jit(solution)/shard_map/ppermute | solution.py:389
  108.9 2.8 %collective-permute-done.23 = bf16[64,1024]{1,0:T(8,128)(2,1)S(1)} collective-permute-done((bf16[64,1024]{1,0:T(8,128)(2,1)S(1)}, bf16[64,1024]{1,0:T(8,128)(2,1)S(1)}, u32[]{:S(2)}, u32[]{:S(2)}) %collective-permute-start.23) | collective-permute-done | bytes 131104 | tf_op jit(solution)/shard_map/ppermute | solution.py:389
  (105 shorter events, 27.8 us)
Async XLA Ops:
  3.8 22.9 %all-to-all-start = ((bf16[16,16,1152]{2,1,0:T(8,128)(2,1)}), bf16[16,16,1152]{2,1,0:T(8,128)(2,1)S(1)}, u32[]{:S(2)}, u32[]{:S(2)}) async-start(bf16[16,16,1152]{2,1,0:T(8,128)(2,1)} %reshape.120), calls=%async_computation | async-start | bytes 1179648 | tf_op jit(solution)/shard_map/all_to_all | solution.py:267
  32.5 8.5 %collective-permute-start = (bf16[64,2048]{1,0:T(8,128)(2,1)}, bf16[64,2048]{1,0:T(8,128)(2,1)S(1)}, u32[]{:S(2)}, u32[]{:S(2)}) collective-permute-start(bf16[64,2048]{1,0:T(8,128)(2,1)} %attend_moved.1.after_any.own_any), channel_id=1, source_target_pairs={{0,16},{16,0},{1,17},{17,1},{2,18},{18,2},{3,19},{19,3},{4,20},{20... | collective-permute-start | bytes 786440 | tf_op jit(solution)/shard_map/ppermute | solution.py:322
  41.8 9.6 %collective-permute-start.2 = (bf16[64,2176]{1,0:T(8,128)(2,1)S(1)}, bf16[64,2176]{1,0:T(8,128)(2,1)S(1)}, u32[]{:S(2)}, u32[]{:S(2)}) collective-permute-start(bf16[64,2176]{1,0:T(8,128)(2,1)S(1)} %get-tuple-element.35.after_any.refs_0_), channel_id=1, source_target_pairs={{0,4},{1,5},{2,6},{3,7},{4,8},{5,9},{6,10},{7,11},{8,12},{9,13},{1... | collective-permute-start | bytes 835592 | tf_op jit(solution)/shard_map/ppermute | solution.py:400
  43.8 8.1 %collective-permute-start.1 = (bf16[64,2176]{1,0:T(8,128)(2,1)S(1)}, bf16[64,2176]{1,0:T(8,128)(2,1)S(1)}, u32[]{:S(2)}, u32[]{:S(2)}) collective-permute-start(bf16[64,2176]{1,0:T(8,128)(2,1)S(1)} %get-tuple-element.35.after_any.refs_0_), channel_id=1, source_target_pairs={{0,2},{1,3},{2,0},{3,1},{4,6},{5,7},{6,4},{7,5},{8,10},{9,11},{10,... | collective-permute-start | bytes 835592 | tf_op jit(solution)/shard_map/ppermute | solution.py:401
  52.0 3.2 %collective-permute-start.3 = (bf16[192,2176]{1,0:T(8,128)(2,1)S(1)}, bf16[192,2176]{1,0:T(8,128)(2,1)S(1)}, u32[]{:S(2)}, u32[]{:S(2)}) collective-permute-start(bf16[192,2176]{1,0:T(8,128)(2,1)S(1)} %pack.3.here_ref), channel_id=1, source_target_pairs={{0,1},{1,0},{2,3},{3,2},{4,5},{5,4},{6,7},{7,6},{8,9},{9,8},{10,11... | collective-permute-start | bytes 2506760 | tf_op jit(solution)/shard_map/ppermute | solution.py:367
  52.1 9.1 %collective-permute-start.10 = (bf16[64,2176]{1,0:T(8,128)(2,1)S(1)}, bf16[64,2176]{1,0:T(8,128)(2,1)S(1)}, u32[]{:S(2)}, u32[]{:S(2)}) collective-permute-start(bf16[64,2176]{1,0:T(8,128)(2,1)S(1)} %collective-permute-done.2.refs_2_), channel_id=1, source_target_pairs={{0,16},{16,0},{1,17},{17,1},{2,18},{18,2},{3,19},{19,3},{4,20},{20... | collective-permute-start | bytes 835592 | tf_op jit(solution)/shard_map/ppermute | solution.py:404
  53.7 10.5 %collective-permute-start.9 = (bf16[64,2176]{1,0:T(8,128)(2,1)S(1)}, bf16[64,2176]{1,0:T(8,128)(2,1)S(1)}, u32[]{:S(2)}, u32[]{:S(2)}) collective-permute-start(bf16[64,2176]{1,0:T(8,128)(2,1)S(1)} %collective-permute-done.2.refs_2_), channel_id=1, source_target_pairs={{0,4},{1,5},{2,6},{3,7},{4,8},{5,9},{6,10},{7,11},{8,12},{9,13},{1... | collective-permute-start | bytes 835592 | tf_op jit(solution)/shard_map/ppermute | solution.py:402
  54.0 10.2 %collective-permute-start.8 = (bf16[64,2176]{1,0:T(8,128)(2,1)S(1)}, bf16[64,2176]{1,0:T(8,128)(2,1)S(1)}, u32[]{:S(2)}, u32[]{:S(2)}) collective-permute-start(bf16[64,2176]{1,0:T(8,128)(2,1)S(1)} %collective-permute-done.2.refs_2_), channel_id=1, source_target_pairs={{0,2},{1,3},{2,0},{3,1},{4,6},{5,7},{6,4},{7,5},{8,10},{9,11},{10,... | collective-permute-start | bytes 835592 | tf_op jit(solution)/shard_map/ppermute | solution.py:403
  64.3 2.4 %collective-permute-start.11 = (bf16[192,2176]{1,0:T(8,128)(2,1)S(1)}, bf16[192,2176]{1,0:T(8,128)(2,1)S(1)}, u32[]{:S(2)}, u32[]{:S(2)}) collective-permute-start(bf16[192,2176]{1,0:T(8,128)(2,1)S(1)} %pack.4.here_ref), channel_id=1, source_target_pairs={{0,1},{1,0},{2,3},{3,2},{4,5},{5,4},{6,7},{7,6},{8,9},{9,8},{10,11... | collective-permute-start | bytes 2506760 | tf_op jit(solution)/shard_map/ppermute | solution.py:367
  64.4 9.1 %collective-permute-start.14 = (bf16[64,2176]{1,0:T(8,128)(2,1)S(1)}, bf16[64,2176]{1,0:T(8,128)(2,1)S(1)}, u32[]{:S(2)}, u32[]{:S(2)}) collective-permute-start(bf16[64,2176]{1,0:T(8,128)(2,1)S(1)} %collective-permute-done.9.refs_1_), channel_id=1, source_target_pairs={{0,2},{1,3},{2,0},{3,1},{4,6},{5,7},{6,4},{7,5},{8,10},{9,11},{10,... | collective-permute-start | bytes 835592 | tf_op jit(solution)/shard_map/ppermute | solution.py:405
  65.9 8.7 %collective-permute-start.13 = (bf16[64,2176]{1,0:T(8,128)(2,1)S(1)}, bf16[64,2176]{1,0:T(8,128)(2,1)S(1)}, u32[]{:S(2)}, u32[]{:S(2)}) collective-permute-start(bf16[64,2176]{1,0:T(8,128)(2,1)S(1)} %collective-permute-done.8.refs_0_), channel_id=1, source_target_pairs={{0,16},{16,0},{1,17},{17,1},{2,18},{18,2},{3,19},{19,3},{4,20},{20... | collective-permute-start | bytes 835592 | tf_op jit(solution)/shard_map/ppermute | solution.py:406
  74.7 2.0 %collective-permute-start.15 = (bf16[128,2176]{1,0:T(8,128)(2,1)S(1)}, bf16[128,2176]{1,0:T(8,128)(2,1)S(1)}, u32[]{:S(2)}, u32[]{:S(2)}) collective-permute-start(bf16[128,2176]{1,0:T(8,128)(2,1)S(1)} %pack.5.here_ref), channel_id=1, source_target_pairs={{0,1},{1,0},{2,3},{3,2},{4,5},{5,4},{6,7},{7,6},{8,9},{9,8},{10,11... | collective-permute-start | bytes 1671176 | tf_op jit(solution)/shard_map/ppermute | solution.py:367
  79.6 2.9 %collective-permute-start.12 = (bf16[192,2048]{1,0:T(8,128)(2,1)S(1)}, bf16[192,2048]{1,0:T(8,128)(2,1)S(1)}, u32[]{:S(2)}, u32[]{:S(2)}) collective-permute-start(bf16[192,2048]{1,0:T(8,128)(2,1)S(1)} %get-tuple-element.48), channel_id=1, source_target_pairs={{0,1},{1,0},{2,3},{3,2},{4,5},{5,4},{6,7},{7,6},{8,9},{9,8},{10,11... | collective-permute-start | bytes 2359304 | tf_op jit(solution)/shard_map/ppermute | solution.py:376
  80.0 12.6 %collective-permute-start.4 = (bf16[192,2048]{1,0:T(8,128)(2,1)S(1)}, bf16[192,2048]{1,0:T(8,128)(2,1)S(1)}, u32[]{:S(2)}, u32[]{:S(2)}) collective-permute-start(bf16[192,2048]{1,0:T(8,128)(2,1)S(1)} %get-tuple-element.39), channel_id=1, source_target_pairs={{0,1},{1,0},{2,3},{3,2},{4,5},{5,4},{6,7},{7,6},{8,9},{9,8},{10,11... | collective-permute-start | bytes 2359304 | tf_op jit(solution)/shard_map/ppermute | solution.py:376
  81.5 8.4 %collective-permute-start.20 = (bf16[64,2048]{1,0:T(8,128)(2,1)S(1)}, bf16[64,2048]{1,0:T(8,128)(2,1)S(1)}, u32[]{:S(2)}, u32[]{:S(2)}) collective-permute-start(bf16[64,2048]{1,0:T(8,128)(2,1)S(1)} %get-tuple-element.54), channel_id=1, source_target_pairs={{0,2},{1,3},{2,0},{3,1},{4,6},{5,7},{6,4},{7,5},{8,10},{9,11},{10,... | collective-permute-start | bytes 786440 | tf_op jit(solution)/shard_map/ppermute | solution.py:414
  82.1 9.6 %collective-permute-start.17 = (bf16[64,2048]{1,0:T(8,128)(2,1)S(1)}, bf16[64,2048]{1,0:T(8,128)(2,1)S(1)}, u32[]{:S(2)}, u32[]{:S(2)}) collective-permute-start(bf16[64,2048]{1,0:T(8,128)(2,1)S(1)} %get-tuple-element.51), channel_id=1, source_target_pairs={{0,16},{16,0},{1,17},{17,1},{2,18},{18,2},{3,19},{19,3},{4,20},{20... | collective-permute-start | bytes 786440 | tf_op jit(solution)/shard_map/ppermute | solution.py:413
  89.9 7.6 %collective-permute-start.21 = (bf16[64,2048]{1,0:T(8,128)(2,1)S(1)}, bf16[64,2048]{1,0:T(8,128)(2,1)S(1)}, u32[]{:S(2)}, u32[]{:S(2)}) collective-permute-start(bf16[64,2048]{1,0:T(8,128)(2,1)S(1)} %join.11), channel_id=1, source_target_pairs={{0,12},{1,13},{2,14},{3,15},{4,0},{5,1},{6,2},{7,3},{8,4},{9,5},{1... | collective-permute-start | bytes 786440 | tf_op jit(solution)/shard_map/ppermute | solution.py:418
  91.8 9.1 %collective-permute-start.19 = (bf16[64,2048]{1,0:T(8,128)(2,1)S(1)}, bf16[64,2048]{1,0:T(8,128)(2,1)S(1)}, u32[]{:S(2)}, u32[]{:S(2)}) collective-permute-start(bf16[64,2048]{1,0:T(8,128)(2,1)S(1)} %join.10), channel_id=1, source_target_pairs={{0,2},{1,3},{2,0},{3,1},{4,6},{5,7},{6,4},{7,5},{8,10},{9,11},{10,... | collective-permute-start | bytes 786440 | tf_op jit(solution)/shard_map/ppermute | solution.py:417
  92.5 11.2 %collective-permute-start.18 = (bf16[64,2048]{1,0:T(8,128)(2,1)S(1)}, bf16[64,2048]{1,0:T(8,128)(2,1)S(1)}, u32[]{:S(2)}, u32[]{:S(2)}) collective-permute-start(bf16[64,2048]{1,0:T(8,128)(2,1)S(1)} %join.8), channel_id=1, source_target_pairs={{0,16},{16,0},{1,17},{17,1},{2,18},{18,2},{3,19},{19,3},{4,20},{20... | collective-permute-start | bytes 786440 | tf_op jit(solution)/shard_map/ppermute | solution.py:420
  92.8 13.9 %collective-permute-start.5 = (bf16[64,1024]{1,0:T(8,128)(2,1)S(1)}, bf16[64,1024]{1,0:T(8,128)(2,1)S(1)}, u32[]{:S(2)}, u32[]{:S(2)}) collective-permute-start(bf16[64,1024]{1,0:T(8,128)(2,1)S(1)} %get-tuple-element.42), channel_id=1, source_target_pairs={{0,16},{16,0},{1,17},{17,1},{2,18},{18,2},{3,19},{19,3},{4,20},{20... | collective-permute-start | bytes 393224 | tf_op jit(solution)/shard_map/ppermute | solution.py:389
  94.9 11.8 %collective-permute-start.6 = (bf16[64,1024]{1,0:T(8,128)(2,1)S(1)}, bf16[64,1024]{1,0:T(8,128)(2,1)S(1)}, u32[]{:S(2)}, u32[]{:S(2)}) collective-permute-start(bf16[64,1024]{1,0:T(8,128)(2,1)S(1)} %get-tuple-element.44), channel_id=1, source_target_pairs={{0,2},{1,3},{2,0},{3,1},{4,6},{5,7},{6,4},{7,5},{8,10},{9,11},{10,... | collective-permute-start | bytes 393224 | tf_op jit(solution)/shard_map/ppermute | solution.py:389
  97.5 9.2 %collective-permute-start.7 = (bf16[64,1024]{1,0:T(8,128)(2,1)S(1)}, bf16[64,1024]{1,0:T(8,128)(2,1)S(1)}, u32[]{:S(2)}, u32[]{:S(2)}) collective-permute-start(bf16[64,1024]{1,0:T(8,128)(2,1)S(1)} %get-tuple-element.45), channel_id=1, source_target_pairs={{0,18},{1,19},{2,16},{3,17},{4,22},{5,23},{6,20},{7,21},{8,26},{9,... | collective-permute-start | bytes 393224 | tf_op jit(solution)/shard_map/ppermute | solution.py:389
  103.8 5.0 %collective-permute-start.22 = (bf16[64,1024]{1,0:T(8,128)(2,1)S(1)}, bf16[64,1024]{1,0:T(8,128)(2,1)S(1)}, u32[]{:S(2)}, u32[]{:S(2)}) collective-permute-start(bf16[64,1024]{1,0:T(8,128)(2,1)S(1)} %get-tuple-element.55), channel_id=1, source_target_pairs={{0,12},{1,13},{2,14},{3,15},{4,0},{5,1},{6,2},{7,3},{8,4},{9,5},{1... | collective-permute-start | bytes 393224 | tf_op jit(solution)/shard_map/ppermute | solution.py:389
  103.9 7.7 %collective-permute-start.23 = (bf16[64,1024]{1,0:T(8,128)(2,1)S(1)}, bf16[64,1024]{1,0:T(8,128)(2,1)S(1)}, u32[]{:S(2)}, u32[]{:S(2)}) collective-permute-start(bf16[64,1024]{1,0:T(8,128)(2,1)S(1)} %get-tuple-element.56), channel_id=1, source_target_pairs={{0,28},{1,29},{2,30},{3,31},{4,16},{5,17},{6,18},{7,19},{8,20},{9,... | collective-permute-start | bytes 393224 | tf_op jit(solution)/shard_map/ppermute | solution.py:389
  (16 other events, 115.0 us)

commit v3 on v2

--- a/solution.py
+++ b/solution.py
@@ -42,6 +42,29 @@
         keys[start : start + count, :width] = ref[:, token * width : (token + 1) * width]
         start += count
     return start
+
+
+def pick_kernel(pieces, moves_ref, cache_any, out_ref, cache, stacked, sems):
+    [copy] = fetch_all((cache_any,), (cache,), sems)
+    ranks, per_rank, wide = out_ref.shape
+    slots = moves_ref.shape[0]
+    resident = cache.shape[0]
+    rows = ranks * per_rank
+    row = lax.broadcasted_iota(jnp.int32, (rows, ranks), 0)
+    rank = lax.broadcasted_iota(jnp.int32, (rows, ranks), 1)
+    chosen = jnp.zeros((rows, ranks), jnp.int32)
+    for slot in range(slots):
+        here = (row // per_rank == rank) & (row % per_rank // pieces == slot)
+        chosen = chosen + jnp.where(here, moves_ref[slot : slot + 1, :], 0)
+    block = jnp.clip(jnp.sum(chosen, axis=1, keepdims=True), 0, resident - 1)
+    at = lax.broadcasted_iota(jnp.int32, (rows, pieces * resident), 0)
+    source = lax.broadcasted_iota(jnp.int32, (rows, pieces * resident), 1)
+    pick = (source // resident == at % pieces) & (source % resident == block)
+    copy.wait()
+    for piece in range(pieces):
+        stacked[piece * resident : (piece + 1) * resident, :] = cache[:, piece * wide : (piece + 1) * wide]
+    picked = dot(pick.astype(F32).astype(BF16), stacked[...]).astype(BF16)
+    out_ref[...] = picked.reshape(ranks, per_rank, wide)
 
 
 def resident_kernel(
@@ -85,15 +108,12 @@
     head_count, nope_dim, latent, rope, block_size, steps = dims
     width = latent + rope
     rows = heads_out.shape[0]
-    got = fetch_all(
-        (moved_any, query_any, bias_any, mixed_any, value_any, proj_any),
-        (moved, query, bias, mixed, value, proj),
-        sems,
-    )
+    got = fetch_all((moved_any, query_any, bias_any), (moved, query, bias), sems)
     keys[:, latent:] = jnp.zeros((keys.shape[0], keys.shape[1] - latent), BF16)
     scale = (nope_dim + rope) ** (-0.5)
     value_dim = value.shape[2]
     got[0].wait()
+    got += fetch_all((mixed_any, value_any, proj_any), (mixed, value, proj), sems.at[pl.ds(3, 3)])
     count = moved.shape[0] * moved.shape[1]
     for half in range(2):
         part = moved[:, :, half * width : (half + 1) * width]
@@ -259,11 +279,21 @@
     def turn(by):
         return [(g, (g + by) % groups) for g in range(groups)]
 
-    sent = jnp.clip(subtree_moves.reshape(-1), 0, resident - 1)
     slots = subtree_moves.shape[2]
-    pick = (sent[:, None] == jnp.arange(resident, dtype=jnp.int32)[None, :]).astype(BF16)
     pieces = block_size // 2
-    outgoing = dot(pick, latent_cache).astype(BF16).reshape(ranks, slots * pieces, 2 * width)
+    outgoing = pl.pallas_call(
+        functools.partial(pick_kernel, pieces),
+        out_shape=jax.ShapeDtypeStruct((ranks, slots * pieces, 2 * width), BF16),
+        in_specs=[WHOLE, ANY],
+        scratch_shapes=[
+            VMEM(latent_cache.shape, BF16),
+            VMEM((pieces * resident, 2 * width), BF16),
+            pltpu.SemaphoreType.DMA((1,)),
+        ],
+        compiler_params=pltpu.CompilerParams(vmem_limit_bytes=16 * 2**20),
+        cost_estimate=cost(0, 4 * 2**20),
+        name="pick",
+    )(subtree_moves[0].T, latent_cache)
     arrived = lax.all_to_all(outgoing, "ep", split_axis=0, concat_axis=0, tiled=True)
 
     place = jnp.arange(table_len, dtype=jnp.int32)
@@ -407,7 +437,6 @@
         early = run_expert([packet, side, near], packet)
         later = run_expert([near_side, two, far], early[0])
         last = run_expert([far_side, two_side], later[0])
-        own_sum, side_sum, near_sum = join(*early, [F32, BF16, F32])
         near_side_sum, two_sum = join(*later, [F32, F32])
         far_side_sum, two_side_sum = join(*last, [BF16, BF16])
         far_side_in = lax.ppermute(far_side_sum, "grp", plane_swap)
@@ -436,11 +465,13 @@
             return [(source, (target + ranks) % (2 * ranks)) for source, target in pairs]
 
         sideways = [(i, i ^ 2) for i in range(2 * ranks)]
-        base, own_other = by_columns(own_kernel, F32, state, own_sum)
-        side_mine, side_other = by_columns(sum_kernel, BF16, side_sum)
+        [near_sum] = join(*early, [F32], 2)
         near_mine, near_other = by_columns(
             sum_kernel, BF16, near_sum, far_in, near_side_in, two_in
         )
+        own_sum, side_sum = join(*early, [F32, BF16], 0, [near_other])
+        base, own_other = by_columns(own_kernel, F32, state, own_sum)
+        side_mine, side_other = by_columns(sum_kernel, BF16, side_sum)
         result = base + send(own_other, "grp", plane_swap)
         result = result + send(side_mine, both_axes, sideways)
         result = result + send(side_other, both_axes, crossed(sideways))

time: 113 us -> 114 us (level)
  waiting for transfers between devices: 48.7 us -> 51.3 us
  Pallas kernels: 23.2 us -> 25.6 us
  matrix products: 1.79 us -> 0 us
  starting transfers between devices: 29.8 us -> 28.1 us
    ppermute x1, waiting for transfers between devices: 1.09 us -> 4.85 us  [local(): two_in = lax.ppermute(two_sum, both_axes, backward)]
    ppermute x1, waiting for transfers between devices: 2.8 us -> 0.44 us  [local(): far_in = lax.ppermute(far_sum, 'grp', plane_swap)]
    unnamed x30 -> x34, local copies, waits for them, and re-layouts: 3.8 us -> 5.76 us
    dot_general x1 -> x0, matrix products: 1.79 us -> none  [dot(): return jnp.dot(a, b, preferred_element_type=F32)]
    pallas_call x0 -> x1, Pallas kernels: none -> 1.78 us  [local(): pl.pallas_call(functools.partial(pick_kernel, pieces), out_shape=jax.Shap...]
    ppermute x5, starting transfers between devices: 8.56 us -> 6.91 us  [send(): return lax.ppermute(value.astype(BF16), axes, pairs).astype(F32)]
  transfers between devices with their start and end apart: 25 -> 25, of which waited for: 18 -> 19; matrix products, arithmetic and copies ran while one was open for 2% -> 2% of each run, Pallas kernels for 13% -> 13%
where the time goes in v3:
time: 114 us
  waiting for transfers between devices  51.3 us (45%)
  starting transfers between devices  28.1 us (25%)
  Pallas kernels  25.6 us (22%)
  local copies, waits for them, and re-layouts  7.09 us (6%)
  other arithmetic  1.48 us (1%)
    pallas_call x3, Pallas kernels, run_expert(): pl.pallas_call(functools.partial(expert_kernel, experts), out_shape=(out,...  10.3 us
    all_to_all x1, waiting for transfers between devices, local(): lax.all_to_all(outgoing, 'ep', split_axis=0, concat_axis=0, tiled=True)  8.66 us
    all_to_all x1, starting transfers between devices, local(): lax.all_to_all(outgoing, 'ep', split_axis=0, concat_axis=0, tiled=True)  7.36 us
    ppermute x1, waiting for transfers between devices, local(): two_side_in = lax.ppermute(two_side_sum, 'ep', side_swap)  7.31 us
    ppermute x5, starting transfers between devices, send(): return lax.ppermute(value.astype(BF16), axes, pairs).astype(F32)  6.91 us
    ppermute x1, waiting for transfers between devices, local(): near = lax.ppermute(packet, both_axes, onward)  6.55 us
    ppermute x5, waiting for transfers between devices, send(): return lax.ppermute(value.astype(BF16), axes, pairs).astype(F32)  5.86 us
    unnamed x34, local copies, waits for them, and re-layouts  5.76 us
  transfers between devices with their start and end apart: 25, of which 19 were waited for; matrix products, arithmetic and copies ran while one was open for 2% of the time, Pallas kernels for 13%

profile of v3, /device:TPU:0, one launch (start us, length us, event | category | flops | bytes accessed | tf_op | source)
XLA Modules:
  0.0 114.0 jit_solution(549391218722734324)
XLA Ops:
  2.0 1.8 %pick.1 = bf16[16,16,1152]{2,1,0:T(8,128)(2,1)} custom-call(s32[2,16]{1,0:T(2,128)S(1)} %bitcast.18, bf16[64,9216]{1,0:T(8,128)(2,1)S(1)} %copy-done.2), custom_call_target="tpu_custom_call" | custom-call | bytes 4194304 | tf_op jit(solution)/shard_map/pick/pallas_call | solution.py:284
  3.8 7.4 %all-to-all-start = ((bf16[16,16,1152]{2,1,0:T(8,128)(2,1)}), bf16[16,16,1152]{2,1,0:T(8,128)(2,1)S(1)}, u32[]{:S(2)}, u32[]{:S(2)}) async-start(bf16[16,16,1152]{2,1,0:T(8,128)(2,1)} %pick.1), calls=%async_computation | async-start | bytes 1179648 | tf_op jit(solution)/shard_map/all_to_all | solution.py:297
  13.4 2.7 %attend_resident.1 = (bf16[512,640]{1,0:T(8,128)(2,1)S(1)}, f32[512,640]{1,0:T(8,128)S(1)}) custom-call(bf16[64,1024]{1,0:T(8,128)(2,1)S(1)} %copy-done.10, bf16[64,512]{1,0:T(8,128)(2,1)S(1)} %copy-done.12, bf16[16,2304]{1,0:T(8,128)(2,1)S(1)} %copy-done.11, bf16[64,9216]{1,0:T(8,128)(2,1)S(1)} %copy-done.3, bf16[8,128,512]{2,1,0:T(8,128)(2,1)S(1)} %copy-done.9, ...), custom_call_target="tpu_custom_call" | custom-call | flops 1283457024 | bytes 8388608 | tf_op jit(solution)/shard_map/attend_resident/pallas_call | solution.py:322
  18.0 8.7 %all-to-all-done.moved_any = bf16[16,16,1152]{2,1,0:T(8,128)(2,1)S(1)} async-done(((bf16[16,16,1152]{2,1,0:T(8,128)(2,1)}), bf16[16,16,1152]{2,1,0:T(8,128)(2,1)S(1)}, u32[]{:S(2)}, u32[]{:S(2)}) %all-to-all-start) | async-done | bytes 589856 | tf_op jit(solution)/shard_map/all_to_all | solution.py:297
  27.5 5.7 %attend_moved.1.after_any.own_any = bf16[64,2048]{1,0:T(8,128)(2,1)} custom-call(bf16[16,16,1152]{2,1,0:T(8,128)(2,1)} %copy-done.13, bf16[512,640]{1,0:T(8,128)(2,1)} %copy-done.4, f32[64,512]{1,0:T(8,128)} %reshape.110.bias_any, f32[512,640]{1,0:T(8,128)} %copy-done.1, bf16[8,512,128]{2,1,0:T(8,128)(2,1)} %value_any.1, bf16[1024,2048]{1,0:T(8,128)(2,1)} %proj_any.1), custom_call_target="tpu_custom_call" | custom-call | flops 603979776 | bytes 10485760 | tf_op jit(solution)/shard_map/attend_moved/pallas_call | solution.py:333
  35.8 3.6 %load.1 = (bf16[704,2048]{1,0:T(8,128)(2,1)S(1)}, bf16[704,2048]{1,0:T(8,128)(2,1)S(1)}, bf16[704,2048]{1,0:T(8,128)(2,1)S(1)}) custom-call(bf16[64,2048]{1,0:T(8,128)(2,1)S(1)} %copy-done, bf16[704,2048]{1,0:T(8,128)(2,1)} %bitcast.19, bf16[704,2048]{1,0:T(8,128)(2,1)} %bitcast.20, bf16[704,2048]{1,0:T(8,128)(2,1)} %bitcast.21), custom_call_target="tpu_custom_call" | custom-call | bytes 12582912 | tf_op jit(solution)/shard_map/load/pallas_call | solution.py:355
  39.4 2.3 %collective-permute-done.refs_0_ = bf16[64,2048]{1,0:T(8,128)(2,1)S(1)} collective-permute-done((bf16[64,2048]{1,0:T(8,128)(2,1)}, bf16[64,2048]{1,0:T(8,128)(2,1)S(1)}, u32[]{:S(2)}, u32[]{:S(2)}) %collective-permute-start) | collective-permute-done | bytes 262176 | tf_op jit(solution)/shard_map/ppermute | solution.py:352
  42.4 2.1 %collective-permute-start.2 = (bf16[64,2176]{1,0:T(8,128)(2,1)S(1)}, bf16[64,2176]{1,0:T(8,128)(2,1)S(1)}, u32[]{:S(2)}, u32[]{:S(2)}) collective-permute-start(bf16[64,2176]{1,0:T(8,128)(2,1)S(1)} %get-tuple-element.34.after_any.refs_0_), channel_id=1, source_target_pairs={{0,4},{1,5},{2,6},{3,7},{4,8},{5,9},{6,10},{7,11},{8,12},{9,13},{1... | collective-permute-start | bytes 835592 | tf_op jit(solution)/shard_map/ppermute | solution.py:430
  45.4 6.6 %collective-permute-done.2.refs_2_ = bf16[64,2176]{1,0:T(8,128)(2,1)S(1)} collective-permute-done((bf16[64,2176]{1,0:T(8,128)(2,1)S(1)}, bf16[64,2176]{1,0:T(8,128)(2,1)S(1)}, u32[]{:S(2)}, u32[]{:S(2)}) %collective-permute-start.2) | collective-permute-done | bytes 278560 | tf_op jit(solution)/shard_map/ppermute | solution.py:430
  52.7 1.6 %collective-permute-start.7 = (bf16[64,2176]{1,0:T(8,128)(2,1)S(1)}, bf16[64,2176]{1,0:T(8,128)(2,1)S(1)}, u32[]{:S(2)}, u32[]{:S(2)}) collective-permute-start(bf16[64,2176]{1,0:T(8,128)(2,1)S(1)} %collective-permute-done.2.refs_2_), channel_id=1, source_target_pairs={{0,16},{16,0},{1,17},{17,1},{2,18},{18,2},{3,19},{19,3},{4,20},{20... | collective-permute-start | bytes 835592 | tf_op jit(solution)/shard_map/ppermute | solution.py:434
  55.8 3.8 %expert.3 = (bf16[192,2048]{1,0:T(8,128)(2,1)S(1)}, bf16[192,2048]{1,0:T(8,128)(2,1)S(1)}) custom-call(bf16[192,2176]{1,0:T(8,128)(2,1)S(1)} %pack.3.here_ref, bf16[192,2176]{1,0:T(8,128)(2,1)S(1)} %collective-permute-done.3.across_ref, bf16[704,2048]{1,0:T(8,128)(2,1)S(1)} %get-tuple-element.35.gate_ref, bf16[704,2048]{1,0:T(8,128)(2,1)S(1)} %get-tuple-element.36.up_ref, ...), custom_call_target="tpu_custom_call" | custom-call | flops 3321888768 | bytes 12582912 | tf_op jit(solution)/shard_map/expert/pallas_call | solution.py:398
  59.7 2.1 %collective-permute-done.7.refs_2_ = bf16[64,2176]{1,0:T(8,128)(2,1)S(1)} collective-permute-done((bf16[64,2176]{1,0:T(8,128)(2,1)S(1)}, bf16[64,2176]{1,0:T(8,128)(2,1)S(1)}, u32[]{:S(2)}, u32[]{:S(2)}) %collective-permute-start.7) | collective-permute-done | bytes 278560 | tf_op jit(solution)/shard_map/ppermute | solution.py:434
  61.8 3.1 %collective-permute-done.6.refs_1_ = bf16[64,2176]{1,0:T(8,128)(2,1)S(1)} collective-permute-done((bf16[64,2176]{1,0:T(8,128)(2,1)S(1)}, bf16[64,2176]{1,0:T(8,128)(2,1)S(1)}, u32[]{:S(2)}, u32[]{:S(2)}) %collective-permute-start.6) | collective-permute-done | bytes 278560 | tf_op jit(solution)/shard_map/ppermute | solution.py:432
  67.4 3.8 %expert.4 = (bf16[192,2048]{1,0:T(8,128)(2,1)S(1)}, bf16[192,2048]{1,0:T(8,128)(2,1)S(1)}) custom-call(bf16[192,2176]{1,0:T(8,128)(2,1)S(1)} %pack.4.here_ref, bf16[192,2176]{1,0:T(8,128)(2,1)S(1)} %collective-permute-done.8.across_ref, bf16[704,2048]{1,0:T(8,128)(2,1)S(1)} %get-tuple-element.35.gate_ref, bf16[704,2048]{1,0:T(8,128)(2,1)S(1)} %get-tuple-element.36.up_ref, ...), custom_call_target="tpu_custom_call" | custom-call | flops 3321888768 | bytes 12582912 | tf_op jit(solution)/shard_map/expert/pallas_call | solution.py:398
  71.3 2.9 %collective-permute-done.11.refs_1_ = bf16[64,2176]{1,0:T(8,128)(2,1)S(1)} collective-permute-done((bf16[64,2176]{1,0:T(8,128)(2,1)S(1)}, bf16[64,2176]{1,0:T(8,128)(2,1)S(1)}, u32[]{:S(2)}, u32[]{:S(2)}) %collective-permute-start.11) | collective-permute-done | bytes 278560 | tf_op jit(solution)/shard_map/ppermute | solution.py:435
  75.4 1.9 %collective-permute-done.12.across_ref = bf16[128,2176]{1,0:T(8,128)(2,1)S(1)} collective-permute-done((bf16[128,2176]{1,0:T(8,128)(2,1)S(1)}, bf16[128,2176]{1,0:T(8,128)(2,1)S(1)}, u32[]{:S(2)}, u32[]{:S(2)}) %collective-permute-start.12) | collective-permute-done | bytes 557088 | tf_op jit(solution)/shard_map/ppermute | solution.py:397
  77.4 2.6 %expert.5 = (bf16[128,2048]{1,0:T(8,128)(2,1)S(1)}, bf16[128,2048]{1,0:T(8,128)(2,1)S(1)}) custom-call(bf16[128,2176]{1,0:T(8,128)(2,1)S(1)} %pack.5.here_ref, bf16[128,2176]{1,0:T(8,128)(2,1)S(1)} %collective-permute-done.12.across_ref, bf16[704,2048]{1,0:T(8,128)(2,1)S(1)} %get-tuple-element.35.gate_ref, bf16[704,2048]{1,0:T(8,128)(2,1)S(1)} %get-tuple-element.36.up_ref, ...), custom_call_target="tpu_custom_call" | custom-call | flops 2214592512 | bytes 12582912 | tf_op jit(solution)/shard_map/expert/pallas_call | solution.py:398
  83.2 7.3 %collective-permute-done.17.back_ref = bf16[64,2048]{1,0:T(8,128)(2,1)S(1)} collective-permute-done((bf16[64,2048]{1,0:T(8,128)(2,1)S(1)}, bf16[64,2048]{1,0:T(8,128)(2,1)S(1)}, u32[]{:S(2)}, u32[]{:S(2)}) %collective-permute-start.17) | collective-permute-done | bytes 262176 | tf_op jit(solution)/shard_map/ppermute | solution.py:443
  90.6 1.8 %collective-permute-start.18 = (bf16[64,2048]{1,0:T(8,128)(2,1)S(1)}, bf16[64,2048]{1,0:T(8,128)(2,1)S(1)}, u32[]{:S(2)}, u32[]{:S(2)}) collective-permute-start(bf16[64,2048]{1,0:T(8,128)(2,1)S(1)} %join.12), channel_id=1, source_target_pairs={{0,12},{1,13},{2,14},{3,15},{4,0},{5,1},{6,2},{7,3},{8,4},{9,5},{1... | collective-permute-start | bytes 786440 | tf_op jit(solution)/shard_map/ppermute | solution.py:447
  93.3 4.8 %collective-permute-done.18.refs_3_ = bf16[64,2048]{1,0:T(8,128)(2,1)S(1)} collective-permute-done((bf16[64,2048]{1,0:T(8,128)(2,1)S(1)}, bf16[64,2048]{1,0:T(8,128)(2,1)S(1)}, u32[]{:S(2)}, u32[]{:S(2)}) %collective-permute-start.18) | collective-permute-done | bytes 262176 | tf_op jit(solution)/shard_map/ppermute | solution.py:447
  100.3 1.9 %collective-permute-start.23 = (bf16[64,1024]{1,0:T(8,128)(2,1)S(1)}, bf16[64,1024]{1,0:T(8,128)(2,1)S(1)}, u32[]{:S(2)}, u32[]{:S(2)}) collective-permute-start(bf16[64,1024]{1,0:T(8,128)(2,1)S(1)} %get-tuple-element.47.refs_0_), channel_id=1, source_target_pairs={{0,28},{1,29},{2,30},{3,31},{4,16},{5,17},{6,18},{7,19},{8,20},{9,... | collective-permute-start | bytes 393224 | tf_op jit(solution)/shard_map/ppermute | solution.py:419
  102.4 3.5 %collective-permute-start.22 = (bf16[64,1024]{1,0:T(8,128)(2,1)S(1)}, bf16[64,1024]{1,0:T(8,128)(2,1)S(1)}, u32[]{:S(2)}, u32[]{:S(2)}) collective-permute-start(bf16[64,1024]{1,0:T(8,128)(2,1)S(1)} %get-tuple-element.54), channel_id=1, source_target_pairs={{0,12},{1,13},{2,14},{3,15},{4,0},{5,1},{6,2},{7,3},{8,4},{9,5},{1... | collective-permute-start | bytes 393224 | tf_op jit(solution)/shard_map/ppermute | solution.py:419
  107.4 2.5 %collective-permute-done.19 = bf16[64,1024]{1,0:T(8,128)(2,1)S(1)} collective-permute-done((bf16[64,1024]{1,0:T(8,128)(2,1)S(1)}, bf16[64,1024]{1,0:T(8,128)(2,1)S(1)}, u32[]{:S(2)}, u32[]{:S(2)}) %collective-permute-start.19) | collective-permute-done | bytes 131104 | tf_op jit(solution)/shard_map/ppermute | solution.py:419
  110.9 2.3 %collective-permute-done.21 = bf16[64,1024]{1,0:T(8,128)(2,1)S(1)} collective-permute-done((bf16[64,1024]{1,0:T(8,128)(2,1)S(1)}, bf16[64,1024]{1,0:T(8,128)(2,1)S(1)}, u32[]{:S(2)}, u32[]{:S(2)}) %collective-permute-start.21) | collective-permute-done | bytes 131104 | tf_op jit(solution)/shard_map/ppermute | solution.py:419
  (106 shorter events, 26.7 us)
Async XLA Ops:
  3.8 22.9 %all-to-all-start = ((bf16[16,16,1152]{2,1,0:T(8,128)(2,1)}), bf16[16,16,1152]{2,1,0:T(8,128)(2,1)S(1)}, u32[]{:S(2)}, u32[]{:S(2)}) async-start(bf16[16,16,1152]{2,1,0:T(8,128)(2,1)} %pick.1), calls=%async_computation | async-start | bytes 1179648 | tf_op jit(solution)/shard_map/all_to_all | solution.py:297
  33.2 8.5 %collective-permute-start = (bf16[64,2048]{1,0:T(8,128)(2,1)}, bf16[64,2048]{1,0:T(8,128)(2,1)S(1)}, u32[]{:S(2)}, u32[]{:S(2)}) collective-permute-start(bf16[64,2048]{1,0:T(8,128)(2,1)} %attend_moved.1.after_any.own_any), channel_id=1, source_target_pairs={{0,16},{16,0},{1,17},{17,1},{2,18},{18,2},{3,19},{19,3},{4,20},{20... | collective-permute-start | bytes 786440 | tf_op jit(solution)/shard_map/ppermute | solution.py:352
  42.4 9.6 %collective-permute-start.2 = (bf16[64,2176]{1,0:T(8,128)(2,1)S(1)}, bf16[64,2176]{1,0:T(8,128)(2,1)S(1)}, u32[]{:S(2)}, u32[]{:S(2)}) collective-permute-start(bf16[64,2176]{1,0:T(8,128)(2,1)S(1)} %get-tuple-element.34.after_any.refs_0_), channel_id=1, source_target_pairs={{0,4},{1,5},{2,6},{3,7},{4,8},{5,9},{6,10},{7,11},{8,12},{9,13},{1... | collective-permute-start | bytes 835592 | tf_op jit(solution)/shard_map/ppermute | solution.py:430
  44.5 8.1 %collective-permute-start.1 = (bf16[64,2176]{1,0:T(8,128)(2,1)S(1)}, bf16[64,2176]{1,0:T(8,128)(2,1)S(1)}, u32[]{:S(2)}, u32[]{:S(2)}) collective-permute-start(bf16[64,2176]{1,0:T(8,128)(2,1)S(1)} %get-tuple-element.34.after_any.refs_0_), channel_id=1, source_target_pairs={{0,2},{1,3},{2,0},{3,1},{4,6},{5,7},{6,4},{7,5},{8,10},{9,11},{10,... | collective-permute-start | bytes 835592 | tf_op jit(solution)/shard_map/ppermute | solution.py:431
  52.7 3.2 %collective-permute-start.3 = (bf16[192,2176]{1,0:T(8,128)(2,1)S(1)}, bf16[192,2176]{1,0:T(8,128)(2,1)S(1)}, u32[]{:S(2)}, u32[]{:S(2)}) collective-permute-start(bf16[192,2176]{1,0:T(8,128)(2,1)S(1)} %pack.3.here_ref), channel_id=1, source_target_pairs={{0,1},{1,0},{2,3},{3,2},{4,5},{5,4},{6,7},{7,6},{8,9},{9,8},{10,11... | collective-permute-start | bytes 2506760 | tf_op jit(solution)/shard_map/ppermute | solution.py:397
  52.7 9.1 %collective-permute-start.7 = (bf16[64,2176]{1,0:T(8,128)(2,1)S(1)}, bf16[64,2176]{1,0:T(8,128)(2,1)S(1)}, u32[]{:S(2)}, u32[]{:S(2)}) collective-permute-start(bf16[64,2176]{1,0:T(8,128)(2,1)S(1)} %collective-permute-done.2.refs_2_), channel_id=1, source_target_pairs={{0,16},{16,0},{1,17},{17,1},{2,18},{18,2},{3,19},{19,3},{4,20},{20... | collective-permute-start | bytes 835592 | tf_op jit(solution)/shard_map/ppermute | solution.py:434
  54.4 10.5 %collective-permute-start.6 = (bf16[64,2176]{1,0:T(8,128)(2,1)S(1)}, bf16[64,2176]{1,0:T(8,128)(2,1)S(1)}, u32[]{:S(2)}, u32[]{:S(2)}) collective-permute-start(bf16[64,2176]{1,0:T(8,128)(2,1)S(1)} %collective-permute-done.2.refs_2_), channel_id=1, source_target_pairs={{0,4},{1,5},{2,6},{3,7},{4,8},{5,9},{6,10},{7,11},{8,12},{9,13},{1... | collective-permute-start | bytes 835592 | tf_op jit(solution)/shard_map/ppermute | solution.py:432
  54.7 10.2 %collective-permute-start.5 = (bf16[64,2176]{1,0:T(8,128)(2,1)S(1)}, bf16[64,2176]{1,0:T(8,128)(2,1)S(1)}, u32[]{:S(2)}, u32[]{:S(2)}) collective-permute-start(bf16[64,2176]{1,0:T(8,128)(2,1)S(1)} %collective-permute-done.2.refs_2_), channel_id=1, source_target_pairs={{0,2},{1,3},{2,0},{3,1},{4,6},{5,7},{6,4},{7,5},{8,10},{9,11},{10,... | collective-permute-start | bytes 835592 | tf_op jit(solution)/shard_map/ppermute | solution.py:433
  65.0 2.4 %collective-permute-start.8 = (bf16[192,2176]{1,0:T(8,128)(2,1)S(1)}, bf16[192,2176]{1,0:T(8,128)(2,1)S(1)}, u32[]{:S(2)}, u32[]{:S(2)}) collective-permute-start(bf16[192,2176]{1,0:T(8,128)(2,1)S(1)} %pack.4.here_ref), channel_id=1, source_target_pairs={{0,1},{1,0},{2,3},{3,2},{4,5},{5,4},{6,7},{7,6},{8,9},{9,8},{10,11... | collective-permute-start | bytes 2506760 | tf_op jit(solution)/shard_map/ppermute | solution.py:397
  65.1 9.1 %collective-permute-start.11 = (bf16[64,2176]{1,0:T(8,128)(2,1)S(1)}, bf16[64,2176]{1,0:T(8,128)(2,1)S(1)}, u32[]{:S(2)}, u32[]{:S(2)}) collective-permute-start(bf16[64,2176]{1,0:T(8,128)(2,1)S(1)} %collective-permute-done.6.refs_1_), channel_id=1, source_target_pairs={{0,2},{1,3},{2,0},{3,1},{4,6},{5,7},{6,4},{7,5},{8,10},{9,11},{10,... | collective-permute-start | bytes 835592 | tf_op jit(solution)/shard_map/ppermute | solution.py:435
  66.6 8.7 %collective-permute-start.10 = (bf16[64,2176]{1,0:T(8,128)(2,1)S(1)}, bf16[64,2176]{1,0:T(8,128)(2,1)S(1)}, u32[]{:S(2)}, u32[]{:S(2)}) collective-permute-start(bf16[64,2176]{1,0:T(8,128)(2,1)S(1)} %collective-permute-done.5.refs_0_), channel_id=1, source_target_pairs={{0,16},{16,0},{1,17},{17,1},{2,18},{18,2},{3,19},{19,3},{4,20},{20... | collective-permute-start | bytes 835592 | tf_op jit(solution)/shard_map/ppermute | solution.py:436
  75.3 2.0 %collective-permute-start.12 = (bf16[128,2176]{1,0:T(8,128)(2,1)S(1)}, bf16[128,2176]{1,0:T(8,128)(2,1)S(1)}, u32[]{:S(2)}, u32[]{:S(2)}) collective-permute-start(bf16[128,2176]{1,0:T(8,128)(2,1)S(1)} %pack.5.here_ref), channel_id=1, source_target_pairs={{0,1},{1,0},{2,3},{3,2},{4,5},{5,4},{6,7},{7,6},{8,9},{9,8},{10,11... | collective-permute-start | bytes 1671176 | tf_op jit(solution)/shard_map/ppermute | solution.py:397
  80.2 2.9 %collective-permute-start.9 = (bf16[192,2048]{1,0:T(8,128)(2,1)S(1)}, bf16[192,2048]{1,0:T(8,128)(2,1)S(1)}, u32[]{:S(2)}, u32[]{:S(2)}) collective-permute-start(bf16[192,2048]{1,0:T(8,128)(2,1)S(1)} %get-tuple-element.40), channel_id=1, source_target_pairs={{0,1},{1,0},{2,3},{3,2},{4,5},{5,4},{6,7},{7,6},{8,9},{9,8},{10,11... | collective-permute-start | bytes 2359304 | tf_op jit(solution)/shard_map/ppermute | solution.py:406
  80.6 12.6 %collective-permute-start.4 = (bf16[192,2048]{1,0:T(8,128)(2,1)S(1)}, bf16[192,2048]{1,0:T(8,128)(2,1)S(1)}, u32[]{:S(2)}, u32[]{:S(2)}) collective-permute-start(bf16[192,2048]{1,0:T(8,128)(2,1)S(1)} %get-tuple-element.38), channel_id=1, source_target_pairs={{0,1},{1,0},{2,3},{3,2},{4,5},{5,4},{6,7},{7,6},{8,9},{9,8},{10,11... | collective-permute-start | bytes 2359304 | tf_op jit(solution)/shard_map/ppermute | solution.py:406
  82.1 8.4 %collective-permute-start.17 = (bf16[64,2048]{1,0:T(8,128)(2,1)S(1)}, bf16[64,2048]{1,0:T(8,128)(2,1)S(1)}, u32[]{:S(2)}, u32[]{:S(2)}) collective-permute-start(bf16[64,2048]{1,0:T(8,128)(2,1)S(1)} %get-tuple-element.46), channel_id=1, source_target_pairs={{0,2},{1,3},{2,0},{3,1},{4,6},{5,7},{6,4},{7,5},{8,10},{9,11},{10,... | collective-permute-start | bytes 786440 | tf_op jit(solution)/shard_map/ppermute | solution.py:443
  82.8 9.6 %collective-permute-start.14 = (bf16[64,2048]{1,0:T(8,128)(2,1)S(1)}, bf16[64,2048]{1,0:T(8,128)(2,1)S(1)}, u32[]{:S(2)}, u32[]{:S(2)}) collective-permute-start(bf16[64,2048]{1,0:T(8,128)(2,1)S(1)} %get-tuple-element.43), channel_id=1, source_target_pairs={{0,16},{16,0},{1,17},{17,1},{2,18},{18,2},{3,19},{19,3},{4,20},{20... | collective-permute-start | bytes 786440 | tf_op jit(solution)/shard_map/ppermute | solution.py:442
  90.6 7.6 %collective-permute-start.18 = (bf16[64,2048]{1,0:T(8,128)(2,1)S(1)}, bf16[64,2048]{1,0:T(8,128)(2,1)S(1)}, u32[]{:S(2)}, u32[]{:S(2)}) collective-permute-start(bf16[64,2048]{1,0:T(8,128)(2,1)S(1)} %join.12), channel_id=1, source_target_pairs={{0,12},{1,13},{2,14},{3,15},{4,0},{5,1},{6,2},{7,3},{8,4},{9,5},{1... | collective-permute-start | bytes 786440 | tf_op jit(solution)/shard_map/ppermute | solution.py:447
  92.4 7.3 %collective-permute-start.16 = (bf16[64,2048]{1,0:T(8,128)(2,1)S(1)}, bf16[64,2048]{1,0:T(8,128)(2,1)S(1)}, u32[]{:S(2)}, u32[]{:S(2)}) collective-permute-start(bf16[64,2048]{1,0:T(8,128)(2,1)S(1)} %join.11), channel_id=1, source_target_pairs={{0,2},{1,3},{2,0},{3,1},{4,6},{5,7},{6,4},{7,5},{8,10},{9,11},{10,... | collective-permute-start | bytes 786440 | tf_op jit(solution)/shard_map/ppermute | solution.py:446
  93.1 7.0 %collective-permute-start.15 = (bf16[64,2048]{1,0:T(8,128)(2,1)S(1)}, bf16[64,2048]{1,0:T(8,128)(2,1)S(1)}, u32[]{:S(2)}, u32[]{:S(2)}) collective-permute-start(bf16[64,2048]{1,0:T(8,128)(2,1)S(1)} %join.9), channel_id=1, source_target_pairs={{0,16},{16,0},{1,17},{17,1},{2,18},{18,2},{3,19},{19,3},{4,20},{20... | collective-permute-start | bytes 786440 | tf_op jit(solution)/shard_map/ppermute | solution.py:449
  100.3 9.6 %collective-permute-start.23 = (bf16[64,1024]{1,0:T(8,128)(2,1)S(1)}, bf16[64,1024]{1,0:T(8,128)(2,1)S(1)}, u32[]{:S(2)}, u32[]{:S(2)}) collective-permute-start(bf16[64,1024]{1,0:T(8,128)(2,1)S(1)} %get-tuple-element.47.refs_0_), channel_id=1, source_target_pairs={{0,28},{1,29},{2,30},{3,31},{4,16},{5,17},{6,18},{7,19},{8,20},{9,... | collective-permute-start | bytes 393224 | tf_op jit(solution)/shard_map/ppermute | solution.py:419
  102.3 7.6 %collective-permute-start.19 = (bf16[64,1024]{1,0:T(8,128)(2,1)S(1)}, bf16[64,1024]{1,0:T(8,128)(2,1)S(1)}, u32[]{:S(2)}, u32[]{:S(2)}) collective-permute-start(bf16[64,1024]{1,0:T(8,128)(2,1)S(1)} %get-tuple-element.50), channel_id=1, source_target_pairs={{0,16},{16,0},{1,17},{17,1},{2,18},{18,2},{3,19},{19,3},{4,20},{20... | collective-permute-start | bytes 393224 | tf_op jit(solution)/shard_map/ppermute | solution.py:419
  102.4 7.5 %collective-permute-start.22 = (bf16[64,1024]{1,0:T(8,128)(2,1)S(1)}, bf16[64,1024]{1,0:T(8,128)(2,1)S(1)}, u32[]{:S(2)}, u32[]{:S(2)}) collective-permute-start(bf16[64,1024]{1,0:T(8,128)(2,1)S(1)} %get-tuple-element.54), channel_id=1, source_target_pairs={{0,12},{1,13},{2,14},{3,15},{4,0},{5,1},{6,2},{7,3},{8,4},{9,5},{1... | collective-permute-start | bytes 393224 | tf_op jit(solution)/shard_map/ppermute | solution.py:419
  105.9 5.0 %collective-permute-start.20 = (bf16[64,1024]{1,0:T(8,128)(2,1)S(1)}, bf16[64,1024]{1,0:T(8,128)(2,1)S(1)}, u32[]{:S(2)}, u32[]{:S(2)}) collective-permute-start(bf16[64,1024]{1,0:T(8,128)(2,1)S(1)} %get-tuple-element.52), channel_id=1, source_target_pairs={{0,2},{1,3},{2,0},{3,1},{4,6},{5,7},{6,4},{7,5},{8,10},{9,11},{10,... | collective-permute-start | bytes 393224 | tf_op jit(solution)/shard_map/ppermute | solution.py:419
  107.4 5.9 %collective-permute-start.21 = (bf16[64,1024]{1,0:T(8,128)(2,1)S(1)}, bf16[64,1024]{1,0:T(8,128)(2,1)S(1)}, u32[]{:S(2)}, u32[]{:S(2)}) collective-permute-start(bf16[64,1024]{1,0:T(8,128)(2,1)S(1)} %get-tuple-element.53), channel_id=1, source_target_pairs={{0,18},{1,19},{2,16},{3,17},{4,22},{5,23},{6,20},{7,21},{8,26},{9,... | collective-permute-start | bytes 393224 | tf_op jit(solution)/shard_map/ppermute | solution.py:419
  (18 other events, 110.1 us)

commit v4 on v3

--- a/solution.py
+++ b/solution.py
@@ -44,8 +44,8 @@
     return start
 
 
-def pick_kernel(pieces, moves_ref, cache_any, out_ref, cache, stacked, sems):
-    [copy] = fetch_all((cache_any,), (cache,), sems)
+def pick_kernel(pieces, moves_any, cache_any, out_ref, moves_ref, cache, stacked, sems):
+    got = fetch_all((moves_any, cache_any), (moves_ref, cache), sems)
     ranks, per_rank, wide = out_ref.shape
     slots = moves_ref.shape[0]
     resident = cache.shape[0]
@@ -53,6 +53,7 @@
     row = lax.broadcasted_iota(jnp.int32, (rows, ranks), 0)
     rank = lax.broadcasted_iota(jnp.int32, (rows, ranks), 1)
     chosen = jnp.zeros((rows, ranks), jnp.int32)
+    got[0].wait()
     for slot in range(slots):
         here = (row // per_rank == rank) & (row % per_rank // pieces == slot)
         chosen = chosen + jnp.where(here, moves_ref[slot : slot + 1, :], 0)
@@ -60,7 +61,7 @@
     at = lax.broadcasted_iota(jnp.int32, (rows, pieces * resident), 0)
     source = lax.broadcasted_iota(jnp.int32, (rows, pieces * resident), 1)
     pick = (source // resident == at % pieces) & (source % resident == block)
-    copy.wait()
+    got[1].wait()
     for piece in range(pieces):
         stacked[piece * resident : (piece + 1) * resident, :] = cache[:, piece * wide : (piece + 1) * wide]
     picked = dot(pick.astype(F32).astype(BF16), stacked[...]).astype(BF16)
@@ -108,12 +109,15 @@
     head_count, nope_dim, latent, rope, block_size, steps = dims
     width = latent + rope
     rows = heads_out.shape[0]
-    got = fetch_all((moved_any, query_any, bias_any), (moved, query, bias), sems)
+    got = fetch_all(
+        (moved_any, query_any, bias_any, mixed_any, value_any, proj_any),
+        (moved, query, bias, mixed, value, proj),
+        sems,
+    )
     keys[:, latent:] = jnp.zeros((keys.shape[0], keys.shape[1] - latent), BF16)
     scale = (nope_dim + rope) ** (-0.5)
     value_dim = value.shape[2]
     got[0].wait()
-    got += fetch_all((mixed_any, value_any, proj_any), (mixed, value, proj), sems.at[pl.ds(3, 3)])
     count = moved.shape[0] * moved.shape[1]
     for half in range(2):
         part = moved[:, :, half * width : (half + 1) * width]
@@ -191,10 +195,10 @@
         copy.wait()
 
 
-def pack_kernel(after_any, *refs):
-    out_ref = refs[-1]
-    count = refs[0].shape[0]
-    for at, ref in enumerate(refs[:-1]):
+def pack_kernel(after_count, *refs):
+    rows_refs, out_ref = refs[after_count:-1], refs[-1]
+    count = rows_refs[0].shape[0]
+    for at, ref in enumerate(rows_refs):
         out_ref[at * count : (at + 1) * count, :] = ref[...]
 
 
@@ -224,9 +228,10 @@
         ref[...] = (near_ref[rows, :].astype(F32) + back_ref[rows, :].astype(F32)).astype(ref.dtype)
 
 
-def own_kernel(state_ref, own_ref, base_ref, other_ref):
-    base_ref[...] = state_ref[...] + own_columns(own_ref, 0)
-    other_ref[...] = own_columns(own_ref, 1).astype(BF16)
+def own_kernel(state_ref, own_ref, side_ref, base_ref, other_ref):
+    mine, other = (own_columns(own_ref, by) + own_columns(side_ref, by).astype(F32) for by in (0, 1))
+    base_ref[...] = state_ref[...] + mine
+    other_ref[...] = other.astype(BF16)
 
 
 def sum_kernel(*refs):
@@ -284,13 +289,14 @@
     outgoing = pl.pallas_call(
         functools.partial(pick_kernel, pieces),
         out_shape=jax.ShapeDtypeStruct((ranks, slots * pieces, 2 * width), BF16),
-        in_specs=[WHOLE, ANY],
+        in_specs=[ANY] * 2,
         scratch_shapes=[
+            VMEM((slots, ranks), jnp.int32),
             VMEM(latent_cache.shape, BF16),
             VMEM((pieces * resident, 2 * width), BF16),
-            pltpu.SemaphoreType.DMA((1,)),
+            pltpu.SemaphoreType.DMA((2,)),
         ],
-        compiler_params=pltpu.CompilerParams(vmem_limit_bytes=16 * 2**20),
+        compiler_params=pltpu.CompilerParams(vmem_limit_bytes=60 * 2**20),
         cost_estimate=cost(0, 4 * 2**20),
         name="pick",
     )(subtree_moves[0].T, latent_cache)
@@ -383,17 +389,17 @@
         name="norm",
     )(share, hidden_in, down_rows, norm_gain[None, :], router_proj.T, expert_ids.T, *shares)
 
-    def run_expert(rows, after):
+    def run_expert(rows, *after):
         half = len(rows) * row_count
         out = jax.ShapeDtypeStruct((half, model), BF16)
         here = pl.pallas_call(
-            pack_kernel,
+            functools.partial(pack_kernel, len(after)),
             out_shape=jax.ShapeDtypeStruct((half, model + extra), BF16),
-            in_specs=[ANY] + [WHOLE] * len(rows),
+            in_specs=[ANY] * len(after) + [WHOLE] * len(rows),
             compiler_params=pltpu.CompilerParams(vmem_limit_bytes=16 * 2**20),
             cost_estimate=cost(0, 2 * half * model * 2),
             name="pack",
-        )(after, *rows)
+        )(*after, *rows)
         across = lax.ppermute(here, "ep", core_swap)
         near, far = pl.pallas_call(
             functools.partial(expert_kernel, experts),
@@ -435,9 +441,11 @@
         two_side = lax.ppermute(two, "ep", side_swap)
         far_side = lax.ppermute(near_side, "grp", plane_swap)
         early = run_expert([packet, side, near], packet)
-        later = run_expert([near_side, two, far], early[0])
-        last = run_expert([far_side, two_side], later[0])
-        near_side_sum, two_sum = join(*later, [F32, F32])
+        later = run_expert([far, near_side, two], early[0])
+        own_sum, side_sum, near_sum = join(*early, [F32, BF16, F32])
+        side_in = lax.ppermute(side_sum, "ep", side_swap)
+        last = run_expert([far_side, two_side], later[0], side_in)
+        near_side_sum, two_sum = join(*later, [F32, F32], 1)
         far_side_sum, two_side_sum = join(*last, [BF16, BF16])
         far_side_in = lax.ppermute(far_side_sum, "grp", plane_swap)
         two_side_in = lax.ppermute(two_side_sum, "ep", side_swap)
@@ -445,7 +453,7 @@
         [two_sum] = join(two_sum, two_side_in, [BF16])
         near_side_in = lax.ppermute(near_side_sum, "ep", side_swap)
         two_in = lax.ppermute(two_sum, both_axes, backward)
-        [far_sum] = join(*later, [BF16], 2, [far_side_in])
+        [far_sum] = join(*later, [BF16], 0, [far_side_in])
         far_in = lax.ppermute(far_sum, "grp", plane_swap)
         part = (row_count, columns)
 
@@ -464,17 +472,11 @@
         def crossed(pairs):
             return [(source, (target + ranks) % (2 * ranks)) for source, target in pairs]
 
-        sideways = [(i, i ^ 2) for i in range(2 * ranks)]
-        [near_sum] = join(*early, [F32], 2)
+        base, own_other = by_columns(own_kernel, F32, state, own_sum, side_in)
         near_mine, near_other = by_columns(
             sum_kernel, BF16, near_sum, far_in, near_side_in, two_in
         )
-        own_sum, side_sum = join(*early, [F32, BF16], 0, [near_other])
-        base, own_other = by_columns(own_kernel, F32, state, own_sum)
-        side_mine, side_other = by_columns(sum_kernel, BF16, side_sum)
         result = base + send(own_other, "grp", plane_swap)
-        result = result + send(side_mine, both_axes, sideways)
-        result = result + send(side_other, both_axes, crossed(sideways))
         result = result + send(near_mine, both_axes, backward)
         result = result + send(near_other, both_axes, crossed(backward))
         return result.astype(BF16)

time: 114 us -> 115 us (level)
  starting transfers between devices: 28.1 us -> 33.2 us
  waiting for transfers between devices: 51.3 us -> 48.8 us
  local copies, waits for them, and re-layouts: 7.09 us -> 5.11 us
    ppermute x0 -> x1, waiting for transfers between devices: none -> 4.74 us  [local(): side_in = lax.ppermute(side_sum, 'ep', side_swap)]
    ppermute x1, waiting for transfers between devices: 4.85 us -> 2.6 us  [local(): two_in = lax.ppermute(two_sum, both_axes, backward)]
    unnamed x34 -> x30, local copies, waits for them, and re-layouts: 5.76 us -> 3.78 us
    ppermute x1, starting transfers between devices: 1.64 us -> 3.55 us  [local(): far = lax.ppermute(near, 'grp', plane_swap)]
    ppermute x5 -> x3, starting transfers between devices: 6.91 us -> 5.37 us  [send(): return lax.ppermute(value.astype(BF16), axes, pairs).astype(F32)]
    ppermute x1, starting transfers between devices: 0.27 us -> 1.74 us  [local(): far_side = lax.ppermute(near_side, 'grp', plane_swap)]
    ppermute x1, starting transfers between devices: 0.28 us -> 1.74 us  [local(): far_side_in = lax.ppermute(far_side_sum, 'grp', plane_swap)]
    ppermute x1, waiting for transfers between devices: 7.31 us -> 5.88 us  [local(): two_side_in = lax.ppermute(two_side_sum, 'ep', side_swap)]
  transfers between devices with their start and end apart: 25 -> 24, of which waited for: 19 -> 17; matrix products, arithmetic and copies ran while one was open for 2% -> 2% of each run, Pallas kernels for 13% -> 13%
where the time goes in v4:
time: 115 us
  waiting for transfers between devices  48.8 us (42%)
  starting transfers between devices  33.2 us (29%)
  Pallas kernels  25.9 us (23%)
  local copies, waits for them, and re-layouts  5.11 us (4%)
  other arithmetic  1.44 us (1%)
    pallas_call x3, Pallas kernels, run_expert(): pl.pallas_call(functools.partial(expert_kernel, experts), out_shape=(out,...  10.3 us
    all_to_all x1, waiting for transfers between devices, local(): lax.all_to_all(outgoing, 'ep', split_axis=0, concat_axis=0, tiled=True)  8.7 us
    all_to_all x1, starting transfers between devices, local(): lax.all_to_all(outgoing, 'ep', split_axis=0, concat_axis=0, tiled=True)  7.38 us
    ppermute x1, waiting for transfers between devices, local(): near = lax.ppermute(packet, both_axes, onward)  6.52 us
    ppermute x1, waiting for transfers between devices, local(): two_side_in = lax.ppermute(two_side_sum, 'ep', side_swap)  5.88 us
    ppermute x3, waiting for transfers between devices, send(): return lax.ppermute(value.astype(BF16), axes, pairs).astype(F32)  5.5 us
    ppermute x3, starting transfers between devices, send(): return lax.ppermute(value.astype(BF16), axes, pairs).astype(F32)  5.37 us
    pallas_call x1, Pallas kernels, local(): pl.pallas_call(functools.partial(moved_kernel, dims), out_shape=jax.Shape...  4.97 us
  transfers between devices with their start and end apart: 24, of which 17 were waited for; matrix products, arithmetic and copies ran while one was open for 2% of the time, Pallas kernels for 13%

profile of v4, /device:TPU:0, one launch (start us, length us, event | category | flops | bytes accessed | tf_op | source)
XLA Modules:
  0.0 114.8 jit_solution(4028659012052022981)
XLA Ops:
  0.0 2.8 %pick.1 = bf16[16,16,1152]{2,1,0:T(8,128)(2,1)} custom-call(s32[2,16]{1,0:T(2,128)} %bitcast.22, bf16[64,9216]{1,0:T(8,128)(2,1)} %cache.1), custom_call_target="tpu_custom_call" | custom-call | bytes 4194304 | tf_op jit(solution)/shard_map/pick/pallas_call | solution.py:289
  2.8 7.4 %all-to-all-start = ((bf16[16,16,1152]{2,1,0:T(8,128)(2,1)}), bf16[16,16,1152]{2,1,0:T(8,128)(2,1)S(1)}, u32[]{:S(2)}, u32[]{:S(2)}) async-start(bf16[16,16,1152]{2,1,0:T(8,128)(2,1)} %pick.1), calls=%async_computation | async-start | bytes 1179648 | tf_op jit(solution)/shard_map/all_to_all | solution.py:303
  12.4 2.7 %attend_resident.1 = (bf16[512,640]{1,0:T(8,128)(2,1)S(1)}, f32[512,640]{1,0:T(8,128)S(1)}) custom-call(bf16[64,1024]{1,0:T(8,128)(2,1)S(1)} %copy-done.8, bf16[64,512]{1,0:T(8,128)(2,1)S(1)} %copy-done.10, bf16[16,2304]{1,0:T(8,128)(2,1)S(1)} %copy-done.9, bf16[64,9216]{1,0:T(8,128)(2,1)S(1)} %copy-done.2, bf16[8,128,512]{2,1,0:T(8,128)(2,1)S(1)} %copy-done.7, ...), custom_call_target="tpu_custom_call" | custom-call | flops 1283457024 | bytes 8388608 | tf_op jit(solution)/shard_map/attend_resident/pallas_call | solution.py:328
  17.1 8.7 %all-to-all-done.moved_any = bf16[16,16,1152]{2,1,0:T(8,128)(2,1)S(1)} async-done(((bf16[16,16,1152]{2,1,0:T(8,128)(2,1)}), bf16[16,16,1152]{2,1,0:T(8,128)(2,1)S(1)}, u32[]{:S(2)}, u32[]{:S(2)}) %all-to-all-start) | async-done | bytes 589856 | tf_op jit(solution)/shard_map/all_to_all | solution.py:303
  26.6 5.0 %attend_moved.1.after_any.own_any = bf16[64,2048]{1,0:T(8,128)(2,1)} custom-call(bf16[16,16,1152]{2,1,0:T(8,128)(2,1)} %copy-done.11, bf16[512,640]{1,0:T(8,128)(2,1)} %copy-done.3, f32[64,512]{1,0:T(8,128)} %reshape.110.bias_any, f32[512,640]{1,0:T(8,128)} %copy-done.1, bf16[8,512,128]{2,1,0:T(8,128)(2,1)} %value_any.1, bf16[1024,2048]{1,0:T(8,128)(2,1)} %proj_any.1), custom_call_target="tpu_custom_call" | custom-call | flops 603979776 | bytes 10485760 | tf_op jit(solution)/shard_map/attend_moved/pallas_call | solution.py:339
  34.2 3.6 %load.1 = (bf16[704,2048]{1,0:T(8,128)(2,1)S(1)}, bf16[704,2048]{1,0:T(8,128)(2,1)S(1)}, bf16[704,2048]{1,0:T(8,128)(2,1)S(1)}) custom-call(bf16[64,2048]{1,0:T(8,128)(2,1)S(1)} %copy-done, bf16[704,2048]{1,0:T(8,128)(2,1)} %bitcast.18, bf16[704,2048]{1,0:T(8,128)(2,1)} %bitcast.19, bf16[704,2048]{1,0:T(8,128)(2,1)} %bitcast.20), custom_call_target="tpu_custom_call" | custom-call | bytes 12582912 | tf_op jit(solution)/shard_map/load/pallas_call | solution.py:361
  37.8 2.3 %collective-permute-done.refs_0_ = bf16[64,2048]{1,0:T(8,128)(2,1)S(1)} collective-permute-done((bf16[64,2048]{1,0:T(8,128)(2,1)}, bf16[64,2048]{1,0:T(8,128)(2,1)S(1)}, u32[]{:S(2)}, u32[]{:S(2)}) %collective-permute-start) | collective-permute-done | bytes 262176 | tf_op jit(solution)/shard_map/ppermute | solution.py:358
  40.8 2.1 %collective-permute-start.2 = (bf16[64,2176]{1,0:T(8,128)(2,1)S(1)}, bf16[64,2176]{1,0:T(8,128)(2,1)S(1)}, u32[]{:S(2)}, u32[]{:S(2)}) collective-permute-start(bf16[64,2176]{1,0:T(8,128)(2,1)S(1)} %get-tuple-element.33.refs_0_.refs_1_), channel_id=1, source_target_pairs={{0,4},{1,5},{2,6},{3,7},{4,8},{5,9},{6,10},{7,11},{8,12},{9,13},{1... | collective-permute-start | bytes 835592 | tf_op jit(solution)/shard_map/ppermute | solution.py:436
  43.8 6.5 %collective-permute-done.2.refs_3_ = bf16[64,2176]{1,0:T(8,128)(2,1)S(1)} collective-permute-done((bf16[64,2176]{1,0:T(8,128)(2,1)S(1)}, bf16[64,2176]{1,0:T(8,128)(2,1)S(1)}, u32[]{:S(2)}, u32[]{:S(2)}) %collective-permute-start.2) | collective-permute-done | bytes 278560 | tf_op jit(solution)/shard_map/ppermute | solution.py:436
  52.9 3.5 %collective-permute-start.7 = (bf16[64,2176]{1,0:T(8,128)(2,1)S(1)}, bf16[64,2176]{1,0:T(8,128)(2,1)S(1)}, u32[]{:S(2)}, u32[]{:S(2)}) collective-permute-start(bf16[64,2176]{1,0:T(8,128)(2,1)S(1)} %collective-permute-done.2.refs_3_), channel_id=1, source_target_pairs={{0,16},{16,0},{1,17},{17,1},{2,18},{18,2},{3,19},{19,3},{4,20},{20... | collective-permute-start | bytes 835592 | tf_op jit(solution)/shard_map/ppermute | solution.py:440
  56.4 3.8 %expert.3 = (bf16[192,2048]{1,0:T(8,128)(2,1)S(1)}, bf16[192,2048]{1,0:T(8,128)(2,1)S(1)}) custom-call(bf16[192,2176]{1,0:T(8,128)(2,1)S(1)} %pack.3.here_ref, bf16[192,2176]{1,0:T(8,128)(2,1)S(1)} %collective-permute-done.3.across_ref, bf16[704,2048]{1,0:T(8,128)(2,1)S(1)} %get-tuple-element.34.gate_ref, bf16[704,2048]{1,0:T(8,128)(2,1)S(1)} %get-tuple-element.35.up_ref, ...), custom_call_target="tpu_custom_call" | custom-call | flops 3321888768 | bytes 12582912 | tf_op jit(solution)/shard_map/expert/pallas_call | solution.py:404
  64.2 1.7 %collective-permute-start.12 = (bf16[64,2176]{1,0:T(8,128)(2,1)S(1)}, bf16[64,2176]{1,0:T(8,128)(2,1)S(1)}, u32[]{:S(2)}, u32[]{:S(2)}) collective-permute-start(bf16[64,2176]{1,0:T(8,128)(2,1)S(1)} %collective-permute-done.8.refs_2_), channel_id=1, source_target_pairs={{0,16},{16,0},{1,17},{17,1},{2,18},{18,2},{3,19},{19,3},{4,20},{20... | collective-permute-start | bytes 835592 | tf_op jit(solution)/shard_map/ppermute | solution.py:442
  67.6 3.8 %expert.4 = (bf16[192,2048]{1,0:T(8,128)(2,1)S(1)}, bf16[192,2048]{1,0:T(8,128)(2,1)S(1)}) custom-call(bf16[192,2176]{1,0:T(8,128)(2,1)S(1)} %pack.4.here_ref, bf16[192,2176]{1,0:T(8,128)(2,1)S(1)} %collective-permute-done.10.across_ref, bf16[704,2048]{1,0:T(8,128)(2,1)S(1)} %get-tuple-element.34.gate_ref, bf16[704,2048]{1,0:T(8,128)(2,1)S(1)} %get-tuple-element.35.up_ref, ...), custom_call_target="tpu_custom_call" | custom-call | flops 3321888768 | bytes 12582912 | tf_op jit(solution)/shard_map/expert/pallas_call | solution.py:404
  73.1 4.7 %collective-permute-done.5.side_ref.refs_1_ = bf16[64,2048]{1,0:T(8,128)(2,1)S(1)} collective-permute-done((bf16[64,2048]{1,0:T(8,128)(2,1)S(1)}, bf16[64,2048]{1,0:T(8,128)(2,1)S(1)}, u32[]{:S(2)}, u32[]{:S(2)}) %collective-permute-start.5) | collective-permute-done | bytes 262176 | tf_op jit(solution)/shard_map/ppermute | solution.py:446
  78.0 1.9 %collective-permute-done.14.across_ref = bf16[128,2176]{1,0:T(8,128)(2,1)S(1)} collective-permute-done((bf16[128,2176]{1,0:T(8,128)(2,1)S(1)}, bf16[128,2176]{1,0:T(8,128)(2,1)S(1)}, u32[]{:S(2)}, u32[]{:S(2)}) %collective-permute-start.14) | collective-permute-done | bytes 557088 | tf_op jit(solution)/shard_map/ppermute | solution.py:403
  79.9 2.6 %expert.5 = (bf16[128,2048]{1,0:T(8,128)(2,1)S(1)}, bf16[128,2048]{1,0:T(8,128)(2,1)S(1)}) custom-call(bf16[128,2176]{1,0:T(8,128)(2,1)S(1)} %pack.5.here_ref, bf16[128,2176]{1,0:T(8,128)(2,1)S(1)} %collective-permute-done.14.across_ref, bf16[704,2048]{1,0:T(8,128)(2,1)S(1)} %get-tuple-element.34.gate_ref, bf16[704,2048]{1,0:T(8,128)(2,1)S(1)} %get-tuple-element.35.up_ref, ...), custom_call_target="tpu_custom_call" | custom-call | flops 2214592512 | bytes 12582912 | tf_op jit(solution)/shard_map/expert/pallas_call | solution.py:404
  87.2 5.9 %collective-permute-done.19.back_ref = bf16[64,2048]{1,0:T(8,128)(2,1)S(1)} collective-permute-done((bf16[64,2048]{1,0:T(8,128)(2,1)S(1)}, bf16[64,2048]{1,0:T(8,128)(2,1)S(1)}, u32[]{:S(2)}, u32[]{:S(2)}) %collective-permute-start.19) | collective-permute-done | bytes 262176 | tf_op jit(solution)/shard_map/ppermute | solution.py:451
  93.1 2.0 %collective-permute-start.20 = (bf16[64,2048]{1,0:T(8,128)(2,1)S(1)}, bf16[64,2048]{1,0:T(8,128)(2,1)S(1)}, u32[]{:S(2)}, u32[]{:S(2)}) collective-permute-start(bf16[64,2048]{1,0:T(8,128)(2,1)S(1)} %join.11), channel_id=1, source_target_pairs={{0,12},{1,13},{2,14},{3,15},{4,0},{5,1},{6,2},{7,3},{8,4},{9,5},{1... | collective-permute-start | bytes 786440 | tf_op jit(solution)/shard_map/ppermute | solution.py:455
  98.1 2.6 %collective-permute-done.20.refs_3_ = bf16[64,2048]{1,0:T(8,128)(2,1)S(1)} collective-permute-done((bf16[64,2048]{1,0:T(8,128)(2,1)S(1)}, bf16[64,2048]{1,0:T(8,128)(2,1)S(1)}, u32[]{:S(2)}, u32[]{:S(2)}) %collective-permute-start.20) | collective-permute-done | bytes 262176 | tf_op jit(solution)/shard_map/ppermute | solution.py:455
  100.7 1.8 %collective-permute-done.18.refs_2_ = bf16[64,2048]{1,0:T(8,128)(2,1)S(1)} collective-permute-done((bf16[64,2048]{1,0:T(8,128)(2,1)S(1)}, bf16[64,2048]{1,0:T(8,128)(2,1)S(1)}, u32[]{:S(2)}, u32[]{:S(2)}) %collective-permute-start.18) | collective-permute-done | bytes 262176 | tf_op jit(solution)/shard_map/ppermute | solution.py:454
  102.5 1.8 %collective-permute-done.17.refs_1_ = bf16[64,2048]{1,0:T(8,128)(2,1)S(1)} collective-permute-done((bf16[64,2048]{1,0:T(8,128)(2,1)S(1)}, bf16[64,2048]{1,0:T(8,128)(2,1)S(1)}, u32[]{:S(2)}, u32[]{:S(2)}) %collective-permute-start.17) | collective-permute-done | bytes 262176 | tf_op jit(solution)/shard_map/ppermute | solution.py:457
  104.4 2.0 %collective-permute-start.21 = (bf16[64,1024]{1,0:T(8,128)(2,1)S(1)}, bf16[64,1024]{1,0:T(8,128)(2,1)S(1)}, u32[]{:S(2)}, u32[]{:S(2)}) collective-permute-start(bf16[64,1024]{1,0:T(8,128)(2,1)S(1)} %get-tuple-element.51), channel_id=1, source_target_pairs={{0,12},{1,13},{2,14},{3,15},{4,0},{5,1},{6,2},{7,3},{8,4},{9,5},{1... | collective-permute-start | bytes 393224 | tf_op jit(solution)/shard_map/ppermute | solution.py:425
  106.4 2.2 %collective-permute-start.22 = (bf16[64,1024]{1,0:T(8,128)(2,1)S(1)}, bf16[64,1024]{1,0:T(8,128)(2,1)S(1)}, u32[]{:S(2)}, u32[]{:S(2)}) collective-permute-start(bf16[64,1024]{1,0:T(8,128)(2,1)S(1)} %get-tuple-element.52), channel_id=1, source_target_pairs={{0,28},{1,29},{2,30},{3,31},{4,16},{5,17},{6,18},{7,19},{8,20},{9,... | collective-permute-start | bytes 393224 | tf_op jit(solution)/shard_map/ppermute | solution.py:425
  109.5 4.6 %collective-permute-done.22 = bf16[64,1024]{1,0:T(8,128)(2,1)S(1)} collective-permute-done((bf16[64,1024]{1,0:T(8,128)(2,1)S(1)}, bf16[64,1024]{1,0:T(8,128)(2,1)S(1)}, u32[]{:S(2)}, u32[]{:S(2)}) %collective-permute-start.22) | collective-permute-done | bytes 131104 | tf_op jit(solution)/shard_map/ppermute | solution.py:425
  (98 shorter events, 28.2 us)
Async XLA Ops:
  2.8 22.9 %all-to-all-start = ((bf16[16,16,1152]{2,1,0:T(8,128)(2,1)}), bf16[16,16,1152]{2,1,0:T(8,128)(2,1)S(1)}, u32[]{:S(2)}, u32[]{:S(2)}) async-start(bf16[16,16,1152]{2,1,0:T(8,128)(2,1)} %pick.1), calls=%async_computation | async-start | bytes 1179648 | tf_op jit(solution)/shard_map/all_to_all | solution.py:303
  31.6 8.5 %collective-permute-start = (bf16[64,2048]{1,0:T(8,128)(2,1)}, bf16[64,2048]{1,0:T(8,128)(2,1)S(1)}, u32[]{:S(2)}, u32[]{:S(2)}) collective-permute-start(bf16[64,2048]{1,0:T(8,128)(2,1)} %attend_moved.1.after_any.own_any), channel_id=1, source_target_pairs={{0,16},{16,0},{1,17},{17,1},{2,18},{18,2},{3,19},{19,3},{4,20},{20... | collective-permute-start | bytes 786440 | tf_op jit(solution)/shard_map/ppermute | solution.py:358
  40.8 9.6 %collective-permute-start.2 = (bf16[64,2176]{1,0:T(8,128)(2,1)S(1)}, bf16[64,2176]{1,0:T(8,128)(2,1)S(1)}, u32[]{:S(2)}, u32[]{:S(2)}) collective-permute-start(bf16[64,2176]{1,0:T(8,128)(2,1)S(1)} %get-tuple-element.33.refs_0_.refs_1_), channel_id=1, source_target_pairs={{0,4},{1,5},{2,6},{3,7},{4,8},{5,9},{6,10},{7,11},{8,12},{9,13},{1... | collective-permute-start | bytes 835592 | tf_op jit(solution)/shard_map/ppermute | solution.py:436
  42.9 8.1 %collective-permute-start.1 = (bf16[64,2176]{1,0:T(8,128)(2,1)S(1)}, bf16[64,2176]{1,0:T(8,128)(2,1)S(1)}, u32[]{:S(2)}, u32[]{:S(2)}) collective-permute-start(bf16[64,2176]{1,0:T(8,128)(2,1)S(1)} %get-tuple-element.33.refs_0_.refs_1_), channel_id=1, source_target_pairs={{0,2},{1,3},{2,0},{3,1},{4,6},{5,7},{6,4},{7,5},{8,10},{9,11},{10,... | collective-permute-start | bytes 835592 | tf_op jit(solution)/shard_map/ppermute | solution.py:437
  51.1 5.4 %collective-permute-start.3 = (bf16[192,2176]{1,0:T(8,128)(2,1)S(1)}, bf16[192,2176]{1,0:T(8,128)(2,1)S(1)}, u32[]{:S(2)}, u32[]{:S(2)}) collective-permute-start(bf16[192,2176]{1,0:T(8,128)(2,1)S(1)} %pack.3.here_ref), channel_id=1, source_target_pairs={{0,1},{1,0},{2,3},{3,2},{4,5},{5,4},{6,7},{7,6},{8,9},{9,8},{10,11... | collective-permute-start | bytes 2506760 | tf_op jit(solution)/shard_map/ppermute | solution.py:403
  51.1 10.9 %collective-permute-start.9 = (bf16[64,2176]{1,0:T(8,128)(2,1)S(1)}, bf16[64,2176]{1,0:T(8,128)(2,1)S(1)}, u32[]{:S(2)}, u32[]{:S(2)}) collective-permute-start(bf16[64,2176]{1,0:T(8,128)(2,1)S(1)} %collective-permute-done.2.refs_3_), channel_id=1, source_target_pairs={{0,4},{1,5},{2,6},{3,7},{4,8},{5,9},{6,10},{7,11},{8,12},{9,13},{1... | collective-permute-start | bytes 835592 | tf_op jit(solution)/shard_map/ppermute | solution.py:438
  51.7 10.3 %collective-permute-start.8 = (bf16[64,2176]{1,0:T(8,128)(2,1)S(1)}, bf16[64,2176]{1,0:T(8,128)(2,1)S(1)}, u32[]{:S(2)}, u32[]{:S(2)}) collective-permute-start(bf16[64,2176]{1,0:T(8,128)(2,1)S(1)} %collective-permute-done.2.refs_3_), channel_id=1, source_target_pairs={{0,2},{1,3},{2,0},{3,1},{4,6},{5,7},{6,4},{7,5},{8,10},{9,11},{10,... | collective-permute-start | bytes 835592 | tf_op jit(solution)/shard_map/ppermute | solution.py:439
  52.9 10.1 %collective-permute-start.7 = (bf16[64,2176]{1,0:T(8,128)(2,1)S(1)}, bf16[64,2176]{1,0:T(8,128)(2,1)S(1)}, u32[]{:S(2)}, u32[]{:S(2)}) collective-permute-start(bf16[64,2176]{1,0:T(8,128)(2,1)S(1)} %collective-permute-done.2.refs_3_), channel_id=1, source_target_pairs={{0,16},{16,0},{1,17},{17,1},{2,18},{18,2},{3,19},{19,3},{4,20},{20... | collective-permute-start | bytes 835592 | tf_op jit(solution)/shard_map/ppermute | solution.py:440
  63.0 4.6 %collective-permute-start.10 = (bf16[192,2176]{1,0:T(8,128)(2,1)S(1)}, bf16[192,2176]{1,0:T(8,128)(2,1)S(1)}, u32[]{:S(2)}, u32[]{:S(2)}) collective-permute-start(bf16[192,2176]{1,0:T(8,128)(2,1)S(1)} %pack.4.here_ref), channel_id=1, source_target_pairs={{0,1},{1,0},{2,3},{3,2},{4,5},{5,4},{6,7},{7,6},{8,9},{9,8},{10,11... | collective-permute-start | bytes 2506760 | tf_op jit(solution)/shard_map/ppermute | solution.py:403
  63.1 3.5 %collective-permute-start.4 = (bf16[192,2048]{1,0:T(8,128)(2,1)S(1)}, bf16[192,2048]{1,0:T(8,128)(2,1)S(1)}, u32[]{:S(2)}, u32[]{:S(2)}) collective-permute-start(bf16[192,2048]{1,0:T(8,128)(2,1)S(1)} %get-tuple-element.37), channel_id=1, source_target_pairs={{0,1},{1,0},{2,3},{3,2},{4,5},{5,4},{6,7},{7,6},{8,9},{9,8},{10,11... | collective-permute-start | bytes 2359304 | tf_op jit(solution)/shard_map/ppermute | solution.py:412
  63.6 9.5 %collective-permute-start.13 = (bf16[64,2176]{1,0:T(8,128)(2,1)S(1)}, bf16[64,2176]{1,0:T(8,128)(2,1)S(1)}, u32[]{:S(2)}, u32[]{:S(2)}) collective-permute-start(bf16[64,2176]{1,0:T(8,128)(2,1)S(1)} %collective-permute-done.9.refs_3_), channel_id=1, source_target_pairs={{0,2},{1,3},{2,0},{3,1},{4,6},{5,7},{6,4},{7,5},{8,10},{9,11},{10,... | collective-permute-start | bytes 835592 | tf_op jit(solution)/shard_map/ppermute | solution.py:441
  64.2 8.9 %collective-permute-start.12 = (bf16[64,2176]{1,0:T(8,128)(2,1)S(1)}, bf16[64,2176]{1,0:T(8,128)(2,1)S(1)}, u32[]{:S(2)}, u32[]{:S(2)}) collective-permute-start(bf16[64,2176]{1,0:T(8,128)(2,1)S(1)} %collective-permute-done.8.refs_2_), channel_id=1, source_target_pairs={{0,16},{16,0},{1,17},{17,1},{2,18},{18,2},{3,19},{19,3},{4,20},{20... | collective-permute-start | bytes 835592 | tf_op jit(solution)/shard_map/ppermute | solution.py:442
  66.7 11.1 %collective-permute-start.5 = (bf16[64,2048]{1,0:T(8,128)(2,1)S(1)}, bf16[64,2048]{1,0:T(8,128)(2,1)S(1)}, u32[]{:S(2)}, u32[]{:S(2)}) collective-permute-start(bf16[64,2048]{1,0:T(8,128)(2,1)S(1)} %get-tuple-element.39), channel_id=1, source_target_pairs={{0,2},{1,3},{2,0},{3,1},{4,6},{5,7},{6,4},{7,5},{8,10},{9,11},{10,... | collective-permute-start | bytes 786440 | tf_op jit(solution)/shard_map/ppermute | solution.py:446
  77.9 2.0 %collective-permute-start.14 = (bf16[128,2176]{1,0:T(8,128)(2,1)S(1)}, bf16[128,2176]{1,0:T(8,128)(2,1)S(1)}, u32[]{:S(2)}, u32[]{:S(2)}) collective-permute-start(bf16[128,2176]{1,0:T(8,128)(2,1)S(1)} %pack.5.here_ref), channel_id=1, source_target_pairs={{0,1},{1,0},{2,3},{3,2},{4,5},{5,4},{6,7},{7,6},{8,9},{9,8},{10,11... | collective-permute-start | bytes 1671176 | tf_op jit(solution)/shard_map/ppermute | solution.py:403
  82.6 2.0 %collective-permute-start.15 = (bf16[128,2048]{1,0:T(8,128)(2,1)S(1)}, bf16[128,2048]{1,0:T(8,128)(2,1)S(1)}, u32[]{:S(2)}, u32[]{:S(2)}) collective-permute-start(bf16[128,2048]{1,0:T(8,128)(2,1)S(1)} %get-tuple-element.46), channel_id=1, source_target_pairs={{0,1},{1,0},{2,3},{3,2},{4,5},{5,4},{6,7},{7,6},{8,9},{9,8},{10,11... | collective-permute-start | bytes 1572872 | tf_op jit(solution)/shard_map/ppermute | solution.py:412
  82.8 4.3 %collective-permute-start.11 = (bf16[192,2048]{1,0:T(8,128)(2,1)S(1)}, bf16[192,2048]{1,0:T(8,128)(2,1)S(1)}, u32[]{:S(2)}, u32[]{:S(2)}) collective-permute-start(bf16[192,2048]{1,0:T(8,128)(2,1)S(1)} %get-tuple-element.44), channel_id=1, source_target_pairs={{0,1},{1,0},{2,3},{3,2},{4,5},{5,4},{6,7},{7,6},{8,9},{9,8},{10,11... | collective-permute-start | bytes 2359304 | tf_op jit(solution)/shard_map/ppermute | solution.py:412
  84.7 8.4 %collective-permute-start.19 = (bf16[64,2048]{1,0:T(8,128)(2,1)S(1)}, bf16[64,2048]{1,0:T(8,128)(2,1)S(1)}, u32[]{:S(2)}, u32[]{:S(2)}) collective-permute-start(bf16[64,2048]{1,0:T(8,128)(2,1)S(1)} %get-tuple-element.50), channel_id=1, source_target_pairs={{0,2},{1,3},{2,0},{3,1},{4,6},{5,7},{6,4},{7,5},{8,10},{9,11},{10,... | collective-permute-start | bytes 786440 | tf_op jit(solution)/shard_map/ppermute | solution.py:451
  85.4 9.8 %collective-permute-start.16 = (bf16[64,2048]{1,0:T(8,128)(2,1)S(1)}, bf16[64,2048]{1,0:T(8,128)(2,1)S(1)}, u32[]{:S(2)}, u32[]{:S(2)}) collective-permute-start(bf16[64,2048]{1,0:T(8,128)(2,1)S(1)} %get-tuple-element.47), channel_id=1, source_target_pairs={{0,16},{16,0},{1,17},{17,1},{2,18},{18,2},{3,19},{19,3},{4,20},{20... | collective-permute-start | bytes 786440 | tf_op jit(solution)/shard_map/ppermute | solution.py:450
  93.1 7.6 %collective-permute-start.20 = (bf16[64,2048]{1,0:T(8,128)(2,1)S(1)}, bf16[64,2048]{1,0:T(8,128)(2,1)S(1)}, u32[]{:S(2)}, u32[]{:S(2)}) collective-permute-start(bf16[64,2048]{1,0:T(8,128)(2,1)S(1)} %join.11), channel_id=1, source_target_pairs={{0,12},{1,13},{2,14},{3,15},{4,0},{5,1},{6,2},{7,3},{8,4},{9,5},{1... | collective-permute-start | bytes 786440 | tf_op jit(solution)/shard_map/ppermute | solution.py:455
  95.2 7.3 %collective-permute-start.18 = (bf16[64,2048]{1,0:T(8,128)(2,1)S(1)}, bf16[64,2048]{1,0:T(8,128)(2,1)S(1)}, u32[]{:S(2)}, u32[]{:S(2)}) collective-permute-start(bf16[64,2048]{1,0:T(8,128)(2,1)S(1)} %join.10), channel_id=1, source_target_pairs={{0,2},{1,3},{2,0},{3,1},{4,6},{5,7},{6,4},{7,5},{8,10},{9,11},{10,... | collective-permute-start | bytes 786440 | tf_op jit(solution)/shard_map/ppermute | solution.py:454
  95.9 8.4 %collective-permute-start.17 = (bf16[64,2048]{1,0:T(8,128)(2,1)S(1)}, bf16[64,2048]{1,0:T(8,128)(2,1)S(1)}, u32[]{:S(2)}, u32[]{:S(2)}) collective-permute-start(bf16[64,2048]{1,0:T(8,128)(2,1)S(1)} %join.8), channel_id=1, source_target_pairs={{0,16},{16,0},{1,17},{17,1},{2,18},{18,2},{3,19},{19,3},{4,20},{20... | collective-permute-start | bytes 786440 | tf_op jit(solution)/shard_map/ppermute | solution.py:457
  96.9 11.7 %collective-permute-start.6 = (bf16[64,1024]{1,0:T(8,128)(2,1)S(1)}, bf16[64,1024]{1,0:T(8,128)(2,1)S(1)}, u32[]{:S(2)}, u32[]{:S(2)}) collective-permute-start(bf16[64,1024]{1,0:T(8,128)(2,1)S(1)} %get-tuple-element.41), channel_id=1, source_target_pairs={{0,16},{16,0},{1,17},{17,1},{2,18},{18,2},{3,19},{19,3},{4,20},{20... | collective-permute-start | bytes 393224 | tf_op jit(solution)/shard_map/ppermute | solution.py:425
  104.4 5.0 %collective-permute-start.21 = (bf16[64,1024]{1,0:T(8,128)(2,1)S(1)}, bf16[64,1024]{1,0:T(8,128)(2,1)S(1)}, u32[]{:S(2)}, u32[]{:S(2)}) collective-permute-start(bf16[64,1024]{1,0:T(8,128)(2,1)S(1)} %get-tuple-element.51), channel_id=1, source_target_pairs={{0,12},{1,13},{2,14},{3,15},{4,0},{5,1},{6,2},{7,3},{8,4},{9,5},{1... | collective-permute-start | bytes 393224 | tf_op jit(solution)/shard_map/ppermute | solution.py:425
  106.4 7.7 %collective-permute-start.22 = (bf16[64,1024]{1,0:T(8,128)(2,1)S(1)}, bf16[64,1024]{1,0:T(8,128)(2,1)S(1)}, u32[]{:S(2)}, u32[]{:S(2)}) collective-permute-start(bf16[64,1024]{1,0:T(8,128)(2,1)S(1)} %get-tuple-element.52), channel_id=1, source_target_pairs={{0,28},{1,29},{2,30},{3,31},{4,16},{5,17},{6,18},{7,19},{8,20},{9,... | collective-permute-start | bytes 393224 | tf_op jit(solution)/shard_map/ppermute | solution.py:425
  (15 other events, 110.8 us)

commit v5 on v4

--- a/solution.py
+++ b/solution.py
@@ -195,14 +195,14 @@
         copy.wait()
 
 
-def pack_kernel(after_count, *refs):
-    rows_refs, out_ref = refs[after_count:-1], refs[-1]
+def pack_kernel(after_any, *refs):
+    rows_refs, out_ref = refs[:-1], refs[-1]
     count = rows_refs[0].shape[0]
     for at, ref in enumerate(rows_refs):
         out_ref[at * count : (at + 1) * count, :] = ref[...]
 
 
-def expert_kernel(experts, here_ref, across_ref, gate_ref, up_ref, down_ref, near_ref, far_ref):
+def expert_kernel(experts, after_any, here_ref, across_ref, gate_ref, up_ref, down_ref, near_ref, *far_refs):
     model = gate_ref.shape[1]
     packet = jnp.concatenate([here_ref[...], across_ref[...]], axis=0)
     rows = packet[:, :model]
@@ -217,15 +217,21 @@
     result = dot(inner, down_ref[...]).astype(BF16)
     half = near_ref.shape[0]
     near_ref[...] = result[:half]
-    far_ref[...] = result[half:]
-
-
-def join_kernel(first, after_count, near_ref, back_ref, *refs):
-    out_refs = refs[after_count:]
+    count = half // len(far_refs)
+    for at, far_ref in enumerate(far_refs):
+        far_ref[...] = result[half + at * count : half + (at + 1) * count]
+
+
+def join_kernel(first, back_count, after_count, near_ref, *refs):
+    back_refs, out_refs = refs[after_count : after_count + back_count], refs[after_count + back_count :]
     count = out_refs[0].shape[0]
+    height = back_refs[0].shape[0]
+    step = min(count, height)
     for at, ref in enumerate(out_refs, first):
-        rows = slice(at * count, (at + 1) * count)
-        ref[...] = (near_ref[rows, :].astype(F32) + back_ref[rows, :].astype(F32)).astype(ref.dtype)
+        for row in range(at * count, (at + 1) * count, step):
+            back = back_refs[row // height][row % height : row % height + step, :].astype(F32)
+            total = near_ref[row : row + step, :].astype(F32) + back
+            ref[row - at * count : row - at * count + step, :] = total.astype(ref.dtype)
 
 
 def own_kernel(state_ref, own_ref, side_ref, base_ref, other_ref):
@@ -389,37 +395,37 @@
         name="norm",
     )(share, hidden_in, down_rows, norm_gain[None, :], router_proj.T, expert_ids.T, *shares)
 
-    def run_expert(rows, *after):
+    def run_expert(rows, after, run_after, pieces=1):
         half = len(rows) * row_count
-        out = jax.ShapeDtypeStruct((half, model), BF16)
+        out = [jax.ShapeDtypeStruct((half // cuts, model), BF16) for cuts in [1] + [pieces] * pieces]
         here = pl.pallas_call(
-            functools.partial(pack_kernel, len(after)),
+            pack_kernel,
             out_shape=jax.ShapeDtypeStruct((half, model + extra), BF16),
-            in_specs=[ANY] * len(after) + [WHOLE] * len(rows),
+            in_specs=[ANY] + [WHOLE] * len(rows),
             compiler_params=pltpu.CompilerParams(vmem_limit_bytes=16 * 2**20),
             cost_estimate=cost(0, 2 * half * model * 2),
             name="pack",
-        )(*after, *rows)
+        )(after, *rows)
         across = lax.ppermute(here, "ep", core_swap)
-        near, far = pl.pallas_call(
+        near, *far = pl.pallas_call(
             functools.partial(expert_kernel, experts),
-            out_shape=(out, out),
-            in_specs=[WHOLE] * 5,
+            out_shape=out,
+            in_specs=[ANY] + [WHOLE] * 5,
             compiler_params=pltpu.CompilerParams(vmem_limit_bytes=24 * 2**20),
             cost_estimate=cost(6 * half * model * gate_rows.shape[0], 12 * 2**20),
             name="expert",
-        )(here, across, gate_rows, up_rows, down_rows)
-        return near, lax.ppermute(far, "ep", core_swap)
+        )(run_after, here, across, gate_rows, up_rows, down_rows)
+        return near, [lax.ppermute(part, "ep", core_swap) for part in far]
 
     def join(near, back, types, first=0, after=()):
         return pl.pallas_call(
-            functools.partial(join_kernel, first, len(after)),
+            functools.partial(join_kernel, first, len(back), len(after)),
             out_shape=[jax.ShapeDtypeStruct((row_count, model), kind) for kind in types],
-            in_specs=[WHOLE] * 2 + [ANY] * len(after),
+            in_specs=[WHOLE] + [ANY] * len(after) + [WHOLE] * len(back),
             compiler_params=pltpu.CompilerParams(vmem_limit_bytes=16 * 2**20),
             cost_estimate=cost(row_count * model, 2**20),
             name="join",
-        )(near, back, *after)
+        )(near, *after, *back)
 
     def send(value, axes, pairs):
         return lax.ppermute(value.astype(BF16), axes, pairs).astype(F32)
@@ -440,21 +446,20 @@
         far = lax.ppermute(near, "grp", plane_swap)
         two_side = lax.ppermute(two, "ep", side_swap)
         far_side = lax.ppermute(near_side, "grp", plane_swap)
-        early = run_expert([packet, side, near], packet)
-        later = run_expert([far, near_side, two], early[0])
+        early = run_expert([packet, side, near], packet, packet)
+        later = run_expert([far, near_side, two], early[0], packet)
         own_sum, side_sum, near_sum = join(*early, [F32, BF16, F32])
         side_in = lax.ppermute(side_sum, "ep", side_swap)
-        last = run_expert([far_side, two_side], later[0], side_in)
-        near_side_sum, two_sum = join(*later, [F32, F32], 1)
-        far_side_sum, two_side_sum = join(*last, [BF16, BF16])
+        far_sum, near_side_sum, two_sum = join(*later, [BF16, F32, F32])
+        far_in = lax.ppermute(far_sum, "grp", plane_swap)
+        last = run_expert([far_side, two_side], later[0], far_sum, 4)
+        far_side_sum, two_side_sum = join(*last, [BF16, BF16], 0, [side_in, far_in])
         far_side_in = lax.ppermute(far_side_sum, "grp", plane_swap)
         two_side_in = lax.ppermute(two_side_sum, "ep", side_swap)
-        [near_side_sum] = join(near_side_sum, far_side_in, [BF16])
-        [two_sum] = join(two_sum, two_side_in, [BF16])
+        [near_side_sum] = join(near_side_sum, [far_side_in], [BF16])
+        [two_sum] = join(two_sum, [two_side_in], [BF16])
         near_side_in = lax.ppermute(near_side_sum, "ep", side_swap)
         two_in = lax.ppermute(two_sum, both_axes, backward)
-        [far_sum] = join(*later, [BF16], 0, [far_side_in])
-        far_in = lax.ppermute(far_sum, "grp", plane_swap)
         part = (row_count, columns)
 
         def by_columns(kernel, first_type, *operands):
@@ -486,7 +491,7 @@
         line.append(lax.ppermute(line[-1], "ep", ring_next))
     totals = []
     for part in line:
-        sums = run_expert([lax.ppermute(part, "ep", side_swap), part], packet)
+        sums = run_expert([lax.ppermute(part, "ep", side_swap), part], packet, packet)
         over, here = join(*sums, [BF16, F32])
         totals.append(here + send(over, "ep", side_swap))
     moving = totals[1 % ring]

time: 115 us -> 113 us (0.983)
  waiting for transfers between devices: 48.8 us -> 41.7 us
  starting transfers between devices: 33.2 us -> 38.1 us
    ppermute x1, waiting for transfers between devices: 5.88 us -> 0.01 us  [local(): two_side_in = lax.ppermute(two_side_sum, 'ep', side_swap)]
    ppermute x1, waiting for transfers between devices: 0.01 us -> 5.17 us  [local(): far_side_in = lax.ppermute(far_side_sum, 'grp', plane_swap)]
    ppermute x1, waiting for transfers between devices: 4.74 us -> 1.96 us  [local(): side_in = lax.ppermute(side_sum, 'ep', side_swap)]
    ppermute x1, waiting for transfers between devices: 1.78 us -> 3.88 us  [local(): near_side_in = lax.ppermute(near_side_sum, 'ep', side_swap)]
    ppermute x3, waiting for transfers between devices: 1.95 us -> 0.01 us  [run_expert(): across = lax.ppermute(here, 'ep', core_swap)]
    ppermute x1, waiting for transfers between devices: 1.83 us -> 0.06 us  [local(): far_in = lax.ppermute(far_sum, 'grp', plane_swap)]
    ppermute x3, starting transfers between devices: 5.37 us -> 6.92 us  [send(): return lax.ppermute(value.astype(BF16), axes, pairs).astype(F32)]
    ppermute x1, waiting for transfers between devices: 2.6 us -> 1.33 us  [local(): two_in = lax.ppermute(two_sum, both_axes, backward)]
  transfers between devices with their start and end apart: 24 -> 27, of which waited for: 17 -> 16; matrix products, arithmetic and copies ran while one was open for 2% -> 2% of each run, Pallas kernels for 13% -> 15%
where the time goes in v5:
time: 113 us
  waiting for transfers between devices  41.7 us (37%)
  starting transfers between devices  38.1 us (34%)
  Pallas kernels  25.9 us (23%)
  local copies, waits for them, and re-layouts  5.11 us (5%)
  other arithmetic  1.44 us (1%)
    pallas_call x3, Pallas kernels, run_expert(): pl.pallas_call(functools.partial(expert_kernel, experts), out_shape=out,...  10.3 us
    all_to_all x1, waiting for transfers between devices, local(): lax.all_to_all(outgoing, 'ep', split_axis=0, concat_axis=0, tiled=True)  8.68 us
    all_to_all x1, starting transfers between devices, local(): lax.all_to_all(outgoing, 'ep', split_axis=0, concat_axis=0, tiled=True)  7.38 us
    ppermute x3, starting transfers between devices, send(): return lax.ppermute(value.astype(BF16), axes, pairs).astype(F32)  6.92 us
    ppermute x1, waiting for transfers between devices, local(): near = lax.ppermute(packet, both_axes, onward)  6.51 us
    ppermute x1, waiting for transfers between devices, local(): far_side_in = lax.ppermute(far_side_sum, 'grp', plane_swap)  5.17 us
    pallas_call x1, Pallas kernels, local(): pl.pallas_call(functools.partial(moved_kernel, dims), out_shape=jax.Shape...  4.96 us
    ppermute x3, waiting for transfers between devices, send(): return lax.ppermute(value.astype(BF16), axes, pairs).astype(F32)  4.57 us
  transfers between devices with their start and end apart: 27, of which 16 were waited for; matrix products, arithmetic and copies ran while one was open for 2% of the time, Pallas kernels for 15%

profile of v5, /device:TPU:0, one launch (start us, length us, event | category | flops | bytes accessed | tf_op | source)
XLA Modules:
  0.0 112.6 jit_solution(17630995870148323150)
XLA Ops:
  0.0 2.8 %pick.1 = bf16[16,16,1152]{2,1,0:T(8,128)(2,1)} custom-call(s32[2,16]{1,0:T(2,128)} %bitcast.22, bf16[64,9216]{1,0:T(8,128)(2,1)} %cache.1), custom_call_target="tpu_custom_call" | custom-call | bytes 4194304 | tf_op jit(solution)/shard_map/pick/pallas_call | solution.py:295
  2.8 7.4 %all-to-all-start = ((bf16[16,16,1152]{2,1,0:T(8,128)(2,1)}), bf16[16,16,1152]{2,1,0:T(8,128)(2,1)S(1)}, u32[]{:S(2)}, u32[]{:S(2)}) async-start(bf16[16,16,1152]{2,1,0:T(8,128)(2,1)} %pick.1), calls=%async_computation | async-start | bytes 1179648 | tf_op jit(solution)/shard_map/all_to_all | solution.py:309
  12.4 2.7 %attend_resident.1 = (bf16[512,640]{1,0:T(8,128)(2,1)S(1)}, f32[512,640]{1,0:T(8,128)S(1)}) custom-call(bf16[64,1024]{1,0:T(8,128)(2,1)S(1)} %copy-done.8, bf16[64,512]{1,0:T(8,128)(2,1)S(1)} %copy-done.10, bf16[16,2304]{1,0:T(8,128)(2,1)S(1)} %copy-done.9, bf16[64,9216]{1,0:T(8,128)(2,1)S(1)} %copy-done.2, bf16[8,128,512]{2,1,0:T(8,128)(2,1)S(1)} %copy-done.7, ...), custom_call_target="tpu_custom_call" | custom-call | flops 1283457024 | bytes 8388608 | tf_op jit(solution)/shard_map/attend_resident/pallas_call | solution.py:334
  17.1 8.7 %all-to-all-done.moved_any = bf16[16,16,1152]{2,1,0:T(8,128)(2,1)S(1)} async-done(((bf16[16,16,1152]{2,1,0:T(8,128)(2,1)}), bf16[16,16,1152]{2,1,0:T(8,128)(2,1)S(1)}, u32[]{:S(2)}, u32[]{:S(2)}) %all-to-all-start) | async-done | bytes 589856 | tf_op jit(solution)/shard_map/all_to_all | solution.py:309
  26.6 5.0 %attend_moved.1.after_any.own_any = bf16[64,2048]{1,0:T(8,128)(2,1)} custom-call(bf16[16,16,1152]{2,1,0:T(8,128)(2,1)} %copy-done.11, bf16[512,640]{1,0:T(8,128)(2,1)} %copy-done.3, f32[64,512]{1,0:T(8,128)} %reshape.110.bias_any, f32[512,640]{1,0:T(8,128)} %copy-done.1, bf16[8,512,128]{2,1,0:T(8,128)(2,1)} %value_any.1, bf16[1024,2048]{1,0:T(8,128)(2,1)} %proj_any.1), custom_call_target="tpu_custom_call" | custom-call | flops 603979776 | bytes 10485760 | tf_op jit(solution)/shard_map/attend_moved/pallas_call | solution.py:345
  34.1 3.6 %load.1 = (bf16[704,2048]{1,0:T(8,128)(2,1)S(1)}, bf16[704,2048]{1,0:T(8,128)(2,1)S(1)}, bf16[704,2048]{1,0:T(8,128)(2,1)S(1)}) custom-call(bf16[64,2048]{1,0:T(8,128)(2,1)S(1)} %copy-done, bf16[704,2048]{1,0:T(8,128)(2,1)} %bitcast.18, bf16[704,2048]{1,0:T(8,128)(2,1)} %bitcast.19, bf16[704,2048]{1,0:T(8,128)(2,1)} %bitcast.20), custom_call_target="tpu_custom_call" | custom-call | bytes 12582912 | tf_op jit(solution)/shard_map/load/pallas_call | solution.py:367
  37.7 2.3 %collective-permute-done.refs_0_ = bf16[64,2048]{1,0:T(8,128)(2,1)S(1)} collective-permute-done((bf16[64,2048]{1,0:T(8,128)(2,1)}, bf16[64,2048]{1,0:T(8,128)(2,1)S(1)}, u32[]{:S(2)}, u32[]{:S(2)}) %collective-permute-start) | collective-permute-done | bytes 262176 | tf_op jit(solution)/shard_map/ppermute | solution.py:364
  40.7 2.1 %collective-permute-start.2 = (bf16[64,2176]{1,0:T(8,128)(2,1)S(1)}, bf16[64,2176]{1,0:T(8,128)(2,1)S(1)}, u32[]{:S(2)}, u32[]{:S(2)}) collective-permute-start(bf16[64,2176]{1,0:T(8,128)(2,1)S(1)} %get-tuple-element.37.after_any.refs_0_), channel_id=1, source_target_pairs={{0,4},{1,5},{2,6},{3,7},{4,8},{5,9},{6,10},{7,11},{8,12},{9,13},{1... | collective-permute-start | bytes 835592 | tf_op jit(solution)/shard_map/ppermute | solution.py:442
  43.8 6.5 %collective-permute-done.2.refs_2_ = bf16[64,2176]{1,0:T(8,128)(2,1)S(1)} collective-permute-done((bf16[64,2176]{1,0:T(8,128)(2,1)S(1)}, bf16[64,2176]{1,0:T(8,128)(2,1)S(1)}, u32[]{:S(2)}, u32[]{:S(2)}) %collective-permute-start.2) | collective-permute-done | bytes 278560 | tf_op jit(solution)/shard_map/ppermute | solution.py:442
  52.9 3.6 %collective-permute-start.7 = (bf16[64,2176]{1,0:T(8,128)(2,1)S(1)}, bf16[64,2176]{1,0:T(8,128)(2,1)S(1)}, u32[]{:S(2)}, u32[]{:S(2)}) collective-permute-start(bf16[64,2176]{1,0:T(8,128)(2,1)S(1)} %collective-permute-done.2.refs_2_), channel_id=1, source_target_pairs={{0,16},{16,0},{1,17},{17,1},{2,18},{18,2},{3,19},{19,3},{4,20},{20... | collective-permute-start | bytes 835592 | tf_op jit(solution)/shard_map/ppermute | solution.py:446
  56.4 3.8 %expert.3 = (bf16[192,2048]{1,0:T(8,128)(2,1)S(1)}, bf16[192,2048]{1,0:T(8,128)(2,1)S(1)}) custom-call(bf16[64,2176]{1,0:T(8,128)(2,1)S(1)} %get-tuple-element.37.after_any.refs_0_, bf16[192,2176]{1,0:T(8,128)(2,1)S(1)} %pack.3.here_ref, bf16[192,2176]{1,0:T(8,128)(2,1)S(1)} %collective-permute-done.3.across_ref, ...), custom_call_target="tpu_custom_call" | custom-call | flops 3321888768 | bytes 12582912 | tf_op jit(solution)/shard_map/expert/pallas_call | solution.py:410
  63.7 1.7 %collective-permute-start.13 = (bf16[64,2176]{1,0:T(8,128)(2,1)S(1)}, bf16[64,2176]{1,0:T(8,128)(2,1)S(1)}, u32[]{:S(2)}, u32[]{:S(2)}) collective-permute-start(bf16[64,2176]{1,0:T(8,128)(2,1)S(1)} %collective-permute-done.8.refs_1_), channel_id=1, source_target_pairs={{0,16},{16,0},{1,17},{17,1},{2,18},{18,2},{3,19},{19,3},{4,20},{20... | collective-permute-start | bytes 835592 | tf_op jit(solution)/shard_map/ppermute | solution.py:448
  65.5 3.9 %expert.4 = (bf16[192,2048]{1,0:T(8,128)(2,1)S(1)}, bf16[192,2048]{1,0:T(8,128)(2,1)S(1)}) custom-call(bf16[64,2176]{1,0:T(8,128)(2,1)S(1)} %get-tuple-element.37.after_any.refs_0_, bf16[192,2176]{1,0:T(8,128)(2,1)S(1)} %pack.4.here_ref, bf16[192,2176]{1,0:T(8,128)(2,1)S(1)} %collective-permute-done.10.across_ref, ...), custom_call_target="tpu_custom_call" | custom-call | flops 3321888768 | bytes 12582912 | tf_op jit(solution)/shard_map/expert/pallas_call | solution.py:410
  69.9 2.2 %collective-permute-done.14.refs_1_ = bf16[64,2176]{1,0:T(8,128)(2,1)S(1)} collective-permute-done((bf16[64,2176]{1,0:T(8,128)(2,1)S(1)}, bf16[64,2176]{1,0:T(8,128)(2,1)S(1)}, u32[]{:S(2)}, u32[]{:S(2)}) %collective-permute-start.14) | collective-permute-done | bytes 278560 | tf_op jit(solution)/shard_map/ppermute | solution.py:447
  74.5 1.8 %collective-permute-start.12 = (bf16[64,2048]{1,0:T(8,128)(2,1)S(1)}, bf16[64,2048]{1,0:T(8,128)(2,1)S(1)}, u32[]{:S(2)}, u32[]{:S(2)}) collective-permute-start(bf16[64,2048]{1,0:T(8,128)(2,1)S(1)} %get-tuple-element.49.after_any), channel_id=1, source_target_pairs={{0,16},{16,0},{1,17},{17,1},{2,18},{18,2},{3,19},{19,3},{4,20},{20... | collective-permute-start | bytes 786440 | tf_op jit(solution)/shard_map/ppermute | solution.py:454
  76.3 2.6 %expert.5 = (bf16[128,2048]{1,0:T(8,128)(2,1)S(1)}, bf16[32,2048]{1,0:T(8,128)(2,1)S(1)}, bf16[32,2048]{1,0:T(8,128)(2,1)S(1)}, bf16[32,2048]{1,0:T(8,128)(2,1)S(1)}, bf16[32,2048]{1,0:T(8,128)(2,1)S(1)}) custom-call(bf16[64,2048]{1,0:T(8,128)(2,1)S(1)} %get-tuple-element.49.after_any, bf16[128,2176]{1,0:T(8,128)(2,1)S(1)} %pack.5.here_ref, ...), custom_call_target="tpu_custom_call" | custom-call | flops 2214592512 | bytes 12582912 | tf_op jit(solution)/shard_map/expert/pallas_call | solution.py:410
  79.6 2.0 %collective-permute-done.5.side_ref.refs_0_ = bf16[64,2048]{1,0:T(8,128)(2,1)S(1)} collective-permute-done((bf16[64,2048]{1,0:T(8,128)(2,1)S(1)}, bf16[64,2048]{1,0:T(8,128)(2,1)S(1)}, u32[]{:S(2)}, u32[]{:S(2)}) %collective-permute-start.5) | collective-permute-done | bytes 262176 | tf_op jit(solution)/shard_map/ppermute | solution.py:452
  83.1 1.8 %collective-permute-start.20 = (bf16[64,2048]{1,0:T(8,128)(2,1)S(1)}, bf16[64,2048]{1,0:T(8,128)(2,1)S(1)}, u32[]{:S(2)}, u32[]{:S(2)}) collective-permute-start(bf16[64,2048]{1,0:T(8,128)(2,1)S(1)} %get-tuple-element.56), channel_id=1, source_target_pairs={{0,16},{16,0},{1,17},{17,1},{2,18},{18,2},{3,19},{19,3},{4,20},{20... | collective-permute-start | bytes 786440 | tf_op jit(solution)/shard_map/ppermute | solution.py:457
  86.3 5.2 %collective-permute-done.20.refs_0_ = bf16[64,2048]{1,0:T(8,128)(2,1)S(1)} collective-permute-done((bf16[64,2048]{1,0:T(8,128)(2,1)S(1)}, bf16[64,2048]{1,0:T(8,128)(2,1)S(1)}, u32[]{:S(2)}, u32[]{:S(2)}) %collective-permute-start.20) | collective-permute-done | bytes 262176 | tf_op jit(solution)/shard_map/ppermute | solution.py:457
  93.1 2.0 %collective-permute-start.23 = (bf16[64,2048]{1,0:T(8,128)(2,1)S(1)}, bf16[64,2048]{1,0:T(8,128)(2,1)S(1)}, u32[]{:S(2)}, u32[]{:S(2)}) collective-permute-start(bf16[64,2048]{1,0:T(8,128)(2,1)S(1)} %join.9), channel_id=1, source_target_pairs={{0,12},{1,13},{2,14},{3,15},{4,0},{5,1},{6,2},{7,3},{8,4},{9,5},{1... | collective-permute-start | bytes 786440 | tf_op jit(solution)/shard_map/ppermute | solution.py:462
  95.2 3.9 %collective-permute-done.21.refs_2_ = bf16[64,2048]{1,0:T(8,128)(2,1)S(1)} collective-permute-done((bf16[64,2048]{1,0:T(8,128)(2,1)S(1)}, bf16[64,2048]{1,0:T(8,128)(2,1)S(1)}, u32[]{:S(2)}, u32[]{:S(2)}) %collective-permute-start.21) | collective-permute-done | bytes 262176 | tf_op jit(solution)/shard_map/ppermute | solution.py:461
  100.5 3.8 %collective-permute-start.24 = (bf16[64,1024]{1,0:T(8,128)(2,1)S(1)}, bf16[64,1024]{1,0:T(8,128)(2,1)S(1)}, u32[]{:S(2)}, u32[]{:S(2)}) collective-permute-start(bf16[64,1024]{1,0:T(8,128)(2,1)S(1)} %get-tuple-element.59), channel_id=1, source_target_pairs={{0,12},{1,13},{2,14},{3,15},{4,0},{5,1},{6,2},{7,3},{8,4},{9,5},{1... | collective-permute-start | bytes 393224 | tf_op jit(solution)/shard_map/ppermute | solution.py:431
  104.2 3.1 %collective-permute-start.25 = (bf16[64,1024]{1,0:T(8,128)(2,1)S(1)}, bf16[64,1024]{1,0:T(8,128)(2,1)S(1)}, u32[]{:S(2)}, u32[]{:S(2)}) collective-permute-start(bf16[64,1024]{1,0:T(8,128)(2,1)S(1)} %get-tuple-element.60), channel_id=1, source_target_pairs={{0,28},{1,29},{2,30},{3,31},{4,16},{5,17},{6,18},{7,19},{8,20},{9,... | collective-permute-start | bytes 393224 | tf_op jit(solution)/shard_map/ppermute | solution.py:431
  108.1 3.8 %collective-permute-done.25 = bf16[64,1024]{1,0:T(8,128)(2,1)S(1)} collective-permute-done((bf16[64,1024]{1,0:T(8,128)(2,1)S(1)}, bf16[64,1024]{1,0:T(8,128)(2,1)S(1)}, u32[]{:S(2)}, u32[]{:S(2)}) %collective-permute-start.25) | collective-permute-done | bytes 131104 | tf_op jit(solution)/shard_map/ppermute | solution.py:431
  (103 shorter events, 26.1 us)
Async XLA Ops:
  2.8 22.9 %all-to-all-start = ((bf16[16,16,1152]{2,1,0:T(8,128)(2,1)}), bf16[16,16,1152]{2,1,0:T(8,128)(2,1)S(1)}, u32[]{:S(2)}, u32[]{:S(2)}) async-start(bf16[16,16,1152]{2,1,0:T(8,128)(2,1)} %pick.1), calls=%async_computation | async-start | bytes 1179648 | tf_op jit(solution)/shard_map/all_to_all | solution.py:309
  31.6 8.5 %collective-permute-start = (bf16[64,2048]{1,0:T(8,128)(2,1)}, bf16[64,2048]{1,0:T(8,128)(2,1)S(1)}, u32[]{:S(2)}, u32[]{:S(2)}) collective-permute-start(bf16[64,2048]{1,0:T(8,128)(2,1)} %attend_moved.1.after_any.own_any), channel_id=1, source_target_pairs={{0,16},{16,0},{1,17},{17,1},{2,18},{18,2},{3,19},{19,3},{4,20},{20... | collective-permute-start | bytes 786440 | tf_op jit(solution)/shard_map/ppermute | solution.py:364
  40.7 9.6 %collective-permute-start.2 = (bf16[64,2176]{1,0:T(8,128)(2,1)S(1)}, bf16[64,2176]{1,0:T(8,128)(2,1)S(1)}, u32[]{:S(2)}, u32[]{:S(2)}) collective-permute-start(bf16[64,2176]{1,0:T(8,128)(2,1)S(1)} %get-tuple-element.37.after_any.refs_0_), channel_id=1, source_target_pairs={{0,4},{1,5},{2,6},{3,7},{4,8},{5,9},{6,10},{7,11},{8,12},{9,13},{1... | collective-permute-start | bytes 835592 | tf_op jit(solution)/shard_map/ppermute | solution.py:442
  42.8 8.1 %collective-permute-start.1 = (bf16[64,2176]{1,0:T(8,128)(2,1)S(1)}, bf16[64,2176]{1,0:T(8,128)(2,1)S(1)}, u32[]{:S(2)}, u32[]{:S(2)}) collective-permute-start(bf16[64,2176]{1,0:T(8,128)(2,1)S(1)} %get-tuple-element.37.after_any.refs_0_), channel_id=1, source_target_pairs={{0,2},{1,3},{2,0},{3,1},{4,6},{5,7},{6,4},{7,5},{8,10},{9,11},{10,... | collective-permute-start | bytes 835592 | tf_op jit(solution)/shard_map/ppermute | solution.py:443
  51.0 5.4 %collective-permute-start.3 = (bf16[192,2176]{1,0:T(8,128)(2,1)S(1)}, bf16[192,2176]{1,0:T(8,128)(2,1)S(1)}, u32[]{:S(2)}, u32[]{:S(2)}) collective-permute-start(bf16[192,2176]{1,0:T(8,128)(2,1)S(1)} %pack.3.here_ref), channel_id=1, source_target_pairs={{0,1},{1,0},{2,3},{3,2},{4,5},{5,4},{6,7},{7,6},{8,9},{9,8},{10,11... | collective-permute-start | bytes 2506760 | tf_op jit(solution)/shard_map/ppermute | solution.py:409
  51.1 10.9 %collective-permute-start.9 = (bf16[64,2176]{1,0:T(8,128)(2,1)S(1)}, bf16[64,2176]{1,0:T(8,128)(2,1)S(1)}, u32[]{:S(2)}, u32[]{:S(2)}) collective-permute-start(bf16[64,2176]{1,0:T(8,128)(2,1)S(1)} %collective-permute-done.2.refs_2_), channel_id=1, source_target_pairs={{0,4},{1,5},{2,6},{3,7},{4,8},{5,9},{6,10},{7,11},{8,12},{9,13},{1... | collective-permute-start | bytes 835592 | tf_op jit(solution)/shard_map/ppermute | solution.py:444
  51.7 10.3 %collective-permute-start.8 = (bf16[64,2176]{1,0:T(8,128)(2,1)S(1)}, bf16[64,2176]{1,0:T(8,128)(2,1)S(1)}, u32[]{:S(2)}, u32[]{:S(2)}) collective-permute-start(bf16[64,2176]{1,0:T(8,128)(2,1)S(1)} %collective-permute-done.2.refs_2_), channel_id=1, source_target_pairs={{0,2},{1,3},{2,0},{3,1},{4,6},{5,7},{6,4},{7,5},{8,10},{9,11},{10,... | collective-permute-start | bytes 835592 | tf_op jit(solution)/shard_map/ppermute | solution.py:445
  52.9 10.1 %collective-permute-start.7 = (bf16[64,2176]{1,0:T(8,128)(2,1)S(1)}, bf16[64,2176]{1,0:T(8,128)(2,1)S(1)}, u32[]{:S(2)}, u32[]{:S(2)}) collective-permute-start(bf16[64,2176]{1,0:T(8,128)(2,1)S(1)} %collective-permute-done.2.refs_2_), channel_id=1, source_target_pairs={{0,16},{16,0},{1,17},{17,1},{2,18},{18,2},{3,19},{19,3},{4,20},{20... | collective-permute-start | bytes 835592 | tf_op jit(solution)/shard_map/ppermute | solution.py:446
  63.1 9.1 %collective-permute-start.14 = (bf16[64,2176]{1,0:T(8,128)(2,1)S(1)}, bf16[64,2176]{1,0:T(8,128)(2,1)S(1)}, u32[]{:S(2)}, u32[]{:S(2)}) collective-permute-start(bf16[64,2176]{1,0:T(8,128)(2,1)S(1)} %collective-permute-done.9.refs_2_), channel_id=1, source_target_pairs={{0,2},{1,3},{2,0},{3,1},{4,6},{5,7},{6,4},{7,5},{8,10},{9,11},{10,... | collective-permute-start | bytes 835592 | tf_op jit(solution)/shard_map/ppermute | solution.py:447
  63.7 8.7 %collective-permute-start.13 = (bf16[64,2176]{1,0:T(8,128)(2,1)S(1)}, bf16[64,2176]{1,0:T(8,128)(2,1)S(1)}, u32[]{:S(2)}, u32[]{:S(2)}) collective-permute-start(bf16[64,2176]{1,0:T(8,128)(2,1)S(1)} %collective-permute-done.8.refs_1_), channel_id=1, source_target_pairs={{0,16},{16,0},{1,17},{17,1},{2,18},{18,2},{3,19},{19,3},{4,20},{20... | collective-permute-start | bytes 835592 | tf_op jit(solution)/shard_map/ppermute | solution.py:448
  65.5 7.1 %collective-permute-start.4 = (bf16[192,2048]{1,0:T(8,128)(2,1)S(1)}, bf16[192,2048]{1,0:T(8,128)(2,1)S(1)}, u32[]{:S(2)}, u32[]{:S(2)}) collective-permute-start(bf16[192,2048]{1,0:T(8,128)(2,1)S(1)} %get-tuple-element.41), channel_id=1, source_target_pairs={{0,1},{1,0},{2,3},{3,2},{4,5},{5,4},{6,7},{7,6},{8,9},{9,8},{10,11... | collective-permute-start | bytes 2359304 | tf_op jit(solution)/shard_map/ppermute | solution.py:418
  69.4 4.9 %collective-permute-start.11 = (bf16[192,2048]{1,0:T(8,128)(2,1)S(1)}, bf16[192,2048]{1,0:T(8,128)(2,1)S(1)}, u32[]{:S(2)}, u32[]{:S(2)}) collective-permute-start(bf16[192,2048]{1,0:T(8,128)(2,1)S(1)} %get-tuple-element.48), channel_id=1, source_target_pairs={{0,1},{1,0},{2,3},{3,2},{4,5},{5,4},{6,7},{7,6},{8,9},{9,8},{10,11... | collective-permute-start | bytes 2359304 | tf_op jit(solution)/shard_map/ppermute | solution.py:418
  72.5 3.8 %collective-permute-start.15 = (bf16[128,2176]{1,0:T(8,128)(2,1)S(1)}, bf16[128,2176]{1,0:T(8,128)(2,1)S(1)}, u32[]{:S(2)}, u32[]{:S(2)}) collective-permute-start(bf16[128,2176]{1,0:T(8,128)(2,1)S(1)} %pack.5.here_ref), channel_id=1, source_target_pairs={{0,1},{1,0},{2,3},{3,2},{4,5},{5,4},{6,7},{7,6},{8,9},{9,8},{10,11... | collective-permute-start | bytes 1671176 | tf_op jit(solution)/shard_map/ppermute | solution.py:409
  72.8 8.8 %collective-permute-start.5 = (bf16[64,2048]{1,0:T(8,128)(2,1)S(1)}, bf16[64,2048]{1,0:T(8,128)(2,1)S(1)}, u32[]{:S(2)}, u32[]{:S(2)}) collective-permute-start(bf16[64,2048]{1,0:T(8,128)(2,1)S(1)} %get-tuple-element.43), channel_id=1, source_target_pairs={{0,2},{1,3},{2,0},{3,1},{4,6},{5,7},{6,4},{7,5},{8,10},{9,11},{10,... | collective-permute-start | bytes 786440 | tf_op jit(solution)/shard_map/ppermute | solution.py:452
  74.5 8.5 %collective-permute-start.12 = (bf16[64,2048]{1,0:T(8,128)(2,1)S(1)}, bf16[64,2048]{1,0:T(8,128)(2,1)S(1)}, u32[]{:S(2)}, u32[]{:S(2)}) collective-permute-start(bf16[64,2048]{1,0:T(8,128)(2,1)S(1)} %get-tuple-element.49.after_any), channel_id=1, source_target_pairs={{0,16},{16,0},{1,17},{17,1},{2,18},{18,2},{3,19},{19,3},{4,20},{20... | collective-permute-start | bytes 786440 | tf_op jit(solution)/shard_map/ppermute | solution.py:454
  78.9 2.6 %collective-permute-start.16 = (bf16[32,2048]{1,0:T(8,128)(2,1)S(1)}, bf16[32,2048]{1,0:T(8,128)(2,1)S(1)}, u32[]{:S(2)}, u32[]{:S(2)}) collective-permute-start(bf16[32,2048]{1,0:T(8,128)(2,1)S(1)} %get-tuple-element.52), channel_id=1, source_target_pairs={{0,1},{1,0},{2,3},{3,2},{4,5},{5,4},{6,7},{7,6},{8,9},{9,8},{10,11... | collective-permute-start | bytes 393224 | tf_op jit(solution)/shard_map/ppermute | solution.py:418
  79.0 2.5 %collective-permute-start.17 = (bf16[32,2048]{1,0:T(8,128)(2,1)S(1)}, bf16[32,2048]{1,0:T(8,128)(2,1)S(1)}, u32[]{:S(2)}, u32[]{:S(2)}) collective-permute-start(bf16[32,2048]{1,0:T(8,128)(2,1)S(1)} %get-tuple-element.53), channel_id=1, source_target_pairs={{0,1},{1,0},{2,3},{3,2},{4,5},{5,4},{6,7},{7,6},{8,9},{9,8},{10,11... | collective-permute-start | bytes 393224 | tf_op jit(solution)/shard_map/ppermute | solution.py:418
  83.1 8.4 %collective-permute-start.20 = (bf16[64,2048]{1,0:T(8,128)(2,1)S(1)}, bf16[64,2048]{1,0:T(8,128)(2,1)S(1)}, u32[]{:S(2)}, u32[]{:S(2)}) collective-permute-start(bf16[64,2048]{1,0:T(8,128)(2,1)S(1)} %get-tuple-element.56), channel_id=1, source_target_pairs={{0,16},{16,0},{1,17},{17,1},{2,18},{18,2},{3,19},{19,3},{4,20},{20... | collective-permute-start | bytes 786440 | tf_op jit(solution)/shard_map/ppermute | solution.py:457
  84.9 8.1 %collective-permute-start.22 = (bf16[64,2048]{1,0:T(8,128)(2,1)S(1)}, bf16[64,2048]{1,0:T(8,128)(2,1)S(1)}, u32[]{:S(2)}, u32[]{:S(2)}) collective-permute-start(bf16[64,2048]{1,0:T(8,128)(2,1)S(1)} %get-tuple-element.58), channel_id=1, source_target_pairs={{0,2},{1,3},{2,0},{3,1},{4,6},{5,7},{6,4},{7,5},{8,10},{9,11},{10,... | collective-permute-start | bytes 786440 | tf_op jit(solution)/shard_map/ppermute | solution.py:458
  91.5 7.5 %collective-permute-start.21 = (bf16[64,2048]{1,0:T(8,128)(2,1)S(1)}, bf16[64,2048]{1,0:T(8,128)(2,1)S(1)}, u32[]{:S(2)}, u32[]{:S(2)}) collective-permute-start(bf16[64,2048]{1,0:T(8,128)(2,1)S(1)} %join.8), channel_id=1, source_target_pairs={{0,2},{1,3},{2,0},{3,1},{4,6},{5,7},{6,4},{7,5},{8,10},{9,11},{10,... | collective-permute-start | bytes 786440 | tf_op jit(solution)/shard_map/ppermute | solution.py:461
  93.1 7.3 %collective-permute-start.23 = (bf16[64,2048]{1,0:T(8,128)(2,1)S(1)}, bf16[64,2048]{1,0:T(8,128)(2,1)S(1)}, u32[]{:S(2)}, u32[]{:S(2)}) collective-permute-start(bf16[64,2048]{1,0:T(8,128)(2,1)S(1)} %join.9), channel_id=1, source_target_pairs={{0,12},{1,13},{2,14},{3,15},{4,0},{5,1},{6,2},{7,3},{8,4},{9,5},{1... | collective-permute-start | bytes 786440 | tf_op jit(solution)/shard_map/ppermute | solution.py:462
  95.1 12.3 %collective-permute-start.6 = (bf16[64,1024]{1,0:T(8,128)(2,1)S(1)}, bf16[64,1024]{1,0:T(8,128)(2,1)S(1)}, u32[]{:S(2)}, u32[]{:S(2)}) collective-permute-start(bf16[64,1024]{1,0:T(8,128)(2,1)S(1)} %get-tuple-element.45), channel_id=1, source_target_pairs={{0,16},{16,0},{1,17},{17,1},{2,18},{18,2},{3,19},{19,3},{4,20},{20... | collective-permute-start | bytes 393224 | tf_op jit(solution)/shard_map/ppermute | solution.py:431
  100.5 7.6 %collective-permute-start.24 = (bf16[64,1024]{1,0:T(8,128)(2,1)S(1)}, bf16[64,1024]{1,0:T(8,128)(2,1)S(1)}, u32[]{:S(2)}, u32[]{:S(2)}) collective-permute-start(bf16[64,1024]{1,0:T(8,128)(2,1)S(1)} %get-tuple-element.59), channel_id=1, source_target_pairs={{0,12},{1,13},{2,14},{3,15},{4,0},{5,1},{6,2},{7,3},{8,4},{9,5},{1... | collective-permute-start | bytes 393224 | tf_op jit(solution)/shard_map/ppermute | solution.py:431
  104.2 7.7 %collective-permute-start.25 = (bf16[64,1024]{1,0:T(8,128)(2,1)S(1)}, bf16[64,1024]{1,0:T(8,128)(2,1)S(1)}, u32[]{:S(2)}, u32[]{:S(2)}) collective-permute-start(bf16[64,1024]{1,0:T(8,128)(2,1)S(1)} %get-tuple-element.60), channel_id=1, source_target_pairs={{0,28},{1,29},{2,30},{3,31},{4,16},{5,17},{6,18},{7,19},{8,20},{9,... | collective-permute-start | bytes 393224 | tf_op jit(solution)/shard_map/ppermute | solution.py:431
  (18 other events, 116.5 us)

commit v6 on v5

--- a/solution.py
+++ b/solution.py
@@ -196,13 +196,13 @@
 
 
 def pack_kernel(after_any, *refs):
-    rows_refs, out_ref = refs[:-1], refs[-1]
-    count = rows_refs[0].shape[0]
-    for at, ref in enumerate(rows_refs):
-        out_ref[at * count : (at + 1) * count, :] = ref[...]
-
-
-def expert_kernel(experts, after_any, here_ref, across_ref, gate_ref, up_ref, down_ref, near_ref, *far_refs):
+    count = refs[0].shape[0]
+    for at, ref in enumerate(refs[:-1]):
+        refs[-1][at * count : (at + 1) * count, :] = ref[...]
+
+
+def expert_kernel(experts, after_any, here_ref, across_ref, gate_ref, up_ref, down_ref, *out_refs):
+    near_ref, *far_refs = out_refs
     model = gate_ref.shape[1]
     packet = jnp.concatenate([here_ref[...], across_ref[...]], axis=0)
     rows = packet[:, :model]
@@ -217,9 +217,9 @@
     result = dot(inner, down_ref[...]).astype(BF16)
     half = near_ref.shape[0]
     near_ref[...] = result[:half]
-    count = half // len(far_refs)
+    height = half // len(far_refs)
     for at, far_ref in enumerate(far_refs):
-        far_ref[...] = result[half + at * count : half + (at + 1) * count]
+        far_ref[...] = result[half + at * height : half + (at + 1) * height]
 
 
 def join_kernel(first, back_count, after_count, near_ref, *refs):
@@ -238,6 +238,13 @@
     mine, other = (own_columns(own_ref, by) + own_columns(side_ref, by).astype(F32) for by in (0, 1))
     base_ref[...] = state_ref[...] + mine
     other_ref[...] = other.astype(BF16)
+
+
+def last_kernel(base_ref, *refs):
+    total = base_ref[...]
+    for ref in refs[:-1]:
+        total = total + ref[...].astype(F32)
+    refs[-1][...] = total.astype(BF16)
 
 
 def sum_kernel(*refs):
@@ -395,9 +402,8 @@
         name="norm",
     )(share, hidden_in, down_rows, norm_gain[None, :], router_proj.T, expert_ids.T, *shares)
 
-    def run_expert(rows, after, run_after, pieces=1):
+    def run_expert(rows, after, run_after, back=1):
         half = len(rows) * row_count
-        out = [jax.ShapeDtypeStruct((half // cuts, model), BF16) for cuts in [1] + [pieces] * pieces]
         here = pl.pallas_call(
             pack_kernel,
             out_shape=jax.ShapeDtypeStruct((half, model + extra), BF16),
@@ -409,7 +415,9 @@
         across = lax.ppermute(here, "ep", core_swap)
         near, *far = pl.pallas_call(
             functools.partial(expert_kernel, experts),
-            out_shape=out,
+            out_shape=[
+                jax.ShapeDtypeStruct((half // cuts, model), BF16) for cuts in [1] + [back] * back
+            ],
             in_specs=[ANY] + [WHOLE] * 5,
             compiler_params=pltpu.CompilerParams(vmem_limit_bytes=24 * 2**20),
             cost_estimate=cost(6 * half * model * gate_rows.shape[0], 12 * 2**20),
@@ -450,14 +458,15 @@
         later = run_expert([far, near_side, two], early[0], packet)
         own_sum, side_sum, near_sum = join(*early, [F32, BF16, F32])
         side_in = lax.ppermute(side_sum, "ep", side_swap)
-        far_sum, near_side_sum, two_sum = join(*later, [BF16, F32, F32])
-        far_in = lax.ppermute(far_sum, "grp", plane_swap)
-        last = run_expert([far_side, two_side], later[0], far_sum, 4)
-        far_side_sum, two_side_sum = join(*last, [BF16, BF16], 0, [side_in, far_in])
+        last = run_expert([far_side, two_side], later[0], side_sum, 2)
+        near_side_sum, two_sum = join(*later, [F32, F32], 1)
+        far_side_sum, two_side_sum = join(*last, [BF16, BF16], 0, [side_in])
         far_side_in = lax.ppermute(far_side_sum, "grp", plane_swap)
         two_side_in = lax.ppermute(two_side_sum, "ep", side_swap)
         [near_side_sum] = join(near_side_sum, [far_side_in], [BF16])
         [two_sum] = join(two_sum, [two_side_in], [BF16])
+        [far_sum] = join(*later, [BF16], 0, [far_side_in])
+        far_in = lax.ppermute(far_sum, "grp", plane_swap)
         near_side_in = lax.ppermute(near_side_sum, "ep", side_swap)
         two_in = lax.ppermute(two_sum, both_axes, backward)
         part = (row_count, columns)
@@ -481,10 +490,17 @@
         near_mine, near_other = by_columns(
             sum_kernel, BF16, near_sum, far_in, near_side_in, two_in
         )
-        result = base + send(own_other, "grp", plane_swap)
-        result = result + send(near_mine, both_axes, backward)
-        result = result + send(near_other, both_axes, crossed(backward))
-        return result.astype(BF16)
+        own_over = lax.ppermute(own_other, "grp", plane_swap)
+        mine_in = lax.ppermute(near_mine, both_axes, backward)
+        other_in = lax.ppermute(near_other, both_axes, crossed(backward))
+        return pl.pallas_call(
+            last_kernel,
+            out_shape=jax.ShapeDtypeStruct(part, BF16),
+            in_specs=[WHOLE] * 4,
+            compiler_params=pltpu.CompilerParams(vmem_limit_bytes=16 * 2**20),
+            cost_estimate=cost(0, 2**20),
+            name="last",
+        )(base, own_over, mine_in, other_in)
 
     line = [packet]
     for _ in range(1, ring):

time: 113 us -> 111 us (0.982)
  starting transfers between devices: 38.1 us -> 34.9 us
  waiting for transfers between devices: 41.7 us -> 43 us
    ppermute x1, waiting for transfers between devices: 5.17 us -> 0.01 us  [local(): far_side_in = lax.ppermute(far_side_sum, 'grp', plane_swap)]
    ppermute x1, waiting for transfers between devices: 0.01 us -> 4.18 us  [local(): two_side_in = lax.ppermute(two_side_sum, 'ep', side_swap)]
    ppermute x1, waiting for transfers between devices: 0.06 us -> 2.6 us  [local(): far_in = lax.ppermute(far_sum, 'grp', plane_swap)]
    ppermute x1, waiting for transfers between devices: 3.88 us -> 1.87 us  [local(): near_side_in = lax.ppermute(near_side_sum, 'ep', side_swap)]
    ppermute x1, starting transfers between devices: 1.81 us -> 0.08 us  [local(): far_in = lax.ppermute(far_sum, 'grp', plane_swap)]
    ppermute x1, waiting for transfers between devices: 1.96 us -> 3.65 us  [local(): side_in = lax.ppermute(side_sum, 'ep', side_swap)]
    ppermute x3, waiting for transfers between devices: 4.57 us -> 5.98 us  [the longest x1 4.56 us: local(): other_in = lax.ppermute(near_other, both_axes, crossed(backward))]
    ppermute x6 -> x4, waiting for transfers between devices: 1.34 us -> 0.01 us  [run_expert(): return (near, [lax.ppermute(part, 'ep', core_swap) for part in far])]
  transfers between devices with their start and end apart: 27 -> 25, of which waited for: 16 -> 15; matrix products, arithmetic and copies ran while one was open for 2% -> 2% of each run, Pallas kernels for 15% -> 16%
where the time goes in v6:
time: 111 us
  waiting for transfers between devices  43 us (39%)
  starting transfers between devices  34.9 us (31%)
  Pallas kernels  26.6 us (24%)
  local copies, waits for them, and re-layouts  5.11 us (5%)
    pallas_call x3, Pallas kernels, run_expert(): pl.pallas_call(functools.partial(expert_kernel, experts), out_shape=[jax....  10.3 us
    all_to_all x1, waiting for transfers between devices, local(): lax.all_to_all(outgoing, 'ep', split_axis=0, concat_axis=0, tiled=True)  8.7 us
    all_to_all x1, starting transfers between devices, local(): lax.all_to_all(outgoing, 'ep', split_axis=0, concat_axis=0, tiled=True)  7.38 us
    ppermute x1, waiting for transfers between devices, local(): near = lax.ppermute(packet, both_axes, onward)  6.55 us
    pallas_call x1, Pallas kernels, local(): pl.pallas_call(functools.partial(moved_kernel, dims), out_shape=jax.Shape...  4.95 us
    ppermute x1, waiting for transfers between devices, local(): other_in = lax.ppermute(near_other, both_axes, crossed(backward))  4.56 us
    ppermute x1, waiting for transfers between devices, local(): two_side_in = lax.ppermute(two_side_sum, 'ep', side_swap)  4.18 us
    unnamed x30, local copies, waits for them, and re-layouts  3.78 us
  transfers between devices with their start and end apart: 25, of which 15 were waited for; matrix products, arithmetic and copies ran while one was open for 2% of the time, Pallas kernels for 16%

profile of v6, /device:TPU:0, one launch (start us, length us, event | category | flops | bytes accessed | tf_op | source)
XLA Modules:
  0.0 110.8 jit_solution(1216567691281373121)
XLA Ops:
  0.0 2.8 %pick.1 = bf16[16,16,1152]{2,1,0:T(8,128)(2,1)} custom-call(s32[2,16]{1,0:T(2,128)} %bitcast.22, bf16[64,9216]{1,0:T(8,128)(2,1)} %cache.1), custom_call_target="tpu_custom_call" | custom-call | bytes 4194304 | tf_op jit(solution)/shard_map/pick/pallas_call | solution.py:302
  2.8 7.4 %all-to-all-start = ((bf16[16,16,1152]{2,1,0:T(8,128)(2,1)}), bf16[16,16,1152]{2,1,0:T(8,128)(2,1)S(1)}, u32[]{:S(2)}, u32[]{:S(2)}) async-start(bf16[16,16,1152]{2,1,0:T(8,128)(2,1)} %pick.1), calls=%async_computation | async-start | bytes 1179648 | tf_op jit(solution)/shard_map/all_to_all | solution.py:316
  12.4 2.7 %attend_resident.1 = (bf16[512,640]{1,0:T(8,128)(2,1)S(1)}, f32[512,640]{1,0:T(8,128)S(1)}) custom-call(bf16[64,1024]{1,0:T(8,128)(2,1)S(1)} %copy-done.8, bf16[64,512]{1,0:T(8,128)(2,1)S(1)} %copy-done.10, bf16[16,2304]{1,0:T(8,128)(2,1)S(1)} %copy-done.9, bf16[64,9216]{1,0:T(8,128)(2,1)S(1)} %copy-done.2, bf16[8,128,512]{2,1,0:T(8,128)(2,1)S(1)} %copy-done.7, ...), custom_call_target="tpu_custom_call" | custom-call | flops 1283457024 | bytes 8388608 | tf_op jit(solution)/shard_map/attend_resident/pallas_call | solution.py:341
  17.1 8.7 %all-to-all-done.moved_any = bf16[16,16,1152]{2,1,0:T(8,128)(2,1)S(1)} async-done(((bf16[16,16,1152]{2,1,0:T(8,128)(2,1)}), bf16[16,16,1152]{2,1,0:T(8,128)(2,1)S(1)}, u32[]{:S(2)}, u32[]{:S(2)}) %all-to-all-start) | async-done | bytes 589856 | tf_op jit(solution)/shard_map/all_to_all | solution.py:316
  26.6 5.0 %attend_moved.1.after_any.own_any = bf16[64,2048]{1,0:T(8,128)(2,1)} custom-call(bf16[16,16,1152]{2,1,0:T(8,128)(2,1)} %copy-done.11, bf16[512,640]{1,0:T(8,128)(2,1)} %copy-done.3, f32[64,512]{1,0:T(8,128)} %reshape.110.bias_any, f32[512,640]{1,0:T(8,128)} %copy-done.1, bf16[8,512,128]{2,1,0:T(8,128)(2,1)} %value_any.1, bf16[1024,2048]{1,0:T(8,128)(2,1)} %proj_any.1), custom_call_target="tpu_custom_call" | custom-call | flops 603979776 | bytes 10485760 | tf_op jit(solution)/shard_map/attend_moved/pallas_call | solution.py:352
  34.1 3.6 %load.1 = (bf16[704,2048]{1,0:T(8,128)(2,1)S(1)}, bf16[704,2048]{1,0:T(8,128)(2,1)S(1)}, bf16[704,2048]{1,0:T(8,128)(2,1)S(1)}) custom-call(bf16[64,2048]{1,0:T(8,128)(2,1)S(1)} %copy-done, bf16[704,2048]{1,0:T(8,128)(2,1)} %bitcast.18, bf16[704,2048]{1,0:T(8,128)(2,1)} %bitcast.19, bf16[704,2048]{1,0:T(8,128)(2,1)} %bitcast.20), custom_call_target="tpu_custom_call" | custom-call | bytes 12582912 | tf_op jit(solution)/shard_map/load/pallas_call | solution.py:374
  37.7 2.3 %collective-permute-done.refs_0_ = bf16[64,2048]{1,0:T(8,128)(2,1)S(1)} collective-permute-done((bf16[64,2048]{1,0:T(8,128)(2,1)}, bf16[64,2048]{1,0:T(8,128)(2,1)S(1)}, u32[]{:S(2)}, u32[]{:S(2)}) %collective-permute-start) | collective-permute-done | bytes 262176 | tf_op jit(solution)/shard_map/ppermute | solution.py:371
  40.8 2.1 %collective-permute-start.2 = (bf16[64,2176]{1,0:T(8,128)(2,1)S(1)}, bf16[64,2176]{1,0:T(8,128)(2,1)S(1)}, u32[]{:S(2)}, u32[]{:S(2)}) collective-permute-start(bf16[64,2176]{1,0:T(8,128)(2,1)S(1)} %get-tuple-element.34.after_any.refs_0_), channel_id=1, source_target_pairs={{0,4},{1,5},{2,6},{3,7},{4,8},{5,9},{6,10},{7,11},{8,12},{9,13},{1... | collective-permute-start | bytes 835592 | tf_op jit(solution)/shard_map/ppermute | solution.py:450
  43.8 6.6 %collective-permute-done.2.refs_2_ = bf16[64,2176]{1,0:T(8,128)(2,1)S(1)} collective-permute-done((bf16[64,2176]{1,0:T(8,128)(2,1)S(1)}, bf16[64,2176]{1,0:T(8,128)(2,1)S(1)}, u32[]{:S(2)}, u32[]{:S(2)}) %collective-permute-start.2) | collective-permute-done | bytes 278560 | tf_op jit(solution)/shard_map/ppermute | solution.py:450
  52.9 3.5 %collective-permute-start.7 = (bf16[64,2176]{1,0:T(8,128)(2,1)S(1)}, bf16[64,2176]{1,0:T(8,128)(2,1)S(1)}, u32[]{:S(2)}, u32[]{:S(2)}) collective-permute-start(bf16[64,2176]{1,0:T(8,128)(2,1)S(1)} %collective-permute-done.2.refs_2_), channel_id=1, source_target_pairs={{0,16},{16,0},{1,17},{17,1},{2,18},{18,2},{3,19},{19,3},{4,20},{20... | collective-permute-start | bytes 835592 | tf_op jit(solution)/shard_map/ppermute | solution.py:454
  56.4 3.9 %expert.3 = (bf16[192,2048]{1,0:T(8,128)(2,1)S(1)}, bf16[192,2048]{1,0:T(8,128)(2,1)S(1)}) custom-call(bf16[64,2176]{1,0:T(8,128)(2,1)S(1)} %get-tuple-element.34.after_any.refs_0_, bf16[192,2176]{1,0:T(8,128)(2,1)S(1)} %pack.3.here_ref, bf16[192,2176]{1,0:T(8,128)(2,1)S(1)} %collective-permute-done.3.across_ref, ...), custom_call_target="tpu_custom_call" | custom-call | flops 3321888768 | bytes 12582912 | tf_op jit(solution)/shard_map/expert/pallas_call | solution.py:416
  63.8 1.7 %collective-permute-start.11 = (bf16[64,2176]{1,0:T(8,128)(2,1)S(1)}, bf16[64,2176]{1,0:T(8,128)(2,1)S(1)}, u32[]{:S(2)}, u32[]{:S(2)}) collective-permute-start(bf16[64,2176]{1,0:T(8,128)(2,1)S(1)} %collective-permute-done.8.refs_1_), channel_id=1, source_target_pairs={{0,16},{16,0},{1,17},{17,1},{2,18},{18,2},{3,19},{19,3},{4,20},{20... | collective-permute-start | bytes 835592 | tf_op jit(solution)/shard_map/ppermute | solution.py:456
  65.5 3.8 %expert.4 = (bf16[192,2048]{1,0:T(8,128)(2,1)S(1)}, bf16[192,2048]{1,0:T(8,128)(2,1)S(1)}) custom-call(bf16[64,2176]{1,0:T(8,128)(2,1)S(1)} %get-tuple-element.34.after_any.refs_0_, bf16[192,2176]{1,0:T(8,128)(2,1)S(1)} %pack.4.here_ref, bf16[192,2176]{1,0:T(8,128)(2,1)S(1)} %collective-permute-done.10.across_ref, ...), custom_call_target="tpu_custom_call" | custom-call | flops 3321888768 | bytes 12582912 | tf_op jit(solution)/shard_map/expert/pallas_call | solution.py:416
  69.4 2.8 %collective-permute-done.12.refs_1_ = bf16[64,2176]{1,0:T(8,128)(2,1)S(1)} collective-permute-done((bf16[64,2176]{1,0:T(8,128)(2,1)S(1)}, bf16[64,2176]{1,0:T(8,128)(2,1)S(1)}, u32[]{:S(2)}, u32[]{:S(2)}) %collective-permute-start.12) | collective-permute-done | bytes 278560 | tf_op jit(solution)/shard_map/ppermute | solution.py:455
  74.8 2.6 %expert.5 = (bf16[128,2048]{1,0:T(8,128)(2,1)S(1)}, bf16[64,2048]{1,0:T(8,128)(2,1)S(1)}, bf16[64,2048]{1,0:T(8,128)(2,1)S(1)}) custom-call(bf16[64,2048]{1,0:T(8,128)(2,1)S(1)} %get-tuple-element.40.after_any, bf16[128,2176]{1,0:T(8,128)(2,1)S(1)} %pack.5.here_ref, bf16[128,2176]{1,0:T(8,128)(2,1)S(1)} %collective-permute-done.13.across_ref, ...), custom_call_target="tpu_custom_call" | custom-call | flops 2214592512 | bytes 12582912 | tf_op jit(solution)/shard_map/expert/pallas_call | solution.py:416
  78.0 3.7 %collective-permute-done.5.side_ref.refs_0_ = bf16[64,2048]{1,0:T(8,128)(2,1)S(1)} collective-permute-done((bf16[64,2048]{1,0:T(8,128)(2,1)S(1)}, bf16[64,2048]{1,0:T(8,128)(2,1)S(1)}, u32[]{:S(2)}, u32[]{:S(2)}) %collective-permute-start.5) | collective-permute-done | bytes 262176 | tf_op jit(solution)/shard_map/ppermute | solution.py:460
  83.3 1.7 %collective-permute-start.16 = (bf16[64,2048]{1,0:T(8,128)(2,1)S(1)}, bf16[64,2048]{1,0:T(8,128)(2,1)S(1)}, u32[]{:S(2)}, u32[]{:S(2)}) collective-permute-start(bf16[64,2048]{1,0:T(8,128)(2,1)S(1)} %get-tuple-element.48), channel_id=1, source_target_pairs={{0,16},{16,0},{1,17},{17,1},{2,18},{18,2},{3,19},{19,3},{4,20},{20... | collective-permute-start | bytes 786440 | tf_op jit(solution)/shard_map/ppermute | solution.py:464
  85.1 4.2 %collective-permute-done.20.refs_0_ = bf16[64,2048]{1,0:T(8,128)(2,1)S(1)} collective-permute-done((bf16[64,2048]{1,0:T(8,128)(2,1)S(1)}, bf16[64,2048]{1,0:T(8,128)(2,1)S(1)}, u32[]{:S(2)}, u32[]{:S(2)}) %collective-permute-start.20) | collective-permute-done | bytes 262176 | tf_op jit(solution)/shard_map/ppermute | solution.py:465
  89.3 2.0 %collective-permute-start.21 = (bf16[64,2048]{1,0:T(8,128)(2,1)S(1)}, bf16[64,2048]{1,0:T(8,128)(2,1)S(1)}, u32[]{:S(2)}, u32[]{:S(2)}) collective-permute-start(bf16[64,2048]{1,0:T(8,128)(2,1)S(1)} %join.11), channel_id=1, source_target_pairs={{0,12},{1,13},{2,14},{3,15},{4,0},{5,1},{6,2},{7,3},{8,4},{9,5},{1... | collective-permute-start | bytes 786440 | tf_op jit(solution)/shard_map/ppermute | solution.py:471
  93.1 2.1 %collective-permute-start.6 = (bf16[64,1024]{1,0:T(8,128)(2,1)S(1)}, bf16[64,1024]{1,0:T(8,128)(2,1)S(1)}, u32[]{:S(2)}, u32[]{:S(2)}) collective-permute-start(bf16[64,1024]{1,0:T(8,128)(2,1)S(1)} %get-tuple-element.42), channel_id=1, source_target_pairs={{0,16},{16,0},{1,17},{17,1},{2,18},{18,2},{3,19},{19,3},{4,20},{20... | collective-permute-start | bytes 393224 | tf_op jit(solution)/shard_map/ppermute | solution.py:493
  95.9 1.9 %collective-permute-done.19.refs_2_ = bf16[64,2048]{1,0:T(8,128)(2,1)S(1)} collective-permute-done((bf16[64,2048]{1,0:T(8,128)(2,1)S(1)}, bf16[64,2048]{1,0:T(8,128)(2,1)S(1)}, u32[]{:S(2)}, u32[]{:S(2)}) %collective-permute-start.19) | collective-permute-done | bytes 262176 | tf_op jit(solution)/shard_map/ppermute | solution.py:470
  97.8 2.6 %collective-permute-done.18.refs_1_ = bf16[64,2048]{1,0:T(8,128)(2,1)S(1)} collective-permute-done((bf16[64,2048]{1,0:T(8,128)(2,1)S(1)}, bf16[64,2048]{1,0:T(8,128)(2,1)S(1)}, u32[]{:S(2)}, u32[]{:S(2)}) %collective-permute-start.18) | collective-permute-done | bytes 262176 | tf_op jit(solution)/shard_map/ppermute | solution.py:469
  100.5 1.9 %collective-permute-start.22 = (bf16[64,1024]{1,0:T(8,128)(2,1)S(1)}, bf16[64,1024]{1,0:T(8,128)(2,1)S(1)}, u32[]{:S(2)}, u32[]{:S(2)}) collective-permute-start(bf16[64,1024]{1,0:T(8,128)(2,1)S(1)} %get-tuple-element.53), channel_id=1, source_target_pairs={{0,12},{1,13},{2,14},{3,15},{4,0},{5,1},{6,2},{7,3},{8,4},{9,5},{1... | collective-permute-start | bytes 393224 | tf_op jit(solution)/shard_map/ppermute | solution.py:494
  105.5 4.6 %collective-permute-done.23.refs_2_ = bf16[64,1024]{1,0:T(8,128)(2,1)S(1)} collective-permute-done((bf16[64,1024]{1,0:T(8,128)(2,1)S(1)}, bf16[64,1024]{1,0:T(8,128)(2,1)S(1)}, u32[]{:S(2)}, u32[]{:S(2)}) %collective-permute-start.23) | collective-permute-done | bytes 131104 | tf_op jit(solution)/shard_map/ppermute | solution.py:495
  (100 shorter events, 26.4 us)
Async XLA Ops:
  2.8 22.9 %all-to-all-start = ((bf16[16,16,1152]{2,1,0:T(8,128)(2,1)}), bf16[16,16,1152]{2,1,0:T(8,128)(2,1)S(1)}, u32[]{:S(2)}, u32[]{:S(2)}) async-start(bf16[16,16,1152]{2,1,0:T(8,128)(2,1)} %pick.1), calls=%async_computation | async-start | bytes 1179648 | tf_op jit(solution)/shard_map/all_to_all | solution.py:316
  31.6 8.5 %collective-permute-start = (bf16[64,2048]{1,0:T(8,128)(2,1)}, bf16[64,2048]{1,0:T(8,128)(2,1)S(1)}, u32[]{:S(2)}, u32[]{:S(2)}) collective-permute-start(bf16[64,2048]{1,0:T(8,128)(2,1)} %attend_moved.1.after_any.own_any), channel_id=1, source_target_pairs={{0,16},{16,0},{1,17},{17,1},{2,18},{18,2},{3,19},{19,3},{4,20},{20... | collective-permute-start | bytes 786440 | tf_op jit(solution)/shard_map/ppermute | solution.py:371
  40.8 9.6 %collective-permute-start.2 = (bf16[64,2176]{1,0:T(8,128)(2,1)S(1)}, bf16[64,2176]{1,0:T(8,128)(2,1)S(1)}, u32[]{:S(2)}, u32[]{:S(2)}) collective-permute-start(bf16[64,2176]{1,0:T(8,128)(2,1)S(1)} %get-tuple-element.34.after_any.refs_0_), channel_id=1, source_target_pairs={{0,4},{1,5},{2,6},{3,7},{4,8},{5,9},{6,10},{7,11},{8,12},{9,13},{1... | collective-permute-start | bytes 835592 | tf_op jit(solution)/shard_map/ppermute | solution.py:450
  42.9 8.1 %collective-permute-start.1 = (bf16[64,2176]{1,0:T(8,128)(2,1)S(1)}, bf16[64,2176]{1,0:T(8,128)(2,1)S(1)}, u32[]{:S(2)}, u32[]{:S(2)}) collective-permute-start(bf16[64,2176]{1,0:T(8,128)(2,1)S(1)} %get-tuple-element.34.after_any.refs_0_), channel_id=1, source_target_pairs={{0,2},{1,3},{2,0},{3,1},{4,6},{5,7},{6,4},{7,5},{8,10},{9,11},{10,... | collective-permute-start | bytes 835592 | tf_op jit(solution)/shard_map/ppermute | solution.py:451
  51.0 5.4 %collective-permute-start.3 = (bf16[192,2176]{1,0:T(8,128)(2,1)S(1)}, bf16[192,2176]{1,0:T(8,128)(2,1)S(1)}, u32[]{:S(2)}, u32[]{:S(2)}) collective-permute-start(bf16[192,2176]{1,0:T(8,128)(2,1)S(1)} %pack.3.here_ref), channel_id=1, source_target_pairs={{0,1},{1,0},{2,3},{3,2},{4,5},{5,4},{6,7},{7,6},{8,9},{9,8},{10,11... | collective-permute-start | bytes 2506760 | tf_op jit(solution)/shard_map/ppermute | solution.py:415
  51.1 10.9 %collective-permute-start.9 = (bf16[64,2176]{1,0:T(8,128)(2,1)S(1)}, bf16[64,2176]{1,0:T(8,128)(2,1)S(1)}, u32[]{:S(2)}, u32[]{:S(2)}) collective-permute-start(bf16[64,2176]{1,0:T(8,128)(2,1)S(1)} %collective-permute-done.2.refs_2_), channel_id=1, source_target_pairs={{0,4},{1,5},{2,6},{3,7},{4,8},{5,9},{6,10},{7,11},{8,12},{9,13},{1... | collective-permute-start | bytes 835592 | tf_op jit(solution)/shard_map/ppermute | solution.py:452
  51.7 10.3 %collective-permute-start.8 = (bf16[64,2176]{1,0:T(8,128)(2,1)S(1)}, bf16[64,2176]{1,0:T(8,128)(2,1)S(1)}, u32[]{:S(2)}, u32[]{:S(2)}) collective-permute-start(bf16[64,2176]{1,0:T(8,128)(2,1)S(1)} %collective-permute-done.2.refs_2_), channel_id=1, source_target_pairs={{0,2},{1,3},{2,0},{3,1},{4,6},{5,7},{6,4},{7,5},{8,10},{9,11},{10,... | collective-permute-start | bytes 835592 | tf_op jit(solution)/shard_map/ppermute | solution.py:453
  52.9 10.1 %collective-permute-start.7 = (bf16[64,2176]{1,0:T(8,128)(2,1)S(1)}, bf16[64,2176]{1,0:T(8,128)(2,1)S(1)}, u32[]{:S(2)}, u32[]{:S(2)}) collective-permute-start(bf16[64,2176]{1,0:T(8,128)(2,1)S(1)} %collective-permute-done.2.refs_2_), channel_id=1, source_target_pairs={{0,16},{16,0},{1,17},{17,1},{2,18},{18,2},{3,19},{19,3},{4,20},{20... | collective-permute-start | bytes 835592 | tf_op jit(solution)/shard_map/ppermute | solution.py:454
  63.0 2.5 %collective-permute-start.10 = (bf16[192,2176]{1,0:T(8,128)(2,1)S(1)}, bf16[192,2176]{1,0:T(8,128)(2,1)S(1)}, u32[]{:S(2)}, u32[]{:S(2)}) collective-permute-start(bf16[192,2176]{1,0:T(8,128)(2,1)S(1)} %pack.4.here_ref), channel_id=1, source_target_pairs={{0,1},{1,0},{2,3},{3,2},{4,5},{5,4},{6,7},{7,6},{8,9},{9,8},{10,11... | collective-permute-start | bytes 2506760 | tf_op jit(solution)/shard_map/ppermute | solution.py:415
  63.1 9.1 %collective-permute-start.12 = (bf16[64,2176]{1,0:T(8,128)(2,1)S(1)}, bf16[64,2176]{1,0:T(8,128)(2,1)S(1)}, u32[]{:S(2)}, u32[]{:S(2)}) collective-permute-start(bf16[64,2176]{1,0:T(8,128)(2,1)S(1)} %collective-permute-done.9.refs_2_), channel_id=1, source_target_pairs={{0,2},{1,3},{2,0},{3,1},{4,6},{5,7},{6,4},{7,5},{8,10},{9,11},{10,... | collective-permute-start | bytes 835592 | tf_op jit(solution)/shard_map/ppermute | solution.py:455
  63.8 8.7 %collective-permute-start.11 = (bf16[64,2176]{1,0:T(8,128)(2,1)S(1)}, bf16[64,2176]{1,0:T(8,128)(2,1)S(1)}, u32[]{:S(2)}, u32[]{:S(2)}) collective-permute-start(bf16[64,2176]{1,0:T(8,128)(2,1)S(1)} %collective-permute-done.8.refs_1_), channel_id=1, source_target_pairs={{0,16},{16,0},{1,17},{17,1},{2,18},{18,2},{3,19},{19,3},{4,20},{20... | collective-permute-start | bytes 835592 | tf_op jit(solution)/shard_map/ppermute | solution.py:456
  65.5 7.6 %collective-permute-start.4 = (bf16[192,2048]{1,0:T(8,128)(2,1)S(1)}, bf16[192,2048]{1,0:T(8,128)(2,1)S(1)}, u32[]{:S(2)}, u32[]{:S(2)}) collective-permute-start(bf16[192,2048]{1,0:T(8,128)(2,1)S(1)} %get-tuple-element.38), channel_id=1, source_target_pairs={{0,1},{1,0},{2,3},{3,2},{4,5},{5,4},{6,7},{7,6},{8,9},{9,8},{10,11... | collective-permute-start | bytes 2359304 | tf_op jit(solution)/shard_map/ppermute | solution.py:426
  72.6 12.4 %collective-permute-start.17 = (bf16[192,2048]{1,0:T(8,128)(2,1)S(1)}, bf16[192,2048]{1,0:T(8,128)(2,1)S(1)}, u32[]{:S(2)}, u32[]{:S(2)}) collective-permute-start(bf16[192,2048]{1,0:T(8,128)(2,1)S(1)} %get-tuple-element.49), channel_id=1, source_target_pairs={{0,1},{1,0},{2,3},{3,2},{4,5},{5,4},{6,7},{7,6},{8,9},{9,8},{10,11... | collective-permute-start | bytes 2359304 | tf_op jit(solution)/shard_map/ppermute | solution.py:426
  73.3 8.4 %collective-permute-start.5 = (bf16[64,2048]{1,0:T(8,128)(2,1)S(1)}, bf16[64,2048]{1,0:T(8,128)(2,1)S(1)}, u32[]{:S(2)}, u32[]{:S(2)}) collective-permute-start(bf16[64,2048]{1,0:T(8,128)(2,1)S(1)} %get-tuple-element.40.after_any), channel_id=1, source_target_pairs={{0,2},{1,3},{2,0},{3,1},{4,6},{5,7},{6,4},{7,5},{8,10},{9,11},{10,... | collective-permute-start | bytes 786440 | tf_op jit(solution)/shard_map/ppermute | solution.py:460
  77.4 4.2 %collective-permute-start.14 = (bf16[64,2048]{1,0:T(8,128)(2,1)S(1)}, bf16[64,2048]{1,0:T(8,128)(2,1)S(1)}, u32[]{:S(2)}, u32[]{:S(2)}) collective-permute-start(bf16[64,2048]{1,0:T(8,128)(2,1)S(1)} %get-tuple-element.46), channel_id=1, source_target_pairs={{0,1},{1,0},{2,3},{3,2},{4,5},{5,4},{6,7},{7,6},{8,9},{9,8},{10,11... | collective-permute-start | bytes 786440 | tf_op jit(solution)/shard_map/ppermute | solution.py:426
  77.5 4.2 %collective-permute-start.15 = (bf16[64,2048]{1,0:T(8,128)(2,1)S(1)}, bf16[64,2048]{1,0:T(8,128)(2,1)S(1)}, u32[]{:S(2)}, u32[]{:S(2)}) collective-permute-start(bf16[64,2048]{1,0:T(8,128)(2,1)S(1)} %get-tuple-element.47), channel_id=1, source_target_pairs={{0,1},{1,0},{2,3},{3,2},{4,5},{5,4},{6,7},{7,6},{8,9},{9,8},{10,11... | collective-permute-start | bytes 786440 | tf_op jit(solution)/shard_map/ppermute | solution.py:426
  81.8 7.5 %collective-permute-start.20 = (bf16[64,2048]{1,0:T(8,128)(2,1)S(1)}, bf16[64,2048]{1,0:T(8,128)(2,1)S(1)}, u32[]{:S(2)}, u32[]{:S(2)}) collective-permute-start(bf16[64,2048]{1,0:T(8,128)(2,1)S(1)} %get-tuple-element.52), channel_id=1, source_target_pairs={{0,2},{1,3},{2,0},{3,1},{4,6},{5,7},{6,4},{7,5},{8,10},{9,11},{10,... | collective-permute-start | bytes 786440 | tf_op jit(solution)/shard_map/ppermute | solution.py:465
  83.3 8.0 %collective-permute-start.16 = (bf16[64,2048]{1,0:T(8,128)(2,1)S(1)}, bf16[64,2048]{1,0:T(8,128)(2,1)S(1)}, u32[]{:S(2)}, u32[]{:S(2)}) collective-permute-start(bf16[64,2048]{1,0:T(8,128)(2,1)S(1)} %get-tuple-element.48), channel_id=1, source_target_pairs={{0,16},{16,0},{1,17},{17,1},{2,18},{18,2},{3,19},{19,3},{4,20},{20... | collective-permute-start | bytes 786440 | tf_op jit(solution)/shard_map/ppermute | solution.py:464
  89.3 6.6 %collective-permute-start.21 = (bf16[64,2048]{1,0:T(8,128)(2,1)S(1)}, bf16[64,2048]{1,0:T(8,128)(2,1)S(1)}, u32[]{:S(2)}, u32[]{:S(2)}) collective-permute-start(bf16[64,2048]{1,0:T(8,128)(2,1)S(1)} %join.11), channel_id=1, source_target_pairs={{0,12},{1,13},{2,14},{3,15},{4,0},{5,1},{6,2},{7,3},{8,4},{9,5},{1... | collective-permute-start | bytes 786440 | tf_op jit(solution)/shard_map/ppermute | solution.py:471
  91.4 6.4 %collective-permute-start.19 = (bf16[64,2048]{1,0:T(8,128)(2,1)S(1)}, bf16[64,2048]{1,0:T(8,128)(2,1)S(1)}, u32[]{:S(2)}, u32[]{:S(2)}) collective-permute-start(bf16[64,2048]{1,0:T(8,128)(2,1)S(1)} %join.10), channel_id=1, source_target_pairs={{0,2},{1,3},{2,0},{3,1},{4,6},{5,7},{6,4},{7,5},{8,10},{9,11},{10,... | collective-permute-start | bytes 786440 | tf_op jit(solution)/shard_map/ppermute | solution.py:470
  92.9 7.4 %collective-permute-start.18 = (bf16[64,2048]{1,0:T(8,128)(2,1)S(1)}, bf16[64,2048]{1,0:T(8,128)(2,1)S(1)}, u32[]{:S(2)}, u32[]{:S(2)}) collective-permute-start(bf16[64,2048]{1,0:T(8,128)(2,1)S(1)} %join.8), channel_id=1, source_target_pairs={{0,16},{16,0},{1,17},{17,1},{2,18},{18,2},{3,19},{19,3},{4,20},{20... | collective-permute-start | bytes 786440 | tf_op jit(solution)/shard_map/ppermute | solution.py:469
  93.1 11.0 %collective-permute-start.6 = (bf16[64,1024]{1,0:T(8,128)(2,1)S(1)}, bf16[64,1024]{1,0:T(8,128)(2,1)S(1)}, u32[]{:S(2)}, u32[]{:S(2)}) collective-permute-start(bf16[64,1024]{1,0:T(8,128)(2,1)S(1)} %get-tuple-element.42), channel_id=1, source_target_pairs={{0,16},{16,0},{1,17},{17,1},{2,18},{18,2},{3,19},{19,3},{4,20},{20... | collective-permute-start | bytes 393224 | tf_op jit(solution)/shard_map/ppermute | solution.py:493
  100.5 5.0 %collective-permute-start.22 = (bf16[64,1024]{1,0:T(8,128)(2,1)S(1)}, bf16[64,1024]{1,0:T(8,128)(2,1)S(1)}, u32[]{:S(2)}, u32[]{:S(2)}) collective-permute-start(bf16[64,1024]{1,0:T(8,128)(2,1)S(1)} %get-tuple-element.53), channel_id=1, source_target_pairs={{0,12},{1,13},{2,14},{3,15},{4,0},{5,1},{6,2},{7,3},{8,4},{9,5},{1... | collective-permute-start | bytes 393224 | tf_op jit(solution)/shard_map/ppermute | solution.py:494
  102.4 7.7 %collective-permute-start.23 = (bf16[64,1024]{1,0:T(8,128)(2,1)S(1)}, bf16[64,1024]{1,0:T(8,128)(2,1)S(1)}, u32[]{:S(2)}, u32[]{:S(2)}) collective-permute-start(bf16[64,1024]{1,0:T(8,128)(2,1)S(1)} %get-tuple-element.54), channel_id=1, source_target_pairs={{0,28},{1,29},{2,30},{3,31},{4,16},{5,17},{6,18},{7,19},{8,20},{9,... | collective-permute-start | bytes 393224 | tf_op jit(solution)/shard_map/ppermute | solution.py:495
  (16 other events, 113.0 us)

commit v7 on v6

--- a/solution.py
+++ b/solution.py
@@ -291,7 +291,13 @@
     ring = ranks // 4
     core_swap = [(i, i ^ 1) for i in range(ranks)]
     side_swap = [(i, i ^ 2) for i in range(ranks)]
-    ring_next = [(i, (i + 4) % ranks) for i in range(ranks)]
+    visit = list(range(0, ring, 2)) + list(range(ring - 1 - ring % 2, 0, -2))
+    turn_of = {chip: at for at, chip in enumerate(visit)}
+
+    def along(rank, by):
+        return visit[(turn_of[rank // 4] + by) % ring] * 4 + rank % 4
+
+    ring_next = [(i, along(i, 1)) for i in range(ranks)]
     both_axes = ("grp", "ep")
 
     def turn(by):
@@ -364,7 +370,7 @@
             VMEM((row_count, head_count * value_absorb.shape[2]), BF16),
             pltpu.SemaphoreType.DMA((6,)),
         ],
-        compiler_params=pltpu.CompilerParams(vmem_limit_bytes=60 * 2**20),
+        compiler_params=pltpu.CompilerParams(vmem_limit_bytes=56 * 2**20),
         cost_estimate=cost(query_rows * moved_bias.shape[1] * (padded + latent), 10 * 2**20),
         name="attend_moved",
     )(arrived, query, moved_bias, mixed, value_absorb, output_proj)
@@ -441,7 +447,7 @@
     if ring == 4 and groups == 2:
         def ring_step(sign):
             return [
-                (g * ranks + i, g * ranks + (i + sign * 4 * (1 - 2 * g)) % ranks)
+                (g * ranks + i, g * ranks + along(i, sign * (1 - 2 * g)))
                 for g in range(2)
                 for i in range(ranks)
             ]
@@ -500,7 +506,7 @@
             compiler_params=pltpu.CompilerParams(vmem_limit_bytes=16 * 2**20),
             cost_estimate=cost(0, 2**20),
             name="last",
-        )(base, own_over, mine_in, other_in)
+        )(base, own_over, other_in, mine_in)
 
     line = [packet]
     for _ in range(1, ring):

time: 111 us -> 109 us (0.982)
  starting transfers between devices: 34.9 us -> 31.2 us
  waiting for transfers between devices: 43 us -> 44.2 us
    ppermute x1, starting transfers between devices: 0.08 us -> 2.13 us  [local(): far_in = lax.ppermute(far_sum, 'grp', plane_swap)]
    ppermute x1, starting transfers between devices: 3.53 us -> 1.52 us  [local(): far = lax.ppermute(near, 'grp', plane_swap)]
    ppermute x1, starting transfers between devices: 2.06 us -> 0.1 us  [local(): own_over = lax.ppermute(own_other, 'grp', plane_swap)]
    ppermute x1, waiting for transfers between devices: 0.75 us -> 2.59 us  [local(): two_in = lax.ppermute(two_sum, both_axes, backward)]
    ppermute x1, waiting for transfers between devices: 1.87 us -> 0.09 us  [local(): near_side_in = lax.ppermute(near_side_sum, 'ep', side_swap)]
    ppermute x1, starting transfers between devices: 0.59 us -> 2.31 us  [local(): two = lax.ppermute(near, both_axes, onward)]
    ppermute x1, waiting for transfers between devices: 2.6 us -> 4.2 us  [local(): far_in = lax.ppermute(far_sum, 'grp', plane_swap)]
    ppermute x1, starting transfers between devices: 1.92 us -> 0.68 us  [local(): mine_in = lax.ppermute(near_mine, both_axes, backward)]
  transfers between devices with their start and end apart: 25 -> 25, of which waited for: 15 -> 17; matrix products, arithmetic and copies ran while one was open for 2% -> 2% of each run, Pallas kernels for 16% -> 16%
where the time goes in v7:
time: 109 us; the launch traced here: 108 us
  waiting for transfers between devices  44.2 us (41%)
  starting transfers between devices  31.2 us (29%)
  Pallas kernels  26.6 us (24%)
  local copies, waits for them, and re-layouts  5.11 us (5%)
    pallas_call x3, Pallas kernels, run_expert(): pl.pallas_call(functools.partial(expert_kernel, experts), out_shape=[jax....  10.3 us
    all_to_all x1, waiting for transfers between devices, local(): lax.all_to_all(outgoing, 'ep', split_axis=0, concat_axis=0, tiled=True)  8.7 us
    all_to_all x1, starting transfers between devices, local(): lax.all_to_all(outgoing, 'ep', split_axis=0, concat_axis=0, tiled=True)  7.38 us
    ppermute x1, waiting for transfers between devices, local(): near = lax.ppermute(packet, both_axes, onward)  6.74 us
    pallas_call x1, Pallas kernels, local(): pl.pallas_call(functools.partial(moved_kernel, dims), out_shape=jax.Shape...  4.95 us
    ppermute x1, waiting for transfers between devices, local(): two_side_in = lax.ppermute(two_side_sum, 'ep', side_swap)  4.4 us
    ppermute x1, waiting for transfers between devices, local(): far_in = lax.ppermute(far_sum, 'grp', plane_swap)  4.2 us
    unnamed x30, local copies, waits for them, and re-layouts  3.78 us
  transfers between devices with their start and end apart: 25, of which 17 were waited for; matrix products, arithmetic and copies ran while one was open for 2% of the time, Pallas kernels for 16%

profile of v7, /device:TPU:0, one launch (start us, length us, event | category | flops | bytes accessed | tf_op | source)
XLA Modules:
  0.0 108.3 jit_solution(9673773665265370243)
XLA Ops:
  0.0 2.8 %pick.1 = bf16[16,16,1152]{2,1,0:T(8,128)(2,1)} custom-call(s32[2,16]{1,0:T(2,128)} %bitcast.22, bf16[64,9216]{1,0:T(8,128)(2,1)} %cache.1), custom_call_target="tpu_custom_call" | custom-call | bytes 4194304 | tf_op jit(solution)/shard_map/pick/pallas_call | solution.py:308
  2.8 7.4 %all-to-all-start = ((bf16[16,16,1152]{2,1,0:T(8,128)(2,1)}), bf16[16,16,1152]{2,1,0:T(8,128)(2,1)S(1)}, u32[]{:S(2)}, u32[]{:S(2)}) async-start(bf16[16,16,1152]{2,1,0:T(8,128)(2,1)} %pick.1), calls=%async_computation | async-start | bytes 1179648 | tf_op jit(solution)/shard_map/all_to_all | solution.py:322
  12.4 2.7 %attend_resident.1 = (bf16[512,640]{1,0:T(8,128)(2,1)S(1)}, f32[512,640]{1,0:T(8,128)S(1)}) custom-call(bf16[64,1024]{1,0:T(8,128)(2,1)S(1)} %copy-done.8, bf16[64,512]{1,0:T(8,128)(2,1)S(1)} %copy-done.10, bf16[16,2304]{1,0:T(8,128)(2,1)S(1)} %copy-done.9, bf16[64,9216]{1,0:T(8,128)(2,1)S(1)} %copy-done.2, bf16[8,128,512]{2,1,0:T(8,128)(2,1)S(1)} %copy-done.7, ...), custom_call_target="tpu_custom_call" | custom-call | flops 1283457024 | bytes 8388608 | tf_op jit(solution)/shard_map/attend_resident/pallas_call | solution.py:347
  17.1 8.7 %all-to-all-done.moved_any = bf16[16,16,1152]{2,1,0:T(8,128)(2,1)S(1)} async-done(((bf16[16,16,1152]{2,1,0:T(8,128)(2,1)}), bf16[16,16,1152]{2,1,0:T(8,128)(2,1)S(1)}, u32[]{:S(2)}, u32[]{:S(2)}) %all-to-all-start) | async-done | bytes 589856 | tf_op jit(solution)/shard_map/all_to_all | solution.py:322
  26.6 5.0 %attend_moved.1.after_any.own_any = bf16[64,2048]{1,0:T(8,128)(2,1)} custom-call(bf16[16,16,1152]{2,1,0:T(8,128)(2,1)} %copy-done.11, bf16[512,640]{1,0:T(8,128)(2,1)} %copy-done.3, f32[64,512]{1,0:T(8,128)} %reshape.110.bias_any, f32[512,640]{1,0:T(8,128)} %copy-done.1, bf16[8,512,128]{2,1,0:T(8,128)(2,1)} %value_any.1, bf16[1024,2048]{1,0:T(8,128)(2,1)} %proj_any.1), custom_call_target="tpu_custom_call" | custom-call | flops 603979776 | bytes 10485760 | tf_op jit(solution)/shard_map/attend_moved/pallas_call | solution.py:358
  31.6 1.6 %collective-permute-start = (bf16[64,2048]{1,0:T(8,128)(2,1)}, bf16[64,2048]{1,0:T(8,128)(2,1)S(1)}, u32[]{:S(2)}, u32[]{:S(2)}) collective-permute-start(bf16[64,2048]{1,0:T(8,128)(2,1)} %attend_moved.1.after_any.own_any), channel_id=1, source_target_pairs={{0,16},{16,0},{1,17},{17,1},{2,18},{18,2},{3,19},{19,3},{4,20},{20... | collective-permute-start | bytes 786440 | tf_op jit(solution)/shard_map/ppermute | solution.py:377
  34.1 3.6 %load.1 = (bf16[704,2048]{1,0:T(8,128)(2,1)S(1)}, bf16[704,2048]{1,0:T(8,128)(2,1)S(1)}, bf16[704,2048]{1,0:T(8,128)(2,1)S(1)}) custom-call(bf16[64,2048]{1,0:T(8,128)(2,1)S(1)} %copy-done, bf16[704,2048]{1,0:T(8,128)(2,1)} %bitcast.18, bf16[704,2048]{1,0:T(8,128)(2,1)} %bitcast.19, bf16[704,2048]{1,0:T(8,128)(2,1)} %bitcast.20), custom_call_target="tpu_custom_call" | custom-call | bytes 12582912 | tf_op jit(solution)/shard_map/load/pallas_call | solution.py:380
  37.7 2.3 %collective-permute-done.refs_0_ = bf16[64,2048]{1,0:T(8,128)(2,1)S(1)} collective-permute-done((bf16[64,2048]{1,0:T(8,128)(2,1)}, bf16[64,2048]{1,0:T(8,128)(2,1)S(1)}, u32[]{:S(2)}, u32[]{:S(2)}) %collective-permute-start) | collective-permute-done | bytes 262176 | tf_op jit(solution)/shard_map/ppermute | solution.py:377
  40.8 2.0 %collective-permute-start.2 = (bf16[64,2176]{1,0:T(8,128)(2,1)S(1)}, bf16[64,2176]{1,0:T(8,128)(2,1)S(1)}, u32[]{:S(2)}, u32[]{:S(2)}) collective-permute-start(bf16[64,2176]{1,0:T(8,128)(2,1)S(1)} %get-tuple-element.34.after_any.refs_0_), channel_id=1, source_target_pairs={{0,8},{1,9},{2,10},{3,11},{4,0},{5,1},{6,2},{7,3},{8,12},{9,13},{1... | collective-permute-start | bytes 835592 | tf_op jit(solution)/shard_map/ppermute | solution.py:456
  42.8 6.7 %collective-permute-done.2.refs_2_ = bf16[64,2176]{1,0:T(8,128)(2,1)S(1)} collective-permute-done((bf16[64,2176]{1,0:T(8,128)(2,1)S(1)}, bf16[64,2176]{1,0:T(8,128)(2,1)S(1)}, u32[]{:S(2)}, u32[]{:S(2)}) %collective-permute-start.2) | collective-permute-done | bytes 278560 | tf_op jit(solution)/shard_map/ppermute | solution.py:456
  49.7 2.3 %collective-permute-start.9 = (bf16[64,2176]{1,0:T(8,128)(2,1)S(1)}, bf16[64,2176]{1,0:T(8,128)(2,1)S(1)}, u32[]{:S(2)}, u32[]{:S(2)}) collective-permute-start(bf16[64,2176]{1,0:T(8,128)(2,1)S(1)} %collective-permute-done.2.refs_2_), channel_id=1, source_target_pairs={{0,8},{1,9},{2,10},{3,11},{4,0},{5,1},{6,2},{7,3},{8,12},{9,13},{1... | collective-permute-start | bytes 835592 | tf_op jit(solution)/shard_map/ppermute | solution.py:458
  54.9 3.8 %expert.3 = (bf16[192,2048]{1,0:T(8,128)(2,1)S(1)}, bf16[192,2048]{1,0:T(8,128)(2,1)S(1)}) custom-call(bf16[64,2176]{1,0:T(8,128)(2,1)S(1)} %get-tuple-element.34.after_any.refs_0_, bf16[192,2176]{1,0:T(8,128)(2,1)S(1)} %pack.3.here_ref, bf16[192,2176]{1,0:T(8,128)(2,1)S(1)} %collective-permute-done.3.across_ref, ...), custom_call_target="tpu_custom_call" | custom-call | flops 3321888768 | bytes 12582912 | tf_op jit(solution)/shard_map/expert/pallas_call | solution.py:422
  62.5 1.5 %collective-permute-start.11 = (bf16[64,2176]{1,0:T(8,128)(2,1)S(1)}, bf16[64,2176]{1,0:T(8,128)(2,1)S(1)}, u32[]{:S(2)}, u32[]{:S(2)}) collective-permute-start(bf16[64,2176]{1,0:T(8,128)(2,1)S(1)} %collective-permute-done.8.refs_1_), channel_id=1, source_target_pairs={{0,16},{16,0},{1,17},{17,1},{2,18},{18,2},{3,19},{19,3},{4,20},{20... | collective-permute-start | bytes 835592 | tf_op jit(solution)/shard_map/ppermute | solution.py:462
  64.1 3.8 %expert.4 = (bf16[192,2048]{1,0:T(8,128)(2,1)S(1)}, bf16[192,2048]{1,0:T(8,128)(2,1)S(1)}) custom-call(bf16[64,2176]{1,0:T(8,128)(2,1)S(1)} %get-tuple-element.34.after_any.refs_0_, bf16[192,2176]{1,0:T(8,128)(2,1)S(1)} %pack.4.here_ref, bf16[192,2176]{1,0:T(8,128)(2,1)S(1)} %collective-permute-done.10.across_ref, ...), custom_call_target="tpu_custom_call" | custom-call | flops 3321888768 | bytes 12582912 | tf_op jit(solution)/shard_map/expert/pallas_call | solution.py:422
  68.0 2.9 %collective-permute-done.12.refs_1_ = bf16[64,2176]{1,0:T(8,128)(2,1)S(1)} collective-permute-done((bf16[64,2176]{1,0:T(8,128)(2,1)S(1)}, bf16[64,2176]{1,0:T(8,128)(2,1)S(1)}, u32[]{:S(2)}, u32[]{:S(2)}) %collective-permute-start.12) | collective-permute-done | bytes 278560 | tf_op jit(solution)/shard_map/ppermute | solution.py:461
  73.5 2.6 %expert.5 = (bf16[128,2048]{1,0:T(8,128)(2,1)S(1)}, bf16[64,2048]{1,0:T(8,128)(2,1)S(1)}, bf16[64,2048]{1,0:T(8,128)(2,1)S(1)}) custom-call(bf16[64,2048]{1,0:T(8,128)(2,1)S(1)} %get-tuple-element.40.after_any, bf16[128,2176]{1,0:T(8,128)(2,1)S(1)} %pack.5.here_ref, bf16[128,2176]{1,0:T(8,128)(2,1)S(1)} %collective-permute-done.13.across_ref, ...), custom_call_target="tpu_custom_call" | custom-call | flops 2214592512 | bytes 12582912 | tf_op jit(solution)/shard_map/expert/pallas_call | solution.py:422
  76.7 3.7 %collective-permute-done.5.side_ref.refs_0_ = bf16[64,2048]{1,0:T(8,128)(2,1)S(1)} collective-permute-done((bf16[64,2048]{1,0:T(8,128)(2,1)S(1)}, bf16[64,2048]{1,0:T(8,128)(2,1)S(1)}, u32[]{:S(2)}, u32[]{:S(2)}) %collective-permute-start.5) | collective-permute-done | bytes 262176 | tf_op jit(solution)/shard_map/ppermute | solution.py:466
  83.6 4.4 %collective-permute-done.20.refs_0_ = bf16[64,2048]{1,0:T(8,128)(2,1)S(1)} collective-permute-done((bf16[64,2048]{1,0:T(8,128)(2,1)S(1)}, bf16[64,2048]{1,0:T(8,128)(2,1)S(1)}, u32[]{:S(2)}, u32[]{:S(2)}) %collective-permute-start.20) | collective-permute-done | bytes 262176 | tf_op jit(solution)/shard_map/ppermute | solution.py:471
  90.7 2.1 %collective-permute-start.18 = (bf16[64,2048]{1,0:T(8,128)(2,1)S(1)}, bf16[64,2048]{1,0:T(8,128)(2,1)S(1)}, u32[]{:S(2)}, u32[]{:S(2)}) collective-permute-start(bf16[64,2048]{1,0:T(8,128)(2,1)S(1)} %join.8), channel_id=1, source_target_pairs={{0,16},{16,0},{1,17},{17,1},{2,18},{18,2},{3,19},{19,3},{4,20},{20... | collective-permute-start | bytes 786440 | tf_op jit(solution)/shard_map/ppermute | solution.py:475
  92.9 2.6 %collective-permute-done.21.refs_3_ = bf16[64,2048]{1,0:T(8,128)(2,1)S(1)} collective-permute-done((bf16[64,2048]{1,0:T(8,128)(2,1)S(1)}, bf16[64,2048]{1,0:T(8,128)(2,1)S(1)}, u32[]{:S(2)}, u32[]{:S(2)}) %collective-permute-start.21) | collective-permute-done | bytes 262176 | tf_op jit(solution)/shard_map/ppermute | solution.py:477
  95.6 4.2 %collective-permute-done.18.refs_1_ = bf16[64,2048]{1,0:T(8,128)(2,1)S(1)} collective-permute-done((bf16[64,2048]{1,0:T(8,128)(2,1)S(1)}, bf16[64,2048]{1,0:T(8,128)(2,1)S(1)}, u32[]{:S(2)}, u32[]{:S(2)}) %collective-permute-start.18) | collective-permute-done | bytes 262176 | tf_op jit(solution)/shard_map/ppermute | solution.py:475
  99.9 1.8 %collective-permute-start.22 = (bf16[64,1024]{1,0:T(8,128)(2,1)S(1)}, bf16[64,1024]{1,0:T(8,128)(2,1)S(1)}, u32[]{:S(2)}, u32[]{:S(2)}) collective-permute-start(bf16[64,1024]{1,0:T(8,128)(2,1)S(1)} %get-tuple-element.53), channel_id=1, source_target_pairs={{0,20},{1,21},{2,22},{3,23},{4,28},{5,29},{6,30},{7,31},{8,16},{9,... | collective-permute-start | bytes 393224 | tf_op jit(solution)/shard_map/ppermute | solution.py:501
  102.4 3.5 %collective-permute-done.22.refs_1_ = bf16[64,1024]{1,0:T(8,128)(2,1)S(1)} collective-permute-done((bf16[64,1024]{1,0:T(8,128)(2,1)S(1)}, bf16[64,1024]{1,0:T(8,128)(2,1)S(1)}, u32[]{:S(2)}, u32[]{:S(2)}) %collective-permute-start.22) | collective-permute-done | bytes 131104 | tf_op jit(solution)/shard_map/ppermute | solution.py:501
  105.9 1.7 %collective-permute-done.23.refs_2_ = bf16[64,1024]{1,0:T(8,128)(2,1)S(1)} collective-permute-done((bf16[64,1024]{1,0:T(8,128)(2,1)S(1)}, bf16[64,1024]{1,0:T(8,128)(2,1)S(1)}, u32[]{:S(2)}, u32[]{:S(2)}) %collective-permute-start.23) | collective-permute-done | bytes 131104 | tf_op jit(solution)/shard_map/ppermute | solution.py:500
  (100 shorter events, 24.2 us)
Async XLA Ops:
  2.8 22.9 %all-to-all-start = ((bf16[16,16,1152]{2,1,0:T(8,128)(2,1)}), bf16[16,16,1152]{2,1,0:T(8,128)(2,1)S(1)}, u32[]{:S(2)}, u32[]{:S(2)}) async-start(bf16[16,16,1152]{2,1,0:T(8,128)(2,1)} %pick.1), calls=%async_computation | async-start | bytes 1179648 | tf_op jit(solution)/shard_map/all_to_all | solution.py:322
  31.6 8.5 %collective-permute-start = (bf16[64,2048]{1,0:T(8,128)(2,1)}, bf16[64,2048]{1,0:T(8,128)(2,1)S(1)}, u32[]{:S(2)}, u32[]{:S(2)}) collective-permute-start(bf16[64,2048]{1,0:T(8,128)(2,1)} %attend_moved.1.after_any.own_any), channel_id=1, source_target_pairs={{0,16},{16,0},{1,17},{17,1},{2,18},{18,2},{3,19},{19,3},{4,20},{20... | collective-permute-start | bytes 786440 | tf_op jit(solution)/shard_map/ppermute | solution.py:377
  40.8 8.7 %collective-permute-start.2 = (bf16[64,2176]{1,0:T(8,128)(2,1)S(1)}, bf16[64,2176]{1,0:T(8,128)(2,1)S(1)}, u32[]{:S(2)}, u32[]{:S(2)}) collective-permute-start(bf16[64,2176]{1,0:T(8,128)(2,1)S(1)} %get-tuple-element.34.after_any.refs_0_), channel_id=1, source_target_pairs={{0,8},{1,9},{2,10},{3,11},{4,0},{5,1},{6,2},{7,3},{8,12},{9,13},{1... | collective-permute-start | bytes 835592 | tf_op jit(solution)/shard_map/ppermute | solution.py:456
  42.8 6.8 %collective-permute-start.1 = (bf16[64,2176]{1,0:T(8,128)(2,1)S(1)}, bf16[64,2176]{1,0:T(8,128)(2,1)S(1)}, u32[]{:S(2)}, u32[]{:S(2)}) collective-permute-start(bf16[64,2176]{1,0:T(8,128)(2,1)S(1)} %get-tuple-element.34.after_any.refs_0_), channel_id=1, source_target_pairs={{0,2},{1,3},{2,0},{3,1},{4,6},{5,7},{6,4},{7,5},{8,10},{9,11},{10,... | collective-permute-start | bytes 835592 | tf_op jit(solution)/shard_map/ppermute | solution.py:457
  49.6 5.3 %collective-permute-start.3 = (bf16[192,2176]{1,0:T(8,128)(2,1)S(1)}, bf16[192,2176]{1,0:T(8,128)(2,1)S(1)}, u32[]{:S(2)}, u32[]{:S(2)}) collective-permute-start(bf16[192,2176]{1,0:T(8,128)(2,1)S(1)} %pack.3.here_ref), channel_id=1, source_target_pairs={{0,1},{1,0},{2,3},{3,2},{4,5},{5,4},{6,7},{7,6},{8,9},{9,8},{10,11... | collective-permute-start | bytes 2506760 | tf_op jit(solution)/shard_map/ppermute | solution.py:421
  49.7 10.0 %collective-permute-start.9 = (bf16[64,2176]{1,0:T(8,128)(2,1)S(1)}, bf16[64,2176]{1,0:T(8,128)(2,1)S(1)}, u32[]{:S(2)}, u32[]{:S(2)}) collective-permute-start(bf16[64,2176]{1,0:T(8,128)(2,1)S(1)} %collective-permute-done.2.refs_2_), channel_id=1, source_target_pairs={{0,8},{1,9},{2,10},{3,11},{4,0},{5,1},{6,2},{7,3},{8,12},{9,13},{1... | collective-permute-start | bytes 835592 | tf_op jit(solution)/shard_map/ppermute | solution.py:458
  52.0 8.5 %collective-permute-start.8 = (bf16[64,2176]{1,0:T(8,128)(2,1)S(1)}, bf16[64,2176]{1,0:T(8,128)(2,1)S(1)}, u32[]{:S(2)}, u32[]{:S(2)}) collective-permute-start(bf16[64,2176]{1,0:T(8,128)(2,1)S(1)} %collective-permute-done.2.refs_2_), channel_id=1, source_target_pairs={{0,2},{1,3},{2,0},{3,1},{4,6},{5,7},{6,4},{7,5},{8,10},{9,11},{10,... | collective-permute-start | bytes 835592 | tf_op jit(solution)/shard_map/ppermute | solution.py:459
  53.4 8.3 %collective-permute-start.7 = (bf16[64,2176]{1,0:T(8,128)(2,1)S(1)}, bf16[64,2176]{1,0:T(8,128)(2,1)S(1)}, u32[]{:S(2)}, u32[]{:S(2)}) collective-permute-start(bf16[64,2176]{1,0:T(8,128)(2,1)S(1)} %collective-permute-done.2.refs_2_), channel_id=1, source_target_pairs={{0,16},{16,0},{1,17},{17,1},{2,18},{18,2},{3,19},{19,3},{4,20},{20... | collective-permute-start | bytes 835592 | tf_op jit(solution)/shard_map/ppermute | solution.py:460
  61.7 2.4 %collective-permute-start.10 = (bf16[192,2176]{1,0:T(8,128)(2,1)S(1)}, bf16[192,2176]{1,0:T(8,128)(2,1)S(1)}, u32[]{:S(2)}, u32[]{:S(2)}) collective-permute-start(bf16[192,2176]{1,0:T(8,128)(2,1)S(1)} %pack.4.here_ref), channel_id=1, source_target_pairs={{0,1},{1,0},{2,3},{3,2},{4,5},{5,4},{6,7},{7,6},{8,9},{9,8},{10,11... | collective-permute-start | bytes 2506760 | tf_op jit(solution)/shard_map/ppermute | solution.py:421
  61.8 9.1 %collective-permute-start.12 = (bf16[64,2176]{1,0:T(8,128)(2,1)S(1)}, bf16[64,2176]{1,0:T(8,128)(2,1)S(1)}, u32[]{:S(2)}, u32[]{:S(2)}) collective-permute-start(bf16[64,2176]{1,0:T(8,128)(2,1)S(1)} %collective-permute-done.9.refs_2_), channel_id=1, source_target_pairs={{0,2},{1,3},{2,0},{3,1},{4,6},{5,7},{6,4},{7,5},{8,10},{9,11},{10,... | collective-permute-start | bytes 835592 | tf_op jit(solution)/shard_map/ppermute | solution.py:461
  62.5 8.7 %collective-permute-start.11 = (bf16[64,2176]{1,0:T(8,128)(2,1)S(1)}, bf16[64,2176]{1,0:T(8,128)(2,1)S(1)}, u32[]{:S(2)}, u32[]{:S(2)}) collective-permute-start(bf16[64,2176]{1,0:T(8,128)(2,1)S(1)} %collective-permute-done.8.refs_1_), channel_id=1, source_target_pairs={{0,16},{16,0},{1,17},{17,1},{2,18},{18,2},{3,19},{19,3},{4,20},{20... | collective-permute-start | bytes 835592 | tf_op jit(solution)/shard_map/ppermute | solution.py:462
  64.0 7.8 %collective-permute-start.4 = (bf16[192,2048]{1,0:T(8,128)(2,1)S(1)}, bf16[192,2048]{1,0:T(8,128)(2,1)S(1)}, u32[]{:S(2)}, u32[]{:S(2)}) collective-permute-start(bf16[192,2048]{1,0:T(8,128)(2,1)S(1)} %get-tuple-element.38), channel_id=1, source_target_pairs={{0,1},{1,0},{2,3},{3,2},{4,5},{5,4},{6,7},{7,6},{8,9},{9,8},{10,11... | collective-permute-start | bytes 2359304 | tf_op jit(solution)/shard_map/ppermute | solution.py:432
  71.3 12.2 %collective-permute-start.17 = (bf16[192,2048]{1,0:T(8,128)(2,1)S(1)}, bf16[192,2048]{1,0:T(8,128)(2,1)S(1)}, u32[]{:S(2)}, u32[]{:S(2)}) collective-permute-start(bf16[192,2048]{1,0:T(8,128)(2,1)S(1)} %get-tuple-element.49), channel_id=1, source_target_pairs={{0,1},{1,0},{2,3},{3,2},{4,5},{5,4},{6,7},{7,6},{8,9},{9,8},{10,11... | collective-permute-start | bytes 2359304 | tf_op jit(solution)/shard_map/ppermute | solution.py:432
  72.0 8.4 %collective-permute-start.5 = (bf16[64,2048]{1,0:T(8,128)(2,1)S(1)}, bf16[64,2048]{1,0:T(8,128)(2,1)S(1)}, u32[]{:S(2)}, u32[]{:S(2)}) collective-permute-start(bf16[64,2048]{1,0:T(8,128)(2,1)S(1)} %get-tuple-element.40.after_any), channel_id=1, source_target_pairs={{0,2},{1,3},{2,0},{3,1},{4,6},{5,7},{6,4},{7,5},{8,10},{9,11},{10,... | collective-permute-start | bytes 786440 | tf_op jit(solution)/shard_map/ppermute | solution.py:466
  76.1 4.2 %collective-permute-start.14 = (bf16[64,2048]{1,0:T(8,128)(2,1)S(1)}, bf16[64,2048]{1,0:T(8,128)(2,1)S(1)}, u32[]{:S(2)}, u32[]{:S(2)}) collective-permute-start(bf16[64,2048]{1,0:T(8,128)(2,1)S(1)} %get-tuple-element.46), channel_id=1, source_target_pairs={{0,1},{1,0},{2,3},{3,2},{4,5},{5,4},{6,7},{7,6},{8,9},{9,8},{10,11... | collective-permute-start | bytes 786440 | tf_op jit(solution)/shard_map/ppermute | solution.py:432
  76.2 4.2 %collective-permute-start.15 = (bf16[64,2048]{1,0:T(8,128)(2,1)S(1)}, bf16[64,2048]{1,0:T(8,128)(2,1)S(1)}, u32[]{:S(2)}, u32[]{:S(2)}) collective-permute-start(bf16[64,2048]{1,0:T(8,128)(2,1)S(1)} %get-tuple-element.47), channel_id=1, source_target_pairs={{0,1},{1,0},{2,3},{3,2},{4,5},{5,4},{6,7},{7,6},{8,9},{9,8},{10,11... | collective-permute-start | bytes 786440 | tf_op jit(solution)/shard_map/ppermute | solution.py:432
  80.5 7.5 %collective-permute-start.20 = (bf16[64,2048]{1,0:T(8,128)(2,1)S(1)}, bf16[64,2048]{1,0:T(8,128)(2,1)S(1)}, u32[]{:S(2)}, u32[]{:S(2)}) collective-permute-start(bf16[64,2048]{1,0:T(8,128)(2,1)S(1)} %get-tuple-element.52), channel_id=1, source_target_pairs={{0,2},{1,3},{2,0},{3,1},{4,6},{5,7},{6,4},{7,5},{8,10},{9,11},{10,... | collective-permute-start | bytes 786440 | tf_op jit(solution)/shard_map/ppermute | solution.py:471
  82.0 7.2 %collective-permute-start.16 = (bf16[64,2048]{1,0:T(8,128)(2,1)S(1)}, bf16[64,2048]{1,0:T(8,128)(2,1)S(1)}, u32[]{:S(2)}, u32[]{:S(2)}) collective-permute-start(bf16[64,2048]{1,0:T(8,128)(2,1)S(1)} %get-tuple-element.48), channel_id=1, source_target_pairs={{0,16},{16,0},{1,17},{17,1},{2,18},{18,2},{3,19},{19,3},{4,20},{20... | collective-permute-start | bytes 786440 | tf_op jit(solution)/shard_map/ppermute | solution.py:470
  88.0 7.5 %collective-permute-start.21 = (bf16[64,2048]{1,0:T(8,128)(2,1)S(1)}, bf16[64,2048]{1,0:T(8,128)(2,1)S(1)}, u32[]{:S(2)}, u32[]{:S(2)}) collective-permute-start(bf16[64,2048]{1,0:T(8,128)(2,1)S(1)} %join.11), channel_id=1, source_target_pairs={{0,4},{1,5},{2,6},{3,7},{4,12},{5,13},{6,14},{7,15},{8,0},{9,1},{1... | collective-permute-start | bytes 786440 | tf_op jit(solution)/shard_map/ppermute | solution.py:477
  89.2 6.4 %collective-permute-start.19 = (bf16[64,2048]{1,0:T(8,128)(2,1)S(1)}, bf16[64,2048]{1,0:T(8,128)(2,1)S(1)}, u32[]{:S(2)}, u32[]{:S(2)}) collective-permute-start(bf16[64,2048]{1,0:T(8,128)(2,1)S(1)} %join.10), channel_id=1, source_target_pairs={{0,2},{1,3},{2,0},{3,1},{4,6},{5,7},{6,4},{7,5},{8,10},{9,11},{10,... | collective-permute-start | bytes 786440 | tf_op jit(solution)/shard_map/ppermute | solution.py:476
  90.7 9.2 %collective-permute-start.18 = (bf16[64,2048]{1,0:T(8,128)(2,1)S(1)}, bf16[64,2048]{1,0:T(8,128)(2,1)S(1)}, u32[]{:S(2)}, u32[]{:S(2)}) collective-permute-start(bf16[64,2048]{1,0:T(8,128)(2,1)S(1)} %join.8), channel_id=1, source_target_pairs={{0,16},{16,0},{1,17},{17,1},{2,18},{18,2},{3,19},{19,3},{4,20},{20... | collective-permute-start | bytes 786440 | tf_op jit(solution)/shard_map/ppermute | solution.py:475
  92.8 9.5 %collective-permute-start.6 = (bf16[64,1024]{1,0:T(8,128)(2,1)S(1)}, bf16[64,1024]{1,0:T(8,128)(2,1)S(1)}, u32[]{:S(2)}, u32[]{:S(2)}) collective-permute-start(bf16[64,1024]{1,0:T(8,128)(2,1)S(1)} %get-tuple-element.42), channel_id=1, source_target_pairs={{0,16},{16,0},{1,17},{17,1},{2,18},{18,2},{3,19},{19,3},{4,20},{20... | collective-permute-start | bytes 393224 | tf_op jit(solution)/shard_map/ppermute | solution.py:499
  99.9 5.9 %collective-permute-start.22 = (bf16[64,1024]{1,0:T(8,128)(2,1)S(1)}, bf16[64,1024]{1,0:T(8,128)(2,1)S(1)}, u32[]{:S(2)}, u32[]{:S(2)}) collective-permute-start(bf16[64,1024]{1,0:T(8,128)(2,1)S(1)} %get-tuple-element.53), channel_id=1, source_target_pairs={{0,20},{1,21},{2,22},{3,23},{4,28},{5,29},{6,30},{7,31},{8,16},{9,... | collective-permute-start | bytes 393224 | tf_op jit(solution)/shard_map/ppermute | solution.py:501
  101.7 5.9 %collective-permute-start.23 = (bf16[64,1024]{1,0:T(8,128)(2,1)S(1)}, bf16[64,1024]{1,0:T(8,128)(2,1)S(1)}, u32[]{:S(2)}, u32[]{:S(2)}) collective-permute-start(bf16[64,1024]{1,0:T(8,128)(2,1)S(1)} %get-tuple-element.54), channel_id=1, source_target_pairs={{0,4},{1,5},{2,6},{3,7},{4,12},{5,13},{6,14},{7,15},{8,0},{9,1},{1... | collective-permute-start | bytes 393224 | tf_op jit(solution)/shard_map/ppermute | solution.py:500
  (16 other events, 113.0 us)

commit v8 on v7

--- a/solution.py
+++ b/solution.py
@@ -234,7 +234,7 @@
             ref[row - at * count : row - at * count + step, :] = total.astype(ref.dtype)
 
 
-def own_kernel(state_ref, own_ref, side_ref, base_ref, other_ref):
+def own_kernel(after_any, state_ref, own_ref, side_ref, base_ref, other_ref):
     mine, other = (own_columns(own_ref, by) + own_columns(side_ref, by).astype(F32) for by in (0, 1))
     base_ref[...] = state_ref[...] + mine
     other_ref[...] = other.astype(BF16)
@@ -477,13 +477,14 @@
         two_in = lax.ppermute(two_sum, both_axes, backward)
         part = (row_count, columns)
 
-        def by_columns(kernel, first_type, *operands):
+        def by_columns(kernel, first_type, after_count, *operands):
             return pl.pallas_call(
                 kernel,
                 out_shape=(
                     jax.ShapeDtypeStruct(part, first_type),
                     jax.ShapeDtypeStruct(part, BF16),
                 ),
+                in_specs=[ANY] * after_count + [WHOLE] * (len(operands) - after_count),
                 compiler_params=pltpu.CompilerParams(vmem_limit_bytes=16 * 2**20),
                 cost_estimate=cost(row_count * model, 2**20),
                 name=kernel.__name__,
@@ -492,10 +493,10 @@
         def crossed(pairs):
             return [(source, (target + ranks) % (2 * ranks)) for source, target in pairs]
 
-        base, own_other = by_columns(own_kernel, F32, state, own_sum, side_in)
         near_mine, near_other = by_columns(
-            sum_kernel, BF16, near_sum, far_in, near_side_in, two_in
+            sum_kernel, BF16, 0, near_sum, near_side_in, two_in, far_in
         )
+        base, own_other = by_columns(own_kernel, F32, 1, near_mine, state, own_sum, side_in)
         own_over = lax.ppermute(own_other, "grp", plane_swap)
         mine_in = lax.ppermute(near_mine, both_axes, backward)
         other_in = lax.ppermute(near_other, both_axes, crossed(backward))
@@ -506,7 +507,7 @@
             compiler_params=pltpu.CompilerParams(vmem_limit_bytes=16 * 2**20),
             cost_estimate=cost(0, 2**20),
             name="last",
-        )(base, own_over, other_in, mine_in)
+        )(base, other_in, mine_in, own_over)
 
     line = [packet]
     for _ in range(1, ring):

time: 109 us -> 108 us (level)
  waiting for transfers between devices: 44.2 us -> 41.4 us
  starting transfers between devices: 31.2 us -> 33.1 us
    ppermute x1, waiting for transfers between devices: 4.2 us -> 1.52 us  [local(): far_in = lax.ppermute(far_sum, 'grp', plane_swap)]
    ppermute x1, starting transfers between devices: 0.1 us -> 2.26 us  [local(): own_over = lax.ppermute(own_other, 'grp', plane_swap)]
  transfers between devices with their start and end apart: 25 -> 25, of which waited for: 17 -> 18; matrix products, arithmetic and copies ran while one was open for 2% -> 2% of each run, Pallas kernels for 16% -> 16%
where the time goes in v8:
time: 108 us; the launch traced here: 107 us
  waiting for transfers between devices  41.4 us (38%)
  starting transfers between devices  33.1 us (31%)
  Pallas kernels  26.6 us (25%)
  local copies, waits for them, and re-layouts  5.11 us (5%)
    pallas_call x3, Pallas kernels, run_expert(): pl.pallas_call(functools.partial(expert_kernel, experts), out_shape=[jax....  10.3 us
    all_to_all x1, waiting for transfers between devices, local(): lax.all_to_all(outgoing, 'ep', split_axis=0, concat_axis=0, tiled=True)  8.7 us
    all_to_all x1, starting transfers between devices, local(): lax.all_to_all(outgoing, 'ep', split_axis=0, concat_axis=0, tiled=True)  7.38 us
    ppermute x1, waiting for transfers between devices, local(): near = lax.ppermute(packet, both_axes, onward)  6.74 us
    pallas_call x1, Pallas kernels, local(): pl.pallas_call(functools.partial(moved_kernel, dims), out_shape=jax.Shape...  4.95 us
    ppermute x1, waiting for transfers between devices, local(): two_side_in = lax.ppermute(two_side_sum, 'ep', side_swap)  4.4 us
    unnamed x30, local copies, waits for them, and re-layouts  3.78 us
    ppermute x1, waiting for transfers between devices, local(): side_in = lax.ppermute(side_sum, 'ep', side_swap)  3.65 us
  transfers between devices with their start and end apart: 25, of which 18 were waited for; matrix products, arithmetic and copies ran while one was open for 2% of the time, Pallas kernels for 16%

profile of v8, /device:TPU:0, one launch (start us, length us, event | category | flops | bytes accessed | tf_op | source)
XLA Modules:
  0.0 107.3 jit_solution(10919859750394898535)
XLA Ops:
  0.0 2.8 %pick.1 = bf16[16,16,1152]{2,1,0:T(8,128)(2,1)} custom-call(s32[2,16]{1,0:T(2,128)} %bitcast.22, bf16[64,9216]{1,0:T(8,128)(2,1)} %cache.1), custom_call_target="tpu_custom_call" | custom-call | bytes 4194304 | tf_op jit(solution)/shard_map/pick/pallas_call | solution.py:308
  2.8 7.4 %all-to-all-start = ((bf16[16,16,1152]{2,1,0:T(8,128)(2,1)}), bf16[16,16,1152]{2,1,0:T(8,128)(2,1)S(1)}, u32[]{:S(2)}, u32[]{:S(2)}) async-start(bf16[16,16,1152]{2,1,0:T(8,128)(2,1)} %pick.1), calls=%async_computation | async-start | bytes 1179648 | tf_op jit(solution)/shard_map/all_to_all | solution.py:322
  12.4 2.7 %attend_resident.1 = (bf16[512,640]{1,0:T(8,128)(2,1)S(1)}, f32[512,640]{1,0:T(8,128)S(1)}) custom-call(bf16[64,1024]{1,0:T(8,128)(2,1)S(1)} %copy-done.8, bf16[64,512]{1,0:T(8,128)(2,1)S(1)} %copy-done.10, bf16[16,2304]{1,0:T(8,128)(2,1)S(1)} %copy-done.9, bf16[64,9216]{1,0:T(8,128)(2,1)S(1)} %copy-done.2, bf16[8,128,512]{2,1,0:T(8,128)(2,1)S(1)} %copy-done.7, ...), custom_call_target="tpu_custom_call" | custom-call | flops 1283457024 | bytes 8388608 | tf_op jit(solution)/shard_map/attend_resident/pallas_call | solution.py:347
  17.1 8.7 %all-to-all-done.moved_any = bf16[16,16,1152]{2,1,0:T(8,128)(2,1)S(1)} async-done(((bf16[16,16,1152]{2,1,0:T(8,128)(2,1)}), bf16[16,16,1152]{2,1,0:T(8,128)(2,1)S(1)}, u32[]{:S(2)}, u32[]{:S(2)}) %all-to-all-start) | async-done | bytes 589856 | tf_op jit(solution)/shard_map/all_to_all | solution.py:322
  26.6 5.0 %attend_moved.1.after_any.own_any = bf16[64,2048]{1,0:T(8,128)(2,1)} custom-call(bf16[16,16,1152]{2,1,0:T(8,128)(2,1)} %copy-done.11, bf16[512,640]{1,0:T(8,128)(2,1)} %copy-done.3, f32[64,512]{1,0:T(8,128)} %reshape.110.bias_any, f32[512,640]{1,0:T(8,128)} %copy-done.1, bf16[8,512,128]{2,1,0:T(8,128)(2,1)} %value_any.1, bf16[1024,2048]{1,0:T(8,128)(2,1)} %proj_any.1), custom_call_target="tpu_custom_call" | custom-call | flops 603979776 | bytes 10485760 | tf_op jit(solution)/shard_map/attend_moved/pallas_call | solution.py:358
  31.6 1.6 %collective-permute-start = (bf16[64,2048]{1,0:T(8,128)(2,1)}, bf16[64,2048]{1,0:T(8,128)(2,1)S(1)}, u32[]{:S(2)}, u32[]{:S(2)}) collective-permute-start(bf16[64,2048]{1,0:T(8,128)(2,1)} %attend_moved.1.after_any.own_any), channel_id=1, source_target_pairs={{0,16},{16,0},{1,17},{17,1},{2,18},{18,2},{3,19},{19,3},{4,20},{20... | collective-permute-start | bytes 786440 | tf_op jit(solution)/shard_map/ppermute | solution.py:377
  34.1 3.6 %load.1 = (bf16[704,2048]{1,0:T(8,128)(2,1)S(1)}, bf16[704,2048]{1,0:T(8,128)(2,1)S(1)}, bf16[704,2048]{1,0:T(8,128)(2,1)S(1)}) custom-call(bf16[64,2048]{1,0:T(8,128)(2,1)S(1)} %copy-done, bf16[704,2048]{1,0:T(8,128)(2,1)} %bitcast.18, bf16[704,2048]{1,0:T(8,128)(2,1)} %bitcast.19, bf16[704,2048]{1,0:T(8,128)(2,1)} %bitcast.20), custom_call_target="tpu_custom_call" | custom-call | bytes 12582912 | tf_op jit(solution)/shard_map/load/pallas_call | solution.py:380
  37.7 2.3 %collective-permute-done.refs_0_ = bf16[64,2048]{1,0:T(8,128)(2,1)S(1)} collective-permute-done((bf16[64,2048]{1,0:T(8,128)(2,1)}, bf16[64,2048]{1,0:T(8,128)(2,1)S(1)}, u32[]{:S(2)}, u32[]{:S(2)}) %collective-permute-start) | collective-permute-done | bytes 262176 | tf_op jit(solution)/shard_map/ppermute | solution.py:377
  40.8 2.0 %collective-permute-start.2 = (bf16[64,2176]{1,0:T(8,128)(2,1)S(1)}, bf16[64,2176]{1,0:T(8,128)(2,1)S(1)}, u32[]{:S(2)}, u32[]{:S(2)}) collective-permute-start(bf16[64,2176]{1,0:T(8,128)(2,1)S(1)} %get-tuple-element.33.after_any.refs_0_), channel_id=1, source_target_pairs={{0,8},{1,9},{2,10},{3,11},{4,0},{5,1},{6,2},{7,3},{8,12},{9,13},{1... | collective-permute-start | bytes 835592 | tf_op jit(solution)/shard_map/ppermute | solution.py:456
  42.8 6.7 %collective-permute-done.2.refs_2_ = bf16[64,2176]{1,0:T(8,128)(2,1)S(1)} collective-permute-done((bf16[64,2176]{1,0:T(8,128)(2,1)S(1)}, bf16[64,2176]{1,0:T(8,128)(2,1)S(1)}, u32[]{:S(2)}, u32[]{:S(2)}) %collective-permute-start.2) | collective-permute-done | bytes 278560 | tf_op jit(solution)/shard_map/ppermute | solution.py:456
  49.7 2.3 %collective-permute-start.7 = (bf16[64,2176]{1,0:T(8,128)(2,1)S(1)}, bf16[64,2176]{1,0:T(8,128)(2,1)S(1)}, u32[]{:S(2)}, u32[]{:S(2)}) collective-permute-start(bf16[64,2176]{1,0:T(8,128)(2,1)S(1)} %collective-permute-done.2.refs_2_), channel_id=1, source_target_pairs={{0,8},{1,9},{2,10},{3,11},{4,0},{5,1},{6,2},{7,3},{8,12},{9,13},{1... | collective-permute-start | bytes 835592 | tf_op jit(solution)/shard_map/ppermute | solution.py:458
  53.4 1.5 %collective-permute-start.5 = (bf16[64,2176]{1,0:T(8,128)(2,1)S(1)}, bf16[64,2176]{1,0:T(8,128)(2,1)S(1)}, u32[]{:S(2)}, u32[]{:S(2)}) collective-permute-start(bf16[64,2176]{1,0:T(8,128)(2,1)S(1)} %collective-permute-done.2.refs_2_), channel_id=1, source_target_pairs={{0,16},{16,0},{1,17},{17,1},{2,18},{18,2},{3,19},{19,3},{4,20},{20... | collective-permute-start | bytes 835592 | tf_op jit(solution)/shard_map/ppermute | solution.py:460
  54.9 3.8 %expert.3 = (bf16[192,2048]{1,0:T(8,128)(2,1)S(1)}, bf16[192,2048]{1,0:T(8,128)(2,1)S(1)}) custom-call(bf16[64,2176]{1,0:T(8,128)(2,1)S(1)} %get-tuple-element.33.after_any.refs_0_, bf16[192,2176]{1,0:T(8,128)(2,1)S(1)} %pack.3.here_ref, bf16[192,2176]{1,0:T(8,128)(2,1)S(1)} %collective-permute-done.3.across_ref, ...), custom_call_target="tpu_custom_call" | custom-call | flops 3321888768 | bytes 12582912 | tf_op jit(solution)/shard_map/expert/pallas_call | solution.py:422
  62.5 1.5 %collective-permute-start.10 = (bf16[64,2176]{1,0:T(8,128)(2,1)S(1)}, bf16[64,2176]{1,0:T(8,128)(2,1)S(1)}, u32[]{:S(2)}, u32[]{:S(2)}) collective-permute-start(bf16[64,2176]{1,0:T(8,128)(2,1)S(1)} %collective-permute-done.6.refs_1_), channel_id=1, source_target_pairs={{0,16},{16,0},{1,17},{17,1},{2,18},{18,2},{3,19},{19,3},{4,20},{20... | collective-permute-start | bytes 835592 | tf_op jit(solution)/shard_map/ppermute | solution.py:462
  64.1 3.8 %expert.4 = (bf16[192,2048]{1,0:T(8,128)(2,1)S(1)}, bf16[192,2048]{1,0:T(8,128)(2,1)S(1)}) custom-call(bf16[64,2176]{1,0:T(8,128)(2,1)S(1)} %get-tuple-element.33.after_any.refs_0_, bf16[192,2176]{1,0:T(8,128)(2,1)S(1)} %pack.4.here_ref, bf16[192,2176]{1,0:T(8,128)(2,1)S(1)} %collective-permute-done.8.across_ref, ...), custom_call_target="tpu_custom_call" | custom-call | flops 3321888768 | bytes 12582912 | tf_op jit(solution)/shard_map/expert/pallas_call | solution.py:422
  68.0 2.9 %collective-permute-done.11.refs_1_ = bf16[64,2176]{1,0:T(8,128)(2,1)S(1)} collective-permute-done((bf16[64,2176]{1,0:T(8,128)(2,1)S(1)}, bf16[64,2176]{1,0:T(8,128)(2,1)S(1)}, u32[]{:S(2)}, u32[]{:S(2)}) %collective-permute-start.11) | collective-permute-done | bytes 278560 | tf_op jit(solution)/shard_map/ppermute | solution.py:461
  73.5 2.6 %expert.5 = (bf16[128,2048]{1,0:T(8,128)(2,1)S(1)}, bf16[64,2048]{1,0:T(8,128)(2,1)S(1)}, bf16[64,2048]{1,0:T(8,128)(2,1)S(1)}) custom-call(bf16[64,2048]{1,0:T(8,128)(2,1)S(1)} %get-tuple-element.42.after_any, bf16[128,2176]{1,0:T(8,128)(2,1)S(1)} %pack.5.here_ref, bf16[128,2176]{1,0:T(8,128)(2,1)S(1)} %collective-permute-done.12.across_ref, ...), custom_call_target="tpu_custom_call" | custom-call | flops 2214592512 | bytes 12582912 | tf_op jit(solution)/shard_map/expert/pallas_call | solution.py:422
  76.7 3.7 %collective-permute-done.13.refs_0_.side_ref = bf16[64,2048]{1,0:T(8,128)(2,1)S(1)} collective-permute-done((bf16[64,2048]{1,0:T(8,128)(2,1)S(1)}, bf16[64,2048]{1,0:T(8,128)(2,1)S(1)}, u32[]{:S(2)}, u32[]{:S(2)}) %collective-permute-start.13) | collective-permute-done | bytes 262176 | tf_op jit(solution)/shard_map/ppermute | solution.py:466
  82.0 1.5 %collective-permute-start.16 = (bf16[64,2048]{1,0:T(8,128)(2,1)S(1)}, bf16[64,2048]{1,0:T(8,128)(2,1)S(1)}, u32[]{:S(2)}, u32[]{:S(2)}) collective-permute-start(bf16[64,2048]{1,0:T(8,128)(2,1)S(1)} %get-tuple-element.46), channel_id=1, source_target_pairs={{0,16},{16,0},{1,17},{17,1},{2,18},{18,2},{3,19},{19,3},{4,20},{20... | collective-permute-start | bytes 786440 | tf_op jit(solution)/shard_map/ppermute | solution.py:470
  83.6 4.4 %collective-permute-done.18.refs_0_ = bf16[64,2048]{1,0:T(8,128)(2,1)S(1)} collective-permute-done((bf16[64,2048]{1,0:T(8,128)(2,1)S(1)}, bf16[64,2048]{1,0:T(8,128)(2,1)S(1)}, u32[]{:S(2)}, u32[]{:S(2)}) %collective-permute-start.18) | collective-permute-done | bytes 262176 | tf_op jit(solution)/shard_map/ppermute | solution.py:471
  90.7 2.1 %collective-permute-start.20 = (bf16[64,2048]{1,0:T(8,128)(2,1)S(1)}, bf16[64,2048]{1,0:T(8,128)(2,1)S(1)}, u32[]{:S(2)}, u32[]{:S(2)}) collective-permute-start(bf16[64,2048]{1,0:T(8,128)(2,1)S(1)} %join.11), channel_id=1, source_target_pairs={{0,16},{16,0},{1,17},{17,1},{2,18},{18,2},{3,19},{19,3},{4,20},{20... | collective-permute-start | bytes 786440 | tf_op jit(solution)/shard_map/ppermute | solution.py:475
  92.8 2.7 %collective-permute-done.19.refs_2_ = bf16[64,2048]{1,0:T(8,128)(2,1)S(1)} collective-permute-done((bf16[64,2048]{1,0:T(8,128)(2,1)S(1)}, bf16[64,2048]{1,0:T(8,128)(2,1)S(1)}, u32[]{:S(2)}, u32[]{:S(2)}) %collective-permute-start.19) | collective-permute-done | bytes 262176 | tf_op jit(solution)/shard_map/ppermute | solution.py:477
  97.3 2.3 %collective-permute-start.23 = (bf16[64,1024]{1,0:T(8,128)(2,1)S(1)}, bf16[64,1024]{1,0:T(8,128)(2,1)S(1)}, u32[]{:S(2)}, u32[]{:S(2)}) collective-permute-start(bf16[64,1024]{1,0:T(8,128)(2,1)S(1)} %get-tuple-element.54), channel_id=1, source_target_pairs={{0,16},{16,0},{1,17},{17,1},{2,18},{18,2},{3,19},{19,3},{4,20},{20... | collective-permute-start | bytes 393224 | tf_op jit(solution)/shard_map/ppermute | solution.py:500
  102.5 2.9 %collective-permute-done.21.refs_0_ = bf16[64,1024]{1,0:T(8,128)(2,1)S(1)} collective-permute-done((bf16[64,1024]{1,0:T(8,128)(2,1)S(1)}, bf16[64,1024]{1,0:T(8,128)(2,1)S(1)}, u32[]{:S(2)}, u32[]{:S(2)}) %collective-permute-start.21) | collective-permute-done | bytes 131104 | tf_op jit(solution)/shard_map/ppermute | solution.py:502
  (100 shorter events, 26.0 us)
Async XLA Ops:
  2.8 22.9 %all-to-all-start = ((bf16[16,16,1152]{2,1,0:T(8,128)(2,1)}), bf16[16,16,1152]{2,1,0:T(8,128)(2,1)S(1)}, u32[]{:S(2)}, u32[]{:S(2)}) async-start(bf16[16,16,1152]{2,1,0:T(8,128)(2,1)} %pick.1), calls=%async_computation | async-start | bytes 1179648 | tf_op jit(solution)/shard_map/all_to_all | solution.py:322
  31.6 8.5 %collective-permute-start = (bf16[64,2048]{1,0:T(8,128)(2,1)}, bf16[64,2048]{1,0:T(8,128)(2,1)S(1)}, u32[]{:S(2)}, u32[]{:S(2)}) collective-permute-start(bf16[64,2048]{1,0:T(8,128)(2,1)} %attend_moved.1.after_any.own_any), channel_id=1, source_target_pairs={{0,16},{16,0},{1,17},{17,1},{2,18},{18,2},{3,19},{19,3},{4,20},{20... | collective-permute-start | bytes 786440 | tf_op jit(solution)/shard_map/ppermute | solution.py:377
  40.8 8.7 %collective-permute-start.2 = (bf16[64,2176]{1,0:T(8,128)(2,1)S(1)}, bf16[64,2176]{1,0:T(8,128)(2,1)S(1)}, u32[]{:S(2)}, u32[]{:S(2)}) collective-permute-start(bf16[64,2176]{1,0:T(8,128)(2,1)S(1)} %get-tuple-element.33.after_any.refs_0_), channel_id=1, source_target_pairs={{0,8},{1,9},{2,10},{3,11},{4,0},{5,1},{6,2},{7,3},{8,12},{9,13},{1... | collective-permute-start | bytes 835592 | tf_op jit(solution)/shard_map/ppermute | solution.py:456
  42.8 6.8 %collective-permute-start.1 = (bf16[64,2176]{1,0:T(8,128)(2,1)S(1)}, bf16[64,2176]{1,0:T(8,128)(2,1)S(1)}, u32[]{:S(2)}, u32[]{:S(2)}) collective-permute-start(bf16[64,2176]{1,0:T(8,128)(2,1)S(1)} %get-tuple-element.33.after_any.refs_0_), channel_id=1, source_target_pairs={{0,2},{1,3},{2,0},{3,1},{4,6},{5,7},{6,4},{7,5},{8,10},{9,11},{10,... | collective-permute-start | bytes 835592 | tf_op jit(solution)/shard_map/ppermute | solution.py:457
  49.6 5.3 %collective-permute-start.3 = (bf16[192,2176]{1,0:T(8,128)(2,1)S(1)}, bf16[192,2176]{1,0:T(8,128)(2,1)S(1)}, u32[]{:S(2)}, u32[]{:S(2)}) collective-permute-start(bf16[192,2176]{1,0:T(8,128)(2,1)S(1)} %pack.3.here_ref), channel_id=1, source_target_pairs={{0,1},{1,0},{2,3},{3,2},{4,5},{5,4},{6,7},{7,6},{8,9},{9,8},{10,11... | collective-permute-start | bytes 2506760 | tf_op jit(solution)/shard_map/ppermute | solution.py:421
  49.7 10.0 %collective-permute-start.7 = (bf16[64,2176]{1,0:T(8,128)(2,1)S(1)}, bf16[64,2176]{1,0:T(8,128)(2,1)S(1)}, u32[]{:S(2)}, u32[]{:S(2)}) collective-permute-start(bf16[64,2176]{1,0:T(8,128)(2,1)S(1)} %collective-permute-done.2.refs_2_), channel_id=1, source_target_pairs={{0,8},{1,9},{2,10},{3,11},{4,0},{5,1},{6,2},{7,3},{8,12},{9,13},{1... | collective-permute-start | bytes 835592 | tf_op jit(solution)/shard_map/ppermute | solution.py:458
  52.0 8.5 %collective-permute-start.6 = (bf16[64,2176]{1,0:T(8,128)(2,1)S(1)}, bf16[64,2176]{1,0:T(8,128)(2,1)S(1)}, u32[]{:S(2)}, u32[]{:S(2)}) collective-permute-start(bf16[64,2176]{1,0:T(8,128)(2,1)S(1)} %collective-permute-done.2.refs_2_), channel_id=1, source_target_pairs={{0,2},{1,3},{2,0},{3,1},{4,6},{5,7},{6,4},{7,5},{8,10},{9,11},{10,... | collective-permute-start | bytes 835592 | tf_op jit(solution)/shard_map/ppermute | solution.py:459
  53.4 8.3 %collective-permute-start.5 = (bf16[64,2176]{1,0:T(8,128)(2,1)S(1)}, bf16[64,2176]{1,0:T(8,128)(2,1)S(1)}, u32[]{:S(2)}, u32[]{:S(2)}) collective-permute-start(bf16[64,2176]{1,0:T(8,128)(2,1)S(1)} %collective-permute-done.2.refs_2_), channel_id=1, source_target_pairs={{0,16},{16,0},{1,17},{17,1},{2,18},{18,2},{3,19},{19,3},{4,20},{20... | collective-permute-start | bytes 835592 | tf_op jit(solution)/shard_map/ppermute | solution.py:460
  61.7 2.4 %collective-permute-start.8 = (bf16[192,2176]{1,0:T(8,128)(2,1)S(1)}, bf16[192,2176]{1,0:T(8,128)(2,1)S(1)}, u32[]{:S(2)}, u32[]{:S(2)}) collective-permute-start(bf16[192,2176]{1,0:T(8,128)(2,1)S(1)} %pack.4.here_ref), channel_id=1, source_target_pairs={{0,1},{1,0},{2,3},{3,2},{4,5},{5,4},{6,7},{7,6},{8,9},{9,8},{10,11... | collective-permute-start | bytes 2506760 | tf_op jit(solution)/shard_map/ppermute | solution.py:421
  61.8 9.1 %collective-permute-start.11 = (bf16[64,2176]{1,0:T(8,128)(2,1)S(1)}, bf16[64,2176]{1,0:T(8,128)(2,1)S(1)}, u32[]{:S(2)}, u32[]{:S(2)}) collective-permute-start(bf16[64,2176]{1,0:T(8,128)(2,1)S(1)} %collective-permute-done.7.refs_2_), channel_id=1, source_target_pairs={{0,2},{1,3},{2,0},{3,1},{4,6},{5,7},{6,4},{7,5},{8,10},{9,11},{10,... | collective-permute-start | bytes 835592 | tf_op jit(solution)/shard_map/ppermute | solution.py:461
  62.5 8.7 %collective-permute-start.10 = (bf16[64,2176]{1,0:T(8,128)(2,1)S(1)}, bf16[64,2176]{1,0:T(8,128)(2,1)S(1)}, u32[]{:S(2)}, u32[]{:S(2)}) collective-permute-start(bf16[64,2176]{1,0:T(8,128)(2,1)S(1)} %collective-permute-done.6.refs_1_), channel_id=1, source_target_pairs={{0,16},{16,0},{1,17},{17,1},{2,18},{18,2},{3,19},{19,3},{4,20},{20... | collective-permute-start | bytes 835592 | tf_op jit(solution)/shard_map/ppermute | solution.py:462
  64.0 7.8 %collective-permute-start.4 = (bf16[192,2048]{1,0:T(8,128)(2,1)S(1)}, bf16[192,2048]{1,0:T(8,128)(2,1)S(1)}, u32[]{:S(2)}, u32[]{:S(2)}) collective-permute-start(bf16[192,2048]{1,0:T(8,128)(2,1)S(1)} %get-tuple-element.37), channel_id=1, source_target_pairs={{0,1},{1,0},{2,3},{3,2},{4,5},{5,4},{6,7},{7,6},{8,9},{9,8},{10,11... | collective-permute-start | bytes 2359304 | tf_op jit(solution)/shard_map/ppermute | solution.py:432
  71.3 12.2 %collective-permute-start.9 = (bf16[192,2048]{1,0:T(8,128)(2,1)S(1)}, bf16[192,2048]{1,0:T(8,128)(2,1)S(1)}, u32[]{:S(2)}, u32[]{:S(2)}) collective-permute-start(bf16[192,2048]{1,0:T(8,128)(2,1)S(1)} %get-tuple-element.40), channel_id=1, source_target_pairs={{0,1},{1,0},{2,3},{3,2},{4,5},{5,4},{6,7},{7,6},{8,9},{9,8},{10,11... | collective-permute-start | bytes 2359304 | tf_op jit(solution)/shard_map/ppermute | solution.py:432
  72.0 8.4 %collective-permute-start.13 = (bf16[64,2048]{1,0:T(8,128)(2,1)S(1)}, bf16[64,2048]{1,0:T(8,128)(2,1)S(1)}, u32[]{:S(2)}, u32[]{:S(2)}) collective-permute-start(bf16[64,2048]{1,0:T(8,128)(2,1)S(1)} %get-tuple-element.42.after_any), channel_id=1, source_target_pairs={{0,2},{1,3},{2,0},{3,1},{4,6},{5,7},{6,4},{7,5},{8,10},{9,11},{10,... | collective-permute-start | bytes 786440 | tf_op jit(solution)/shard_map/ppermute | solution.py:466
  76.1 4.2 %collective-permute-start.14 = (bf16[64,2048]{1,0:T(8,128)(2,1)S(1)}, bf16[64,2048]{1,0:T(8,128)(2,1)S(1)}, u32[]{:S(2)}, u32[]{:S(2)}) collective-permute-start(bf16[64,2048]{1,0:T(8,128)(2,1)S(1)} %get-tuple-element.44), channel_id=1, source_target_pairs={{0,1},{1,0},{2,3},{3,2},{4,5},{5,4},{6,7},{7,6},{8,9},{9,8},{10,11... | collective-permute-start | bytes 786440 | tf_op jit(solution)/shard_map/ppermute | solution.py:432
  76.2 4.2 %collective-permute-start.15 = (bf16[64,2048]{1,0:T(8,128)(2,1)S(1)}, bf16[64,2048]{1,0:T(8,128)(2,1)S(1)}, u32[]{:S(2)}, u32[]{:S(2)}) collective-permute-start(bf16[64,2048]{1,0:T(8,128)(2,1)S(1)} %get-tuple-element.45), channel_id=1, source_target_pairs={{0,1},{1,0},{2,3},{3,2},{4,5},{5,4},{6,7},{7,6},{8,9},{9,8},{10,11... | collective-permute-start | bytes 786440 | tf_op jit(solution)/shard_map/ppermute | solution.py:432
  80.5 7.5 %collective-permute-start.18 = (bf16[64,2048]{1,0:T(8,128)(2,1)S(1)}, bf16[64,2048]{1,0:T(8,128)(2,1)S(1)}, u32[]{:S(2)}, u32[]{:S(2)}) collective-permute-start(bf16[64,2048]{1,0:T(8,128)(2,1)S(1)} %get-tuple-element.48), channel_id=1, source_target_pairs={{0,2},{1,3},{2,0},{3,1},{4,6},{5,7},{6,4},{7,5},{8,10},{9,11},{10,... | collective-permute-start | bytes 786440 | tf_op jit(solution)/shard_map/ppermute | solution.py:471
  82.0 7.2 %collective-permute-start.16 = (bf16[64,2048]{1,0:T(8,128)(2,1)S(1)}, bf16[64,2048]{1,0:T(8,128)(2,1)S(1)}, u32[]{:S(2)}, u32[]{:S(2)}) collective-permute-start(bf16[64,2048]{1,0:T(8,128)(2,1)S(1)} %get-tuple-element.46), channel_id=1, source_target_pairs={{0,16},{16,0},{1,17},{17,1},{2,18},{18,2},{3,19},{19,3},{4,20},{20... | collective-permute-start | bytes 786440 | tf_op jit(solution)/shard_map/ppermute | solution.py:470
  88.0 7.5 %collective-permute-start.19 = (bf16[64,2048]{1,0:T(8,128)(2,1)S(1)}, bf16[64,2048]{1,0:T(8,128)(2,1)S(1)}, u32[]{:S(2)}, u32[]{:S(2)}) collective-permute-start(bf16[64,2048]{1,0:T(8,128)(2,1)S(1)} %join.10), channel_id=1, source_target_pairs={{0,4},{1,5},{2,6},{3,7},{4,12},{5,13},{6,14},{7,15},{8,0},{9,1},{1... | collective-permute-start | bytes 786440 | tf_op jit(solution)/shard_map/ppermute | solution.py:477
  89.2 6.4 %collective-permute-start.17 = (bf16[64,2048]{1,0:T(8,128)(2,1)S(1)}, bf16[64,2048]{1,0:T(8,128)(2,1)S(1)}, u32[]{:S(2)}, u32[]{:S(2)}) collective-permute-start(bf16[64,2048]{1,0:T(8,128)(2,1)S(1)} %join.9), channel_id=1, source_target_pairs={{0,2},{1,3},{2,0},{3,1},{4,6},{5,7},{6,4},{7,5},{8,10},{9,11},{10,... | collective-permute-start | bytes 786440 | tf_op jit(solution)/shard_map/ppermute | solution.py:476
  90.7 6.5 %collective-permute-start.20 = (bf16[64,2048]{1,0:T(8,128)(2,1)S(1)}, bf16[64,2048]{1,0:T(8,128)(2,1)S(1)}, u32[]{:S(2)}, u32[]{:S(2)}) collective-permute-start(bf16[64,2048]{1,0:T(8,128)(2,1)S(1)} %join.11), channel_id=1, source_target_pairs={{0,16},{16,0},{1,17},{17,1},{2,18},{18,2},{3,19},{19,3},{4,20},{20... | collective-permute-start | bytes 786440 | tf_op jit(solution)/shard_map/ppermute | solution.py:475
  97.3 5.2 %collective-permute-start.23 = (bf16[64,1024]{1,0:T(8,128)(2,1)S(1)}, bf16[64,1024]{1,0:T(8,128)(2,1)S(1)}, u32[]{:S(2)}, u32[]{:S(2)}) collective-permute-start(bf16[64,1024]{1,0:T(8,128)(2,1)S(1)} %get-tuple-element.54), channel_id=1, source_target_pairs={{0,16},{16,0},{1,17},{17,1},{2,18},{18,2},{3,19},{19,3},{4,20},{20... | collective-permute-start | bytes 393224 | tf_op jit(solution)/shard_map/ppermute | solution.py:500
  99.6 5.9 %collective-permute-start.21 = (bf16[64,1024]{1,0:T(8,128)(2,1)S(1)}, bf16[64,1024]{1,0:T(8,128)(2,1)S(1)}, u32[]{:S(2)}, u32[]{:S(2)}) collective-permute-start(bf16[64,1024]{1,0:T(8,128)(2,1)S(1)} %get-tuple-element.53), channel_id=1, source_target_pairs={{0,20},{1,21},{2,22},{3,23},{4,28},{5,29},{6,30},{7,31},{8,16},{9,... | collective-permute-start | bytes 393224 | tf_op jit(solution)/shard_map/ppermute | solution.py:502
  100.7 5.9 %collective-permute-start.22 = (bf16[64,1024]{1,0:T(8,128)(2,1)S(1)}, bf16[64,1024]{1,0:T(8,128)(2,1)S(1)}, u32[]{:S(2)}, u32[]{:S(2)}) collective-permute-start(bf16[64,1024]{1,0:T(8,128)(2,1)S(1)} %get-tuple-element.49.after_any), channel_id=1, source_target_pairs={{0,4},{1,5},{2,6},{3,7},{4,12},{5,13},{6,14},{7,15},{8,0},{9,1},{1... | collective-permute-start | bytes 393224 | tf_op jit(solution)/shard_map/ppermute | solution.py:501
  (16 other events, 113.0 us)

commit v9 on v8

--- a/solution.py
+++ b/solution.py
@@ -69,7 +69,7 @@
 
 
 def resident_kernel(
-    dims, nope, rope_rows, fresh, cache, absorb, bias_ref,
+    dims, nope, rope_rows, fresh, cache, absorb, value, bias_ref,
     query_ref, mixed_ref,
     keys,
 ):
@@ -96,9 +96,13 @@
         peak = jnp.max(score, axis=1, keepdims=True)
         weight = jnp.exp(score - peak)
         total = jnp.sum(weight, axis=1, keepdims=True)
-        mixed_ref[first : first + part, :latent] = dot(weight.astype(BF16), keys[:, :latent])
+        mixed = dot(weight.astype(BF16), keys[:, :latent]).astype(BF16)
+        value_dim = value.shape[2]
+        for at in range(0, part, rows):
+            here = slice(first + at, first + at + rows)
+            mixed_ref[here, :value_dim] = dot(mixed[at : at + rows], value[(first + at) // rows])
         lane = lax.broadcasted_iota(jnp.int32, (part, 128), 1)
-        mixed_ref[first : first + part, latent:] = jnp.where(lane < 64, peak, total)
+        mixed_ref[first : first + part, value_dim:] = jnp.where(lane < 64, peak, total)
 
 
 def moved_kernel(
@@ -132,18 +136,20 @@
         score = score.reshape(group * rows, -1)
         if first == 0:
             got[3].wait()
-        before = mixed[at, latent : latent + 1]
+        before = mixed[at, value_dim : value_dim + 1]
         peak = jnp.maximum(jnp.max(score, axis=1, keepdims=True), before)
         weight = jnp.exp(score - peak)
         keep = jnp.exp(before - peak)
-        total = jnp.sum(weight, axis=1, keepdims=True) + mixed[at, latent + 64 : latent + 65] * keep
-        joined = dot(weight.astype(BF16), keys[:, :latent]) + mixed[at, :latent] * keep
-        joined = (joined / total).astype(BF16)
+        total = jnp.sum(weight, axis=1, keepdims=True)
+        total = total + mixed[at, value_dim + 64 : value_dim + 65] * keep
+        joined = dot(weight.astype(BF16), keys[:, :latent]).astype(BF16)
         if first == 0:
             got[4].wait()
         for head in range(first, first + group):
-            own = joined[(head - first) * rows : (head - first + 1) * rows]
-            heads_out[:, head * value_dim : (head + 1) * value_dim] = dot(own, value[head]).astype(BF16)
+            own = slice((head - first) * rows, (head - first + 1) * rows)
+            both = dot(joined[own], value[head])
+            both = both + mixed[head * rows : (head + 1) * rows, :value_dim] * keep[own]
+            heads_out[:, head * value_dim : (head + 1) * value_dim] = (both / total[own]).astype(BF16)
     got[5].wait()
     share_ref[...] = dot(heads_out[...], proj[...]).astype(BF16)
 
@@ -348,13 +354,13 @@
         functools.partial(resident_kernel, dims),
         out_shape=(
             jax.ShapeDtypeStruct((query_rows, padded), BF16),
-            jax.ShapeDtypeStruct((query_rows, latent + 128), F32),
+            jax.ShapeDtypeStruct((query_rows, value_absorb.shape[2] + 128), F32),
         ),
         scratch_shapes=[VMEM((near_bias.shape[1], padded), BF16)],
         compiler_params=pltpu.CompilerParams(vmem_limit_bytes=16 * 2**20),
         cost_estimate=cost(query_rows * near_bias.shape[1] * (padded + latent), 8 * 2**20),
         name="attend_resident",
-    )(query_nope, query_rope, new_latent, latent_cache, key_absorb, near_bias)
+    )(query_nope, query_rope, new_latent, latent_cache, key_absorb, value_absorb, near_bias)
     share = pl.pallas_call(
         functools.partial(moved_kernel, dims),
         out_shape=jax.ShapeDtypeStruct((row_count, model), BF16),

time: 108 us -> 117 us (1.083)
  local copies, waits for them, and re-layouts: 5.11 us -> 16.3 us
  waiting for transfers between devices: 41.4 us -> 33.3 us
  other arithmetic: 0.72 us -> 5.72 us
    all_to_all x1, waiting for transfers between devices: 8.7 us -> 0.01 us  [local(): lax.all_to_all(outgoing, 'ep', split_axis=0, concat_axis=0, tiled=True)]
    gt x4, local copies, waits for them, and re-layouts: 0.18 us -> 4.23 us  [local(): limit[:, None, :resident] > token[None, :, None]]
    ppermute x1, waiting for transfers between devices: 6.74 us -> 4.08 us  [local(): near = lax.ppermute(packet, both_axes, onward)]
    ppermute x1, waiting for transfers between devices: 0.01 us -> 2.05 us  [local(): side = lax.ppermute(packet, 'ep', side_swap)]
    slice x2, local copies, waits for them, and re-layouts: 0.15 us -> 2.04 us  [local(): by_key = jnp.repeat(limit[:, resident:], pieces, axis=1)]
    ppermute x1, starting transfers between devices: 0.01 us -> 1.46 us  [local(): side = lax.ppermute(packet, 'ep', side_swap)]
    reshape x1, local copies, waits for them, and re-layouts: 0.04 us -> 1.5 us  [local(): jnp.repeat(near_open, steps, axis=0)]
    gt x1, local copies, waits for them, and re-layouts: 0.07 us -> 1.43 us  [local(): by_key > at_token[None]]
  transfers between devices with their start and end apart: 25 -> 25, of which waited for: 18 -> 18; matrix products, arithmetic and copies ran while one was open for 2% -> 17% of each run, Pallas kernels for 16% -> 15%
where the time goes in v9:
time: 117 us; the launch traced here: 116 us
  starting transfers between devices  33.4 us (29%)
  waiting for transfers between devices  33.3 us (28%)
  Pallas kernels  27 us (23%)
  local copies, waits for them, and re-layouts  16.3 us (14%)
  other arithmetic  5.72 us (5%)
    pallas_call x3, Pallas kernels, run_expert(): pl.pallas_call(functools.partial(expert_kernel, experts), out_shape=[jax....  10.3 us
    all_to_all x1, starting transfers between devices, local(): lax.all_to_all(outgoing, 'ep', split_axis=0, concat_axis=0, tiled=True)  7.43 us
    pallas_call x1, Pallas kernels, local(): pl.pallas_call(functools.partial(moved_kernel, dims), out_shape=jax.Shape...  4.94 us
    ppermute x1, waiting for transfers between devices, local(): two_side_in = lax.ppermute(two_side_sum, 'ep', side_swap)  4.4 us
    gt x4, local copies, waits for them, and re-layouts, local(): limit[:, None, :resident] > token[None, :, None]  4.23 us
    ppermute x1, waiting for transfers between devices, local(): near = lax.ppermute(packet, both_axes, onward)  4.08 us
    ppermute x1, waiting for transfers between devices, local(): two_in = lax.ppermute(two_sum, both_axes, backward)  3.66 us
    ppermute x1, waiting for transfers between devices, local(): side_in = lax.ppermute(side_sum, 'ep', side_swap)  3.6 us
  transfers between devices with their start and end apart: 25, of which 18 were waited for; matrix products, arithmetic and copies ran while one was open for 17% of the time, Pallas kernels for 15%

profile of v9, /device:TPU:0, one launch (start us, length us, event | category | flops | bytes accessed | tf_op | source)
XLA Modules:
  0.0 116.0 jit_solution(135730598870031941)
XLA Ops:
  0.0 2.8 %pick.1 = bf16[16,16,1152]{2,1,0:T(8,128)(2,1)} custom-call(s32[2,16]{1,0:T(2,128)} %bitcast.22, bf16[64,9216]{1,0:T(8,128)(2,1)} %cache.1), custom_call_target="tpu_custom_call" | custom-call | bytes 4194304 | tf_op jit(solution)/shard_map/pick/pallas_call | solution.py:314
  2.8 7.4 %all-to-all-start = ((bf16[16,16,1152]{2,1,0:T(8,128)(2,1)}), bf16[16,16,1152]{2,1,0:T(8,128)(2,1)}, u32[]{:S(2)}, u32[]{:S(2)}) async-start(bf16[16,16,1152]{2,1,0:T(8,128)(2,1)} %pick.1), calls=%async_computation | async-start | bytes 1179648 | tf_op jit(solution)/shard_map/all_to_all | solution.py:328
  21.7 1.6 %reshape.110.bias_any = f32[64,512]{1,0:T(8,128)} reshape(f32[16,4,512]{2,1,0:T(4,128)} %broadcast_in_dim.61) | data formatting | bytes 262144 | tf_op jit(solution)/shard_map/reshape | solution.py:348
  24.0 1.6 %gt.37 = s32[16,1024]{1,0:T(8,128)} reshape(s32[16,16,64]{2,1,0:T(8,128)} %gt.36) | data formatting | bytes 131072 | tf_op jit(solution)/shard_map/gt | solution.py:342
  29.7 3.0 %attend_resident.1 = (bf16[512,640]{1,0:T(8,128)(2,1)S(1)}, f32[512,256]{1,0:T(8,128)S(1)}) custom-call(bf16[64,1024]{1,0:T(8,128)(2,1)S(1)} %copy-done.9, bf16[64,512]{1,0:T(8,128)(2,1)S(1)} %copy-done.11, bf16[16,2304]{1,0:T(8,128)(2,1)S(1)} %copy-done.10, bf16[64,9216]{1,0:T(8,128)(2,1)S(1)} %copy-done.1, bf16[8,128,512]{2,1,0:T(8,128)(2,1)S(1)} %copy-done.8, ...), custom_call_target="tpu_custom_call" | custom-call | flops 1283457024 | bytes 8388608 | tf_op jit(solution)/shard_map/attend_resident/pallas_call | solution.py:353
  34.4 4.9 %attend_moved.1.after_any.own_any = bf16[64,2048]{1,0:T(8,128)(2,1)} custom-call(bf16[16,16,1152]{2,1,0:T(8,128)(2,1)} %all-to-all-done.moved_any, bf16[512,640]{1,0:T(8,128)(2,1)} %copy-done.3, f32[64,512]{1,0:T(8,128)} %reshape.110.bias_any, f32[512,256]{1,0:T(8,128)} %copy-done.4, bf16[8,512,128]{2,1,0:T(8,128)(2,1)} %value_any.1, bf16[1024,2048]{1,0:T(8,128)(2,1)} %proj_any.1), custom_call_target="tpu_custom_call" | custom-call | flops 603979776 | bytes 10485760 | tf_op jit(solution)/shard_map/attend_moved/pallas_call | solution.py:364
  39.4 1.6 %collective-permute-start = (bf16[64,2048]{1,0:T(8,128)(2,1)}, bf16[64,2048]{1,0:T(8,128)(2,1)S(1)}, u32[]{:S(2)}, u32[]{:S(2)}) collective-permute-start(bf16[64,2048]{1,0:T(8,128)(2,1)} %attend_moved.1.after_any.own_any), channel_id=1, source_target_pairs={{0,16},{16,0},{1,17},{17,1},{2,18},{18,2},{3,19},{19,3},{4,20},{20... | collective-permute-start | bytes 786440 | tf_op jit(solution)/shard_map/ppermute | solution.py:383
  41.9 3.6 %load.1 = (bf16[704,2048]{1,0:T(8,128)(2,1)S(1)}, bf16[704,2048]{1,0:T(8,128)(2,1)S(1)}, bf16[704,2048]{1,0:T(8,128)(2,1)S(1)}) custom-call(bf16[64,2048]{1,0:T(8,128)(2,1)S(1)} %copy-done, bf16[704,2048]{1,0:T(8,128)(2,1)} %bitcast.18, bf16[704,2048]{1,0:T(8,128)(2,1)} %bitcast.19, bf16[704,2048]{1,0:T(8,128)(2,1)} %bitcast.20), custom_call_target="tpu_custom_call" | custom-call | bytes 12582912 | tf_op jit(solution)/shard_map/load/pallas_call | solution.py:386
  45.5 2.7 %collective-permute-done.refs_0_ = bf16[64,2048]{1,0:T(8,128)(2,1)S(1)} collective-permute-done((bf16[64,2048]{1,0:T(8,128)(2,1)}, bf16[64,2048]{1,0:T(8,128)(2,1)S(1)}, u32[]{:S(2)}, u32[]{:S(2)}) %collective-permute-start) | collective-permute-done | bytes 262176 | tf_op jit(solution)/shard_map/ppermute | solution.py:383
  48.9 2.6 %collective-permute-start.2 = (bf16[64,2176]{1,0:T(8,128)(2,1)S(1)}, bf16[64,2176]{1,0:T(8,128)(2,1)S(1)}, u32[]{:S(2)}, u32[]{:S(2)}) collective-permute-start(bf16[64,2176]{1,0:T(8,128)(2,1)S(1)} %get-tuple-element.33.after_any.refs_0_), channel_id=1, source_target_pairs={{0,8},{1,9},{2,10},{3,11},{4,0},{5,1},{6,2},{7,3},{8,12},{9,13},{1... | collective-permute-start | bytes 835592 | tf_op jit(solution)/shard_map/ppermute | solution.py:462
  53.0 4.1 %collective-permute-done.2.refs_2_ = bf16[64,2176]{1,0:T(8,128)(2,1)S(1)} collective-permute-done((bf16[64,2176]{1,0:T(8,128)(2,1)S(1)}, bf16[64,2176]{1,0:T(8,128)(2,1)S(1)}, u32[]{:S(2)}, u32[]{:S(2)}) %collective-permute-start.2) | collective-permute-done | bytes 278560 | tf_op jit(solution)/shard_map/ppermute | solution.py:462
  57.0 2.1 %collective-permute-done.1.refs_1_ = bf16[64,2176]{1,0:T(8,128)(2,1)S(1)} collective-permute-done((bf16[64,2176]{1,0:T(8,128)(2,1)S(1)}, bf16[64,2176]{1,0:T(8,128)(2,1)S(1)}, u32[]{:S(2)}, u32[]{:S(2)}) %collective-permute-start.1) | collective-permute-done | bytes 278560 | tf_op jit(solution)/shard_map/ppermute | solution.py:463
  59.2 1.7 %collective-permute-start.7 = (bf16[64,2176]{1,0:T(8,128)(2,1)S(1)}, bf16[64,2176]{1,0:T(8,128)(2,1)S(1)}, u32[]{:S(2)}, u32[]{:S(2)}) collective-permute-start(bf16[64,2176]{1,0:T(8,128)(2,1)S(1)} %collective-permute-done.2.refs_2_), channel_id=1, source_target_pairs={{0,8},{1,9},{2,10},{3,11},{4,0},{5,1},{6,2},{7,3},{8,12},{9,13},{1... | collective-permute-start | bytes 835592 | tf_op jit(solution)/shard_map/ppermute | solution.py:464
  63.9 3.8 %expert.3 = (bf16[192,2048]{1,0:T(8,128)(2,1)S(1)}, bf16[192,2048]{1,0:T(8,128)(2,1)S(1)}) custom-call(bf16[64,2176]{1,0:T(8,128)(2,1)S(1)} %get-tuple-element.33.after_any.refs_0_, bf16[192,2176]{1,0:T(8,128)(2,1)S(1)} %pack.3.here_ref, bf16[192,2176]{1,0:T(8,128)(2,1)S(1)} %collective-permute-done.3.across_ref, ...), custom_call_target="tpu_custom_call" | custom-call | flops 3321888768 | bytes 12582912 | tf_op jit(solution)/shard_map/expert/pallas_call | solution.py:428
  73.2 3.8 %expert.4 = (bf16[192,2048]{1,0:T(8,128)(2,1)S(1)}, bf16[192,2048]{1,0:T(8,128)(2,1)S(1)}) custom-call(bf16[64,2176]{1,0:T(8,128)(2,1)S(1)} %get-tuple-element.33.after_any.refs_0_, bf16[192,2176]{1,0:T(8,128)(2,1)S(1)} %pack.4.here_ref, bf16[192,2176]{1,0:T(8,128)(2,1)S(1)} %collective-permute-done.8.across_ref, ...), custom_call_target="tpu_custom_call" | custom-call | flops 3321888768 | bytes 12582912 | tf_op jit(solution)/shard_map/expert/pallas_call | solution.py:428
  77.0 2.9 %collective-permute-done.11.refs_1_ = bf16[64,2176]{1,0:T(8,128)(2,1)S(1)} collective-permute-done((bf16[64,2176]{1,0:T(8,128)(2,1)S(1)}, bf16[64,2176]{1,0:T(8,128)(2,1)S(1)}, u32[]{:S(2)}, u32[]{:S(2)}) %collective-permute-start.11) | collective-permute-done | bytes 278560 | tf_op jit(solution)/shard_map/ppermute | solution.py:467
  82.5 2.6 %expert.5 = (bf16[128,2048]{1,0:T(8,128)(2,1)S(1)}, bf16[64,2048]{1,0:T(8,128)(2,1)S(1)}, bf16[64,2048]{1,0:T(8,128)(2,1)S(1)}) custom-call(bf16[64,2048]{1,0:T(8,128)(2,1)S(1)} %get-tuple-element.42.after_any, bf16[128,2176]{1,0:T(8,128)(2,1)S(1)} %pack.5.here_ref, bf16[128,2176]{1,0:T(8,128)(2,1)S(1)} %collective-permute-done.12.across_ref, ...), custom_call_target="tpu_custom_call" | custom-call | flops 2214592512 | bytes 12582912 | tf_op jit(solution)/shard_map/expert/pallas_call | solution.py:428
  85.7 3.6 %collective-permute-done.13.refs_0_.side_ref = bf16[64,2048]{1,0:T(8,128)(2,1)S(1)} collective-permute-done((bf16[64,2048]{1,0:T(8,128)(2,1)S(1)}, bf16[64,2048]{1,0:T(8,128)(2,1)S(1)}, u32[]{:S(2)}, u32[]{:S(2)}) %collective-permute-start.13) | collective-permute-done | bytes 262176 | tf_op jit(solution)/shard_map/ppermute | solution.py:472
  92.6 4.4 %collective-permute-done.18.refs_0_ = bf16[64,2048]{1,0:T(8,128)(2,1)S(1)} collective-permute-done((bf16[64,2048]{1,0:T(8,128)(2,1)S(1)}, bf16[64,2048]{1,0:T(8,128)(2,1)S(1)}, u32[]{:S(2)}, u32[]{:S(2)}) %collective-permute-start.18) | collective-permute-done | bytes 262176 | tf_op jit(solution)/shard_map/ppermute | solution.py:477
  100.9 3.7 %collective-permute-done.19.refs_2_ = bf16[64,2048]{1,0:T(8,128)(2,1)S(1)} collective-permute-done((bf16[64,2048]{1,0:T(8,128)(2,1)S(1)}, bf16[64,2048]{1,0:T(8,128)(2,1)S(1)}, u32[]{:S(2)}, u32[]{:S(2)}) %collective-permute-start.19) | collective-permute-done | bytes 262176 | tf_op jit(solution)/shard_map/ppermute | solution.py:483
  104.7 1.6 %collective-permute-done.20.refs_3_ = bf16[64,2048]{1,0:T(8,128)(2,1)S(1)} collective-permute-done((bf16[64,2048]{1,0:T(8,128)(2,1)S(1)}, bf16[64,2048]{1,0:T(8,128)(2,1)S(1)}, u32[]{:S(2)}, u32[]{:S(2)}) %collective-permute-start.20) | collective-permute-done | bytes 262176 | tf_op jit(solution)/shard_map/ppermute | solution.py:481
  108.8 1.9 %collective-permute-start.22 = (bf16[64,1024]{1,0:T(8,128)(2,1)S(1)}, bf16[64,1024]{1,0:T(8,128)(2,1)S(1)}, u32[]{:S(2)}, u32[]{:S(2)}) collective-permute-start(bf16[64,1024]{1,0:T(8,128)(2,1)S(1)} %get-tuple-element.49.after_any), channel_id=1, source_target_pairs={{0,4},{1,5},{2,6},{3,7},{4,12},{5,13},{6,14},{7,15},{8,0},{9,1},{1... | collective-permute-start | bytes 393224 | tf_op jit(solution)/shard_map/ppermute | solution.py:507
  111.5 2.0 %collective-permute-done.21.refs_0_ = bf16[64,1024]{1,0:T(8,128)(2,1)S(1)} collective-permute-done((bf16[64,1024]{1,0:T(8,128)(2,1)S(1)}, bf16[64,1024]{1,0:T(8,128)(2,1)S(1)}, u32[]{:S(2)}, u32[]{:S(2)}) %collective-permute-start.21) | collective-permute-done | bytes 131104 | tf_op jit(solution)/shard_map/ppermute | solution.py:508
  113.5 1.7 %collective-permute-done.22.refs_1_ = bf16[64,1024]{1,0:T(8,128)(2,1)S(1)} collective-permute-done((bf16[64,1024]{1,0:T(8,128)(2,1)S(1)}, bf16[64,1024]{1,0:T(8,128)(2,1)S(1)}, u32[]{:S(2)}, u32[]{:S(2)}) %collective-permute-start.22) | collective-permute-done | bytes 131104 | tf_op jit(solution)/shard_map/ppermute | solution.py:507
  (98 shorter events, 43.8 us)
Async XLA Ops:
  2.8 31.6 %all-to-all-start = ((bf16[16,16,1152]{2,1,0:T(8,128)(2,1)}), bf16[16,16,1152]{2,1,0:T(8,128)(2,1)}, u32[]{:S(2)}, u32[]{:S(2)}) async-start(bf16[16,16,1152]{2,1,0:T(8,128)(2,1)} %pick.1), calls=%async_computation | async-start | bytes 1179648 | tf_op jit(solution)/shard_map/all_to_all | solution.py:328
  39.4 8.8 %collective-permute-start = (bf16[64,2048]{1,0:T(8,128)(2,1)}, bf16[64,2048]{1,0:T(8,128)(2,1)S(1)}, u32[]{:S(2)}, u32[]{:S(2)}) collective-permute-start(bf16[64,2048]{1,0:T(8,128)(2,1)} %attend_moved.1.after_any.own_any), channel_id=1, source_target_pairs={{0,16},{16,0},{1,17},{17,1},{2,18},{18,2},{3,19},{19,3},{4,20},{20... | collective-permute-start | bytes 786440 | tf_op jit(solution)/shard_map/ppermute | solution.py:383
  48.9 8.2 %collective-permute-start.2 = (bf16[64,2176]{1,0:T(8,128)(2,1)S(1)}, bf16[64,2176]{1,0:T(8,128)(2,1)S(1)}, u32[]{:S(2)}, u32[]{:S(2)}) collective-permute-start(bf16[64,2176]{1,0:T(8,128)(2,1)S(1)} %get-tuple-element.33.after_any.refs_0_), channel_id=1, source_target_pairs={{0,8},{1,9},{2,10},{3,11},{4,0},{5,1},{6,2},{7,3},{8,12},{9,13},{1... | collective-permute-start | bytes 835592 | tf_op jit(solution)/shard_map/ppermute | solution.py:462
  51.5 7.6 %collective-permute-start.1 = (bf16[64,2176]{1,0:T(8,128)(2,1)S(1)}, bf16[64,2176]{1,0:T(8,128)(2,1)S(1)}, u32[]{:S(2)}, u32[]{:S(2)}) collective-permute-start(bf16[64,2176]{1,0:T(8,128)(2,1)S(1)} %get-tuple-element.33.after_any.refs_0_), channel_id=1, source_target_pairs={{0,2},{1,3},{2,0},{3,1},{4,6},{5,7},{6,4},{7,5},{8,10},{9,11},{10,... | collective-permute-start | bytes 835592 | tf_op jit(solution)/shard_map/ppermute | solution.py:463
  59.2 4.7 %collective-permute-start.3 = (bf16[192,2176]{1,0:T(8,128)(2,1)S(1)}, bf16[192,2176]{1,0:T(8,128)(2,1)S(1)}, u32[]{:S(2)}, u32[]{:S(2)}) collective-permute-start(bf16[192,2176]{1,0:T(8,128)(2,1)S(1)} %pack.3.here_ref), channel_id=1, source_target_pairs={{0,1},{1,0},{2,3},{3,2},{4,5},{5,4},{6,7},{7,6},{8,9},{9,8},{10,11... | collective-permute-start | bytes 2506760 | tf_op jit(solution)/shard_map/ppermute | solution.py:427
  59.2 9.1 %collective-permute-start.7 = (bf16[64,2176]{1,0:T(8,128)(2,1)S(1)}, bf16[64,2176]{1,0:T(8,128)(2,1)S(1)}, u32[]{:S(2)}, u32[]{:S(2)}) collective-permute-start(bf16[64,2176]{1,0:T(8,128)(2,1)S(1)} %collective-permute-done.2.refs_2_), channel_id=1, source_target_pairs={{0,8},{1,9},{2,10},{3,11},{4,0},{5,1},{6,2},{7,3},{8,12},{9,13},{1... | collective-permute-start | bytes 835592 | tf_op jit(solution)/shard_map/ppermute | solution.py:464
  61.0 8.5 %collective-permute-start.6 = (bf16[64,2176]{1,0:T(8,128)(2,1)S(1)}, bf16[64,2176]{1,0:T(8,128)(2,1)S(1)}, u32[]{:S(2)}, u32[]{:S(2)}) collective-permute-start(bf16[64,2176]{1,0:T(8,128)(2,1)S(1)} %collective-permute-done.2.refs_2_), channel_id=1, source_target_pairs={{0,2},{1,3},{2,0},{3,1},{4,6},{5,7},{6,4},{7,5},{8,10},{9,11},{10,... | collective-permute-start | bytes 835592 | tf_op jit(solution)/shard_map/ppermute | solution.py:465
  62.4 8.3 %collective-permute-start.5 = (bf16[64,2176]{1,0:T(8,128)(2,1)S(1)}, bf16[64,2176]{1,0:T(8,128)(2,1)S(1)}, u32[]{:S(2)}, u32[]{:S(2)}) collective-permute-start(bf16[64,2176]{1,0:T(8,128)(2,1)S(1)} %collective-permute-done.2.refs_2_), channel_id=1, source_target_pairs={{0,16},{16,0},{1,17},{17,1},{2,18},{18,2},{3,19},{19,3},{4,20},{20... | collective-permute-start | bytes 835592 | tf_op jit(solution)/shard_map/ppermute | solution.py:466
  70.8 2.4 %collective-permute-start.8 = (bf16[192,2176]{1,0:T(8,128)(2,1)S(1)}, bf16[192,2176]{1,0:T(8,128)(2,1)S(1)}, u32[]{:S(2)}, u32[]{:S(2)}) collective-permute-start(bf16[192,2176]{1,0:T(8,128)(2,1)S(1)} %pack.4.here_ref), channel_id=1, source_target_pairs={{0,1},{1,0},{2,3},{3,2},{4,5},{5,4},{6,7},{7,6},{8,9},{9,8},{10,11... | collective-permute-start | bytes 2506760 | tf_op jit(solution)/shard_map/ppermute | solution.py:427
  70.8 9.1 %collective-permute-start.11 = (bf16[64,2176]{1,0:T(8,128)(2,1)S(1)}, bf16[64,2176]{1,0:T(8,128)(2,1)S(1)}, u32[]{:S(2)}, u32[]{:S(2)}) collective-permute-start(bf16[64,2176]{1,0:T(8,128)(2,1)S(1)} %collective-permute-done.7.refs_2_), channel_id=1, source_target_pairs={{0,2},{1,3},{2,0},{3,1},{4,6},{5,7},{6,4},{7,5},{8,10},{9,11},{10,... | collective-permute-start | bytes 835592 | tf_op jit(solution)/shard_map/ppermute | solution.py:467
  71.5 8.7 %collective-permute-start.10 = (bf16[64,2176]{1,0:T(8,128)(2,1)S(1)}, bf16[64,2176]{1,0:T(8,128)(2,1)S(1)}, u32[]{:S(2)}, u32[]{:S(2)}) collective-permute-start(bf16[64,2176]{1,0:T(8,128)(2,1)S(1)} %collective-permute-done.6.refs_1_), channel_id=1, source_target_pairs={{0,16},{16,0},{1,17},{17,1},{2,18},{18,2},{3,19},{19,3},{4,20},{20... | collective-permute-start | bytes 835592 | tf_op jit(solution)/shard_map/ppermute | solution.py:468
  72.9 7.9 %collective-permute-start.4 = (bf16[192,2048]{1,0:T(8,128)(2,1)S(1)}, bf16[192,2048]{1,0:T(8,128)(2,1)S(1)}, u32[]{:S(2)}, u32[]{:S(2)}) collective-permute-start(bf16[192,2048]{1,0:T(8,128)(2,1)S(1)} %get-tuple-element.37), channel_id=1, source_target_pairs={{0,1},{1,0},{2,3},{3,2},{4,5},{5,4},{6,7},{7,6},{8,9},{9,8},{10,11... | collective-permute-start | bytes 2359304 | tf_op jit(solution)/shard_map/ppermute | solution.py:438
  80.3 12.2 %collective-permute-start.9 = (bf16[192,2048]{1,0:T(8,128)(2,1)S(1)}, bf16[192,2048]{1,0:T(8,128)(2,1)S(1)}, u32[]{:S(2)}, u32[]{:S(2)}) collective-permute-start(bf16[192,2048]{1,0:T(8,128)(2,1)S(1)} %get-tuple-element.40), channel_id=1, source_target_pairs={{0,1},{1,0},{2,3},{3,2},{4,5},{5,4},{6,7},{7,6},{8,9},{9,8},{10,11... | collective-permute-start | bytes 2359304 | tf_op jit(solution)/shard_map/ppermute | solution.py:438
  81.0 8.4 %collective-permute-start.13 = (bf16[64,2048]{1,0:T(8,128)(2,1)S(1)}, bf16[64,2048]{1,0:T(8,128)(2,1)S(1)}, u32[]{:S(2)}, u32[]{:S(2)}) collective-permute-start(bf16[64,2048]{1,0:T(8,128)(2,1)S(1)} %get-tuple-element.42.after_any), channel_id=1, source_target_pairs={{0,2},{1,3},{2,0},{3,1},{4,6},{5,7},{6,4},{7,5},{8,10},{9,11},{10,... | collective-permute-start | bytes 786440 | tf_op jit(solution)/shard_map/ppermute | solution.py:472
  85.2 4.2 %collective-permute-start.14 = (bf16[64,2048]{1,0:T(8,128)(2,1)S(1)}, bf16[64,2048]{1,0:T(8,128)(2,1)S(1)}, u32[]{:S(2)}, u32[]{:S(2)}) collective-permute-start(bf16[64,2048]{1,0:T(8,128)(2,1)S(1)} %get-tuple-element.44), channel_id=1, source_target_pairs={{0,1},{1,0},{2,3},{3,2},{4,5},{5,4},{6,7},{7,6},{8,9},{9,8},{10,11... | collective-permute-start | bytes 786440 | tf_op jit(solution)/shard_map/ppermute | solution.py:438
  85.2 4.1 %collective-permute-start.15 = (bf16[64,2048]{1,0:T(8,128)(2,1)S(1)}, bf16[64,2048]{1,0:T(8,128)(2,1)S(1)}, u32[]{:S(2)}, u32[]{:S(2)}) collective-permute-start(bf16[64,2048]{1,0:T(8,128)(2,1)S(1)} %get-tuple-element.45), channel_id=1, source_target_pairs={{0,1},{1,0},{2,3},{3,2},{4,5},{5,4},{6,7},{7,6},{8,9},{9,8},{10,11... | collective-permute-start | bytes 786440 | tf_op jit(solution)/shard_map/ppermute | solution.py:438
  89.5 7.5 %collective-permute-start.18 = (bf16[64,2048]{1,0:T(8,128)(2,1)S(1)}, bf16[64,2048]{1,0:T(8,128)(2,1)S(1)}, u32[]{:S(2)}, u32[]{:S(2)}) collective-permute-start(bf16[64,2048]{1,0:T(8,128)(2,1)S(1)} %get-tuple-element.48), channel_id=1, source_target_pairs={{0,2},{1,3},{2,0},{3,1},{4,6},{5,7},{6,4},{7,5},{8,10},{9,11},{10,... | collective-permute-start | bytes 786440 | tf_op jit(solution)/shard_map/ppermute | solution.py:477
  91.0 7.2 %collective-permute-start.16 = (bf16[64,2048]{1,0:T(8,128)(2,1)S(1)}, bf16[64,2048]{1,0:T(8,128)(2,1)S(1)}, u32[]{:S(2)}, u32[]{:S(2)}) collective-permute-start(bf16[64,2048]{1,0:T(8,128)(2,1)S(1)} %get-tuple-element.46), channel_id=1, source_target_pairs={{0,16},{16,0},{1,17},{17,1},{2,18},{18,2},{3,19},{19,3},{4,20},{20... | collective-permute-start | bytes 786440 | tf_op jit(solution)/shard_map/ppermute | solution.py:476
  97.0 7.5 %collective-permute-start.19 = (bf16[64,2048]{1,0:T(8,128)(2,1)S(1)}, bf16[64,2048]{1,0:T(8,128)(2,1)S(1)}, u32[]{:S(2)}, u32[]{:S(2)}) collective-permute-start(bf16[64,2048]{1,0:T(8,128)(2,1)S(1)} %join.10), channel_id=1, source_target_pairs={{0,4},{1,5},{2,6},{3,7},{4,12},{5,13},{6,14},{7,15},{8,0},{9,1},{1... | collective-permute-start | bytes 786440 | tf_op jit(solution)/shard_map/ppermute | solution.py:483
  98.2 6.4 %collective-permute-start.17 = (bf16[64,2048]{1,0:T(8,128)(2,1)S(1)}, bf16[64,2048]{1,0:T(8,128)(2,1)S(1)}, u32[]{:S(2)}, u32[]{:S(2)}) collective-permute-start(bf16[64,2048]{1,0:T(8,128)(2,1)S(1)} %join.9), channel_id=1, source_target_pairs={{0,2},{1,3},{2,0},{3,1},{4,6},{5,7},{6,4},{7,5},{8,10},{9,11},{10,... | collective-permute-start | bytes 786440 | tf_op jit(solution)/shard_map/ppermute | solution.py:482
  99.6 6.6 %collective-permute-start.20 = (bf16[64,2048]{1,0:T(8,128)(2,1)S(1)}, bf16[64,2048]{1,0:T(8,128)(2,1)S(1)}, u32[]{:S(2)}, u32[]{:S(2)}) collective-permute-start(bf16[64,2048]{1,0:T(8,128)(2,1)S(1)} %join.11), channel_id=1, source_target_pairs={{0,16},{16,0},{1,17},{17,1},{2,18},{18,2},{3,19},{19,3},{4,20},{20... | collective-permute-start | bytes 786440 | tf_op jit(solution)/shard_map/ppermute | solution.py:481
  106.5 5.0 %collective-permute-start.23 = (bf16[64,1024]{1,0:T(8,128)(2,1)S(1)}, bf16[64,1024]{1,0:T(8,128)(2,1)S(1)}, u32[]{:S(2)}, u32[]{:S(2)}) collective-permute-start(bf16[64,1024]{1,0:T(8,128)(2,1)S(1)} %get-tuple-element.54), channel_id=1, source_target_pairs={{0,16},{16,0},{1,17},{17,1},{2,18},{18,2},{3,19},{19,3},{4,20},{20... | collective-permute-start | bytes 393224 | tf_op jit(solution)/shard_map/ppermute | solution.py:506
  107.7 5.9 %collective-permute-start.21 = (bf16[64,1024]{1,0:T(8,128)(2,1)S(1)}, bf16[64,1024]{1,0:T(8,128)(2,1)S(1)}, u32[]{:S(2)}, u32[]{:S(2)}) collective-permute-start(bf16[64,1024]{1,0:T(8,128)(2,1)S(1)} %get-tuple-element.53), channel_id=1, source_target_pairs={{0,20},{1,21},{2,22},{3,23},{4,28},{5,29},{6,30},{7,31},{8,16},{9,... | collective-permute-start | bytes 393224 | tf_op jit(solution)/shard_map/ppermute | solution.py:508
  108.8 6.5 %collective-permute-start.22 = (bf16[64,1024]{1,0:T(8,128)(2,1)S(1)}, bf16[64,1024]{1,0:T(8,128)(2,1)S(1)}, u32[]{:S(2)}, u32[]{:S(2)}) collective-permute-start(bf16[64,1024]{1,0:T(8,128)(2,1)S(1)} %get-tuple-element.49.after_any), channel_id=1, source_target_pairs={{0,4},{1,5},{2,6},{3,7},{4,12},{5,13},{6,14},{7,15},{8,0},{9,1},{1... | collective-permute-start | bytes 393224 | tf_op jit(solution)/shard_map/ppermute | solution.py:507
  (15 other events, 219.1 us)

commit v10 on v8

--- a/solution.py
+++ b/solution.py
@@ -240,11 +240,11 @@
     other_ref[...] = other.astype(BF16)
 
 
-def last_kernel(base_ref, *refs):
-    total = base_ref[...]
-    for ref in refs[:-1]:
-        total = total + ref[...].astype(F32)
-    refs[-1][...] = total.astype(BF16)
+def last_kernel(base_ref, other_ref, mine_ref, upper_ref, lower_ref, out_ref):
+    middle = upper_ref.shape[0]
+    for rows, ref in ((slice(0, middle), upper_ref), (slice(middle, 2 * middle), lower_ref)):
+        total = base_ref[rows, :] + other_ref[rows, :].astype(F32) + mine_ref[rows, :].astype(F32)
+        out_ref[rows, :] = (total + ref[...].astype(F32)).astype(BF16)
 
 
 def sum_kernel(*refs):
@@ -497,17 +497,20 @@
             sum_kernel, BF16, 0, near_sum, near_side_in, two_in, far_in
         )
         base, own_other = by_columns(own_kernel, F32, 1, near_mine, state, own_sum, side_in)
-        own_over = lax.ppermute(own_other, "grp", plane_swap)
+        middle = row_count // 2
+        own_over = [
+            lax.ppermute(own_other[half : half + middle], "grp", plane_swap) for half in (0, middle)
+        ]
         mine_in = lax.ppermute(near_mine, both_axes, backward)
         other_in = lax.ppermute(near_other, both_axes, crossed(backward))
         return pl.pallas_call(
             last_kernel,
             out_shape=jax.ShapeDtypeStruct(part, BF16),
-            in_specs=[WHOLE] * 4,
+            in_specs=[WHOLE] * 5,
             compiler_params=pltpu.CompilerParams(vmem_limit_bytes=16 * 2**20),
             cost_estimate=cost(0, 2**20),
             name="last",
-        )(base, other_in, mine_in, own_over)
+        )(base, other_in, mine_in, *own_over)
 
     line = [packet]
     for _ in range(1, ring):

time: 108 us -> 107 us (level)
  waiting for transfers between devices: 41.4 us -> 39.4 us
  starting transfers between devices: 33.1 us -> 35 us
    ppermute x1, waiting for transfers between devices: 2.92 us -> 0.01 us  [local(): other_in = lax.ppermute(near_other, both_axes, crossed(backward))]
    ppermute x1 -> x2, waiting for transfers between devices: 0.83 us -> 2.94 us  [local(): lax.ppermute(own_other[half:half + middle], 'grp', plane_swap)]
    ppermute x1, waiting for transfers between devices: 1.13 us -> 0.01 us  [local(): mine_in = lax.ppermute(near_mine, both_axes, backward)]
    ppermute x1, starting transfers between devices: 0.99 us -> 2.08 us  [local(): mine_in = lax.ppermute(near_mine, both_axes, backward)]
    ppermute x1 -> x2, starting transfers between devices: 2.26 us -> 2.09 us  [local(): lax.ppermute(own_other[half:half + middle], 'grp', plane_swap)]
  transfers between devices with their start and end apart: 25 -> 26, of which waited for: 18 -> 17; matrix products, arithmetic and copies ran while one was open for 2% -> 2% of each run, Pallas kernels for 16% -> 16%
where the time goes in v10:
time: 107 us
  waiting for transfers between devices  39.4 us (37%)
  starting transfers between devices  35 us (33%)
  Pallas kernels  26.6 us (25%)
  local copies, waits for them, and re-layouts  5.12 us (5%)
    pallas_call x3, Pallas kernels, run_expert(): pl.pallas_call(functools.partial(expert_kernel, experts), out_shape=[jax....  10.3 us
    all_to_all x1, waiting for transfers between devices, local(): lax.all_to_all(outgoing, 'ep', split_axis=0, concat_axis=0, tiled=True)  8.68 us
    all_to_all x1, starting transfers between devices, local(): lax.all_to_all(outgoing, 'ep', split_axis=0, concat_axis=0, tiled=True)  7.38 us
    ppermute x1, waiting for transfers between devices, local(): near = lax.ppermute(packet, both_axes, onward)  6.73 us
    pallas_call x1, Pallas kernels, local(): pl.pallas_call(functools.partial(moved_kernel, dims), out_shape=jax.Shape...  4.96 us
    ppermute x1, waiting for transfers between devices, local(): two_side_in = lax.ppermute(two_side_sum, 'ep', side_swap)  4.37 us
    unnamed x30, local copies, waits for them, and re-layouts  3.78 us
    ppermute x1, waiting for transfers between devices, local(): side_in = lax.ppermute(side_sum, 'ep', side_swap)  3.62 us
  transfers between devices with their start and end apart: 26, of which 17 were waited for; matrix products, arithmetic and copies ran while one was open for 2% of the time, Pallas kernels for 16%

profile of v10, /device:TPU:0, one launch (start us, length us, event | category | flops | bytes accessed | tf_op | source)
XLA Modules:
  0.0 107.2 jit_solution(5082223622935824158)
XLA Ops:
  0.0 2.8 %pick.1 = bf16[16,16,1152]{2,1,0:T(8,128)(2,1)} custom-call(s32[2,16]{1,0:T(2,128)} %bitcast.22, bf16[64,9216]{1,0:T(8,128)(2,1)} %cache.1), custom_call_target="tpu_custom_call" | custom-call | bytes 4194304 | tf_op jit(solution)/shard_map/pick/pallas_call | solution.py:308
  2.8 7.4 %all-to-all-start = ((bf16[16,16,1152]{2,1,0:T(8,128)(2,1)}), bf16[16,16,1152]{2,1,0:T(8,128)(2,1)S(1)}, u32[]{:S(2)}, u32[]{:S(2)}) async-start(bf16[16,16,1152]{2,1,0:T(8,128)(2,1)} %pick.1), calls=%async_computation | async-start | bytes 1179648 | tf_op jit(solution)/shard_map/all_to_all | solution.py:322
  12.4 2.7 %attend_resident.1 = (bf16[512,640]{1,0:T(8,128)(2,1)S(1)}, f32[512,640]{1,0:T(8,128)S(1)}) custom-call(bf16[64,1024]{1,0:T(8,128)(2,1)S(1)} %copy-done.8, bf16[64,512]{1,0:T(8,128)(2,1)S(1)} %copy-done.10, bf16[16,2304]{1,0:T(8,128)(2,1)S(1)} %copy-done.9, bf16[64,9216]{1,0:T(8,128)(2,1)S(1)} %copy-done.2, bf16[8,128,512]{2,1,0:T(8,128)(2,1)S(1)} %copy-done.7, ...), custom_call_target="tpu_custom_call" | custom-call | flops 1283457024 | bytes 8388608 | tf_op jit(solution)/shard_map/attend_resident/pallas_call | solution.py:347
  17.1 8.7 %all-to-all-done.moved_any = bf16[16,16,1152]{2,1,0:T(8,128)(2,1)S(1)} async-done(((bf16[16,16,1152]{2,1,0:T(8,128)(2,1)}), bf16[16,16,1152]{2,1,0:T(8,128)(2,1)S(1)}, u32[]{:S(2)}, u32[]{:S(2)}) %all-to-all-start) | async-done | bytes 589856 | tf_op jit(solution)/shard_map/all_to_all | solution.py:322
  26.6 5.0 %attend_moved.1.after_any.own_any = bf16[64,2048]{1,0:T(8,128)(2,1)} custom-call(bf16[16,16,1152]{2,1,0:T(8,128)(2,1)} %copy-done.11, bf16[512,640]{1,0:T(8,128)(2,1)} %copy-done.3, f32[64,512]{1,0:T(8,128)} %reshape.110.bias_any, f32[512,640]{1,0:T(8,128)} %copy-done.1, bf16[8,512,128]{2,1,0:T(8,128)(2,1)} %value_any.1, bf16[1024,2048]{1,0:T(8,128)(2,1)} %proj_any.1), custom_call_target="tpu_custom_call" | custom-call | flops 603979776 | bytes 10485760 | tf_op jit(solution)/shard_map/attend_moved/pallas_call | solution.py:358
  31.6 1.6 %collective-permute-start = (bf16[64,2048]{1,0:T(8,128)(2,1)}, bf16[64,2048]{1,0:T(8,128)(2,1)S(1)}, u32[]{:S(2)}, u32[]{:S(2)}) collective-permute-start(bf16[64,2048]{1,0:T(8,128)(2,1)} %attend_moved.1.after_any.own_any), channel_id=1, source_target_pairs={{0,16},{16,0},{1,17},{17,1},{2,18},{18,2},{3,19},{19,3},{4,20},{20... | collective-permute-start | bytes 786440 | tf_op jit(solution)/shard_map/ppermute | solution.py:377
  34.1 3.6 %load.1 = (bf16[704,2048]{1,0:T(8,128)(2,1)S(1)}, bf16[704,2048]{1,0:T(8,128)(2,1)S(1)}, bf16[704,2048]{1,0:T(8,128)(2,1)S(1)}) custom-call(bf16[64,2048]{1,0:T(8,128)(2,1)S(1)} %copy-done, bf16[704,2048]{1,0:T(8,128)(2,1)} %bitcast.18, bf16[704,2048]{1,0:T(8,128)(2,1)} %bitcast.19, bf16[704,2048]{1,0:T(8,128)(2,1)} %bitcast.20), custom_call_target="tpu_custom_call" | custom-call | bytes 12582912 | tf_op jit(solution)/shard_map/load/pallas_call | solution.py:380
  37.7 2.3 %collective-permute-done.refs_0_ = bf16[64,2048]{1,0:T(8,128)(2,1)S(1)} collective-permute-done((bf16[64,2048]{1,0:T(8,128)(2,1)}, bf16[64,2048]{1,0:T(8,128)(2,1)S(1)}, u32[]{:S(2)}, u32[]{:S(2)}) %collective-permute-start) | collective-permute-done | bytes 262176 | tf_op jit(solution)/shard_map/ppermute | solution.py:377
  40.7 2.0 %collective-permute-start.2 = (bf16[64,2176]{1,0:T(8,128)(2,1)S(1)}, bf16[64,2176]{1,0:T(8,128)(2,1)S(1)}, u32[]{:S(2)}, u32[]{:S(2)}) collective-permute-start(bf16[64,2176]{1,0:T(8,128)(2,1)S(1)} %get-tuple-element.33.after_any.refs_0_), channel_id=1, source_target_pairs={{0,8},{1,9},{2,10},{3,11},{4,0},{5,1},{6,2},{7,3},{8,12},{9,13},{1... | collective-permute-start | bytes 835592 | tf_op jit(solution)/shard_map/ppermute | solution.py:456
  42.8 6.7 %collective-permute-done.2.refs_2_ = bf16[64,2176]{1,0:T(8,128)(2,1)S(1)} collective-permute-done((bf16[64,2176]{1,0:T(8,128)(2,1)S(1)}, bf16[64,2176]{1,0:T(8,128)(2,1)S(1)}, u32[]{:S(2)}, u32[]{:S(2)}) %collective-permute-start.2) | collective-permute-done | bytes 278560 | tf_op jit(solution)/shard_map/ppermute | solution.py:456
  49.6 2.3 %collective-permute-start.7 = (bf16[64,2176]{1,0:T(8,128)(2,1)S(1)}, bf16[64,2176]{1,0:T(8,128)(2,1)S(1)}, u32[]{:S(2)}, u32[]{:S(2)}) collective-permute-start(bf16[64,2176]{1,0:T(8,128)(2,1)S(1)} %collective-permute-done.2.refs_2_), channel_id=1, source_target_pairs={{0,8},{1,9},{2,10},{3,11},{4,0},{5,1},{6,2},{7,3},{8,12},{9,13},{1... | collective-permute-start | bytes 835592 | tf_op jit(solution)/shard_map/ppermute | solution.py:458
  53.4 1.5 %collective-permute-start.5 = (bf16[64,2176]{1,0:T(8,128)(2,1)S(1)}, bf16[64,2176]{1,0:T(8,128)(2,1)S(1)}, u32[]{:S(2)}, u32[]{:S(2)}) collective-permute-start(bf16[64,2176]{1,0:T(8,128)(2,1)S(1)} %collective-permute-done.2.refs_2_), channel_id=1, source_target_pairs={{0,16},{16,0},{1,17},{17,1},{2,18},{18,2},{3,19},{19,3},{4,20},{20... | collective-permute-start | bytes 835592 | tf_op jit(solution)/shard_map/ppermute | solution.py:460
  54.9 3.8 %expert.3 = (bf16[192,2048]{1,0:T(8,128)(2,1)S(1)}, bf16[192,2048]{1,0:T(8,128)(2,1)S(1)}) custom-call(bf16[64,2176]{1,0:T(8,128)(2,1)S(1)} %get-tuple-element.33.after_any.refs_0_, bf16[192,2176]{1,0:T(8,128)(2,1)S(1)} %pack.3.here_ref, bf16[192,2176]{1,0:T(8,128)(2,1)S(1)} %collective-permute-done.3.across_ref, ...), custom_call_target="tpu_custom_call" | custom-call | flops 3321888768 | bytes 12582912 | tf_op jit(solution)/shard_map/expert/pallas_call | solution.py:422
  64.1 3.8 %expert.4 = (bf16[192,2048]{1,0:T(8,128)(2,1)S(1)}, bf16[192,2048]{1,0:T(8,128)(2,1)S(1)}) custom-call(bf16[64,2176]{1,0:T(8,128)(2,1)S(1)} %get-tuple-element.33.after_any.refs_0_, bf16[192,2176]{1,0:T(8,128)(2,1)S(1)} %pack.4.here_ref, bf16[192,2176]{1,0:T(8,128)(2,1)S(1)} %collective-permute-done.8.across_ref, ...), custom_call_target="tpu_custom_call" | custom-call | flops 3321888768 | bytes 12582912 | tf_op jit(solution)/shard_map/expert/pallas_call | solution.py:422
  68.0 2.9 %collective-permute-done.11.refs_1_ = bf16[64,2176]{1,0:T(8,128)(2,1)S(1)} collective-permute-done((bf16[64,2176]{1,0:T(8,128)(2,1)S(1)}, bf16[64,2176]{1,0:T(8,128)(2,1)S(1)}, u32[]{:S(2)}, u32[]{:S(2)}) %collective-permute-start.11) | collective-permute-done | bytes 278560 | tf_op jit(solution)/shard_map/ppermute | solution.py:461
  73.5 2.6 %expert.5 = (bf16[128,2048]{1,0:T(8,128)(2,1)S(1)}, bf16[64,2048]{1,0:T(8,128)(2,1)S(1)}, bf16[64,2048]{1,0:T(8,128)(2,1)S(1)}) custom-call(bf16[64,2048]{1,0:T(8,128)(2,1)S(1)} %get-tuple-element.42.after_any, bf16[128,2176]{1,0:T(8,128)(2,1)S(1)} %pack.5.here_ref, bf16[128,2176]{1,0:T(8,128)(2,1)S(1)} %collective-permute-done.12.across_ref, ...), custom_call_target="tpu_custom_call" | custom-call | flops 2214592512 | bytes 12582912 | tf_op jit(solution)/shard_map/expert/pallas_call | solution.py:422
  76.7 3.6 %collective-permute-done.13.refs_0_.side_ref = bf16[64,2048]{1,0:T(8,128)(2,1)S(1)} collective-permute-done((bf16[64,2048]{1,0:T(8,128)(2,1)S(1)}, bf16[64,2048]{1,0:T(8,128)(2,1)S(1)}, u32[]{:S(2)}, u32[]{:S(2)}) %collective-permute-start.13) | collective-permute-done | bytes 262176 | tf_op jit(solution)/shard_map/ppermute | solution.py:466
  83.6 4.4 %collective-permute-done.18.refs_0_ = bf16[64,2048]{1,0:T(8,128)(2,1)S(1)} collective-permute-done((bf16[64,2048]{1,0:T(8,128)(2,1)S(1)}, bf16[64,2048]{1,0:T(8,128)(2,1)S(1)}, u32[]{:S(2)}, u32[]{:S(2)}) %collective-permute-start.18) | collective-permute-done | bytes 262176 | tf_op jit(solution)/shard_map/ppermute | solution.py:471
  90.7 2.1 %collective-permute-start.20 = (bf16[64,2048]{1,0:T(8,128)(2,1)S(1)}, bf16[64,2048]{1,0:T(8,128)(2,1)S(1)}, u32[]{:S(2)}, u32[]{:S(2)}) collective-permute-start(bf16[64,2048]{1,0:T(8,128)(2,1)S(1)} %join.11), channel_id=1, source_target_pairs={{0,16},{16,0},{1,17},{17,1},{2,18},{18,2},{3,19},{19,3},{4,20},{20... | collective-permute-start | bytes 786440 | tf_op jit(solution)/shard_map/ppermute | solution.py:475
  92.7 2.8 %collective-permute-done.19.refs_2_ = bf16[64,2048]{1,0:T(8,128)(2,1)S(1)} collective-permute-done((bf16[64,2048]{1,0:T(8,128)(2,1)S(1)}, bf16[64,2048]{1,0:T(8,128)(2,1)S(1)}, u32[]{:S(2)}, u32[]{:S(2)}) %collective-permute-start.19) | collective-permute-done | bytes 262176 | tf_op jit(solution)/shard_map/ppermute | solution.py:477
  97.2 2.1 %collective-permute-start.21 = (bf16[64,1024]{1,0:T(8,128)(2,1)S(1)}, bf16[64,1024]{1,0:T(8,128)(2,1)S(1)}, u32[]{:S(2)}, u32[]{:S(2)}) collective-permute-start(bf16[64,1024]{1,0:T(8,128)(2,1)S(1)} %get-tuple-element.53), channel_id=1, source_target_pairs={{0,20},{1,21},{2,22},{3,23},{4,28},{5,29},{6,30},{7,31},{8,16},{9,... | collective-permute-start | bytes 393224 | tf_op jit(solution)/shard_map/ppermute | solution.py:505
  99.3 2.1 %collective-permute-start.22 = (bf16[64,1024]{1,0:T(8,128)(2,1)S(1)}, bf16[64,1024]{1,0:T(8,128)(2,1)S(1)}, u32[]{:S(2)}, u32[]{:S(2)}) collective-permute-start(bf16[64,1024]{1,0:T(8,128)(2,1)S(1)} %get-tuple-element.49.after_any), channel_id=1, source_target_pairs={{0,4},{1,5},{2,6},{3,7},{4,12},{5,13},{6,14},{7,15},{8,0},{9,1},{1... | collective-permute-start | bytes 393224 | tf_op jit(solution)/shard_map/ppermute | solution.py:504
  101.6 2.0 %collective-permute-start.23 = (bf16[32,1024]{1,0:T(8,128)(2,1)S(1)}, bf16[32,1024]{1,0:T(8,128)(2,1)S(1)}, u32[]{:S(2)}, u32[]{:S(2)}) collective-permute-start(bf16[32,1024]{1,0:T(8,128)(2,1)S(1)} %get-tuple-element.56), channel_id=1, source_target_pairs={{0,16},{16,0},{1,17},{17,1},{2,18},{18,2},{3,19},{19,3},{4,20},{20... | collective-permute-start | bytes 196616 | tf_op jit(solution)/shard_map/ppermute | solution.py:502
  103.6 2.2 %collective-permute-done.24.lower_ref = bf16[32,1024]{1,0:T(8,128)(2,1)S(1)} collective-permute-done((bf16[32,1024]{1,0:T(8,128)(2,1)S(1)}, bf16[32,1024]{1,0:T(8,128)(2,1)S(1)}, u32[]{:S(2)}, u32[]{:S(2)}) %collective-permute-start.24) | collective-permute-done | bytes 65568 | tf_op jit(solution)/shard_map/ppermute | solution.py:502
  (103 shorter events, 25.9 us)
Async XLA Ops:
  2.8 22.9 %all-to-all-start = ((bf16[16,16,1152]{2,1,0:T(8,128)(2,1)}), bf16[16,16,1152]{2,1,0:T(8,128)(2,1)S(1)}, u32[]{:S(2)}, u32[]{:S(2)}) async-start(bf16[16,16,1152]{2,1,0:T(8,128)(2,1)} %pick.1), calls=%async_computation | async-start | bytes 1179648 | tf_op jit(solution)/shard_map/all_to_all | solution.py:322
  31.6 8.5 %collective-permute-start = (bf16[64,2048]{1,0:T(8,128)(2,1)}, bf16[64,2048]{1,0:T(8,128)(2,1)S(1)}, u32[]{:S(2)}, u32[]{:S(2)}) collective-permute-start(bf16[64,2048]{1,0:T(8,128)(2,1)} %attend_moved.1.after_any.own_any), channel_id=1, source_target_pairs={{0,16},{16,0},{1,17},{17,1},{2,18},{18,2},{3,19},{19,3},{4,20},{20... | collective-permute-start | bytes 786440 | tf_op jit(solution)/shard_map/ppermute | solution.py:377
  40.7 8.7 %collective-permute-start.2 = (bf16[64,2176]{1,0:T(8,128)(2,1)S(1)}, bf16[64,2176]{1,0:T(8,128)(2,1)S(1)}, u32[]{:S(2)}, u32[]{:S(2)}) collective-permute-start(bf16[64,2176]{1,0:T(8,128)(2,1)S(1)} %get-tuple-element.33.after_any.refs_0_), channel_id=1, source_target_pairs={{0,8},{1,9},{2,10},{3,11},{4,0},{5,1},{6,2},{7,3},{8,12},{9,13},{1... | collective-permute-start | bytes 835592 | tf_op jit(solution)/shard_map/ppermute | solution.py:456
  42.8 6.7 %collective-permute-start.1 = (bf16[64,2176]{1,0:T(8,128)(2,1)S(1)}, bf16[64,2176]{1,0:T(8,128)(2,1)S(1)}, u32[]{:S(2)}, u32[]{:S(2)}) collective-permute-start(bf16[64,2176]{1,0:T(8,128)(2,1)S(1)} %get-tuple-element.33.after_any.refs_0_), channel_id=1, source_target_pairs={{0,2},{1,3},{2,0},{3,1},{4,6},{5,7},{6,4},{7,5},{8,10},{9,11},{10,... | collective-permute-start | bytes 835592 | tf_op jit(solution)/shard_map/ppermute | solution.py:457
  49.6 5.4 %collective-permute-start.3 = (bf16[192,2176]{1,0:T(8,128)(2,1)S(1)}, bf16[192,2176]{1,0:T(8,128)(2,1)S(1)}, u32[]{:S(2)}, u32[]{:S(2)}) collective-permute-start(bf16[192,2176]{1,0:T(8,128)(2,1)S(1)} %pack.3.here_ref), channel_id=1, source_target_pairs={{0,1},{1,0},{2,3},{3,2},{4,5},{5,4},{6,7},{7,6},{8,9},{9,8},{10,11... | collective-permute-start | bytes 2506760 | tf_op jit(solution)/shard_map/ppermute | solution.py:421
  49.6 9.9 %collective-permute-start.7 = (bf16[64,2176]{1,0:T(8,128)(2,1)S(1)}, bf16[64,2176]{1,0:T(8,128)(2,1)S(1)}, u32[]{:S(2)}, u32[]{:S(2)}) collective-permute-start(bf16[64,2176]{1,0:T(8,128)(2,1)S(1)} %collective-permute-done.2.refs_2_), channel_id=1, source_target_pairs={{0,8},{1,9},{2,10},{3,11},{4,0},{5,1},{6,2},{7,3},{8,12},{9,13},{1... | collective-permute-start | bytes 835592 | tf_op jit(solution)/shard_map/ppermute | solution.py:458
  52.0 8.5 %collective-permute-start.6 = (bf16[64,2176]{1,0:T(8,128)(2,1)S(1)}, bf16[64,2176]{1,0:T(8,128)(2,1)S(1)}, u32[]{:S(2)}, u32[]{:S(2)}) collective-permute-start(bf16[64,2176]{1,0:T(8,128)(2,1)S(1)} %collective-permute-done.2.refs_2_), channel_id=1, source_target_pairs={{0,2},{1,3},{2,0},{3,1},{4,6},{5,7},{6,4},{7,5},{8,10},{9,11},{10,... | collective-permute-start | bytes 835592 | tf_op jit(solution)/shard_map/ppermute | solution.py:459
  53.4 8.3 %collective-permute-start.5 = (bf16[64,2176]{1,0:T(8,128)(2,1)S(1)}, bf16[64,2176]{1,0:T(8,128)(2,1)S(1)}, u32[]{:S(2)}, u32[]{:S(2)}) collective-permute-start(bf16[64,2176]{1,0:T(8,128)(2,1)S(1)} %collective-permute-done.2.refs_2_), channel_id=1, source_target_pairs={{0,16},{16,0},{1,17},{17,1},{2,18},{18,2},{3,19},{19,3},{4,20},{20... | collective-permute-start | bytes 835592 | tf_op jit(solution)/shard_map/ppermute | solution.py:460
  61.8 9.1 %collective-permute-start.11 = (bf16[64,2176]{1,0:T(8,128)(2,1)S(1)}, bf16[64,2176]{1,0:T(8,128)(2,1)S(1)}, u32[]{:S(2)}, u32[]{:S(2)}) collective-permute-start(bf16[64,2176]{1,0:T(8,128)(2,1)S(1)} %collective-permute-done.7.refs_2_), channel_id=1, source_target_pairs={{0,2},{1,3},{2,0},{3,1},{4,6},{5,7},{6,4},{7,5},{8,10},{9,11},{10,... | collective-permute-start | bytes 835592 | tf_op jit(solution)/shard_map/ppermute | solution.py:461
  62.5 8.7 %collective-permute-start.10 = (bf16[64,2176]{1,0:T(8,128)(2,1)S(1)}, bf16[64,2176]{1,0:T(8,128)(2,1)S(1)}, u32[]{:S(2)}, u32[]{:S(2)}) collective-permute-start(bf16[64,2176]{1,0:T(8,128)(2,1)S(1)} %collective-permute-done.6.refs_1_), channel_id=1, source_target_pairs={{0,16},{16,0},{1,17},{17,1},{2,18},{18,2},{3,19},{19,3},{4,20},{20... | collective-permute-start | bytes 835592 | tf_op jit(solution)/shard_map/ppermute | solution.py:462
  64.0 7.8 %collective-permute-start.4 = (bf16[192,2048]{1,0:T(8,128)(2,1)S(1)}, bf16[192,2048]{1,0:T(8,128)(2,1)S(1)}, u32[]{:S(2)}, u32[]{:S(2)}) collective-permute-start(bf16[192,2048]{1,0:T(8,128)(2,1)S(1)} %get-tuple-element.37), channel_id=1, source_target_pairs={{0,1},{1,0},{2,3},{3,2},{4,5},{5,4},{6,7},{7,6},{8,9},{9,8},{10,11... | collective-permute-start | bytes 2359304 | tf_op jit(solution)/shard_map/ppermute | solution.py:432
  71.3 12.2 %collective-permute-start.9 = (bf16[192,2048]{1,0:T(8,128)(2,1)S(1)}, bf16[192,2048]{1,0:T(8,128)(2,1)S(1)}, u32[]{:S(2)}, u32[]{:S(2)}) collective-permute-start(bf16[192,2048]{1,0:T(8,128)(2,1)S(1)} %get-tuple-element.40), channel_id=1, source_target_pairs={{0,1},{1,0},{2,3},{3,2},{4,5},{5,4},{6,7},{7,6},{8,9},{9,8},{10,11... | collective-permute-start | bytes 2359304 | tf_op jit(solution)/shard_map/ppermute | solution.py:432
  72.0 8.4 %collective-permute-start.13 = (bf16[64,2048]{1,0:T(8,128)(2,1)S(1)}, bf16[64,2048]{1,0:T(8,128)(2,1)S(1)}, u32[]{:S(2)}, u32[]{:S(2)}) collective-permute-start(bf16[64,2048]{1,0:T(8,128)(2,1)S(1)} %get-tuple-element.42.after_any), channel_id=1, source_target_pairs={{0,2},{1,3},{2,0},{3,1},{4,6},{5,7},{6,4},{7,5},{8,10},{9,11},{10,... | collective-permute-start | bytes 786440 | tf_op jit(solution)/shard_map/ppermute | solution.py:466
  76.1 4.2 %collective-permute-start.14 = (bf16[64,2048]{1,0:T(8,128)(2,1)S(1)}, bf16[64,2048]{1,0:T(8,128)(2,1)S(1)}, u32[]{:S(2)}, u32[]{:S(2)}) collective-permute-start(bf16[64,2048]{1,0:T(8,128)(2,1)S(1)} %get-tuple-element.44), channel_id=1, source_target_pairs={{0,1},{1,0},{2,3},{3,2},{4,5},{5,4},{6,7},{7,6},{8,9},{9,8},{10,11... | collective-permute-start | bytes 786440 | tf_op jit(solution)/shard_map/ppermute | solution.py:432
  76.2 4.1 %collective-permute-start.15 = (bf16[64,2048]{1,0:T(8,128)(2,1)S(1)}, bf16[64,2048]{1,0:T(8,128)(2,1)S(1)}, u32[]{:S(2)}, u32[]{:S(2)}) collective-permute-start(bf16[64,2048]{1,0:T(8,128)(2,1)S(1)} %get-tuple-element.45), channel_id=1, source_target_pairs={{0,1},{1,0},{2,3},{3,2},{4,5},{5,4},{6,7},{7,6},{8,9},{9,8},{10,11... | collective-permute-start | bytes 786440 | tf_op jit(solution)/shard_map/ppermute | solution.py:432
  80.5 7.5 %collective-permute-start.18 = (bf16[64,2048]{1,0:T(8,128)(2,1)S(1)}, bf16[64,2048]{1,0:T(8,128)(2,1)S(1)}, u32[]{:S(2)}, u32[]{:S(2)}) collective-permute-start(bf16[64,2048]{1,0:T(8,128)(2,1)S(1)} %get-tuple-element.48), channel_id=1, source_target_pairs={{0,2},{1,3},{2,0},{3,1},{4,6},{5,7},{6,4},{7,5},{8,10},{9,11},{10,... | collective-permute-start | bytes 786440 | tf_op jit(solution)/shard_map/ppermute | solution.py:471
  82.0 7.2 %collective-permute-start.16 = (bf16[64,2048]{1,0:T(8,128)(2,1)S(1)}, bf16[64,2048]{1,0:T(8,128)(2,1)S(1)}, u32[]{:S(2)}, u32[]{:S(2)}) collective-permute-start(bf16[64,2048]{1,0:T(8,128)(2,1)S(1)} %get-tuple-element.46), channel_id=1, source_target_pairs={{0,16},{16,0},{1,17},{17,1},{2,18},{18,2},{3,19},{19,3},{4,20},{20... | collective-permute-start | bytes 786440 | tf_op jit(solution)/shard_map/ppermute | solution.py:470
  88.0 7.5 %collective-permute-start.19 = (bf16[64,2048]{1,0:T(8,128)(2,1)S(1)}, bf16[64,2048]{1,0:T(8,128)(2,1)S(1)}, u32[]{:S(2)}, u32[]{:S(2)}) collective-permute-start(bf16[64,2048]{1,0:T(8,128)(2,1)S(1)} %join.10), channel_id=1, source_target_pairs={{0,4},{1,5},{2,6},{3,7},{4,12},{5,13},{6,14},{7,15},{8,0},{9,1},{1... | collective-permute-start | bytes 786440 | tf_op jit(solution)/shard_map/ppermute | solution.py:477
  89.2 6.4 %collective-permute-start.17 = (bf16[64,2048]{1,0:T(8,128)(2,1)S(1)}, bf16[64,2048]{1,0:T(8,128)(2,1)S(1)}, u32[]{:S(2)}, u32[]{:S(2)}) collective-permute-start(bf16[64,2048]{1,0:T(8,128)(2,1)S(1)} %join.9), channel_id=1, source_target_pairs={{0,2},{1,3},{2,0},{3,1},{4,6},{5,7},{6,4},{7,5},{8,10},{9,11},{10,... | collective-permute-start | bytes 786440 | tf_op jit(solution)/shard_map/ppermute | solution.py:476
  90.7 6.4 %collective-permute-start.20 = (bf16[64,2048]{1,0:T(8,128)(2,1)S(1)}, bf16[64,2048]{1,0:T(8,128)(2,1)S(1)}, u32[]{:S(2)}, u32[]{:S(2)}) collective-permute-start(bf16[64,2048]{1,0:T(8,128)(2,1)S(1)} %join.11), channel_id=1, source_target_pairs={{0,16},{16,0},{1,17},{17,1},{2,18},{18,2},{3,19},{19,3},{4,20},{20... | collective-permute-start | bytes 786440 | tf_op jit(solution)/shard_map/ppermute | solution.py:475
  97.2 9.3 %collective-permute-start.21 = (bf16[64,1024]{1,0:T(8,128)(2,1)S(1)}, bf16[64,1024]{1,0:T(8,128)(2,1)S(1)}, u32[]{:S(2)}, u32[]{:S(2)}) collective-permute-start(bf16[64,1024]{1,0:T(8,128)(2,1)S(1)} %get-tuple-element.53), channel_id=1, source_target_pairs={{0,20},{1,21},{2,22},{3,23},{4,28},{5,29},{6,30},{7,31},{8,16},{9,... | collective-permute-start | bytes 393224 | tf_op jit(solution)/shard_map/ppermute | solution.py:505
  99.3 7.2 %collective-permute-start.22 = (bf16[64,1024]{1,0:T(8,128)(2,1)S(1)}, bf16[64,1024]{1,0:T(8,128)(2,1)S(1)}, u32[]{:S(2)}, u32[]{:S(2)}) collective-permute-start(bf16[64,1024]{1,0:T(8,128)(2,1)S(1)} %get-tuple-element.49.after_any), channel_id=1, source_target_pairs={{0,4},{1,5},{2,6},{3,7},{4,12},{5,13},{6,14},{7,15},{8,0},{9,1},{1... | collective-permute-start | bytes 393224 | tf_op jit(solution)/shard_map/ppermute | solution.py:504
  101.5 4.3 %collective-permute-start.24 = (bf16[32,1024]{1,0:T(8,128)(2,1)S(1)}, bf16[32,1024]{1,0:T(8,128)(2,1)S(1)}, u32[]{:S(2)}, u32[]{:S(2)}) collective-permute-start(bf16[32,1024]{1,0:T(8,128)(2,1)S(1)} %get-tuple-element.55), channel_id=1, source_target_pairs={{0,16},{16,0},{1,17},{17,1},{2,18},{18,2},{3,19},{19,3},{4,20},{20... | collective-permute-start | bytes 196616 | tf_op jit(solution)/shard_map/ppermute | solution.py:502
  101.6 4.9 %collective-permute-start.23 = (bf16[32,1024]{1,0:T(8,128)(2,1)S(1)}, bf16[32,1024]{1,0:T(8,128)(2,1)S(1)}, u32[]{:S(2)}, u32[]{:S(2)}) collective-permute-start(bf16[32,1024]{1,0:T(8,128)(2,1)S(1)} %get-tuple-element.56), channel_id=1, source_target_pairs={{0,16},{16,0},{1,17},{17,1},{2,18},{18,2},{3,19},{19,3},{4,20},{20... | collective-permute-start | bytes 196616 | tf_op jit(solution)/shard_map/ppermute | solution.py:502
  (17 other events, 115.3 us)

commit v11 on v10

--- a/solution.py
+++ b/solution.py
@@ -102,28 +102,27 @@
 
 
 def moved_kernel(
-    dims, moved_any, query_any, bias_any, mixed_any, value_any, proj_any,
+    dims, moved, query_any, bias_any, mixed_any, value_any, proj_any,
     share_ref,
-    moved, query, bias, mixed, value, proj, keys, heads_out, sems,
+    query, bias, mixed, value, proj, keys, heads_out, sems,
 ):
     head_count, nope_dim, latent, rope, block_size, steps = dims
     width = latent + rope
     rows = heads_out.shape[0]
     got = fetch_all(
-        (moved_any, query_any, bias_any, mixed_any, value_any, proj_any),
-        (moved, query, bias, mixed, value, proj),
+        (query_any, bias_any, mixed_any, value_any, proj_any),
+        (query, bias, mixed, value, proj),
         sems,
     )
     keys[:, latent:] = jnp.zeros((keys.shape[0], keys.shape[1] - latent), BF16)
     scale = (nope_dim + rope) ** (-0.5)
     value_dim = value.shape[2]
-    got[0].wait()
     count = moved.shape[0] * moved.shape[1]
     for half in range(2):
         part = moved[:, :, half * width : (half + 1) * width]
         keys[half * count : (half + 1) * count, :width] = part.reshape(count, width)
+    got[0].wait()
     got[1].wait()
-    got[2].wait()
     group = min(4, head_count)
     for first in range(0, head_count, group):
         at = slice(first * rows, (first + group) * rows)
@@ -131,7 +130,7 @@
         score = score.reshape(group, rows, -1) * scale + bias[...][None]
         score = score.reshape(group * rows, -1)
         if first == 0:
-            got[3].wait()
+            got[2].wait()
         before = mixed[at, latent : latent + 1]
         peak = jnp.maximum(jnp.max(score, axis=1, keepdims=True), before)
         weight = jnp.exp(score - peak)
@@ -140,11 +139,11 @@
         joined = dot(weight.astype(BF16), keys[:, :latent]) + mixed[at, :latent] * keep
         joined = (joined / total).astype(BF16)
         if first == 0:
-            got[4].wait()
+            got[3].wait()
         for head in range(first, first + group):
             own = joined[(head - first) * rows : (head - first + 1) * rows]
             heads_out[:, head * value_dim : (head + 1) * value_dim] = dot(own, value[head]).astype(BF16)
-    got[5].wait()
+    got[4].wait()
     share_ref[...] = dot(heads_out[...], proj[...]).astype(BF16)
 
 
@@ -358,9 +357,8 @@
     share = pl.pallas_call(
         functools.partial(moved_kernel, dims),
         out_shape=jax.ShapeDtypeStruct((row_count, model), BF16),
-        in_specs=[ANY] * 6,
+        in_specs=[WHOLE] + [ANY] * 5,
         scratch_shapes=[
-            VMEM(arrived.shape, BF16),
             VMEM(query.shape, BF16),
             VMEM(moved_bias.shape, F32),
             VMEM(mixed.shape, F32),
@@ -368,7 +366,7 @@
             VMEM(output_proj.shape, BF16),
             VMEM((moved_bias.shape[1], padded), BF16),
             VMEM((row_count, head_count * value_absorb.shape[2]), BF16),
-            pltpu.SemaphoreType.DMA((6,)),
+            pltpu.SemaphoreType.DMA((5,)),
         ],
         compiler_params=pltpu.CompilerParams(vmem_limit_bytes=56 * 2**20),
         cost_estimate=cost(query_rows * moved_bias.shape[1] * (padded + latent), 10 * 2**20),

time: 107 us -> 108 us (level)
  no operation moved by 1% of the time
where the time goes in v11:
time: 108 us
  waiting for transfers between devices  39.5 us (37%)
  starting transfers between devices  34.9 us (32%)
  Pallas kernels  27.6 us (26%)
  local copies, waits for them, and re-layouts  5.12 us (5%)
    pallas_call x3, Pallas kernels, run_expert(): pl.pallas_call(functools.partial(expert_kernel, experts), out_shape=[jax....  10.3 us
    all_to_all x1, waiting for transfers between devices, local(): lax.all_to_all(outgoing, 'ep', split_axis=0, concat_axis=0, tiled=True)  8.68 us
    all_to_all x1, starting transfers between devices, local(): lax.all_to_all(outgoing, 'ep', split_axis=0, concat_axis=0, tiled=True)  7.38 us
    ppermute x1, waiting for transfers between devices, local(): near = lax.ppermute(packet, both_axes, onward)  6.73 us
    pallas_call x1, Pallas kernels, local(): pl.pallas_call(functools.partial(moved_kernel, dims), out_shape=jax.Shape...  5.89 us
    ppermute x1, waiting for transfers between devices, local(): two_side_in = lax.ppermute(two_side_sum, 'ep', side_swap)  4.4 us
    unnamed x30, local copies, waits for them, and re-layouts  3.78 us
    ppermute x1, waiting for transfers between devices, local(): side_in = lax.ppermute(side_sum, 'ep', side_swap)  3.61 us
  transfers between devices with their start and end apart: 26, of which 17 were waited for; matrix products, arithmetic and copies ran while one was open for 2% of the time, Pallas kernels for 16%

profile of v11, /device:TPU:0, one launch (start us, length us, event | category | flops | bytes accessed | tf_op | source)
XLA Modules:
  0.0 108.1 jit_solution(461493083802048930)
XLA Ops:
  0.0 2.8 %pick.1 = bf16[16,16,1152]{2,1,0:T(8,128)(2,1)} custom-call(s32[2,16]{1,0:T(2,128)} %bitcast.22, bf16[64,9216]{1,0:T(8,128)(2,1)} %cache.1), custom_call_target="tpu_custom_call" | custom-call | bytes 4194304 | tf_op jit(solution)/shard_map/pick/pallas_call | solution.py:307
  2.8 7.4 %all-to-all-start = ((bf16[16,16,1152]{2,1,0:T(8,128)(2,1)}), bf16[16,16,1152]{2,1,0:T(8,128)(2,1)S(1)}, u32[]{:S(2)}, u32[]{:S(2)}) async-start(bf16[16,16,1152]{2,1,0:T(8,128)(2,1)} %pick.1), calls=%async_computation | async-start | bytes 1179648 | tf_op jit(solution)/shard_map/all_to_all | solution.py:321
  12.4 2.7 %attend_resident.1 = (bf16[512,640]{1,0:T(8,128)(2,1)S(1)}, f32[512,640]{1,0:T(8,128)S(1)}) custom-call(bf16[64,1024]{1,0:T(8,128)(2,1)S(1)} %copy-done.8, bf16[64,512]{1,0:T(8,128)(2,1)S(1)} %copy-done.10, bf16[16,2304]{1,0:T(8,128)(2,1)S(1)} %copy-done.9, bf16[64,9216]{1,0:T(8,128)(2,1)S(1)} %copy-done.2, bf16[8,128,512]{2,1,0:T(8,128)(2,1)S(1)} %copy-done.7, ...), custom_call_target="tpu_custom_call" | custom-call | flops 1283457024 | bytes 8388608 | tf_op jit(solution)/shard_map/attend_resident/pallas_call | solution.py:346
  17.1 8.7 %all-to-all-done.moved = bf16[16,16,1152]{2,1,0:T(8,128)(2,1)S(1)} async-done(((bf16[16,16,1152]{2,1,0:T(8,128)(2,1)}), bf16[16,16,1152]{2,1,0:T(8,128)(2,1)S(1)}, u32[]{:S(2)}, u32[]{:S(2)}) %all-to-all-start) | async-done | bytes 589856 | tf_op jit(solution)/shard_map/all_to_all | solution.py:321
  26.6 5.9 %attend_moved.1.after_any.own_any = bf16[64,2048]{1,0:T(8,128)(2,1)} custom-call(bf16[16,16,1152]{2,1,0:T(8,128)(2,1)} %copy-done.11, bf16[512,640]{1,0:T(8,128)(2,1)} %copy-done.3, f32[64,512]{1,0:T(8,128)} %reshape.110.bias_any, f32[512,640]{1,0:T(8,128)} %copy-done.1, bf16[8,512,128]{2,1,0:T(8,128)(2,1)} %value_any.1, bf16[1024,2048]{1,0:T(8,128)(2,1)} %proj_any.1), custom_call_target="tpu_custom_call" | custom-call | flops 603979776 | bytes 10485760 | tf_op jit(solution)/shard_map/attend_moved/pallas_call | solution.py:357
  32.5 1.6 %collective-permute-start = (bf16[64,2048]{1,0:T(8,128)(2,1)}, bf16[64,2048]{1,0:T(8,128)(2,1)S(1)}, u32[]{:S(2)}, u32[]{:S(2)}) collective-permute-start(bf16[64,2048]{1,0:T(8,128)(2,1)} %attend_moved.1.after_any.own_any), channel_id=1, source_target_pairs={{0,16},{16,0},{1,17},{17,1},{2,18},{18,2},{3,19},{19,3},{4,20},{20... | collective-permute-start | bytes 786440 | tf_op jit(solution)/shard_map/ppermute | solution.py:375
  35.0 3.6 %load.1 = (bf16[704,2048]{1,0:T(8,128)(2,1)S(1)}, bf16[704,2048]{1,0:T(8,128)(2,1)S(1)}, bf16[704,2048]{1,0:T(8,128)(2,1)S(1)}) custom-call(bf16[64,2048]{1,0:T(8,128)(2,1)S(1)} %copy-done, bf16[704,2048]{1,0:T(8,128)(2,1)} %bitcast.18, bf16[704,2048]{1,0:T(8,128)(2,1)} %bitcast.19, bf16[704,2048]{1,0:T(8,128)(2,1)} %bitcast.20), custom_call_target="tpu_custom_call" | custom-call | bytes 12582912 | tf_op jit(solution)/shard_map/load/pallas_call | solution.py:378
  38.7 2.3 %collective-permute-done.refs_0_ = bf16[64,2048]{1,0:T(8,128)(2,1)S(1)} collective-permute-done((bf16[64,2048]{1,0:T(8,128)(2,1)}, bf16[64,2048]{1,0:T(8,128)(2,1)S(1)}, u32[]{:S(2)}, u32[]{:S(2)}) %collective-permute-start) | collective-permute-done | bytes 262176 | tf_op jit(solution)/shard_map/ppermute | solution.py:375
  41.7 2.0 %collective-permute-start.2 = (bf16[64,2176]{1,0:T(8,128)(2,1)S(1)}, bf16[64,2176]{1,0:T(8,128)(2,1)S(1)}, u32[]{:S(2)}, u32[]{:S(2)}) collective-permute-start(bf16[64,2176]{1,0:T(8,128)(2,1)S(1)} %get-tuple-element.33.after_any.refs_0_), channel_id=1, source_target_pairs={{0,8},{1,9},{2,10},{3,11},{4,0},{5,1},{6,2},{7,3},{8,12},{9,13},{1... | collective-permute-start | bytes 835592 | tf_op jit(solution)/shard_map/ppermute | solution.py:454
  43.7 6.7 %collective-permute-done.2.refs_2_ = bf16[64,2176]{1,0:T(8,128)(2,1)S(1)} collective-permute-done((bf16[64,2176]{1,0:T(8,128)(2,1)S(1)}, bf16[64,2176]{1,0:T(8,128)(2,1)S(1)}, u32[]{:S(2)}, u32[]{:S(2)}) %collective-permute-start.2) | collective-permute-done | bytes 278560 | tf_op jit(solution)/shard_map/ppermute | solution.py:454
  50.6 2.3 %collective-permute-start.7 = (bf16[64,2176]{1,0:T(8,128)(2,1)S(1)}, bf16[64,2176]{1,0:T(8,128)(2,1)S(1)}, u32[]{:S(2)}, u32[]{:S(2)}) collective-permute-start(bf16[64,2176]{1,0:T(8,128)(2,1)S(1)} %collective-permute-done.2.refs_2_), channel_id=1, source_target_pairs={{0,8},{1,9},{2,10},{3,11},{4,0},{5,1},{6,2},{7,3},{8,12},{9,13},{1... | collective-permute-start | bytes 835592 | tf_op jit(solution)/shard_map/ppermute | solution.py:456
  55.8 3.9 %expert.3 = (bf16[192,2048]{1,0:T(8,128)(2,1)S(1)}, bf16[192,2048]{1,0:T(8,128)(2,1)S(1)}) custom-call(bf16[64,2176]{1,0:T(8,128)(2,1)S(1)} %get-tuple-element.33.after_any.refs_0_, bf16[192,2176]{1,0:T(8,128)(2,1)S(1)} %pack.3.here_ref, bf16[192,2176]{1,0:T(8,128)(2,1)S(1)} %collective-permute-done.3.across_ref, ...), custom_call_target="tpu_custom_call" | custom-call | flops 3321888768 | bytes 12582912 | tf_op jit(solution)/shard_map/expert/pallas_call | solution.py:420
  63.4 1.5 %collective-permute-start.10 = (bf16[64,2176]{1,0:T(8,128)(2,1)S(1)}, bf16[64,2176]{1,0:T(8,128)(2,1)S(1)}, u32[]{:S(2)}, u32[]{:S(2)}) collective-permute-start(bf16[64,2176]{1,0:T(8,128)(2,1)S(1)} %collective-permute-done.6.refs_1_), channel_id=1, source_target_pairs={{0,16},{16,0},{1,17},{17,1},{2,18},{18,2},{3,19},{19,3},{4,20},{20... | collective-permute-start | bytes 835592 | tf_op jit(solution)/shard_map/ppermute | solution.py:460
  65.1 3.8 %expert.4 = (bf16[192,2048]{1,0:T(8,128)(2,1)S(1)}, bf16[192,2048]{1,0:T(8,128)(2,1)S(1)}) custom-call(bf16[64,2176]{1,0:T(8,128)(2,1)S(1)} %get-tuple-element.33.after_any.refs_0_, bf16[192,2176]{1,0:T(8,128)(2,1)S(1)} %pack.4.here_ref, bf16[192,2176]{1,0:T(8,128)(2,1)S(1)} %collective-permute-done.8.across_ref, ...), custom_call_target="tpu_custom_call" | custom-call | flops 3321888768 | bytes 12582912 | tf_op jit(solution)/shard_map/expert/pallas_call | solution.py:420
  68.9 2.9 %collective-permute-done.11.refs_1_ = bf16[64,2176]{1,0:T(8,128)(2,1)S(1)} collective-permute-done((bf16[64,2176]{1,0:T(8,128)(2,1)S(1)}, bf16[64,2176]{1,0:T(8,128)(2,1)S(1)}, u32[]{:S(2)}, u32[]{:S(2)}) %collective-permute-start.11) | collective-permute-done | bytes 278560 | tf_op jit(solution)/shard_map/ppermute | solution.py:459
  74.4 2.6 %expert.5 = (bf16[128,2048]{1,0:T(8,128)(2,1)S(1)}, bf16[64,2048]{1,0:T(8,128)(2,1)S(1)}, bf16[64,2048]{1,0:T(8,128)(2,1)S(1)}) custom-call(bf16[64,2048]{1,0:T(8,128)(2,1)S(1)} %get-tuple-element.42.after_any, bf16[128,2176]{1,0:T(8,128)(2,1)S(1)} %pack.5.here_ref, bf16[128,2176]{1,0:T(8,128)(2,1)S(1)} %collective-permute-done.12.across_ref, ...), custom_call_target="tpu_custom_call" | custom-call | flops 2214592512 | bytes 12582912 | tf_op jit(solution)/shard_map/expert/pallas_call | solution.py:420
  77.6 3.6 %collective-permute-done.13.refs_0_.side_ref = bf16[64,2048]{1,0:T(8,128)(2,1)S(1)} collective-permute-done((bf16[64,2048]{1,0:T(8,128)(2,1)S(1)}, bf16[64,2048]{1,0:T(8,128)(2,1)S(1)}, u32[]{:S(2)}, u32[]{:S(2)}) %collective-permute-start.13) | collective-permute-done | bytes 262176 | tf_op jit(solution)/shard_map/ppermute | solution.py:464
  84.5 4.4 %collective-permute-done.18.refs_0_ = bf16[64,2048]{1,0:T(8,128)(2,1)S(1)} collective-permute-done((bf16[64,2048]{1,0:T(8,128)(2,1)S(1)}, bf16[64,2048]{1,0:T(8,128)(2,1)S(1)}, u32[]{:S(2)}, u32[]{:S(2)}) %collective-permute-start.18) | collective-permute-done | bytes 262176 | tf_op jit(solution)/shard_map/ppermute | solution.py:469
  91.6 2.1 %collective-permute-start.20 = (bf16[64,2048]{1,0:T(8,128)(2,1)S(1)}, bf16[64,2048]{1,0:T(8,128)(2,1)S(1)}, u32[]{:S(2)}, u32[]{:S(2)}) collective-permute-start(bf16[64,2048]{1,0:T(8,128)(2,1)S(1)} %join.11), channel_id=1, source_target_pairs={{0,16},{16,0},{1,17},{17,1},{2,18},{18,2},{3,19},{19,3},{4,20},{20... | collective-permute-start | bytes 786440 | tf_op jit(solution)/shard_map/ppermute | solution.py:473
  93.7 2.7 %collective-permute-done.19.refs_2_ = bf16[64,2048]{1,0:T(8,128)(2,1)S(1)} collective-permute-done((bf16[64,2048]{1,0:T(8,128)(2,1)S(1)}, bf16[64,2048]{1,0:T(8,128)(2,1)S(1)}, u32[]{:S(2)}, u32[]{:S(2)}) %collective-permute-start.19) | collective-permute-done | bytes 262176 | tf_op jit(solution)/shard_map/ppermute | solution.py:475
  98.2 2.0 %collective-permute-start.21 = (bf16[64,1024]{1,0:T(8,128)(2,1)S(1)}, bf16[64,1024]{1,0:T(8,128)(2,1)S(1)}, u32[]{:S(2)}, u32[]{:S(2)}) collective-permute-start(bf16[64,1024]{1,0:T(8,128)(2,1)S(1)} %get-tuple-element.53), channel_id=1, source_target_pairs={{0,20},{1,21},{2,22},{3,23},{4,28},{5,29},{6,30},{7,31},{8,16},{9,... | collective-permute-start | bytes 393224 | tf_op jit(solution)/shard_map/ppermute | solution.py:503
  100.2 2.1 %collective-permute-start.22 = (bf16[64,1024]{1,0:T(8,128)(2,1)S(1)}, bf16[64,1024]{1,0:T(8,128)(2,1)S(1)}, u32[]{:S(2)}, u32[]{:S(2)}) collective-permute-start(bf16[64,1024]{1,0:T(8,128)(2,1)S(1)} %get-tuple-element.49.after_any), channel_id=1, source_target_pairs={{0,4},{1,5},{2,6},{3,7},{4,12},{5,13},{6,14},{7,15},{8,0},{9,1},{1... | collective-permute-start | bytes 393224 | tf_op jit(solution)/shard_map/ppermute | solution.py:502
  102.5 1.9 %collective-permute-start.23 = (bf16[32,1024]{1,0:T(8,128)(2,1)S(1)}, bf16[32,1024]{1,0:T(8,128)(2,1)S(1)}, u32[]{:S(2)}, u32[]{:S(2)}) collective-permute-start(bf16[32,1024]{1,0:T(8,128)(2,1)S(1)} %get-tuple-element.56), channel_id=1, source_target_pairs={{0,16},{16,0},{1,17},{17,1},{2,18},{18,2},{3,19},{19,3},{4,20},{20... | collective-permute-start | bytes 196616 | tf_op jit(solution)/shard_map/ppermute | solution.py:500
  104.5 2.2 %collective-permute-done.24.lower_ref = bf16[32,1024]{1,0:T(8,128)(2,1)S(1)} collective-permute-done((bf16[32,1024]{1,0:T(8,128)(2,1)S(1)}, bf16[32,1024]{1,0:T(8,128)(2,1)S(1)}, u32[]{:S(2)}, u32[]{:S(2)}) %collective-permute-start.24) | collective-permute-done | bytes 65568 | tf_op jit(solution)/shard_map/ppermute | solution.py:500
  (103 shorter events, 25.9 us)
Async XLA Ops:
  2.8 22.9 %all-to-all-start = ((bf16[16,16,1152]{2,1,0:T(8,128)(2,1)}), bf16[16,16,1152]{2,1,0:T(8,128)(2,1)S(1)}, u32[]{:S(2)}, u32[]{:S(2)}) async-start(bf16[16,16,1152]{2,1,0:T(8,128)(2,1)} %pick.1), calls=%async_computation | async-start | bytes 1179648 | tf_op jit(solution)/shard_map/all_to_all | solution.py:321
  32.5 8.5 %collective-permute-start = (bf16[64,2048]{1,0:T(8,128)(2,1)}, bf16[64,2048]{1,0:T(8,128)(2,1)S(1)}, u32[]{:S(2)}, u32[]{:S(2)}) collective-permute-start(bf16[64,2048]{1,0:T(8,128)(2,1)} %attend_moved.1.after_any.own_any), channel_id=1, source_target_pairs={{0,16},{16,0},{1,17},{17,1},{2,18},{18,2},{3,19},{19,3},{4,20},{20... | collective-permute-start | bytes 786440 | tf_op jit(solution)/shard_map/ppermute | solution.py:375
  41.7 8.8 %collective-permute-start.2 = (bf16[64,2176]{1,0:T(8,128)(2,1)S(1)}, bf16[64,2176]{1,0:T(8,128)(2,1)S(1)}, u32[]{:S(2)}, u32[]{:S(2)}) collective-permute-start(bf16[64,2176]{1,0:T(8,128)(2,1)S(1)} %get-tuple-element.33.after_any.refs_0_), channel_id=1, source_target_pairs={{0,8},{1,9},{2,10},{3,11},{4,0},{5,1},{6,2},{7,3},{8,12},{9,13},{1... | collective-permute-start | bytes 835592 | tf_op jit(solution)/shard_map/ppermute | solution.py:454
  43.7 6.8 %collective-permute-start.1 = (bf16[64,2176]{1,0:T(8,128)(2,1)S(1)}, bf16[64,2176]{1,0:T(8,128)(2,1)S(1)}, u32[]{:S(2)}, u32[]{:S(2)}) collective-permute-start(bf16[64,2176]{1,0:T(8,128)(2,1)S(1)} %get-tuple-element.33.after_any.refs_0_), channel_id=1, source_target_pairs={{0,2},{1,3},{2,0},{3,1},{4,6},{5,7},{6,4},{7,5},{8,10},{9,11},{10,... | collective-permute-start | bytes 835592 | tf_op jit(solution)/shard_map/ppermute | solution.py:455
  50.5 5.3 %collective-permute-start.3 = (bf16[192,2176]{1,0:T(8,128)(2,1)S(1)}, bf16[192,2176]{1,0:T(8,128)(2,1)S(1)}, u32[]{:S(2)}, u32[]{:S(2)}) collective-permute-start(bf16[192,2176]{1,0:T(8,128)(2,1)S(1)} %pack.3.here_ref), channel_id=1, source_target_pairs={{0,1},{1,0},{2,3},{3,2},{4,5},{5,4},{6,7},{7,6},{8,9},{9,8},{10,11... | collective-permute-start | bytes 2506760 | tf_op jit(solution)/shard_map/ppermute | solution.py:419
  50.6 9.9 %collective-permute-start.7 = (bf16[64,2176]{1,0:T(8,128)(2,1)S(1)}, bf16[64,2176]{1,0:T(8,128)(2,1)S(1)}, u32[]{:S(2)}, u32[]{:S(2)}) collective-permute-start(bf16[64,2176]{1,0:T(8,128)(2,1)S(1)} %collective-permute-done.2.refs_2_), channel_id=1, source_target_pairs={{0,8},{1,9},{2,10},{3,11},{4,0},{5,1},{6,2},{7,3},{8,12},{9,13},{1... | collective-permute-start | bytes 835592 | tf_op jit(solution)/shard_map/ppermute | solution.py:456
  52.9 8.5 %collective-permute-start.6 = (bf16[64,2176]{1,0:T(8,128)(2,1)S(1)}, bf16[64,2176]{1,0:T(8,128)(2,1)S(1)}, u32[]{:S(2)}, u32[]{:S(2)}) collective-permute-start(bf16[64,2176]{1,0:T(8,128)(2,1)S(1)} %collective-permute-done.2.refs_2_), channel_id=1, source_target_pairs={{0,2},{1,3},{2,0},{3,1},{4,6},{5,7},{6,4},{7,5},{8,10},{9,11},{10,... | collective-permute-start | bytes 835592 | tf_op jit(solution)/shard_map/ppermute | solution.py:457
  54.3 8.3 %collective-permute-start.5 = (bf16[64,2176]{1,0:T(8,128)(2,1)S(1)}, bf16[64,2176]{1,0:T(8,128)(2,1)S(1)}, u32[]{:S(2)}, u32[]{:S(2)}) collective-permute-start(bf16[64,2176]{1,0:T(8,128)(2,1)S(1)} %collective-permute-done.2.refs_2_), channel_id=1, source_target_pairs={{0,16},{16,0},{1,17},{17,1},{2,18},{18,2},{3,19},{19,3},{4,20},{20... | collective-permute-start | bytes 835592 | tf_op jit(solution)/shard_map/ppermute | solution.py:458
  62.7 9.1 %collective-permute-start.11 = (bf16[64,2176]{1,0:T(8,128)(2,1)S(1)}, bf16[64,2176]{1,0:T(8,128)(2,1)S(1)}, u32[]{:S(2)}, u32[]{:S(2)}) collective-permute-start(bf16[64,2176]{1,0:T(8,128)(2,1)S(1)} %collective-permute-done.7.refs_2_), channel_id=1, source_target_pairs={{0,2},{1,3},{2,0},{3,1},{4,6},{5,7},{6,4},{7,5},{8,10},{9,11},{10,... | collective-permute-start | bytes 835592 | tf_op jit(solution)/shard_map/ppermute | solution.py:459
  63.4 8.7 %collective-permute-start.10 = (bf16[64,2176]{1,0:T(8,128)(2,1)S(1)}, bf16[64,2176]{1,0:T(8,128)(2,1)S(1)}, u32[]{:S(2)}, u32[]{:S(2)}) collective-permute-start(bf16[64,2176]{1,0:T(8,128)(2,1)S(1)} %collective-permute-done.6.refs_1_), channel_id=1, source_target_pairs={{0,16},{16,0},{1,17},{17,1},{2,18},{18,2},{3,19},{19,3},{4,20},{20... | collective-permute-start | bytes 835592 | tf_op jit(solution)/shard_map/ppermute | solution.py:460
  64.9 7.8 %collective-permute-start.4 = (bf16[192,2048]{1,0:T(8,128)(2,1)S(1)}, bf16[192,2048]{1,0:T(8,128)(2,1)S(1)}, u32[]{:S(2)}, u32[]{:S(2)}) collective-permute-start(bf16[192,2048]{1,0:T(8,128)(2,1)S(1)} %get-tuple-element.37), channel_id=1, source_target_pairs={{0,1},{1,0},{2,3},{3,2},{4,5},{5,4},{6,7},{7,6},{8,9},{9,8},{10,11... | collective-permute-start | bytes 2359304 | tf_op jit(solution)/shard_map/ppermute | solution.py:430
  72.2 12.2 %collective-permute-start.9 = (bf16[192,2048]{1,0:T(8,128)(2,1)S(1)}, bf16[192,2048]{1,0:T(8,128)(2,1)S(1)}, u32[]{:S(2)}, u32[]{:S(2)}) collective-permute-start(bf16[192,2048]{1,0:T(8,128)(2,1)S(1)} %get-tuple-element.40), channel_id=1, source_target_pairs={{0,1},{1,0},{2,3},{3,2},{4,5},{5,4},{6,7},{7,6},{8,9},{9,8},{10,11... | collective-permute-start | bytes 2359304 | tf_op jit(solution)/shard_map/ppermute | solution.py:430
  72.9 8.4 %collective-permute-start.13 = (bf16[64,2048]{1,0:T(8,128)(2,1)S(1)}, bf16[64,2048]{1,0:T(8,128)(2,1)S(1)}, u32[]{:S(2)}, u32[]{:S(2)}) collective-permute-start(bf16[64,2048]{1,0:T(8,128)(2,1)S(1)} %get-tuple-element.42.after_any), channel_id=1, source_target_pairs={{0,2},{1,3},{2,0},{3,1},{4,6},{5,7},{6,4},{7,5},{8,10},{9,11},{10,... | collective-permute-start | bytes 786440 | tf_op jit(solution)/shard_map/ppermute | solution.py:464
  77.1 4.2 %collective-permute-start.14 = (bf16[64,2048]{1,0:T(8,128)(2,1)S(1)}, bf16[64,2048]{1,0:T(8,128)(2,1)S(1)}, u32[]{:S(2)}, u32[]{:S(2)}) collective-permute-start(bf16[64,2048]{1,0:T(8,128)(2,1)S(1)} %get-tuple-element.44), channel_id=1, source_target_pairs={{0,1},{1,0},{2,3},{3,2},{4,5},{5,4},{6,7},{7,6},{8,9},{9,8},{10,11... | collective-permute-start | bytes 786440 | tf_op jit(solution)/shard_map/ppermute | solution.py:430
  77.1 4.1 %collective-permute-start.15 = (bf16[64,2048]{1,0:T(8,128)(2,1)S(1)}, bf16[64,2048]{1,0:T(8,128)(2,1)S(1)}, u32[]{:S(2)}, u32[]{:S(2)}) collective-permute-start(bf16[64,2048]{1,0:T(8,128)(2,1)S(1)} %get-tuple-element.45), channel_id=1, source_target_pairs={{0,1},{1,0},{2,3},{3,2},{4,5},{5,4},{6,7},{7,6},{8,9},{9,8},{10,11... | collective-permute-start | bytes 786440 | tf_op jit(solution)/shard_map/ppermute | solution.py:430
  81.4 7.5 %collective-permute-start.18 = (bf16[64,2048]{1,0:T(8,128)(2,1)S(1)}, bf16[64,2048]{1,0:T(8,128)(2,1)S(1)}, u32[]{:S(2)}, u32[]{:S(2)}) collective-permute-start(bf16[64,2048]{1,0:T(8,128)(2,1)S(1)} %get-tuple-element.48), channel_id=1, source_target_pairs={{0,2},{1,3},{2,0},{3,1},{4,6},{5,7},{6,4},{7,5},{8,10},{9,11},{10,... | collective-permute-start | bytes 786440 | tf_op jit(solution)/shard_map/ppermute | solution.py:469
  82.9 7.2 %collective-permute-start.16 = (bf16[64,2048]{1,0:T(8,128)(2,1)S(1)}, bf16[64,2048]{1,0:T(8,128)(2,1)S(1)}, u32[]{:S(2)}, u32[]{:S(2)}) collective-permute-start(bf16[64,2048]{1,0:T(8,128)(2,1)S(1)} %get-tuple-element.46), channel_id=1, source_target_pairs={{0,16},{16,0},{1,17},{17,1},{2,18},{18,2},{3,19},{19,3},{4,20},{20... | collective-permute-start | bytes 786440 | tf_op jit(solution)/shard_map/ppermute | solution.py:468
  89.0 7.5 %collective-permute-start.19 = (bf16[64,2048]{1,0:T(8,128)(2,1)S(1)}, bf16[64,2048]{1,0:T(8,128)(2,1)S(1)}, u32[]{:S(2)}, u32[]{:S(2)}) collective-permute-start(bf16[64,2048]{1,0:T(8,128)(2,1)S(1)} %join.10), channel_id=1, source_target_pairs={{0,4},{1,5},{2,6},{3,7},{4,12},{5,13},{6,14},{7,15},{8,0},{9,1},{1... | collective-permute-start | bytes 786440 | tf_op jit(solution)/shard_map/ppermute | solution.py:475
  90.1 6.4 %collective-permute-start.17 = (bf16[64,2048]{1,0:T(8,128)(2,1)S(1)}, bf16[64,2048]{1,0:T(8,128)(2,1)S(1)}, u32[]{:S(2)}, u32[]{:S(2)}) collective-permute-start(bf16[64,2048]{1,0:T(8,128)(2,1)S(1)} %join.9), channel_id=1, source_target_pairs={{0,2},{1,3},{2,0},{3,1},{4,6},{5,7},{6,4},{7,5},{8,10},{9,11},{10,... | collective-permute-start | bytes 786440 | tf_op jit(solution)/shard_map/ppermute | solution.py:474
  91.6 6.5 %collective-permute-start.20 = (bf16[64,2048]{1,0:T(8,128)(2,1)S(1)}, bf16[64,2048]{1,0:T(8,128)(2,1)S(1)}, u32[]{:S(2)}, u32[]{:S(2)}) collective-permute-start(bf16[64,2048]{1,0:T(8,128)(2,1)S(1)} %join.11), channel_id=1, source_target_pairs={{0,16},{16,0},{1,17},{17,1},{2,18},{18,2},{3,19},{19,3},{4,20},{20... | collective-permute-start | bytes 786440 | tf_op jit(solution)/shard_map/ppermute | solution.py:473
  98.2 9.2 %collective-permute-start.21 = (bf16[64,1024]{1,0:T(8,128)(2,1)S(1)}, bf16[64,1024]{1,0:T(8,128)(2,1)S(1)}, u32[]{:S(2)}, u32[]{:S(2)}) collective-permute-start(bf16[64,1024]{1,0:T(8,128)(2,1)S(1)} %get-tuple-element.53), channel_id=1, source_target_pairs={{0,20},{1,21},{2,22},{3,23},{4,28},{5,29},{6,30},{7,31},{8,16},{9,... | collective-permute-start | bytes 393224 | tf_op jit(solution)/shard_map/ppermute | solution.py:503
  100.2 7.2 %collective-permute-start.22 = (bf16[64,1024]{1,0:T(8,128)(2,1)S(1)}, bf16[64,1024]{1,0:T(8,128)(2,1)S(1)}, u32[]{:S(2)}, u32[]{:S(2)}) collective-permute-start(bf16[64,1024]{1,0:T(8,128)(2,1)S(1)} %get-tuple-element.49.after_any), channel_id=1, source_target_pairs={{0,4},{1,5},{2,6},{3,7},{4,12},{5,13},{6,14},{7,15},{8,0},{9,1},{1... | collective-permute-start | bytes 393224 | tf_op jit(solution)/shard_map/ppermute | solution.py:502
  102.4 4.3 %collective-permute-start.24 = (bf16[32,1024]{1,0:T(8,128)(2,1)S(1)}, bf16[32,1024]{1,0:T(8,128)(2,1)S(1)}, u32[]{:S(2)}, u32[]{:S(2)}) collective-permute-start(bf16[32,1024]{1,0:T(8,128)(2,1)S(1)} %get-tuple-element.55), channel_id=1, source_target_pairs={{0,16},{16,0},{1,17},{17,1},{2,18},{18,2},{3,19},{19,3},{4,20},{20... | collective-permute-start | bytes 196616 | tf_op jit(solution)/shard_map/ppermute | solution.py:500
  102.5 4.9 %collective-permute-start.23 = (bf16[32,1024]{1,0:T(8,128)(2,1)S(1)}, bf16[32,1024]{1,0:T(8,128)(2,1)S(1)}, u32[]{:S(2)}, u32[]{:S(2)}) collective-permute-start(bf16[32,1024]{1,0:T(8,128)(2,1)S(1)} %get-tuple-element.56), channel_id=1, source_target_pairs={{0,16},{16,0},{1,17},{17,1},{2,18},{18,2},{3,19},{19,3},{4,20},{20... | collective-permute-start | bytes 196616 | tf_op jit(solution)/shard_map/ppermute | solution.py:500
  (17 other events, 116.3 us)

commit v12 on v10

--- a/solution.py
+++ b/solution.py
@@ -44,11 +44,16 @@
     return start
 
 
-def pick_kernel(pieces, moves_any, cache_any, out_ref, moves_ref, cache, stacked, sems):
-    got = fetch_all((moves_any, cache_any), (moves_ref, cache), sems)
+def pick_kernel(pieces, moves_any, cache_any, out_ref, moves_ref, stacked, sems):
     ranks, per_rank, wide = out_ref.shape
     slots = moves_ref.shape[0]
-    resident = cache.shape[0]
+    resident = cache_any.shape[0]
+    got = fetch_all(
+        [moves_any] + [cache_any.at[:, piece * wide : (piece + 1) * wide] for piece in range(pieces)],
+        [moves_ref]
+        + [stacked.at[piece * resident : (piece + 1) * resident] for piece in range(pieces)],
+        sems,
+    )
     rows = ranks * per_rank
     row = lax.broadcasted_iota(jnp.int32, (rows, ranks), 0)
     rank = lax.broadcasted_iota(jnp.int32, (rows, ranks), 1)
@@ -61,9 +66,8 @@
     at = lax.broadcasted_iota(jnp.int32, (rows, pieces * resident), 0)
     source = lax.broadcasted_iota(jnp.int32, (rows, pieces * resident), 1)
     pick = (source // resident == at % pieces) & (source % resident == block)
-    got[1].wait()
-    for piece in range(pieces):
-        stacked[piece * resident : (piece + 1) * resident, :] = cache[:, piece * wide : (piece + 1) * wide]
+    for copy in got[1:]:
+        copy.wait()
     picked = dot(pick.astype(F32).astype(BF16), stacked[...]).astype(BF16)
     out_ref[...] = picked.reshape(ranks, per_rank, wide)
 
@@ -109,9 +113,11 @@
     head_count, nope_dim, latent, rope, block_size, steps = dims
     width = latent + rope
     rows = heads_out.shape[0]
+    middle = proj.shape[1] // 2
+    halves = (slice(0, middle), slice(middle, 2 * middle))
     got = fetch_all(
-        (moved_any, query_any, bias_any, mixed_any, value_any, proj_any),
-        (moved, query, bias, mixed, value, proj),
+        [moved_any, query_any, bias_any, mixed_any, value_any] + [proj_any.at[:, at] for at in halves],
+        [moved, query, bias, mixed, value] + [proj.at[:, at] for at in halves],
         sems,
     )
     keys[:, latent:] = jnp.zeros((keys.shape[0], keys.shape[1] - latent), BF16)
@@ -144,8 +150,9 @@
         for head in range(first, first + group):
             own = joined[(head - first) * rows : (head - first + 1) * rows]
             heads_out[:, head * value_dim : (head + 1) * value_dim] = dot(own, value[head]).astype(BF16)
-    got[5].wait()
-    share_ref[...] = dot(heads_out[...], proj[...]).astype(BF16)
+    for at, copy in zip(halves, got[5:]):
+        copy.wait()
+        share_ref[:, at] = dot(heads_out[...], proj[:, at]).astype(BF16)
 
 
 def own_columns(ref, shift):
@@ -311,9 +318,8 @@
         in_specs=[ANY] * 2,
         scratch_shapes=[
             VMEM((slots, ranks), jnp.int32),
-            VMEM(latent_cache.shape, BF16),
             VMEM((pieces * resident, 2 * width), BF16),
-            pltpu.SemaphoreType.DMA((2,)),
+            pltpu.SemaphoreType.DMA((1 + pieces,)),
         ],
         compiler_params=pltpu.CompilerParams(vmem_limit_bytes=60 * 2**20),
         cost_estimate=cost(0, 4 * 2**20),
@@ -368,7 +374,7 @@
             VMEM(output_proj.shape, BF16),
             VMEM((moved_bias.shape[1], padded), BF16),
             VMEM((row_count, head_count * value_absorb.shape[2]), BF16),
-            pltpu.SemaphoreType.DMA((6,)),
+            pltpu.SemaphoreType.DMA((7,)),
         ],
         compiler_params=pltpu.CompilerParams(vmem_limit_bytes=56 * 2**20),
         cost_estimate=cost(query_rows * moved_bias.shape[1] * (padded + latent), 10 * 2**20),

time: 107 us -> 108 us (level)
  no operation moved by 1% of the time
where the time goes in v12:
time: 108 us; the launch traced here: 107 us
  waiting for transfers between devices  39.4 us (36%)
  starting transfers between devices  35 us (32%)
  Pallas kernels  26.9 us (25%)
  local copies, waits for them, and re-layouts  5.12 us (5%)
    pallas_call x3, Pallas kernels, run_expert(): pl.pallas_call(functools.partial(expert_kernel, experts), out_shape=[jax....  10.3 us
    all_to_all x1, waiting for transfers between devices, local(): lax.all_to_all(outgoing, 'ep', split_axis=0, concat_axis=0, tiled=True)  8.68 us
    all_to_all x1, starting transfers between devices, local(): lax.all_to_all(outgoing, 'ep', split_axis=0, concat_axis=0, tiled=True)  7.39 us
    ppermute x1, waiting for transfers between devices, local(): near = lax.ppermute(packet, both_axes, onward)  6.73 us
    pallas_call x1, Pallas kernels, local(): pl.pallas_call(functools.partial(moved_kernel, dims), out_shape=jax.Shape...  5.09 us
    ppermute x1, waiting for transfers between devices, local(): two_side_in = lax.ppermute(two_side_sum, 'ep', side_swap)  4.37 us
    unnamed x30, local copies, waits for them, and re-layouts  3.78 us
    ppermute x1, waiting for transfers between devices, local(): side_in = lax.ppermute(side_sum, 'ep', side_swap)  3.62 us
  transfers between devices with their start and end apart: 26, of which 17 were waited for; matrix products, arithmetic and copies ran while one was open for 2% of the time, Pallas kernels for 16%

profile of v12, /device:TPU:0, one launch (start us, length us, event | category | flops | bytes accessed | tf_op | source)
XLA Modules:
  0.0 107.5 jit_solution(14799991736658242071)
XLA Ops:
  0.0 2.9 %pick.1 = bf16[16,16,1152]{2,1,0:T(8,128)(2,1)} custom-call(s32[2,16]{1,0:T(2,128)} %bitcast.22, bf16[64,9216]{1,0:T(8,128)(2,1)} %cache.1), custom_call_target="tpu_custom_call" | custom-call | bytes 4194304 | tf_op jit(solution)/shard_map/pick/pallas_call | solution.py:315
  2.9 7.4 %all-to-all-start = ((bf16[16,16,1152]{2,1,0:T(8,128)(2,1)}), bf16[16,16,1152]{2,1,0:T(8,128)(2,1)S(1)}, u32[]{:S(2)}, u32[]{:S(2)}) async-start(bf16[16,16,1152]{2,1,0:T(8,128)(2,1)} %pick.1), calls=%async_computation | async-start | bytes 1179648 | tf_op jit(solution)/shard_map/all_to_all | solution.py:328
  12.5 2.7 %attend_resident.1 = (bf16[512,640]{1,0:T(8,128)(2,1)S(1)}, f32[512,640]{1,0:T(8,128)S(1)}) custom-call(bf16[64,1024]{1,0:T(8,128)(2,1)S(1)} %copy-done.8, bf16[64,512]{1,0:T(8,128)(2,1)S(1)} %copy-done.10, bf16[16,2304]{1,0:T(8,128)(2,1)S(1)} %copy-done.9, bf16[64,9216]{1,0:T(8,128)(2,1)S(1)} %copy-done.2, bf16[8,128,512]{2,1,0:T(8,128)(2,1)S(1)} %copy-done.7, ...), custom_call_target="tpu_custom_call" | custom-call | flops 1283457024 | bytes 8388608 | tf_op jit(solution)/shard_map/attend_resident/pallas_call | solution.py:353
  17.2 8.7 %all-to-all-done.moved_any = bf16[16,16,1152]{2,1,0:T(8,128)(2,1)S(1)} async-done(((bf16[16,16,1152]{2,1,0:T(8,128)(2,1)}), bf16[16,16,1152]{2,1,0:T(8,128)(2,1)S(1)}, u32[]{:S(2)}, u32[]{:S(2)}) %all-to-all-start) | async-done | bytes 589856 | tf_op jit(solution)/shard_map/all_to_all | solution.py:328
  26.7 5.1 %attend_moved.1.after_any.own_any = bf16[64,2048]{1,0:T(8,128)(2,1)} custom-call(bf16[16,16,1152]{2,1,0:T(8,128)(2,1)} %copy-done.11, bf16[512,640]{1,0:T(8,128)(2,1)} %copy-done.3, f32[64,512]{1,0:T(8,128)} %reshape.110.bias_any, f32[512,640]{1,0:T(8,128)} %copy-done.1, bf16[8,512,128]{2,1,0:T(8,128)(2,1)} %value_any.1, bf16[1024,2048]{1,0:T(8,128)(2,1)} %proj_any.1), custom_call_target="tpu_custom_call" | custom-call | flops 603979776 | bytes 10485760 | tf_op jit(solution)/shard_map/attend_moved/pallas_call | solution.py:364
  31.8 1.6 %collective-permute-start = (bf16[64,2048]{1,0:T(8,128)(2,1)}, bf16[64,2048]{1,0:T(8,128)(2,1)S(1)}, u32[]{:S(2)}, u32[]{:S(2)}) collective-permute-start(bf16[64,2048]{1,0:T(8,128)(2,1)} %attend_moved.1.after_any.own_any), channel_id=1, source_target_pairs={{0,16},{16,0},{1,17},{17,1},{2,18},{18,2},{3,19},{19,3},{4,20},{20... | collective-permute-start | bytes 786440 | tf_op jit(solution)/shard_map/ppermute | solution.py:383
  34.4 3.6 %load.1 = (bf16[704,2048]{1,0:T(8,128)(2,1)S(1)}, bf16[704,2048]{1,0:T(8,128)(2,1)S(1)}, bf16[704,2048]{1,0:T(8,128)(2,1)S(1)}) custom-call(bf16[64,2048]{1,0:T(8,128)(2,1)S(1)} %copy-done, bf16[704,2048]{1,0:T(8,128)(2,1)} %bitcast.18, bf16[704,2048]{1,0:T(8,128)(2,1)} %bitcast.19, bf16[704,2048]{1,0:T(8,128)(2,1)} %bitcast.20), custom_call_target="tpu_custom_call" | custom-call | bytes 12582912 | tf_op jit(solution)/shard_map/load/pallas_call | solution.py:386
  38.0 2.3 %collective-permute-done.refs_0_ = bf16[64,2048]{1,0:T(8,128)(2,1)S(1)} collective-permute-done((bf16[64,2048]{1,0:T(8,128)(2,1)}, bf16[64,2048]{1,0:T(8,128)(2,1)S(1)}, u32[]{:S(2)}, u32[]{:S(2)}) %collective-permute-start) | collective-permute-done | bytes 262176 | tf_op jit(solution)/shard_map/ppermute | solution.py:383
  41.0 2.0 %collective-permute-start.2 = (bf16[64,2176]{1,0:T(8,128)(2,1)S(1)}, bf16[64,2176]{1,0:T(8,128)(2,1)S(1)}, u32[]{:S(2)}, u32[]{:S(2)}) collective-permute-start(bf16[64,2176]{1,0:T(8,128)(2,1)S(1)} %get-tuple-element.33.after_any.refs_0_), channel_id=1, source_target_pairs={{0,8},{1,9},{2,10},{3,11},{4,0},{5,1},{6,2},{7,3},{8,12},{9,13},{1... | collective-permute-start | bytes 835592 | tf_op jit(solution)/shard_map/ppermute | solution.py:462
  43.0 6.7 %collective-permute-done.2.refs_2_ = bf16[64,2176]{1,0:T(8,128)(2,1)S(1)} collective-permute-done((bf16[64,2176]{1,0:T(8,128)(2,1)S(1)}, bf16[64,2176]{1,0:T(8,128)(2,1)S(1)}, u32[]{:S(2)}, u32[]{:S(2)}) %collective-permute-start.2) | collective-permute-done | bytes 278560 | tf_op jit(solution)/shard_map/ppermute | solution.py:462
  49.9 2.3 %collective-permute-start.7 = (bf16[64,2176]{1,0:T(8,128)(2,1)S(1)}, bf16[64,2176]{1,0:T(8,128)(2,1)S(1)}, u32[]{:S(2)}, u32[]{:S(2)}) collective-permute-start(bf16[64,2176]{1,0:T(8,128)(2,1)S(1)} %collective-permute-done.2.refs_2_), channel_id=1, source_target_pairs={{0,8},{1,9},{2,10},{3,11},{4,0},{5,1},{6,2},{7,3},{8,12},{9,13},{1... | collective-permute-start | bytes 835592 | tf_op jit(solution)/shard_map/ppermute | solution.py:464
  53.6 1.5 %collective-permute-start.5 = (bf16[64,2176]{1,0:T(8,128)(2,1)S(1)}, bf16[64,2176]{1,0:T(8,128)(2,1)S(1)}, u32[]{:S(2)}, u32[]{:S(2)}) collective-permute-start(bf16[64,2176]{1,0:T(8,128)(2,1)S(1)} %collective-permute-done.2.refs_2_), channel_id=1, source_target_pairs={{0,16},{16,0},{1,17},{17,1},{2,18},{18,2},{3,19},{19,3},{4,20},{20... | collective-permute-start | bytes 835592 | tf_op jit(solution)/shard_map/ppermute | solution.py:466
  55.2 3.8 %expert.3 = (bf16[192,2048]{1,0:T(8,128)(2,1)S(1)}, bf16[192,2048]{1,0:T(8,128)(2,1)S(1)}) custom-call(bf16[64,2176]{1,0:T(8,128)(2,1)S(1)} %get-tuple-element.33.after_any.refs_0_, bf16[192,2176]{1,0:T(8,128)(2,1)S(1)} %pack.3.here_ref, bf16[192,2176]{1,0:T(8,128)(2,1)S(1)} %collective-permute-done.3.across_ref, ...), custom_call_target="tpu_custom_call" | custom-call | flops 3321888768 | bytes 12582912 | tf_op jit(solution)/shard_map/expert/pallas_call | solution.py:428
  64.4 3.8 %expert.4 = (bf16[192,2048]{1,0:T(8,128)(2,1)S(1)}, bf16[192,2048]{1,0:T(8,128)(2,1)S(1)}) custom-call(bf16[64,2176]{1,0:T(8,128)(2,1)S(1)} %get-tuple-element.33.after_any.refs_0_, bf16[192,2176]{1,0:T(8,128)(2,1)S(1)} %pack.4.here_ref, bf16[192,2176]{1,0:T(8,128)(2,1)S(1)} %collective-permute-done.8.across_ref, ...), custom_call_target="tpu_custom_call" | custom-call | flops 3321888768 | bytes 12582912 | tf_op jit(solution)/shard_map/expert/pallas_call | solution.py:428
  68.3 2.9 %collective-permute-done.11.refs_1_ = bf16[64,2176]{1,0:T(8,128)(2,1)S(1)} collective-permute-done((bf16[64,2176]{1,0:T(8,128)(2,1)S(1)}, bf16[64,2176]{1,0:T(8,128)(2,1)S(1)}, u32[]{:S(2)}, u32[]{:S(2)}) %collective-permute-start.11) | collective-permute-done | bytes 278560 | tf_op jit(solution)/shard_map/ppermute | solution.py:467
  73.7 2.6 %expert.5 = (bf16[128,2048]{1,0:T(8,128)(2,1)S(1)}, bf16[64,2048]{1,0:T(8,128)(2,1)S(1)}, bf16[64,2048]{1,0:T(8,128)(2,1)S(1)}) custom-call(bf16[64,2048]{1,0:T(8,128)(2,1)S(1)} %get-tuple-element.42.after_any, bf16[128,2176]{1,0:T(8,128)(2,1)S(1)} %pack.5.here_ref, bf16[128,2176]{1,0:T(8,128)(2,1)S(1)} %collective-permute-done.12.across_ref, ...), custom_call_target="tpu_custom_call" | custom-call | flops 2214592512 | bytes 12582912 | tf_op jit(solution)/shard_map/expert/pallas_call | solution.py:428
  77.0 3.6 %collective-permute-done.13.refs_0_.side_ref = bf16[64,2048]{1,0:T(8,128)(2,1)S(1)} collective-permute-done((bf16[64,2048]{1,0:T(8,128)(2,1)S(1)}, bf16[64,2048]{1,0:T(8,128)(2,1)S(1)}, u32[]{:S(2)}, u32[]{:S(2)}) %collective-permute-start.13) | collective-permute-done | bytes 262176 | tf_op jit(solution)/shard_map/ppermute | solution.py:472
  83.9 4.4 %collective-permute-done.18.refs_0_ = bf16[64,2048]{1,0:T(8,128)(2,1)S(1)} collective-permute-done((bf16[64,2048]{1,0:T(8,128)(2,1)S(1)}, bf16[64,2048]{1,0:T(8,128)(2,1)S(1)}, u32[]{:S(2)}, u32[]{:S(2)}) %collective-permute-start.18) | collective-permute-done | bytes 262176 | tf_op jit(solution)/shard_map/ppermute | solution.py:477
  90.9 2.1 %collective-permute-start.20 = (bf16[64,2048]{1,0:T(8,128)(2,1)S(1)}, bf16[64,2048]{1,0:T(8,128)(2,1)S(1)}, u32[]{:S(2)}, u32[]{:S(2)}) collective-permute-start(bf16[64,2048]{1,0:T(8,128)(2,1)S(1)} %join.11), channel_id=1, source_target_pairs={{0,16},{16,0},{1,17},{17,1},{2,18},{18,2},{3,19},{19,3},{4,20},{20... | collective-permute-start | bytes 786440 | tf_op jit(solution)/shard_map/ppermute | solution.py:481
  93.0 2.8 %collective-permute-done.19.refs_2_ = bf16[64,2048]{1,0:T(8,128)(2,1)S(1)} collective-permute-done((bf16[64,2048]{1,0:T(8,128)(2,1)S(1)}, bf16[64,2048]{1,0:T(8,128)(2,1)S(1)}, u32[]{:S(2)}, u32[]{:S(2)}) %collective-permute-start.19) | collective-permute-done | bytes 262176 | tf_op jit(solution)/shard_map/ppermute | solution.py:483
  97.5 2.1 %collective-permute-start.21 = (bf16[64,1024]{1,0:T(8,128)(2,1)S(1)}, bf16[64,1024]{1,0:T(8,128)(2,1)S(1)}, u32[]{:S(2)}, u32[]{:S(2)}) collective-permute-start(bf16[64,1024]{1,0:T(8,128)(2,1)S(1)} %get-tuple-element.53), channel_id=1, source_target_pairs={{0,20},{1,21},{2,22},{3,23},{4,28},{5,29},{6,30},{7,31},{8,16},{9,... | collective-permute-start | bytes 393224 | tf_op jit(solution)/shard_map/ppermute | solution.py:511
  99.6 2.1 %collective-permute-start.22 = (bf16[64,1024]{1,0:T(8,128)(2,1)S(1)}, bf16[64,1024]{1,0:T(8,128)(2,1)S(1)}, u32[]{:S(2)}, u32[]{:S(2)}) collective-permute-start(bf16[64,1024]{1,0:T(8,128)(2,1)S(1)} %get-tuple-element.49.after_any), channel_id=1, source_target_pairs={{0,4},{1,5},{2,6},{3,7},{4,12},{5,13},{6,14},{7,15},{8,0},{9,1},{1... | collective-permute-start | bytes 393224 | tf_op jit(solution)/shard_map/ppermute | solution.py:510
  101.9 2.0 %collective-permute-start.23 = (bf16[32,1024]{1,0:T(8,128)(2,1)S(1)}, bf16[32,1024]{1,0:T(8,128)(2,1)S(1)}, u32[]{:S(2)}, u32[]{:S(2)}) collective-permute-start(bf16[32,1024]{1,0:T(8,128)(2,1)S(1)} %get-tuple-element.56), channel_id=1, source_target_pairs={{0,16},{16,0},{1,17},{17,1},{2,18},{18,2},{3,19},{19,3},{4,20},{20... | collective-permute-start | bytes 196616 | tf_op jit(solution)/shard_map/ppermute | solution.py:508
  103.8 2.2 %collective-permute-done.24.lower_ref = bf16[32,1024]{1,0:T(8,128)(2,1)S(1)} collective-permute-done((bf16[32,1024]{1,0:T(8,128)(2,1)S(1)}, bf16[32,1024]{1,0:T(8,128)(2,1)S(1)}, u32[]{:S(2)}, u32[]{:S(2)}) %collective-permute-start.24) | collective-permute-done | bytes 65568 | tf_op jit(solution)/shard_map/ppermute | solution.py:508
  (103 shorter events, 25.9 us)
Async XLA Ops:
  2.9 22.9 %all-to-all-start = ((bf16[16,16,1152]{2,1,0:T(8,128)(2,1)}), bf16[16,16,1152]{2,1,0:T(8,128)(2,1)S(1)}, u32[]{:S(2)}, u32[]{:S(2)}) async-start(bf16[16,16,1152]{2,1,0:T(8,128)(2,1)} %pick.1), calls=%async_computation | async-start | bytes 1179648 | tf_op jit(solution)/shard_map/all_to_all | solution.py:328
  31.8 8.5 %collective-permute-start = (bf16[64,2048]{1,0:T(8,128)(2,1)}, bf16[64,2048]{1,0:T(8,128)(2,1)S(1)}, u32[]{:S(2)}, u32[]{:S(2)}) collective-permute-start(bf16[64,2048]{1,0:T(8,128)(2,1)} %attend_moved.1.after_any.own_any), channel_id=1, source_target_pairs={{0,16},{16,0},{1,17},{17,1},{2,18},{18,2},{3,19},{19,3},{4,20},{20... | collective-permute-start | bytes 786440 | tf_op jit(solution)/shard_map/ppermute | solution.py:383
  41.0 8.7 %collective-permute-start.2 = (bf16[64,2176]{1,0:T(8,128)(2,1)S(1)}, bf16[64,2176]{1,0:T(8,128)(2,1)S(1)}, u32[]{:S(2)}, u32[]{:S(2)}) collective-permute-start(bf16[64,2176]{1,0:T(8,128)(2,1)S(1)} %get-tuple-element.33.after_any.refs_0_), channel_id=1, source_target_pairs={{0,8},{1,9},{2,10},{3,11},{4,0},{5,1},{6,2},{7,3},{8,12},{9,13},{1... | collective-permute-start | bytes 835592 | tf_op jit(solution)/shard_map/ppermute | solution.py:462
  43.0 6.7 %collective-permute-start.1 = (bf16[64,2176]{1,0:T(8,128)(2,1)S(1)}, bf16[64,2176]{1,0:T(8,128)(2,1)S(1)}, u32[]{:S(2)}, u32[]{:S(2)}) collective-permute-start(bf16[64,2176]{1,0:T(8,128)(2,1)S(1)} %get-tuple-element.33.after_any.refs_0_), channel_id=1, source_target_pairs={{0,2},{1,3},{2,0},{3,1},{4,6},{5,7},{6,4},{7,5},{8,10},{9,11},{10,... | collective-permute-start | bytes 835592 | tf_op jit(solution)/shard_map/ppermute | solution.py:463
  49.8 5.4 %collective-permute-start.3 = (bf16[192,2176]{1,0:T(8,128)(2,1)S(1)}, bf16[192,2176]{1,0:T(8,128)(2,1)S(1)}, u32[]{:S(2)}, u32[]{:S(2)}) collective-permute-start(bf16[192,2176]{1,0:T(8,128)(2,1)S(1)} %pack.3.here_ref), channel_id=1, source_target_pairs={{0,1},{1,0},{2,3},{3,2},{4,5},{5,4},{6,7},{7,6},{8,9},{9,8},{10,11... | collective-permute-start | bytes 2506760 | tf_op jit(solution)/shard_map/ppermute | solution.py:427
  49.9 9.9 %collective-permute-start.7 = (bf16[64,2176]{1,0:T(8,128)(2,1)S(1)}, bf16[64,2176]{1,0:T(8,128)(2,1)S(1)}, u32[]{:S(2)}, u32[]{:S(2)}) collective-permute-start(bf16[64,2176]{1,0:T(8,128)(2,1)S(1)} %collective-permute-done.2.refs_2_), channel_id=1, source_target_pairs={{0,8},{1,9},{2,10},{3,11},{4,0},{5,1},{6,2},{7,3},{8,12},{9,13},{1... | collective-permute-start | bytes 835592 | tf_op jit(solution)/shard_map/ppermute | solution.py:464
  52.2 8.5 %collective-permute-start.6 = (bf16[64,2176]{1,0:T(8,128)(2,1)S(1)}, bf16[64,2176]{1,0:T(8,128)(2,1)S(1)}, u32[]{:S(2)}, u32[]{:S(2)}) collective-permute-start(bf16[64,2176]{1,0:T(8,128)(2,1)S(1)} %collective-permute-done.2.refs_2_), channel_id=1, source_target_pairs={{0,2},{1,3},{2,0},{3,1},{4,6},{5,7},{6,4},{7,5},{8,10},{9,11},{10,... | collective-permute-start | bytes 835592 | tf_op jit(solution)/shard_map/ppermute | solution.py:465
  53.6 8.3 %collective-permute-start.5 = (bf16[64,2176]{1,0:T(8,128)(2,1)S(1)}, bf16[64,2176]{1,0:T(8,128)(2,1)S(1)}, u32[]{:S(2)}, u32[]{:S(2)}) collective-permute-start(bf16[64,2176]{1,0:T(8,128)(2,1)S(1)} %collective-permute-done.2.refs_2_), channel_id=1, source_target_pairs={{0,16},{16,0},{1,17},{17,1},{2,18},{18,2},{3,19},{19,3},{4,20},{20... | collective-permute-start | bytes 835592 | tf_op jit(solution)/shard_map/ppermute | solution.py:466
  62.1 9.1 %collective-permute-start.11 = (bf16[64,2176]{1,0:T(8,128)(2,1)S(1)}, bf16[64,2176]{1,0:T(8,128)(2,1)S(1)}, u32[]{:S(2)}, u32[]{:S(2)}) collective-permute-start(bf16[64,2176]{1,0:T(8,128)(2,1)S(1)} %collective-permute-done.7.refs_2_), channel_id=1, source_target_pairs={{0,2},{1,3},{2,0},{3,1},{4,6},{5,7},{6,4},{7,5},{8,10},{9,11},{10,... | collective-permute-start | bytes 835592 | tf_op jit(solution)/shard_map/ppermute | solution.py:467
  62.7 8.7 %collective-permute-start.10 = (bf16[64,2176]{1,0:T(8,128)(2,1)S(1)}, bf16[64,2176]{1,0:T(8,128)(2,1)S(1)}, u32[]{:S(2)}, u32[]{:S(2)}) collective-permute-start(bf16[64,2176]{1,0:T(8,128)(2,1)S(1)} %collective-permute-done.6.refs_1_), channel_id=1, source_target_pairs={{0,16},{16,0},{1,17},{17,1},{2,18},{18,2},{3,19},{19,3},{4,20},{20... | collective-permute-start | bytes 835592 | tf_op jit(solution)/shard_map/ppermute | solution.py:468
  64.2 7.8 %collective-permute-start.4 = (bf16[192,2048]{1,0:T(8,128)(2,1)S(1)}, bf16[192,2048]{1,0:T(8,128)(2,1)S(1)}, u32[]{:S(2)}, u32[]{:S(2)}) collective-permute-start(bf16[192,2048]{1,0:T(8,128)(2,1)S(1)} %get-tuple-element.37), channel_id=1, source_target_pairs={{0,1},{1,0},{2,3},{3,2},{4,5},{5,4},{6,7},{7,6},{8,9},{9,8},{10,11... | collective-permute-start | bytes 2359304 | tf_op jit(solution)/shard_map/ppermute | solution.py:438
  71.6 12.2 %collective-permute-start.9 = (bf16[192,2048]{1,0:T(8,128)(2,1)S(1)}, bf16[192,2048]{1,0:T(8,128)(2,1)S(1)}, u32[]{:S(2)}, u32[]{:S(2)}) collective-permute-start(bf16[192,2048]{1,0:T(8,128)(2,1)S(1)} %get-tuple-element.40), channel_id=1, source_target_pairs={{0,1},{1,0},{2,3},{3,2},{4,5},{5,4},{6,7},{7,6},{8,9},{9,8},{10,11... | collective-permute-start | bytes 2359304 | tf_op jit(solution)/shard_map/ppermute | solution.py:438
  72.2 8.4 %collective-permute-start.13 = (bf16[64,2048]{1,0:T(8,128)(2,1)S(1)}, bf16[64,2048]{1,0:T(8,128)(2,1)S(1)}, u32[]{:S(2)}, u32[]{:S(2)}) collective-permute-start(bf16[64,2048]{1,0:T(8,128)(2,1)S(1)} %get-tuple-element.42.after_any), channel_id=1, source_target_pairs={{0,2},{1,3},{2,0},{3,1},{4,6},{5,7},{6,4},{7,5},{8,10},{9,11},{10,... | collective-permute-start | bytes 786440 | tf_op jit(solution)/shard_map/ppermute | solution.py:472
  76.4 4.2 %collective-permute-start.14 = (bf16[64,2048]{1,0:T(8,128)(2,1)S(1)}, bf16[64,2048]{1,0:T(8,128)(2,1)S(1)}, u32[]{:S(2)}, u32[]{:S(2)}) collective-permute-start(bf16[64,2048]{1,0:T(8,128)(2,1)S(1)} %get-tuple-element.44), channel_id=1, source_target_pairs={{0,1},{1,0},{2,3},{3,2},{4,5},{5,4},{6,7},{7,6},{8,9},{9,8},{10,11... | collective-permute-start | bytes 786440 | tf_op jit(solution)/shard_map/ppermute | solution.py:438
  76.5 4.1 %collective-permute-start.15 = (bf16[64,2048]{1,0:T(8,128)(2,1)S(1)}, bf16[64,2048]{1,0:T(8,128)(2,1)S(1)}, u32[]{:S(2)}, u32[]{:S(2)}) collective-permute-start(bf16[64,2048]{1,0:T(8,128)(2,1)S(1)} %get-tuple-element.45), channel_id=1, source_target_pairs={{0,1},{1,0},{2,3},{3,2},{4,5},{5,4},{6,7},{7,6},{8,9},{9,8},{10,11... | collective-permute-start | bytes 786440 | tf_op jit(solution)/shard_map/ppermute | solution.py:438
  80.7 7.5 %collective-permute-start.18 = (bf16[64,2048]{1,0:T(8,128)(2,1)S(1)}, bf16[64,2048]{1,0:T(8,128)(2,1)S(1)}, u32[]{:S(2)}, u32[]{:S(2)}) collective-permute-start(bf16[64,2048]{1,0:T(8,128)(2,1)S(1)} %get-tuple-element.48), channel_id=1, source_target_pairs={{0,2},{1,3},{2,0},{3,1},{4,6},{5,7},{6,4},{7,5},{8,10},{9,11},{10,... | collective-permute-start | bytes 786440 | tf_op jit(solution)/shard_map/ppermute | solution.py:477
  82.2 7.2 %collective-permute-start.16 = (bf16[64,2048]{1,0:T(8,128)(2,1)S(1)}, bf16[64,2048]{1,0:T(8,128)(2,1)S(1)}, u32[]{:S(2)}, u32[]{:S(2)}) collective-permute-start(bf16[64,2048]{1,0:T(8,128)(2,1)S(1)} %get-tuple-element.46), channel_id=1, source_target_pairs={{0,16},{16,0},{1,17},{17,1},{2,18},{18,2},{3,19},{19,3},{4,20},{20... | collective-permute-start | bytes 786440 | tf_op jit(solution)/shard_map/ppermute | solution.py:476
  88.3 7.5 %collective-permute-start.19 = (bf16[64,2048]{1,0:T(8,128)(2,1)S(1)}, bf16[64,2048]{1,0:T(8,128)(2,1)S(1)}, u32[]{:S(2)}, u32[]{:S(2)}) collective-permute-start(bf16[64,2048]{1,0:T(8,128)(2,1)S(1)} %join.10), channel_id=1, source_target_pairs={{0,4},{1,5},{2,6},{3,7},{4,12},{5,13},{6,14},{7,15},{8,0},{9,1},{1... | collective-permute-start | bytes 786440 | tf_op jit(solution)/shard_map/ppermute | solution.py:483
  89.4 6.4 %collective-permute-start.17 = (bf16[64,2048]{1,0:T(8,128)(2,1)S(1)}, bf16[64,2048]{1,0:T(8,128)(2,1)S(1)}, u32[]{:S(2)}, u32[]{:S(2)}) collective-permute-start(bf16[64,2048]{1,0:T(8,128)(2,1)S(1)} %join.9), channel_id=1, source_target_pairs={{0,2},{1,3},{2,0},{3,1},{4,6},{5,7},{6,4},{7,5},{8,10},{9,11},{10,... | collective-permute-start | bytes 786440 | tf_op jit(solution)/shard_map/ppermute | solution.py:482
  90.9 6.4 %collective-permute-start.20 = (bf16[64,2048]{1,0:T(8,128)(2,1)S(1)}, bf16[64,2048]{1,0:T(8,128)(2,1)S(1)}, u32[]{:S(2)}, u32[]{:S(2)}) collective-permute-start(bf16[64,2048]{1,0:T(8,128)(2,1)S(1)} %join.11), channel_id=1, source_target_pairs={{0,16},{16,0},{1,17},{17,1},{2,18},{18,2},{3,19},{19,3},{4,20},{20... | collective-permute-start | bytes 786440 | tf_op jit(solution)/shard_map/ppermute | solution.py:481
  97.5 9.3 %collective-permute-start.21 = (bf16[64,1024]{1,0:T(8,128)(2,1)S(1)}, bf16[64,1024]{1,0:T(8,128)(2,1)S(1)}, u32[]{:S(2)}, u32[]{:S(2)}) collective-permute-start(bf16[64,1024]{1,0:T(8,128)(2,1)S(1)} %get-tuple-element.53), channel_id=1, source_target_pairs={{0,20},{1,21},{2,22},{3,23},{4,28},{5,29},{6,30},{7,31},{8,16},{9,... | collective-permute-start | bytes 393224 | tf_op jit(solution)/shard_map/ppermute | solution.py:511
  99.6 7.2 %collective-permute-start.22 = (bf16[64,1024]{1,0:T(8,128)(2,1)S(1)}, bf16[64,1024]{1,0:T(8,128)(2,1)S(1)}, u32[]{:S(2)}, u32[]{:S(2)}) collective-permute-start(bf16[64,1024]{1,0:T(8,128)(2,1)S(1)} %get-tuple-element.49.after_any), channel_id=1, source_target_pairs={{0,4},{1,5},{2,6},{3,7},{4,12},{5,13},{6,14},{7,15},{8,0},{9,1},{1... | collective-permute-start | bytes 393224 | tf_op jit(solution)/shard_map/ppermute | solution.py:510
  101.7 4.3 %collective-permute-start.24 = (bf16[32,1024]{1,0:T(8,128)(2,1)S(1)}, bf16[32,1024]{1,0:T(8,128)(2,1)S(1)}, u32[]{:S(2)}, u32[]{:S(2)}) collective-permute-start(bf16[32,1024]{1,0:T(8,128)(2,1)S(1)} %get-tuple-element.55), channel_id=1, source_target_pairs={{0,16},{16,0},{1,17},{17,1},{2,18},{18,2},{3,19},{19,3},{4,20},{20... | collective-permute-start | bytes 196616 | tf_op jit(solution)/shard_map/ppermute | solution.py:508
  101.9 4.9 %collective-permute-start.23 = (bf16[32,1024]{1,0:T(8,128)(2,1)S(1)}, bf16[32,1024]{1,0:T(8,128)(2,1)S(1)}, u32[]{:S(2)}, u32[]{:S(2)}) collective-permute-start(bf16[32,1024]{1,0:T(8,128)(2,1)S(1)} %get-tuple-element.56), channel_id=1, source_target_pairs={{0,16},{16,0},{1,17},{17,1},{2,18},{18,2},{3,19},{19,3},{4,20},{20... | collective-permute-start | bytes 196616 | tf_op jit(solution)/shard_map/ppermute | solution.py:508
  (17 other events, 116.3 us)

commit v13 on v10

--- a/solution.py
+++ b/solution.py
@@ -124,7 +124,7 @@
         keys[half * count : (half + 1) * count, :width] = part.reshape(count, width)
     got[1].wait()
     got[2].wait()
-    group = min(4, head_count)
+    group = min(8, head_count)
     for first in range(0, head_count, group):
         at = slice(first * rows, (first + group) * rows)
         score = dot_rows(query[at, :], keys[...])

time: 107 us -> 107 us (level)
  no operation moved by 1% of the time
where the time goes in v13:
time: 107 us
  waiting for transfers between devices  39.4 us (37%)
  starting transfers between devices  35 us (33%)
  Pallas kernels  26.6 us (25%)
  local copies, waits for them, and re-layouts  5.12 us (5%)
    pallas_call x3, Pallas kernels, run_expert(): pl.pallas_call(functools.partial(expert_kernel, experts), out_shape=[jax....  10.3 us
    all_to_all x1, waiting for transfers between devices, local(): lax.all_to_all(outgoing, 'ep', split_axis=0, concat_axis=0, tiled=True)  8.68 us
    all_to_all x1, starting transfers between devices, local(): lax.all_to_all(outgoing, 'ep', split_axis=0, concat_axis=0, tiled=True)  7.38 us
    ppermute x1, waiting for transfers between devices, local(): near = lax.ppermute(packet, both_axes, onward)  6.74 us
    pallas_call x1, Pallas kernels, local(): pl.pallas_call(functools.partial(moved_kernel, dims), out_shape=jax.Shape...  4.94 us
    ppermute x1, waiting for transfers between devices, local(): two_side_in = lax.ppermute(two_side_sum, 'ep', side_swap)  4.38 us
    unnamed x30, local copies, waits for them, and re-layouts  3.78 us
    ppermute x1, waiting for transfers between devices, local(): side_in = lax.ppermute(side_sum, 'ep', side_swap)  3.63 us
  transfers between devices with their start and end apart: 26, of which 17 were waited for; matrix products, arithmetic and copies ran while one was open for 2% of the time, Pallas kernels for 16%

profile of v13, /device:TPU:0, one launch (start us, length us, event | category | flops | bytes accessed | tf_op | source)
XLA Modules:
  0.0 107.2 jit_solution(6970389128527932663)
XLA Ops:
  0.0 2.8 %pick.1 = bf16[16,16,1152]{2,1,0:T(8,128)(2,1)} custom-call(s32[2,16]{1,0:T(2,128)} %bitcast.22, bf16[64,9216]{1,0:T(8,128)(2,1)} %cache.1), custom_call_target="tpu_custom_call" | custom-call | bytes 4194304 | tf_op jit(solution)/shard_map/pick/pallas_call | solution.py:308
  2.8 7.4 %all-to-all-start = ((bf16[16,16,1152]{2,1,0:T(8,128)(2,1)}), bf16[16,16,1152]{2,1,0:T(8,128)(2,1)S(1)}, u32[]{:S(2)}, u32[]{:S(2)}) async-start(bf16[16,16,1152]{2,1,0:T(8,128)(2,1)} %pick.1), calls=%async_computation | async-start | bytes 1179648 | tf_op jit(solution)/shard_map/all_to_all | solution.py:322
  12.4 2.7 %attend_resident.1 = (bf16[512,640]{1,0:T(8,128)(2,1)S(1)}, f32[512,640]{1,0:T(8,128)S(1)}) custom-call(bf16[64,1024]{1,0:T(8,128)(2,1)S(1)} %copy-done.8, bf16[64,512]{1,0:T(8,128)(2,1)S(1)} %copy-done.10, bf16[16,2304]{1,0:T(8,128)(2,1)S(1)} %copy-done.9, bf16[64,9216]{1,0:T(8,128)(2,1)S(1)} %copy-done.2, bf16[8,128,512]{2,1,0:T(8,128)(2,1)S(1)} %copy-done.7, ...), custom_call_target="tpu_custom_call" | custom-call | flops 1283457024 | bytes 8388608 | tf_op jit(solution)/shard_map/attend_resident/pallas_call | solution.py:347
  17.1 8.7 %all-to-all-done.moved_any = bf16[16,16,1152]{2,1,0:T(8,128)(2,1)S(1)} async-done(((bf16[16,16,1152]{2,1,0:T(8,128)(2,1)}), bf16[16,16,1152]{2,1,0:T(8,128)(2,1)S(1)}, u32[]{:S(2)}, u32[]{:S(2)}) %all-to-all-start) | async-done | bytes 589856 | tf_op jit(solution)/shard_map/all_to_all | solution.py:322
  26.6 4.9 %attend_moved.1.after_any.own_any = bf16[64,2048]{1,0:T(8,128)(2,1)} custom-call(bf16[16,16,1152]{2,1,0:T(8,128)(2,1)} %copy-done.11, bf16[512,640]{1,0:T(8,128)(2,1)} %copy-done.3, f32[64,512]{1,0:T(8,128)} %reshape.110.bias_any, f32[512,640]{1,0:T(8,128)} %copy-done.1, bf16[8,512,128]{2,1,0:T(8,128)(2,1)} %value_any.1, bf16[1024,2048]{1,0:T(8,128)(2,1)} %proj_any.1), custom_call_target="tpu_custom_call" | custom-call | flops 603979776 | bytes 10485760 | tf_op jit(solution)/shard_map/attend_moved/pallas_call | solution.py:358
  31.5 1.6 %collective-permute-start = (bf16[64,2048]{1,0:T(8,128)(2,1)}, bf16[64,2048]{1,0:T(8,128)(2,1)S(1)}, u32[]{:S(2)}, u32[]{:S(2)}) collective-permute-start(bf16[64,2048]{1,0:T(8,128)(2,1)} %attend_moved.1.after_any.own_any), channel_id=1, source_target_pairs={{0,16},{16,0},{1,17},{17,1},{2,18},{18,2},{3,19},{19,3},{4,20},{20... | collective-permute-start | bytes 786440 | tf_op jit(solution)/shard_map/ppermute | solution.py:377
  34.1 3.6 %load.1 = (bf16[704,2048]{1,0:T(8,128)(2,1)S(1)}, bf16[704,2048]{1,0:T(8,128)(2,1)S(1)}, bf16[704,2048]{1,0:T(8,128)(2,1)S(1)}) custom-call(bf16[64,2048]{1,0:T(8,128)(2,1)S(1)} %copy-done, bf16[704,2048]{1,0:T(8,128)(2,1)} %bitcast.18, bf16[704,2048]{1,0:T(8,128)(2,1)} %bitcast.19, bf16[704,2048]{1,0:T(8,128)(2,1)} %bitcast.20), custom_call_target="tpu_custom_call" | custom-call | bytes 12582912 | tf_op jit(solution)/shard_map/load/pallas_call | solution.py:380
  37.7 2.3 %collective-permute-done.refs_0_ = bf16[64,2048]{1,0:T(8,128)(2,1)S(1)} collective-permute-done((bf16[64,2048]{1,0:T(8,128)(2,1)}, bf16[64,2048]{1,0:T(8,128)(2,1)S(1)}, u32[]{:S(2)}, u32[]{:S(2)}) %collective-permute-start) | collective-permute-done | bytes 262176 | tf_op jit(solution)/shard_map/ppermute | solution.py:377
  40.7 2.0 %collective-permute-start.2 = (bf16[64,2176]{1,0:T(8,128)(2,1)S(1)}, bf16[64,2176]{1,0:T(8,128)(2,1)S(1)}, u32[]{:S(2)}, u32[]{:S(2)}) collective-permute-start(bf16[64,2176]{1,0:T(8,128)(2,1)S(1)} %get-tuple-element.33.after_any.refs_0_), channel_id=1, source_target_pairs={{0,8},{1,9},{2,10},{3,11},{4,0},{5,1},{6,2},{7,3},{8,12},{9,13},{1... | collective-permute-start | bytes 835592 | tf_op jit(solution)/shard_map/ppermute | solution.py:456
  42.7 6.7 %collective-permute-done.2.refs_2_ = bf16[64,2176]{1,0:T(8,128)(2,1)S(1)} collective-permute-done((bf16[64,2176]{1,0:T(8,128)(2,1)S(1)}, bf16[64,2176]{1,0:T(8,128)(2,1)S(1)}, u32[]{:S(2)}, u32[]{:S(2)}) %collective-permute-start.2) | collective-permute-done | bytes 278560 | tf_op jit(solution)/shard_map/ppermute | solution.py:456
  49.6 2.3 %collective-permute-start.7 = (bf16[64,2176]{1,0:T(8,128)(2,1)S(1)}, bf16[64,2176]{1,0:T(8,128)(2,1)S(1)}, u32[]{:S(2)}, u32[]{:S(2)}) collective-permute-start(bf16[64,2176]{1,0:T(8,128)(2,1)S(1)} %collective-permute-done.2.refs_2_), channel_id=1, source_target_pairs={{0,8},{1,9},{2,10},{3,11},{4,0},{5,1},{6,2},{7,3},{8,12},{9,13},{1... | collective-permute-start | bytes 835592 | tf_op jit(solution)/shard_map/ppermute | solution.py:458
  53.4 1.5 %collective-permute-start.5 = (bf16[64,2176]{1,0:T(8,128)(2,1)S(1)}, bf16[64,2176]{1,0:T(8,128)(2,1)S(1)}, u32[]{:S(2)}, u32[]{:S(2)}) collective-permute-start(bf16[64,2176]{1,0:T(8,128)(2,1)S(1)} %collective-permute-done.2.refs_2_), channel_id=1, source_target_pairs={{0,16},{16,0},{1,17},{17,1},{2,18},{18,2},{3,19},{19,3},{4,20},{20... | collective-permute-start | bytes 835592 | tf_op jit(solution)/shard_map/ppermute | solution.py:460
  54.9 3.8 %expert.3 = (bf16[192,2048]{1,0:T(8,128)(2,1)S(1)}, bf16[192,2048]{1,0:T(8,128)(2,1)S(1)}) custom-call(bf16[64,2176]{1,0:T(8,128)(2,1)S(1)} %get-tuple-element.33.after_any.refs_0_, bf16[192,2176]{1,0:T(8,128)(2,1)S(1)} %pack.3.here_ref, bf16[192,2176]{1,0:T(8,128)(2,1)S(1)} %collective-permute-done.3.across_ref, ...), custom_call_target="tpu_custom_call" | custom-call | flops 3321888768 | bytes 12582912 | tf_op jit(solution)/shard_map/expert/pallas_call | solution.py:422
  64.1 3.8 %expert.4 = (bf16[192,2048]{1,0:T(8,128)(2,1)S(1)}, bf16[192,2048]{1,0:T(8,128)(2,1)S(1)}) custom-call(bf16[64,2176]{1,0:T(8,128)(2,1)S(1)} %get-tuple-element.33.after_any.refs_0_, bf16[192,2176]{1,0:T(8,128)(2,1)S(1)} %pack.4.here_ref, bf16[192,2176]{1,0:T(8,128)(2,1)S(1)} %collective-permute-done.8.across_ref, ...), custom_call_target="tpu_custom_call" | custom-call | flops 3321888768 | bytes 12582912 | tf_op jit(solution)/shard_map/expert/pallas_call | solution.py:422
  68.0 2.9 %collective-permute-done.11.refs_1_ = bf16[64,2176]{1,0:T(8,128)(2,1)S(1)} collective-permute-done((bf16[64,2176]{1,0:T(8,128)(2,1)S(1)}, bf16[64,2176]{1,0:T(8,128)(2,1)S(1)}, u32[]{:S(2)}, u32[]{:S(2)}) %collective-permute-start.11) | collective-permute-done | bytes 278560 | tf_op jit(solution)/shard_map/ppermute | solution.py:461
  73.5 2.6 %expert.5 = (bf16[128,2048]{1,0:T(8,128)(2,1)S(1)}, bf16[64,2048]{1,0:T(8,128)(2,1)S(1)}, bf16[64,2048]{1,0:T(8,128)(2,1)S(1)}) custom-call(bf16[64,2048]{1,0:T(8,128)(2,1)S(1)} %get-tuple-element.42.after_any, bf16[128,2176]{1,0:T(8,128)(2,1)S(1)} %pack.5.here_ref, bf16[128,2176]{1,0:T(8,128)(2,1)S(1)} %collective-permute-done.12.across_ref, ...), custom_call_target="tpu_custom_call" | custom-call | flops 2214592512 | bytes 12582912 | tf_op jit(solution)/shard_map/expert/pallas_call | solution.py:422
  76.7 3.6 %collective-permute-done.13.refs_0_.side_ref = bf16[64,2048]{1,0:T(8,128)(2,1)S(1)} collective-permute-done((bf16[64,2048]{1,0:T(8,128)(2,1)S(1)}, bf16[64,2048]{1,0:T(8,128)(2,1)S(1)}, u32[]{:S(2)}, u32[]{:S(2)}) %collective-permute-start.13) | collective-permute-done | bytes 262176 | tf_op jit(solution)/shard_map/ppermute | solution.py:466
  83.6 4.4 %collective-permute-done.18.refs_0_ = bf16[64,2048]{1,0:T(8,128)(2,1)S(1)} collective-permute-done((bf16[64,2048]{1,0:T(8,128)(2,1)S(1)}, bf16[64,2048]{1,0:T(8,128)(2,1)S(1)}, u32[]{:S(2)}, u32[]{:S(2)}) %collective-permute-start.18) | collective-permute-done | bytes 262176 | tf_op jit(solution)/shard_map/ppermute | solution.py:471
  90.6 2.1 %collective-permute-start.20 = (bf16[64,2048]{1,0:T(8,128)(2,1)S(1)}, bf16[64,2048]{1,0:T(8,128)(2,1)S(1)}, u32[]{:S(2)}, u32[]{:S(2)}) collective-permute-start(bf16[64,2048]{1,0:T(8,128)(2,1)S(1)} %join.11), channel_id=1, source_target_pairs={{0,16},{16,0},{1,17},{17,1},{2,18},{18,2},{3,19},{19,3},{4,20},{20... | collective-permute-start | bytes 786440 | tf_op jit(solution)/shard_map/ppermute | solution.py:475
  92.7 2.7 %collective-permute-done.19.refs_2_ = bf16[64,2048]{1,0:T(8,128)(2,1)S(1)} collective-permute-done((bf16[64,2048]{1,0:T(8,128)(2,1)S(1)}, bf16[64,2048]{1,0:T(8,128)(2,1)S(1)}, u32[]{:S(2)}, u32[]{:S(2)}) %collective-permute-start.19) | collective-permute-done | bytes 262176 | tf_op jit(solution)/shard_map/ppermute | solution.py:477
  97.2 2.1 %collective-permute-start.21 = (bf16[64,1024]{1,0:T(8,128)(2,1)S(1)}, bf16[64,1024]{1,0:T(8,128)(2,1)S(1)}, u32[]{:S(2)}, u32[]{:S(2)}) collective-permute-start(bf16[64,1024]{1,0:T(8,128)(2,1)S(1)} %get-tuple-element.53), channel_id=1, source_target_pairs={{0,20},{1,21},{2,22},{3,23},{4,28},{5,29},{6,30},{7,31},{8,16},{9,... | collective-permute-start | bytes 393224 | tf_op jit(solution)/shard_map/ppermute | solution.py:505
  99.3 2.1 %collective-permute-start.22 = (bf16[64,1024]{1,0:T(8,128)(2,1)S(1)}, bf16[64,1024]{1,0:T(8,128)(2,1)S(1)}, u32[]{:S(2)}, u32[]{:S(2)}) collective-permute-start(bf16[64,1024]{1,0:T(8,128)(2,1)S(1)} %get-tuple-element.49.after_any), channel_id=1, source_target_pairs={{0,4},{1,5},{2,6},{3,7},{4,12},{5,13},{6,14},{7,15},{8,0},{9,1},{1... | collective-permute-start | bytes 393224 | tf_op jit(solution)/shard_map/ppermute | solution.py:504
  101.6 1.9 %collective-permute-start.23 = (bf16[32,1024]{1,0:T(8,128)(2,1)S(1)}, bf16[32,1024]{1,0:T(8,128)(2,1)S(1)}, u32[]{:S(2)}, u32[]{:S(2)}) collective-permute-start(bf16[32,1024]{1,0:T(8,128)(2,1)S(1)} %get-tuple-element.56), channel_id=1, source_target_pairs={{0,16},{16,0},{1,17},{17,1},{2,18},{18,2},{3,19},{19,3},{4,20},{20... | collective-permute-start | bytes 196616 | tf_op jit(solution)/shard_map/ppermute | solution.py:502
  103.5 2.2 %collective-permute-done.24.lower_ref = bf16[32,1024]{1,0:T(8,128)(2,1)S(1)} collective-permute-done((bf16[32,1024]{1,0:T(8,128)(2,1)S(1)}, bf16[32,1024]{1,0:T(8,128)(2,1)S(1)}, u32[]{:S(2)}, u32[]{:S(2)}) %collective-permute-start.24) | collective-permute-done | bytes 65568 | tf_op jit(solution)/shard_map/ppermute | solution.py:502
  (103 shorter events, 25.9 us)
Async XLA Ops:
  2.8 22.9 %all-to-all-start = ((bf16[16,16,1152]{2,1,0:T(8,128)(2,1)}), bf16[16,16,1152]{2,1,0:T(8,128)(2,1)S(1)}, u32[]{:S(2)}, u32[]{:S(2)}) async-start(bf16[16,16,1152]{2,1,0:T(8,128)(2,1)} %pick.1), calls=%async_computation | async-start | bytes 1179648 | tf_op jit(solution)/shard_map/all_to_all | solution.py:322
  31.5 8.5 %collective-permute-start = (bf16[64,2048]{1,0:T(8,128)(2,1)}, bf16[64,2048]{1,0:T(8,128)(2,1)S(1)}, u32[]{:S(2)}, u32[]{:S(2)}) collective-permute-start(bf16[64,2048]{1,0:T(8,128)(2,1)} %attend_moved.1.after_any.own_any), channel_id=1, source_target_pairs={{0,16},{16,0},{1,17},{17,1},{2,18},{18,2},{3,19},{19,3},{4,20},{20... | collective-permute-start | bytes 786440 | tf_op jit(solution)/shard_map/ppermute | solution.py:377
  40.7 8.8 %collective-permute-start.2 = (bf16[64,2176]{1,0:T(8,128)(2,1)S(1)}, bf16[64,2176]{1,0:T(8,128)(2,1)S(1)}, u32[]{:S(2)}, u32[]{:S(2)}) collective-permute-start(bf16[64,2176]{1,0:T(8,128)(2,1)S(1)} %get-tuple-element.33.after_any.refs_0_), channel_id=1, source_target_pairs={{0,8},{1,9},{2,10},{3,11},{4,0},{5,1},{6,2},{7,3},{8,12},{9,13},{1... | collective-permute-start | bytes 835592 | tf_op jit(solution)/shard_map/ppermute | solution.py:456
  42.7 6.8 %collective-permute-start.1 = (bf16[64,2176]{1,0:T(8,128)(2,1)S(1)}, bf16[64,2176]{1,0:T(8,128)(2,1)S(1)}, u32[]{:S(2)}, u32[]{:S(2)}) collective-permute-start(bf16[64,2176]{1,0:T(8,128)(2,1)S(1)} %get-tuple-element.33.after_any.refs_0_), channel_id=1, source_target_pairs={{0,2},{1,3},{2,0},{3,1},{4,6},{5,7},{6,4},{7,5},{8,10},{9,11},{10,... | collective-permute-start | bytes 835592 | tf_op jit(solution)/shard_map/ppermute | solution.py:457
  49.6 5.3 %collective-permute-start.3 = (bf16[192,2176]{1,0:T(8,128)(2,1)S(1)}, bf16[192,2176]{1,0:T(8,128)(2,1)S(1)}, u32[]{:S(2)}, u32[]{:S(2)}) collective-permute-start(bf16[192,2176]{1,0:T(8,128)(2,1)S(1)} %pack.3.here_ref), channel_id=1, source_target_pairs={{0,1},{1,0},{2,3},{3,2},{4,5},{5,4},{6,7},{7,6},{8,9},{9,8},{10,11... | collective-permute-start | bytes 2506760 | tf_op jit(solution)/shard_map/ppermute | solution.py:421
  49.6 9.9 %collective-permute-start.7 = (bf16[64,2176]{1,0:T(8,128)(2,1)S(1)}, bf16[64,2176]{1,0:T(8,128)(2,1)S(1)}, u32[]{:S(2)}, u32[]{:S(2)}) collective-permute-start(bf16[64,2176]{1,0:T(8,128)(2,1)S(1)} %collective-permute-done.2.refs_2_), channel_id=1, source_target_pairs={{0,8},{1,9},{2,10},{3,11},{4,0},{5,1},{6,2},{7,3},{8,12},{9,13},{1... | collective-permute-start | bytes 835592 | tf_op jit(solution)/shard_map/ppermute | solution.py:458
  51.9 8.5 %collective-permute-start.6 = (bf16[64,2176]{1,0:T(8,128)(2,1)S(1)}, bf16[64,2176]{1,0:T(8,128)(2,1)S(1)}, u32[]{:S(2)}, u32[]{:S(2)}) collective-permute-start(bf16[64,2176]{1,0:T(8,128)(2,1)S(1)} %collective-permute-done.2.refs_2_), channel_id=1, source_target_pairs={{0,2},{1,3},{2,0},{3,1},{4,6},{5,7},{6,4},{7,5},{8,10},{9,11},{10,... | collective-permute-start | bytes 835592 | tf_op jit(solution)/shard_map/ppermute | solution.py:459
  53.4 8.3 %collective-permute-start.5 = (bf16[64,2176]{1,0:T(8,128)(2,1)S(1)}, bf16[64,2176]{1,0:T(8,128)(2,1)S(1)}, u32[]{:S(2)}, u32[]{:S(2)}) collective-permute-start(bf16[64,2176]{1,0:T(8,128)(2,1)S(1)} %collective-permute-done.2.refs_2_), channel_id=1, source_target_pairs={{0,16},{16,0},{1,17},{17,1},{2,18},{18,2},{3,19},{19,3},{4,20},{20... | collective-permute-start | bytes 835592 | tf_op jit(solution)/shard_map/ppermute | solution.py:460
  61.8 9.1 %collective-permute-start.11 = (bf16[64,2176]{1,0:T(8,128)(2,1)S(1)}, bf16[64,2176]{1,0:T(8,128)(2,1)S(1)}, u32[]{:S(2)}, u32[]{:S(2)}) collective-permute-start(bf16[64,2176]{1,0:T(8,128)(2,1)S(1)} %collective-permute-done.7.refs_2_), channel_id=1, source_target_pairs={{0,2},{1,3},{2,0},{3,1},{4,6},{5,7},{6,4},{7,5},{8,10},{9,11},{10,... | collective-permute-start | bytes 835592 | tf_op jit(solution)/shard_map/ppermute | solution.py:461
  62.4 8.7 %collective-permute-start.10 = (bf16[64,2176]{1,0:T(8,128)(2,1)S(1)}, bf16[64,2176]{1,0:T(8,128)(2,1)S(1)}, u32[]{:S(2)}, u32[]{:S(2)}) collective-permute-start(bf16[64,2176]{1,0:T(8,128)(2,1)S(1)} %collective-permute-done.6.refs_1_), channel_id=1, source_target_pairs={{0,16},{16,0},{1,17},{17,1},{2,18},{18,2},{3,19},{19,3},{4,20},{20... | collective-permute-start | bytes 835592 | tf_op jit(solution)/shard_map/ppermute | solution.py:462
  64.0 7.8 %collective-permute-start.4 = (bf16[192,2048]{1,0:T(8,128)(2,1)S(1)}, bf16[192,2048]{1,0:T(8,128)(2,1)S(1)}, u32[]{:S(2)}, u32[]{:S(2)}) collective-permute-start(bf16[192,2048]{1,0:T(8,128)(2,1)S(1)} %get-tuple-element.37), channel_id=1, source_target_pairs={{0,1},{1,0},{2,3},{3,2},{4,5},{5,4},{6,7},{7,6},{8,9},{9,8},{10,11... | collective-permute-start | bytes 2359304 | tf_op jit(solution)/shard_map/ppermute | solution.py:432
  71.3 12.2 %collective-permute-start.9 = (bf16[192,2048]{1,0:T(8,128)(2,1)S(1)}, bf16[192,2048]{1,0:T(8,128)(2,1)S(1)}, u32[]{:S(2)}, u32[]{:S(2)}) collective-permute-start(bf16[192,2048]{1,0:T(8,128)(2,1)S(1)} %get-tuple-element.40), channel_id=1, source_target_pairs={{0,1},{1,0},{2,3},{3,2},{4,5},{5,4},{6,7},{7,6},{8,9},{9,8},{10,11... | collective-permute-start | bytes 2359304 | tf_op jit(solution)/shard_map/ppermute | solution.py:432
  72.0 8.4 %collective-permute-start.13 = (bf16[64,2048]{1,0:T(8,128)(2,1)S(1)}, bf16[64,2048]{1,0:T(8,128)(2,1)S(1)}, u32[]{:S(2)}, u32[]{:S(2)}) collective-permute-start(bf16[64,2048]{1,0:T(8,128)(2,1)S(1)} %get-tuple-element.42.after_any), channel_id=1, source_target_pairs={{0,2},{1,3},{2,0},{3,1},{4,6},{5,7},{6,4},{7,5},{8,10},{9,11},{10,... | collective-permute-start | bytes 786440 | tf_op jit(solution)/shard_map/ppermute | solution.py:466
  76.1 4.2 %collective-permute-start.14 = (bf16[64,2048]{1,0:T(8,128)(2,1)S(1)}, bf16[64,2048]{1,0:T(8,128)(2,1)S(1)}, u32[]{:S(2)}, u32[]{:S(2)}) collective-permute-start(bf16[64,2048]{1,0:T(8,128)(2,1)S(1)} %get-tuple-element.44), channel_id=1, source_target_pairs={{0,1},{1,0},{2,3},{3,2},{4,5},{5,4},{6,7},{7,6},{8,9},{9,8},{10,11... | collective-permute-start | bytes 786440 | tf_op jit(solution)/shard_map/ppermute | solution.py:432
  76.2 4.1 %collective-permute-start.15 = (bf16[64,2048]{1,0:T(8,128)(2,1)S(1)}, bf16[64,2048]{1,0:T(8,128)(2,1)S(1)}, u32[]{:S(2)}, u32[]{:S(2)}) collective-permute-start(bf16[64,2048]{1,0:T(8,128)(2,1)S(1)} %get-tuple-element.45), channel_id=1, source_target_pairs={{0,1},{1,0},{2,3},{3,2},{4,5},{5,4},{6,7},{7,6},{8,9},{9,8},{10,11... | collective-permute-start | bytes 786440 | tf_op jit(solution)/shard_map/ppermute | solution.py:432
  80.5 7.5 %collective-permute-start.18 = (bf16[64,2048]{1,0:T(8,128)(2,1)S(1)}, bf16[64,2048]{1,0:T(8,128)(2,1)S(1)}, u32[]{:S(2)}, u32[]{:S(2)}) collective-permute-start(bf16[64,2048]{1,0:T(8,128)(2,1)S(1)} %get-tuple-element.48), channel_id=1, source_target_pairs={{0,2},{1,3},{2,0},{3,1},{4,6},{5,7},{6,4},{7,5},{8,10},{9,11},{10,... | collective-permute-start | bytes 786440 | tf_op jit(solution)/shard_map/ppermute | solution.py:471
  82.0 7.2 %collective-permute-start.16 = (bf16[64,2048]{1,0:T(8,128)(2,1)S(1)}, bf16[64,2048]{1,0:T(8,128)(2,1)S(1)}, u32[]{:S(2)}, u32[]{:S(2)}) collective-permute-start(bf16[64,2048]{1,0:T(8,128)(2,1)S(1)} %get-tuple-element.46), channel_id=1, source_target_pairs={{0,16},{16,0},{1,17},{17,1},{2,18},{18,2},{3,19},{19,3},{4,20},{20... | collective-permute-start | bytes 786440 | tf_op jit(solution)/shard_map/ppermute | solution.py:470
  88.0 7.5 %collective-permute-start.19 = (bf16[64,2048]{1,0:T(8,128)(2,1)S(1)}, bf16[64,2048]{1,0:T(8,128)(2,1)S(1)}, u32[]{:S(2)}, u32[]{:S(2)}) collective-permute-start(bf16[64,2048]{1,0:T(8,128)(2,1)S(1)} %join.10), channel_id=1, source_target_pairs={{0,4},{1,5},{2,6},{3,7},{4,12},{5,13},{6,14},{7,15},{8,0},{9,1},{1... | collective-permute-start | bytes 786440 | tf_op jit(solution)/shard_map/ppermute | solution.py:477
  89.2 6.4 %collective-permute-start.17 = (bf16[64,2048]{1,0:T(8,128)(2,1)S(1)}, bf16[64,2048]{1,0:T(8,128)(2,1)S(1)}, u32[]{:S(2)}, u32[]{:S(2)}) collective-permute-start(bf16[64,2048]{1,0:T(8,128)(2,1)S(1)} %join.9), channel_id=1, source_target_pairs={{0,2},{1,3},{2,0},{3,1},{4,6},{5,7},{6,4},{7,5},{8,10},{9,11},{10,... | collective-permute-start | bytes 786440 | tf_op jit(solution)/shard_map/ppermute | solution.py:476
  90.6 6.5 %collective-permute-start.20 = (bf16[64,2048]{1,0:T(8,128)(2,1)S(1)}, bf16[64,2048]{1,0:T(8,128)(2,1)S(1)}, u32[]{:S(2)}, u32[]{:S(2)}) collective-permute-start(bf16[64,2048]{1,0:T(8,128)(2,1)S(1)} %join.11), channel_id=1, source_target_pairs={{0,16},{16,0},{1,17},{17,1},{2,18},{18,2},{3,19},{19,3},{4,20},{20... | collective-permute-start | bytes 786440 | tf_op jit(solution)/shard_map/ppermute | solution.py:475
  97.2 9.3 %collective-permute-start.21 = (bf16[64,1024]{1,0:T(8,128)(2,1)S(1)}, bf16[64,1024]{1,0:T(8,128)(2,1)S(1)}, u32[]{:S(2)}, u32[]{:S(2)}) collective-permute-start(bf16[64,1024]{1,0:T(8,128)(2,1)S(1)} %get-tuple-element.53), channel_id=1, source_target_pairs={{0,20},{1,21},{2,22},{3,23},{4,28},{5,29},{6,30},{7,31},{8,16},{9,... | collective-permute-start | bytes 393224 | tf_op jit(solution)/shard_map/ppermute | solution.py:505
  99.3 7.2 %collective-permute-start.22 = (bf16[64,1024]{1,0:T(8,128)(2,1)S(1)}, bf16[64,1024]{1,0:T(8,128)(2,1)S(1)}, u32[]{:S(2)}, u32[]{:S(2)}) collective-permute-start(bf16[64,1024]{1,0:T(8,128)(2,1)S(1)} %get-tuple-element.49.after_any), channel_id=1, source_target_pairs={{0,4},{1,5},{2,6},{3,7},{4,12},{5,13},{6,14},{7,15},{8,0},{9,1},{1... | collective-permute-start | bytes 393224 | tf_op jit(solution)/shard_map/ppermute | solution.py:504
  101.5 4.3 %collective-permute-start.24 = (bf16[32,1024]{1,0:T(8,128)(2,1)S(1)}, bf16[32,1024]{1,0:T(8,128)(2,1)S(1)}, u32[]{:S(2)}, u32[]{:S(2)}) collective-permute-start(bf16[32,1024]{1,0:T(8,128)(2,1)S(1)} %get-tuple-element.55), channel_id=1, source_target_pairs={{0,16},{16,0},{1,17},{17,1},{2,18},{18,2},{3,19},{19,3},{4,20},{20... | collective-permute-start | bytes 196616 | tf_op jit(solution)/shard_map/ppermute | solution.py:502
  101.6 4.9 %collective-permute-start.23 = (bf16[32,1024]{1,0:T(8,128)(2,1)S(1)}, bf16[32,1024]{1,0:T(8,128)(2,1)S(1)}, u32[]{:S(2)}, u32[]{:S(2)}) collective-permute-start(bf16[32,1024]{1,0:T(8,128)(2,1)S(1)} %get-tuple-element.56), channel_id=1, source_target_pairs={{0,16},{16,0},{1,17},{17,1},{2,18},{18,2},{3,19},{19,3},{4,20},{20... | collective-permute-start | bytes 196616 | tf_op jit(solution)/shard_map/ppermute | solution.py:502
  (17 other events, 115.3 us)
